TPU v7x, 32 devices: a whole 2x2x4 slice. The times are simulated.
32 devices in a mesh: groups: 2 (over y), lat: 4 (over z), lon: 2 (over x), rep: 2 (over core).
Axes of the slice: x: 2, y: 2, z: 4, core: 2. Of those that a mesh axis runs over, the one named last changes fastest.
Arguments:
- grid_in: bfloat16 [32768, 227], P(('groups', 'lat', 'lon')), parts along dimension 0, may hold values from -6 to 6
- w_embed: bfloat16 [227, 512], P(None, 'rep'), may hold values from -0.375 to 0.375
- interp_tiles: bfloat16 [256, 128, 128], P(('groups', 'lat', 'lon')), parts along dimension 0, may hold values from -0.5 to 0.5
- route_device: int32 [256, 1], P(('groups', 'lat', 'lon')), parts along dimension 0, may hold values from 0 to 7, as said below
- route_slot: int32 [256], P(('groups', 'lat', 'lon')), parts along dimension 0, may hold values from 0 to 3
- mesh_embed: bfloat16 [8192, 512], P(('groups', 'lat', 'lon'), 'rep'), parts along dimension 0, may hold values from -36 to 36
- w_up: bfloat16 [512, 512], P(None, 'rep'), may hold values from -0.25 to 0.25
- w_down: bfloat16 [512, 512], P('rep'), may hold values from -0.25 to 0.25
- w_out: bfloat16 [512, 227], P('rep'), may hold values from -0.25 to 0.25
- cotangent: bfloat16 [32768, 227], P(('groups', 'lat', 'lon')), parts along dimension 0, may hold values from -6 to 6
Outputs:
- grid_out: bfloat16 [32768, 227], P(('groups', 'lat', 'lon', 'rep')), parts along dimension 0
- grad_out: float32 [1024, 227], P(('groups', 'rep')), parts along dimension 0
- grad_up: float32 [1024, 512], P('groups', 'rep'), parts along dimension 0
- grad_down: float32 [1024, 512], P(('groups', 'rep')), parts along dimension 0
- grad_mesh: float32 [8192, 512], P(('groups', 'lat', 'lon'), 'rep'), parts along dimension 0
There are 2 independent parts, one for each index of `groups`. A program takes and returns all parts, laid end to end along the dimension named above; an argument that names none is the same for every part. Nothing has to cross between parts.
Inputs may be any that keep to these rules, and one draw needn't show every extreme that they name: `route_device`: grid blocks of a band and sector name only patches of the same band or an adjacent band, in the same sector or the next sector eastward (cyclically). Among the 16 blocks of one band and sector at most 4 name the same patch, and their own patch is named by exactly 4 of them.
All inputs are finite; a program needn't handle non-finite values.
Results may differ from a plain program's by a relative error of at most 0.0088.
Values may be sent and summed in bfloat16 or wider, within the bound.
No kernel may reach another device: no remote copies, remote signals or barrier semaphores. Data moves between devices by JAX's collectives and lax.ppermute only.
A program may use at most 64 MiB of HBM per device.

v0:
```python
import jax
import jax.numpy as jnp
from jax import lax
from jax.sharding import PartitionSpec as P


def passed_along(value, axis, steps):
    count = lax.axis_size(axis)
    pairs = [(source, (source + steps) % count) for source in range(count)]
    return lax.ppermute(value, axis, pairs)


def with_halo(x, sides, width):
    for axis, dim in sides:
        devices, length = (lax.axis_size(axis), x.shape[dim])
        up = [(i, (i + 1) % devices) for i in range(devices - 1)]
        down = [(j, i) for i, j in up]
        last = lax.slice_in_dim(x, length - width, length, axis=dim)
        initial = lax.slice_in_dim(x, 0, width, axis=dim)
        before = lax.ppermute(last, axis, up)
        after = lax.ppermute(initial, axis, down)
        x = jnp.concatenate([before, x, after], axis=dim)
    return x


def sigmoid_linear(values):
    return values * jax.nn.sigmoid(values)


def layer_norm(values):
    centered = values - jnp.mean(values, axis=-1, keepdims=True)
    inverse_std = lax.rsqrt(jnp.mean(centered * centered, axis=-1, keepdims=True) + 1e-05)
    return (centered * inverse_std, inverse_std)


def contract_rows(left, right):
    return lax.dot_general(
        left, right, (((0,), (0,)), ((), ())), preferred_element_type=jnp.float32
    )


def contract_last(left, right):
    return lax.dot_general(
        left, right, (((1,), (1,)), ((), ())), preferred_element_type=jnp.float32
    )


def deliver_sums(packed):
    moved = passed_along(packed[:, 1], "lon", 1)
    column = packed[:, 0] + moved
    padded = with_halo(jnp.stack([column[0], column[2]]), (("lat", 0),), 1)
    total = column[1] + padded[0] + padded[3]
    return total


def fetch_neighbours(mesh_out):
    east = passed_along(mesh_out, "lon", -1)
    padded = with_halo(jnp.stack([mesh_out, east])[None], (("lat", 0),), 1)
    return padded


def per_device(
    grid_in,
    w_embed,
    interp_tiles,
    route_device,
    route_slot,
    mesh_embed,
    w_up,
    w_down,
    w_out,
    cotangent,
):
    lon_count = lax.axis_size("lon")
    blocks = interp_tiles.shape[0]
    tile_rows = interp_tiles.shape[1]
    grid_rows = grid_in.shape[0]
    local_width = w_embed.shape[1]
    mesh_blocks = mesh_embed.shape[0] // tile_rows
    node_rows = mesh_embed.shape[0]
    table_rows = 6 * mesh_blocks
    target = route_device[:, 0]
    band_index = target // lon_count - lax.axis_index("lat") + 1
    sector_index = (target % lon_count - lax.axis_index("lon") + lon_count) % lon_count
    position = (band_index * 2 + sector_index) * mesh_blocks + route_slot
    selector = (position[None, :] == jnp.arange(table_rows, dtype=jnp.int32)[:, None]).astype(
        jnp.bfloat16
    )
    preact = jnp.dot(grid_in, w_embed, preferred_element_type=jnp.float32)
    hidden = sigmoid_linear(preact).astype(jnp.bfloat16)
    messages = jnp.einsum(
        "bgn,bgl->bnl",
        interp_tiles,
        hidden.reshape(blocks, tile_rows, local_width),
        preferred_element_type=jnp.float32,
    ).astype(jnp.bfloat16)
    packed = jnp.dot(
        selector,
        messages.reshape(blocks, tile_rows * local_width),
        preferred_element_type=jnp.float32,
    ).reshape(3, 2, node_rows, local_width)
    node_sum = deliver_sums(packed)
    node_state = (mesh_embed.astype(jnp.float32) + node_sum).astype(jnp.bfloat16)
    state_full = lax.all_gather(node_state, "rep", axis=1, tiled=True)
    norm_exact, inverse_std = layer_norm(state_full.astype(jnp.float32))
    normed = norm_exact.astype(jnp.bfloat16)
    hidden_pre = jnp.dot(normed, w_up, preferred_element_type=jnp.float32)
    hidden_act = sigmoid_linear(hidden_pre).astype(jnp.bfloat16)
    partial_value = jnp.dot(hidden_act, w_down, preferred_element_type=jnp.float32)
    update = lax.psum_scatter(partial_value, "rep", scatter_dimension=1, tiled=True)
    mesh_out = (node_state.astype(jnp.float32) + update).astype(jnp.bfloat16)
    neighbours = fetch_neighbours(mesh_out).reshape(table_rows, tile_rows, local_width)
    mesh_picked = jnp.take(neighbours, position, axis=0)
    decoded = jnp.einsum(
        "bgn,bnl->bgl", interp_tiles, mesh_picked, preferred_element_type=jnp.float32
    ).reshape(grid_rows, local_width)
    grid_latent = (hidden.astype(jnp.float32) + decoded).astype(jnp.bfloat16)
    out_terms = jnp.dot(grid_latent, w_out, preferred_element_type=jnp.float32)
    grid_out = lax.psum_scatter(out_terms, "rep", scatter_dimension=0, tiled=True).astype(
        jnp.bfloat16
    )
    grid_grad = contract_last(cotangent, w_out).astype(jnp.bfloat16)
    grad_out = contract_rows(grid_latent, cotangent)
    back_msgs = jnp.einsum(
        "bgn,bgl->bnl",
        interp_tiles,
        grid_grad.reshape(blocks, tile_rows, local_width),
        preferred_element_type=jnp.float32,
    ).astype(jnp.bfloat16)
    grad_packed = jnp.dot(
        selector,
        back_msgs.reshape(blocks, tile_rows * local_width),
        preferred_element_type=jnp.float32,
    ).reshape(3, 2, node_rows, local_width)
    node_grad = deliver_sums(grad_packed).astype(jnp.bfloat16)
    grad_full = lax.all_gather(node_grad, "rep", axis=1, tiled=True)
    grad_down = contract_rows(hidden_act, grad_full)
    act_grad = contract_last(grad_full, w_down)
    squash = jax.nn.sigmoid(hidden_pre)
    pre_grad = (act_grad * squash * (1.0 + hidden_pre * (1.0 - squash))).astype(jnp.bfloat16)
    grad_up = contract_rows(normed, pre_grad)
    norm_grad = lax.psum(contract_last(pre_grad, w_up).astype(jnp.bfloat16), "rep").astype(
        jnp.float32
    )
    centered_grad = (
        norm_grad
        - jnp.mean(norm_grad, axis=-1, keepdims=True)
        - norm_exact * jnp.mean(norm_grad * norm_exact, axis=-1, keepdims=True)
    )
    state_grad = lax.dynamic_slice_in_dim(
        inverse_std * centered_grad, lax.axis_index("rep") * local_width, local_width, 1
    )
    grad_mesh = node_grad.astype(jnp.float32) + state_grad
    grad_out, grad_up, grad_down = lax.psum((grad_out, grad_up, grad_down), ("lat", "lon"))
    return (grid_out, grad_out, grad_up, grad_down, grad_mesh)


def solution(mesh):
    placed = (
        P(("groups", "lat", "lon"), None),
        P(None, "rep"),
        P(("groups", "lat", "lon"), None, None),
        P(("groups", "lat", "lon"), None),
        P(("groups", "lat", "lon")),
        P(("groups", "lat", "lon"), "rep"),
        P(None, "rep"),
        P("rep", None),
        P("rep", None),
        P(("groups", "lat", "lon"), None),
    )
    return jax.shard_map(
        per_device,
        mesh=mesh,
        in_specs=placed,
        out_specs=(
            P(("groups", "lat", "lon", "rep"), None),
            P(("groups", "rep"), None),
            P("groups", "rep"),
            P(("groups", "rep"), None),
            P(("groups", "lat", "lon"), "rep"),
        ),
        check_vma=False,
    )
```

profile of v0, /device:TPU:0, one launch (start us, length us, event | category | flops | bytes accessed | tf_op | source)
XLA Modules:
  0.0 280.6 jit_solution(10803819497223891228)
XLA Ops:
  7.2 2.1 multiply_convert_fusion
  12.8 2.2 fusion.31
  15.1 4.6 %reshape.67 = f32[3,2,512,256]{3,2,1,0:T(8,128)} reshape(f32[24,32768]{1,0:T(8,128)} %fusion.31) | data formatting | bytes 6291456 | tf_op jit(solution)/shard_map/reshape | solution.py:101
  19.6 2.7 slice_bitcast_fusion.2
  22.4 2.9 %collective-permute-start = (f32[3,512,256]{2,1,0:T(8,128)}, f32[3,512,256]{2,1,0:T(8,128)}, u32[]{:S(2)}, u32[]{:S(2)}) collective-permute-start(f32[3,512,256]{2,1,0:T(8,128)} %slice_bitcast_fusion.2), channel_id=1, source_target_pairs={{0,2},{2,0},{1,3},{3,1},{4,6},{6,4},{5,7},{7,5},{8,10},{10,8},{9,1... | collective-permute-start | bytes 4718600 | tf_op jit(solution)/shard_map/ppermute | solution.py:10
  28.0 31.9 %collective-permute-done = f32[3,512,256]{2,1,0:T(8,128)} collective-permute-done((f32[3,512,256]{2,1,0:T(8,128)}, f32[3,512,256]{2,1,0:T(8,128)}, u32[]{:S(2)}, u32[]{:S(2)}) %collective-permute-start) | collective-permute-done | bytes 1572896 | tf_op jit(solution)/shard_map/ppermute | solution.py:10
  60.0 2.1 fusion.2
  64.4 5.4 %collective-permute-start.1 = (f32[1,512,256]{2,1,0:T(8,128)}, f32[1,512,256]{2,1,0:T(8,128)}, u32[]{:S(2)}, u32[]{:S(2)}) collective-permute-start(f32[1,512,256]{2,1,0:T(8,128)} %get-tuple-element.14), channel_id=1, source_target_pairs={{0,4},{4,8},{8,12},{1,5},{5,9},{9,13},{2,6},{6,10},{10,14},{3,7},{... | collective-permute-start | bytes 1572872 | tf_op jit(solution)/shard_map/ppermute | solution.py:20
  69.8 2.2 fusion.30
  72.0 4.6 %reshape.72 = f32[3,2,512,256]{3,2,1,0:T(8,128)} reshape(f32[24,32768]{1,0:T(8,128)} %fusion.30) | data formatting | bytes 6291456 | tf_op jit(solution)/shard_map/reshape | solution.py:134
  76.6 2.7 slice_bitcast_fusion
  82.4 2.3 all_gather.6
  87.8 26.8 %collective-permute-done.6 = f32[3,512,256]{2,1,0:T(8,128)} collective-permute-done((f32[3,512,256]{2,1,0:T(8,128)}, f32[3,512,256]{2,1,0:T(8,128)}, u32[]{:S(2)}, u32[]{:S(2)}) %collective-permute-start.6) | collective-permute-done | bytes 1572896 | tf_op jit(solution)/shard_map/ppermute | solution.py:10
  120.2 5.4 %collective-permute-start.7 = (f32[1,512,256]{2,1,0:T(8,128)}, f32[1,512,256]{2,1,0:T(8,128)}, u32[]{:S(2)}, u32[]{:S(2)}) collective-permute-start(f32[1,512,256]{2,1,0:T(8,128)} %get-tuple-element.12), channel_id=1, source_target_pairs={{0,4},{4,8},{8,12},{1,5},{5,9},{9,13},{2,6},{6,10},{10,14},{3,7},{... | collective-permute-start | bytes 1572872 | tf_op jit(solution)/shard_map/ppermute | solution.py:20
  128.2 4.4 %collective-permute-done.8 = f32[1,512,256]{2,1,0:T(8,128)S(1)} collective-permute-done((f32[1,512,256]{2,1,0:T(8,128)}, f32[1,512,256]{2,1,0:T(8,128)S(1)}, u32[]{:S(2)}, u32[]{:S(2)}) %collective-permute-start.8) | collective-permute-done | bytes 524320 | tf_op jit(solution)/shard_map/ppermute | solution.py:21
  136.6 5.8 %collective-permute-start.4 = (bf16[1,2,512,256]{3,2,1,0:T(8,128)(2,1)S(1)}, bf16[1,2,512,256]{3,2,1,0:T(8,128)(2,1)}, u32[]{:S(2)}, u32[]{:S(2)}) collective-permute-start(bf16[1,2,512,256]{3,2,1,0:T(8,128)(2,1)S(1)} %maximum_bitcast_fusion), channel_id=1, source_target_pairs={{0,4},{4,8},{8,12},{1,5},{5,9},{9,13},{2,6},{6,10},{10,14},{3,7},{... | collective-permute-start | bytes 1572872 | tf_op jit(solution)/shard_map/ppermute | solution.py:20
  142.4 2.2 all-gather
  149.5 2.5 pad_maximum_fusion
  152.0 2.2 gather_fusion
  157.6 2.3 fusion.26
  159.9 2.2 fusion.22
  163.2 2.7 all-reduce.4.cloned.1.call-done
  168.8 10.0 %reduce-scatter.5.cloned.1.call-done = f32[1024,227]{0,1:T(8,128)} async-done(((f32[2048,227]{0,1:T(8,128)}), f32[1024,227]{0,1:T(8,128)}) %reduce-scatter.5.cloned.1.call-update) | async-done | bytes 929808 | tf_op jit(solution)/shard_map/reduce_scatter | solution.py:119
  180.8 87.8 %all-reduce.6.cloned.1.call-done = (f32[256,227]{0,1:T(8,128)}, f32[512,256]{1,0:T(8,128)}, f32[256,512]{1,0:T(8,128)}) async-done(((f32[256,227]{0,1:T(8,128)}, f32[512,256]{1,0:T(8,128)}, f32[256,512]{1,0:T(8,128)}), (f32[256,227]{0,1:T(8,128)}, f32[512,256]{1,0:T(8,128)}, f32[256,512]{1,0:T(8,128)})) %all-reduce.6.cloned.1.call-update) | async-done | bytes 1281040 | tf_op jit(solution)/shard_map/psum | solution.py:154
  (95 shorter events, 46.4 us)
Async XLA Ops:
  7.2 18.1 %copy-start = (bf16[2048,227]{0,1:T(8,128)(2,1)S(1)}, bf16[2048,227]{0,1:T(8,128)(2,1)}, u32[]{:S(2)}) copy-start(bf16[2048,227]{0,1:T(8,128)(2,1)} %param.19) | copy-start | bytes 2789380
  7.2 118.4 %reduce-scatter.3.cloned.1.call-start = ((), (), s32[]{:S(2)}) async-start(), calls=%async_computation.2 | async-start | bytes 1572864 | tf_op jit(solution)/shard_map/reduce_scatter | solution.py:110
  9.4 3.4 %copy-start.14 = (s32[16]{0:T(128)S(1)}, s32[16]{0:T(128)}, u32[]{:S(2)}) copy-start(s32[16]{0:T(128)} %param.14) | copy-start | bytes 196
  9.4 3.4 %copy-start.15 = (s32[16,1]{0,1:T(1,128)S(1)}, s32[16,1]{0,1:T(1,128)}, u32[]{:S(2)}) copy-start(s32[16,1]{0,1:T(1,128)} %param.13) | copy-start | bytes 196
  19.6 5.7 %copy-start.9 = (bf16[256,227]{0,1:T(8,128)(2,1)S(1)}, bf16[256,227]{0,1:T(8,128)(2,1)}, u32[]{:S(2)}) copy-start(bf16[256,227]{0,1:T(8,128)(2,1)} %param.18) | copy-start | bytes 348676
  22.4 37.6 %collective-permute-start = (f32[3,512,256]{2,1,0:T(8,128)}, f32[3,512,256]{2,1,0:T(8,128)}, u32[]{:S(2)}, u32[]{:S(2)}) collective-permute-start(f32[3,512,256]{2,1,0:T(8,128)} %slice_bitcast_fusion.2), channel_id=1, source_target_pairs={{0,2},{2,0},{1,3},{3,1},{4,6},{6,4},{5,7},{7,5},{8,10},{10,8},{9,1... | collective-permute-start | bytes 4718600 | tf_op jit(solution)/shard_map/ppermute | solution.py:10
  62.1 7.7 %copy-start.3 = (bf16[2,8,128,256]{3,1,2,0:T(8,128)(2,1)S(1)}, bf16[2,8,128,256]{3,1,2,0:T(8,128)(2,1)}, u32[]{:S(2)}) copy-start(bf16[2,8,128,256]{3,1,2,0:T(8,128)(2,1)} %copy.34) | copy-start | bytes 3145732
  63.1 17.9 %collective-permute-start.2 = (f32[1,512,256]{2,1,0:T(8,128)}, f32[1,512,256]{2,1,0:T(8,128)}, u32[]{:S(2)}, u32[]{:S(2)}) collective-permute-start(f32[1,512,256]{2,1,0:T(8,128)} %get-tuple-element.15), channel_id=1, source_target_pairs={{4,0},{8,4},{12,8},{5,1},{9,5},{13,9},{6,2},{10,6},{14,10},{7,3},{... | collective-permute-start | bytes 1572872 | tf_op jit(solution)/shard_map/ppermute | solution.py:21
  64.4 16.6 %collective-permute-start.1 = (f32[1,512,256]{2,1,0:T(8,128)}, f32[1,512,256]{2,1,0:T(8,128)}, u32[]{:S(2)}, u32[]{:S(2)}) collective-permute-start(f32[1,512,256]{2,1,0:T(8,128)} %get-tuple-element.14), channel_id=1, source_target_pairs={{0,4},{4,8},{8,12},{1,5},{5,9},{9,13},{2,6},{6,10},{10,14},{3,7},{... | collective-permute-start | bytes 1572872 | tf_op jit(solution)/shard_map/ppermute | solution.py:20
  76.6 4.5 %copy-start.13 = (bf16[512,256]{1,0:T(8,128)(2,1)S(1)}, bf16[512,256]{1,0:T(8,128)(2,1)}, u32[]{:S(2)}) copy-start(bf16[512,256]{1,0:T(8,128)(2,1)} %param.15) | copy-start | bytes 786436
  79.3 5.9 %copy-start.10 = (bf16[512,256]{1,0:T(8,128)(2,1)S(1)}, bf16[512,256]{1,0:T(8,128)(2,1)}, u32[]{:S(2)}) copy-start(bf16[512,256]{1,0:T(8,128)(2,1)} %param.16) | copy-start | bytes 786436
  79.3 35.3 %collective-permute-start.6 = (f32[3,512,256]{2,1,0:T(8,128)}, f32[3,512,256]{2,1,0:T(8,128)}, u32[]{:S(2)}, u32[]{:S(2)}) collective-permute-start(f32[3,512,256]{2,1,0:T(8,128)} %slice_bitcast_fusion), channel_id=1, source_target_pairs={{0,2},{2,0},{1,3},{3,1},{4,6},{6,4},{5,7},{7,5},{8,10},{10,8},{9,1... | collective-permute-start | bytes 4718600 | tf_op jit(solution)/shard_map/ppermute | solution.py:10
  82.4 4.0 %copy-start.16 = (bf16[256,512]{1,0:T(8,128)(2,1)S(1)}, bf16[256,512]{1,0:T(8,128)(2,1)}, u32[]{:S(2)}) copy-start(bf16[256,512]{1,0:T(8,128)(2,1)} %param.17) | copy-start | bytes 786436
  87.8 78.2 %all-reduce.4.cloned.1.call-start = ((), (), s32[]{:S(2)}) async-start(), calls=%async_computation.4 | async-start | bytes 1048576 | tf_op jit(solution)/shard_map/psum | solution.py:142
  118.9 13.7 %collective-permute-start.8 = (f32[1,512,256]{2,1,0:T(8,128)}, f32[1,512,256]{2,1,0:T(8,128)S(1)}, u32[]{:S(2)}, u32[]{:S(2)}) collective-permute-start(f32[1,512,256]{2,1,0:T(8,128)} %get-tuple-element.13), channel_id=1, source_target_pairs={{4,0},{8,4},{12,8},{5,1},{9,5},{13,9},{6,2},{10,6},{14,10},{7,3},{... | collective-permute-start | bytes 1572872 | tf_op jit(solution)/shard_map/ppermute | solution.py:21
  120.2 13.7 %collective-permute-start.7 = (f32[1,512,256]{2,1,0:T(8,128)}, f32[1,512,256]{2,1,0:T(8,128)}, u32[]{:S(2)}, u32[]{:S(2)}) collective-permute-start(f32[1,512,256]{2,1,0:T(8,128)} %get-tuple-element.12), channel_id=1, source_target_pairs={{0,4},{4,8},{8,12},{1,5},{5,9},{9,13},{2,6},{6,10},{10,14},{3,7},{... | collective-permute-start | bytes 1572872 | tf_op jit(solution)/shard_map/ppermute | solution.py:20
  126.7 17.9 %copy-start.17 = (bf16[256,512]{1,0:T(8,128)(2,1)S(1)}, bf16[256,512]{1,0:T(8,128)(2,1)}, u32[]{:S(2)}) copy-start(bf16[256,512]{1,0:T(8,128)(2,1)} %param.17) | copy-start | bytes 786436
  126.7 17.9 %copy-start.19 = (f32[512,256]{1,0:T(8,128)S(1)}, f32[512,256]{1,0:T(8,128)}, u32[]{:S(2)}) copy-start(f32[512,256]{1,0:T(8,128)} %copy-done.18) | copy-start | bytes 1572868
  126.7 8.5 %collective-permute-start.3 = (bf16[512,256]{1,0:T(8,128)(2,1)S(1)}, bf16[512,256]{1,0:T(8,128)(2,1)S(1)}, u32[]{:S(2)}, u32[]{:S(2)}) collective-permute-start(bf16[512,256]{1,0:T(8,128)(2,1)S(1)} %add_convert_fusion), channel_id=1, source_target_pairs={{0,2},{2,0},{1,3},{3,1},{4,6},{6,4},{5,7},{7,5},{8,10},{10,8},{9,1... | collective-permute-start | bytes 786440 | tf_op jit(solution)/shard_map/ppermute | solution.py:10
  135.3 13.2 %collective-permute-start.5 = (bf16[1,2,512,256]{3,2,1,0:T(8,128)(2,1)S(1)}, bf16[1,2,512,256]{3,2,1,0:T(8,128)(2,1)}, u32[]{:S(2)}, u32[]{:S(2)}) collective-permute-start(bf16[1,2,512,256]{3,2,1,0:T(8,128)(2,1)S(1)} %maximum_bitcast_fusion), channel_id=1, source_target_pairs={{4,0},{8,4},{12,8},{5,1},{9,5},{13,9},{6,2},{10,6},{14,10},{7,3},{... | collective-permute-start | bytes 1572872 | tf_op jit(solution)/shard_map/ppermute | solution.py:21
  136.6 12.9 %collective-permute-start.4 = (bf16[1,2,512,256]{3,2,1,0:T(8,128)(2,1)S(1)}, bf16[1,2,512,256]{3,2,1,0:T(8,128)(2,1)}, u32[]{:S(2)}, u32[]{:S(2)}) collective-permute-start(bf16[1,2,512,256]{3,2,1,0:T(8,128)(2,1)S(1)} %maximum_bitcast_fusion), channel_id=1, source_target_pairs={{0,4},{4,8},{8,12},{1,5},{5,9},{9,13},{2,6},{6,10},{10,14},{3,7},{... | collective-permute-start | bytes 1572872 | tf_op jit(solution)/shard_map/ppermute | solution.py:20
  146.8 32.0 %reduce-scatter.5.cloned.1.call-start = ((), (), s32[]{:S(2)}) async-start(), calls=%async_computation.3 | async-start | bytes 2850816 | tf_op jit(solution)/shard_map/reduce_scatter | solution.py:119
  157.5 2.4 copy-start.8
  157.5 111.1 %all-reduce.6.cloned.1.call-start = ((), (), s32[]{:S(2)}) async-start(), calls=%async_computation.5 | async-start | bytes 2572288 | tf_op jit(solution)/shard_map/psum | solution.py:154
  (9 other events, 12.2 us)
Sparse Core Ops, SparseCore 0:
  87.9 10.0 reduce-scatter.2
  147.0 18.9 all-reduce.3
  168.2 10.5 reduce-scatter.4
  183.6 84.9 all-reduce.5
where the time goes:
time: 282 us; the launch traced here: 281 us
  waiting for transfers between devices  168 us (60%)
  local copies, waits for them, and re-layouts  31.3 us (11%)
  starting transfers between devices  26.7 us (9%)
  matrix products  20.1 us (7%)
  other arithmetic  16.2 us (6%)
  between operations  14.1 us (5%)
  blocking collectives  4.48 us (2%)
    psum x1, waiting for transfers between devices, per_device(): lax.psum((grad_out, grad_up, grad_down), ('lat', 'lon'))  87.8 us
    ppermute x3, waiting for transfers between devices, passed_along(): return lax.ppermute(value, axis, pairs)  58.8 us
    ppermute x3, starting transfers between devices, with_halo(): before = lax.ppermute(last, axis, up)  16.5 us
    unnamed x45, local copies, waits for them, and re-layouts  12.5 us
    reduce_scatter x1, waiting for transfers between devices, per_device(): lax.psum_scatter(out_terms, 'rep', scatter_dimension=0, tiled=True)  9.96 us
    ppermute x3, starting transfers between devices, passed_along(): return lax.ppermute(value, axis, pairs)  6.18 us
    ppermute x3, waiting for transfers between devices, with_halo(): after = lax.ppermute(initial, axis, down)  5.96 us
  transfers between devices with their start and end apart: 13, of which 9 were waited for; matrix products, arithmetic and copies ran while one was open for 14% of the time, Pallas kernels for 0%

commit v1 on v0

v1 whole, which is shorter than its diff:
```python
import jax
import jax.numpy as jnp
from jax import lax
from jax.experimental import pallas as pl
from jax.experimental.pallas import tpu as pltpu
from jax.sharding import PartitionSpec as P

F32 = jnp.float32
BF16 = jnp.bfloat16
VMEM_BYTES = 40 * 1024 * 1024
STEPS = 4


def dot(left, right):
    return jnp.dot(left, right, preferred_element_type=F32)


def dot_rows(left, right):
    return lax.dot_general(left, right, (((0,), (0,)), ((), ())), preferred_element_type=F32)


def dot_last(left, right):
    return lax.dot_general(left, right, (((1,), (1,)), ((), ())), preferred_element_type=F32)


def sigmoid(values):
    return 0.5 * jnp.tanh(0.5 * values) + 0.5


def vmem():
    return pl.BlockSpec(memory_space=pltpu.VMEM)


def smem():
    return pl.BlockSpec(memory_space=pltpu.SMEM)


def params(semantics=None):
    return pltpu.CompilerParams(vmem_limit_bytes=VMEM_BYTES, dimension_semantics=semantics)


def cost(flops, nbytes, transcendentals=0):
    return pl.CostEstimate(
        flops=int(flops), bytes_accessed=int(nbytes), transcendentals=int(transcendentals)
    )


def node_half(tile, r):
    half = tile.shape[1] // 2
    return jnp.where(r == 0, tile[:, :half], tile[:, half:])


def add_messages(pos_ref, first, count, tiles_ref, rows_of, r, total):
    for i in range(count):
        part = node_half(tiles_ref[i], r)
        where = pos_ref[first + i]
        total[where] += dot_rows(part, rows_of(i))


def write_packed(total, outs):
    per = total.shape[0] // 3
    for k, out in enumerate(outs):
        block = total[k * per : (k + 1) * per]
        out[...] = block.reshape(out.shape).astype(out.dtype)


def back_kernel(pos_ref, where_ref, tiles_ref, cot_ref, own_ref, even_ref, odd_ref, total):
    step = pl.program_id(0)
    count, rows = tiles_ref.shape[0], tiles_ref.shape[1]
    channels = cot_ref.shape[1]
    r = where_ref[0]

    @pl.when(step == 0)
    def _():
        total[...] = jnp.zeros_like(total)

    for i in range(count):
        part = node_half(tiles_ref[i], r)
        where = pos_ref[step * count + i]
        total[where, :, :channels] += dot_rows(part, cot_ref[i * rows : (i + 1) * rows, :])

    @pl.when(step == pl.num_programs(0) - 1)
    def _():
        write_packed(total, (own_ref, even_ref, odd_ref))


def encode_kernel(
    pos_ref, where_ref, grid_ref, tiles_ref, mine_ref, other_ref,
    own_ref, even_ref, odd_ref, hidden_ref, total, hold,
):
    step = pl.program_id(0)
    count, rows = tiles_ref.shape[0], tiles_ref.shape[1]
    width = mine_ref.shape[1]
    r = where_ref[0]

    @pl.when(step == 0)
    def _():
        total[...] = jnp.zeros_like(total)

    grid = grid_ref[...]
    for k, weight_ref in enumerate((mine_ref, other_ref)):
        preact = dot(grid, weight_ref[...])
        hold[:, k * width : (k + 1) * width] = (preact * sigmoid(preact)).astype(BF16)
    for i in range(count):
        part = node_half(tiles_ref[i], r)
        where = pos_ref[step * count + i]
        total[where] += dot_rows(part, hold[i * rows : (i + 1) * rows, :])

    half_steps = pl.num_programs(0) // 2

    @pl.when(step // half_steps == r)
    def _():
        at = pl.multiple_of((step % half_steps) * hold.shape[0], hold.shape[0])
        hidden_ref[pl.ds(at, hold.shape[0]), :] = hold[...]

    @pl.when(step == pl.num_programs(0) - 1)
    def _():
        write_packed(total, (own_ref, even_ref, odd_ref))


def local_kernel(hidden_ref, cot_ref, mine_ref, other_ref, base_ref, grad_ref):
    width = mine_ref.shape[0]
    hidden = hidden_ref[...]
    base_ref[...] = dot(hidden[:, :width], mine_ref[...]) + dot(hidden[:, width:], other_ref[...])
    grad_ref[...] = dot_rows(hidden, cot_ref[...])


def update_kernel(
    where_ref, sums_ref, even_ref, odd_ref, moved_ref, embed_ref, embed_other_ref,
    up_ref, up_other_ref, down_ref, down_other_ref, out_ref, out_other_ref,
    proj_ref, mesh_ref, norm_ref, inv_ref, pre_ref, act_ref,
):
    r = where_ref[0]
    nodes, latent = moved_ref.shape
    width = latent // 2
    channels = out_ref.shape[1]
    first = pl.multiple_of(r * width, width)
    second = pl.multiple_of((1 - r) * width, width)
    sums = (
        sums_ref[0].astype(F32) + even_ref[0].astype(F32)
        + odd_ref[0].astype(F32) + moved_ref[...].astype(F32)
    )
    embed = jnp.concatenate(
        [embed_ref[:, r].reshape(nodes, width), embed_other_ref[:, r].reshape(nodes, width)], axis=1
    )
    state = (embed.astype(F32) + sums).astype(BF16).astype(F32)
    centered = state - jnp.mean(state, axis=-1, keepdims=True)
    inverse = lax.rsqrt(jnp.mean(centered * centered, axis=-1, keepdims=True) + 1e-05)
    norm = centered * inverse
    normed = norm.astype(BF16)
    norm_ref[...] = norm
    inv_ref[...] = jnp.broadcast_to(inverse, inv_ref.shape)
    normed_own, normed_oth = normed[:, :width], normed[:, width:]
    update_own = jnp.zeros((nodes, width), F32)
    update_oth = jnp.zeros((nodes, width), F32)
    for k, (u_ref, d_ref) in enumerate(((up_ref, down_ref), (up_other_ref, down_other_ref))):
        hidden = dot(normed_own, u_ref[pl.ds(first, width), :]) + dot(
            normed_oth, u_ref[pl.ds(second, width), :]
        )
        act = (hidden * sigmoid(hidden)).astype(BF16)
        pre_ref[:, k * width : (k + 1) * width] = hidden
        act_ref[:, k * width : (k + 1) * width] = act
        update_own += dot(act, d_ref[:, pl.ds(first, width)])
        update_oth += dot(act, d_ref[:, pl.ds(second, width)])
    mesh = (state + jnp.concatenate([update_own, update_oth], axis=1)).astype(BF16)
    mesh_ref[...] = mesh
    proj = dot(mesh[:, :width], out_ref[...]) + dot(mesh[:, width:], out_other_ref[...])
    proj_ref[...] = jnp.zeros_like(proj_ref)
    proj_ref[:, :channels] = proj.astype(BF16)


def grads_kernel(
    where_ref, sums_ref, even_ref, odd_ref, moved_ref, local_ref,
    mesh_ref, norm_ref, inv_ref, pre_ref, act_ref,
    up_ref, up_other_ref, down_ref, down_other_ref, out_ref, out_other_ref,
    keep_ref, give_ref, grad_keep_ref, grad_give_ref,
):
    r = where_ref[0]
    latent = norm_ref.shape[1]
    width = latent // 2
    channels = out_ref.shape[1]
    first = pl.multiple_of(r * width, width)
    second = pl.multiple_of((1 - r) * width, width)
    cot = (
        sums_ref[0].astype(F32) + even_ref[0].astype(F32)
        + odd_ref[0].astype(F32) + moved_ref[...].astype(F32)
    )[:, :channels].astype(BF16)
    grad_own = dot_last(cot, out_ref[...]).astype(BF16)
    grad_oth = dot_last(cot, out_other_ref[...]).astype(BF16)
    norm = norm_ref[...]
    normed = norm.astype(BF16)
    mesh = mesh_ref[...]
    back_own = jnp.zeros(grad_own.shape, F32)
    back_oth = jnp.zeros(grad_own.shape, F32)
    sides = (
        (up_ref, down_ref, keep_ref, 0),
        (up_other_ref, down_other_ref, give_ref, 1),
    )
    for u_ref, d_ref, o_ref, k in sides:
        cols = slice(k * width, (k + 1) * width)
        hidden = pre_ref[:, cols]
        act_grad = dot_last(grad_own, d_ref[:, pl.ds(first, width)]) + dot_last(
            grad_oth, d_ref[:, pl.ds(second, width)]
        )
        squash = sigmoid(hidden)
        pre_grad = (act_grad * squash * (1.0 + hidden * (1.0 - squash))).astype(BF16)
        o_ref[pl.ds(first, width), :] = dot_rows(normed[:, :width], pre_grad).astype(o_ref.dtype)
        o_ref[pl.ds(second, width), :] = dot_rows(normed[:, width:], pre_grad).astype(o_ref.dtype)
        back_own += dot_last(pre_grad, u_ref[pl.ds(first, width), :])
        back_oth += dot_last(pre_grad, u_ref[pl.ds(second, width), :])
        o_ref[latent:, :] = jnp.zeros((latent, width), o_ref.dtype)
        o_ref[latent : latent + width, :channels] = dot_rows(act_ref[:, cols], cot).astype(
            o_ref.dtype
        )
        o_ref[latent + width :, :channels] = (
            dot_rows(mesh[:, cols], cot) + local_ref[cols, :]
        ).astype(o_ref.dtype)
    back = jnp.concatenate([back_own, back_oth], axis=1)
    centered = (
        back - jnp.mean(back, axis=-1, keepdims=True)
        - norm * jnp.mean(back * norm, axis=-1, keepdims=True)
    )
    state_grad = inv_ref[:, :1] * centered
    grad_keep_ref[...] = grad_own.astype(F32) + state_grad[:, :width]
    grad_give_ref[...] = (grad_oth.astype(F32) + state_grad[:, width:]).astype(grad_give_ref.dtype)


def decode_kernel(
    pos_ref, where_ref, tiles_ref, base_ref, *refs
):
    mine, theirs, out_ref, picked = refs[:3], refs[3:6], refs[6], refs[7]
    r = where_ref[0]
    count, rows = tiles_ref.shape[0], tiles_ref.shape[1]
    half = rows // 2
    channels = out_ref.shape[1]
    blocks = count // 2
    for i in range(blocks):
        b = r * blocks + i
        at = pos_ref[b]
        per = mine[0].shape[0]
        for k in range(3):
            @pl.when(at // per == k)
            def _(k=k, i=i, at=at):
                where = at - k * per
                picked[i, pl.ds(pl.multiple_of(r * half, half), half), :] = mine[k][where]
                picked[i, pl.ds(pl.multiple_of((1 - r) * half, half), half), :] = theirs[k][where]
    for i in range(blocks):
        rows_at = slice(i * rows, (i + 1) * rows)
        decoded = dot(tiles_ref[r * blocks + i], picked[i])
        out_ref[rows_at, :] = (base_ref[rows_at, :] + decoded[:, :channels]).astype(out_ref.dtype)


def along(axis, count, partner):
    pairs = []
    for source in range(count):
        to = partner(source)
        pairs.append((source, to if 0 <= to < count else source))
    return lambda value: lax.ppermute(value, axis, pairs)


def summed_over(value, order):
    held = []
    for axis, distance, halve in order:
        count = lax.axis_size(axis)
        swap = along(axis, count, lambda i: i ^ distance)
        if not halve:
            value = (value.astype(F32) + swap(value).astype(F32)).astype(BF16)
            continue
        bit = (lax.axis_index(axis) // distance) % 2
        rows = value.shape[0] // 2
        keep = lax.dynamic_slice_in_dim(value, bit * rows, rows, 0)
        give = lax.dynamic_slice_in_dim(value, (1 - bit) * rows, rows, 0)
        value = (keep.astype(F32) + swap(give).astype(F32)).astype(BF16)
        held.append((swap, bit))
    for swap, bit in reversed(held):
        other = swap(value)
        value = jnp.where(
            bit == 0,
            jnp.concatenate([value, other], axis=0),
            jnp.concatenate([other, value], axis=0),
        )
    return value


def distances(count):
    found, distance = [], 1
    while distance < count:
        found.append(distance)
        distance *= 2
    return found


def per_device(
    grid_in, w_embed, interp_tiles, route_device, route_slot,
    mesh_embed, w_up, w_down, w_out, cotangent,
):
    lat_count, lon_count = lax.axis_size("lat"), lax.axis_size("lon")
    lat, lon, r = lax.axis_index("lat"), lax.axis_index("lon"), lax.axis_index("rep")
    blocks, tile_rows = interp_tiles.shape[:2]
    grid_rows, channels = grid_in.shape
    width = w_embed.shape[1]
    latent = 2 * width
    padded = -(-channels // 128) * 128
    slots = mesh_embed.shape[0] // tile_rows
    half = tile_rows // 2
    nodes = slots * half

    swap_rep = along("rep", 2, lambda i: 1 - i)
    to_even = along("lat", lat_count, lambda i: i ^ 1)
    to_odd = along("lat", lat_count, lambda i: ((i + 1) ^ 1) - 1)
    east_pairs = [(i, (i + 1) % lon_count) for i in range(lon_count)]
    west_pairs = [(j, i) for i, j in east_pairs]

    target = route_device[:, 0]
    band_step = target // lon_count - lat
    sector_step = (target % lon_count - lon + lon_count) % lon_count
    even_step = 1 - 2 * (lat % 2)
    along_lat = jnp.where(band_step == 0, 0, jnp.where(band_step == even_step, 1, 2))
    position = ((along_lat * 2 + sector_step) * slots + route_slot).astype(jnp.int32)
    where = jnp.stack([r, r]).astype(jnp.int32)

    packed = lambda cols: [jax.ShapeDtypeStruct((2, nodes, cols), BF16)] * 3
    per_step = blocks // STEPS
    step_rows = per_step * tile_rows
    packed_spec = lambda cols: [pl.BlockSpec((2, nodes, cols), lambda i: (0, 0, 0))] * 3
    tiles_spec = pl.BlockSpec((per_step, tile_rows, tile_rows), lambda i: (i, 0, 0))
    rows_spec = pl.BlockSpec((step_rows, channels), lambda i: (i, 0))

    embed_other = swap_rep(w_embed)

    back = pl.pallas_call(
        back_kernel,
        grid=(STEPS,),
        in_specs=[smem(), smem(), tiles_spec, rows_spec],
        out_specs=packed_spec(padded),
        out_shape=packed(padded),
        scratch_shapes=[pltpu.VMEM((6 * slots, half, padded), F32)],
        compiler_params=params(("arbitrary",)),
        cost_estimate=cost(2 * grid_rows * half * padded, 3e6),
        name="back_messages",
    )(position, where, interp_tiles, cotangent)

    full = lambda shape: pl.BlockSpec(shape, lambda i: (0,) * len(shape))
    own, even, odd, hidden = pl.pallas_call(
        encode_kernel,
        grid=(STEPS,),
        in_specs=[
            smem(), smem(), rows_spec, tiles_spec, full((channels, width)), full((channels, width)),
        ],
        out_specs=packed_spec(latent) + [full((grid_rows // 2, latent))],
        out_shape=packed(latent) + [jax.ShapeDtypeStruct((grid_rows // 2, latent), BF16)],
        scratch_shapes=[
            pltpu.VMEM((6 * slots, half, latent), F32),
            pltpu.VMEM((step_rows, latent), BF16),
        ],
        compiler_params=params(("arbitrary",)),
        cost_estimate=cost(2 * grid_rows * latent * (channels + half), 5e6, grid_rows * latent),
        name="encode",
    )(position, where, grid_in, interp_tiles, w_embed, embed_other)

    even_in, odd_in = to_even(even), to_odd(odd)
    w_up_s, w_down_s, w_out_s, mesh_s, hidden = lax.optimization_barrier(
        (w_up, w_down, w_out, mesh_embed, hidden)
    )
    out_other = swap_rep(w_out_s)
    up_other = swap_rep(w_up_s)
    down_other = swap_rep(w_down_s)
    mesh_other = swap_rep(mesh_s)
    back_own, back_even, back_odd = back
    back_even_in, back_odd_in = to_even(back_even), to_odd(back_odd)

    cot_mine = lax.dynamic_slice_in_dim(cotangent, r * (grid_rows // 2), grid_rows // 2, 0)
    base, local_grad = pl.pallas_call(
        local_kernel,
        in_specs=[vmem()] * 4,
        out_specs=[vmem()] * 2,
        out_shape=[
            jax.ShapeDtypeStruct((grid_rows // 2, channels), F32),
            jax.ShapeDtypeStruct((latent, channels), F32),
        ],
        compiler_params=params(),
        cost_estimate=cost(2 * grid_rows * latent * channels, 4e6),
        name="local_terms",
    )(hidden, cot_mine, w_out, out_other)

    def to_east(a, b, c):
        total = a[1].astype(F32) + b[1].astype(F32) + c[1].astype(F32)
        return lax.ppermute(total.astype(BF16), "lon", east_pairs)

    moved = to_east(own, even_in, odd_in)
    weights = (w_up, up_other, w_down, down_other, w_out, out_other)
    embed_shape = (slots, 2, half, width)
    row_specs = [vmem()] * 6
    proj, mesh_out, norm, inverse, hidden_pre, hidden_act = pl.pallas_call(
        update_kernel,
        in_specs=[smem()] + [vmem()] * 12,
        out_specs=row_specs,
        out_shape=[
            jax.ShapeDtypeStruct((nodes, padded), BF16),
            jax.ShapeDtypeStruct((nodes, latent), BF16),
            jax.ShapeDtypeStruct((nodes, latent), F32),
            jax.ShapeDtypeStruct((nodes, 128), F32),
            jax.ShapeDtypeStruct((nodes, latent), F32),
            jax.ShapeDtypeStruct((nodes, latent), BF16),
        ],
        compiler_params=params(),
        cost_estimate=cost(5 * nodes * latent * latent, 4e6, nodes * latent),
        name="node_update",
    )(
        where, own, even_in, odd_in, moved,
        mesh_embed.reshape(embed_shape), mesh_other.reshape(embed_shape), *weights,
    )

    east = lax.ppermute(proj, "lon", west_pairs)
    pair = jnp.stack([proj, east])
    pair_even, pair_odd = to_even(pair), to_odd(pair)

    back_moved = to_east(back_own, back_even_in, back_odd_in)
    keep, give, mesh_keep, mesh_give = pl.pallas_call(
        grads_kernel,
        in_specs=[smem()] + [vmem()] * 16,
        out_specs=[vmem()] * 4,
        out_shape=[
            jax.ShapeDtypeStruct((2 * latent, width), F32),
            jax.ShapeDtypeStruct((2 * latent, width), BF16),
            jax.ShapeDtypeStruct((nodes, width), F32),
            jax.ShapeDtypeStruct((nodes, width), F32),
        ],
        compiler_params=params(),
        cost_estimate=cost(10 * nodes * latent * latent, 7e6, nodes * latent),
        name="node_grads",
    )(
        where, back_own, back_even_in, back_odd_in, back_moved, local_grad,
        mesh_out, norm, inverse, hidden_pre, hidden_act, *weights,
    )

    given = swap_rep(give)
    order = [("lon", d, True) for d in distances(lon_count)]
    order += [("lat", d, d == 1) for d in distances(lat_count)]
    grads = summed_over((keep + given.astype(F32)).astype(BF16), order)

    mesh_got = swap_rep(mesh_give)
    parts = [part.reshape(slots, half, width) for part in (mesh_keep, mesh_got)]
    grad_mesh = jnp.where(
        r == 0, jnp.stack(parts, axis=1), jnp.stack(parts[::-1], axis=1)
    ).reshape(mesh_embed.shape)

    tables = (pair, pair_even, pair_odd)
    table_shape = (2 * slots, half, padded)
    grid_out = pl.pallas_call(
        decode_kernel,
        in_specs=[smem(), smem()] + [vmem()] * 8,
        out_specs=vmem(),
        out_shape=jax.ShapeDtypeStruct((grid_rows // 2, channels), BF16),
        scratch_shapes=[pltpu.VMEM((blocks // 2, tile_rows, padded), BF16)],
        compiler_params=params(),
        cost_estimate=cost(grid_rows * tile_rows * padded, 4e6),
        name="decode",
    )(
        position, where, interp_tiles, base,
        *[table.reshape(table_shape) for table in tables],
        *[swap_rep(table).reshape(table_shape) for table in tables],
    )

    grad_up = grads[:latent].astype(F32)
    grad_out = grads[latent + width :, :channels].astype(F32)
    down_terms = grads[latent : latent + width, :channels]
    w_out_full = jnp.where(
        r == 0,
        jnp.concatenate([w_out, out_other], axis=0),
        jnp.concatenate([out_other, w_out], axis=0),
    )
    grad_down = dot_last(down_terms, w_out_full)
    return (grid_out, grad_out, grad_up, grad_down, grad_mesh)


def solution(mesh):
    patch = ("groups", "lat", "lon")
    placed = (
        P(patch, None),
        P(None, "rep"),
        P(patch, None, None),
        P(patch, None),
        P(patch),
        P(patch, "rep"),
        P(None, "rep"),
        P("rep", None),
        P("rep", None),
        P(patch, None),
    )
    return jax.shard_map(
        per_device,
        mesh=mesh,
        in_specs=placed,
        out_specs=(
            P(("groups", "lat", "lon", "rep"), None),
            P(("groups", "rep"), None),
            P("groups", "rep"),
            P(("groups", "rep"), None),
            P(patch, "rep"),
        ),
        check_vma=False,
    )
```

time: 282 us -> 89.4 us (0.32)
  waiting for transfers between devices: 168 us -> 22.4 us
  local copies, waits for them, and re-layouts: 31.3 us -> 12.1 us
  matrix products: 20.1 us -> 1.06 us
  Pallas kernels: 0 us -> 14.7 us
  between operations: 14.1 us -> 0.87 us
  other arithmetic: 16.2 us -> 6.2 us
  starting transfers between devices: 26.7 us -> 31.4 us
  blocking collectives: 4.48 us -> 0 us
    psum x2 -> x0, waiting for transfers between devices: 90.5 us -> none  [the longest x1 87.8 us: per_device(): lax.psum((grad_out, grad_up, grad_down), ('lat', 'lon'))]
    ppermute x9 -> x24, waiting for transfers between devices: 67.1 us -> 22.4 us  [the longest x21 20.7 us: along(): return lambda value: lax.ppermute(value, axis, pairs)]
    dot_general x15 -> x1, matrix products: 20.1 us -> 1.06 us  [dot_last(): lax.dot_general(left, right, (((1,), (1,)), ((), ())), preferred_element_...]
    pallas_call x0 -> x6, Pallas kernels: none -> 14.7 us  [the longest x1 4.33 us: per_device(): pl.pallas_call(encode_kernel, grid=(STEPS,), in_specs=[smem(), smem(), ro...]
    reduce_scatter x2 -> x0, waiting for transfers between devices: 9.98 us -> none  [the longest x1 9.96 us: per_device(): lax.psum_scatter(out_terms, 'rep', scatter_dimension=0, tiled=True)]
    reshape x2 -> x0, local copies, waits for them, and re-layouts: 9.12 us -> none  [the longest x1 4.56 us: per_device(): packed = jnp.dot(selector, messages.reshape(blocks, tile_rows * local_wid...]
    squeeze x2 -> x0, local copies, waits for them, and re-layouts: 5.45 us -> none  [deliver_sums(): moved = passed_along(packed[:, 1], 'lon', 1)]
    add x3 -> x1, other arithmetic: 5.24 us -> 0.02 us  [per_device(): (along_lat * 2 + sector_step) * slots + route_slot]
  transfers between devices with their start and end apart: 13 -> 24, of which waited for: 9 -> 9; matrix products, arithmetic and copies ran while one was open for 14% -> 12% of each run, Pallas kernels for 0% -> 8%
where the time goes in v1:
time: 89.4 us; the launch traced here: 88.8 us
  starting transfers between devices  31.4 us (35%)
  waiting for transfers between devices  22.4 us (25%)
  Pallas kernels  14.7 us (16%)
  local copies, waits for them, and re-layouts  12.1 us (14%)
  other arithmetic  6.2 us (7%)
  matrix products  1.06 us (1%)
    ppermute x21, starting transfers between devices, along(): return lambda value: lax.ppermute(value, axis, pairs)  27.9 us
    ppermute x21, waiting for transfers between devices, along(): return lambda value: lax.ppermute(value, axis, pairs)  20.7 us
    unnamed x41, local copies, waits for them, and re-layouts  10.5 us
    pallas_call x1, Pallas kernels, per_device(): pl.pallas_call(encode_kernel, grid=(STEPS,), in_specs=[smem(), smem(), ro...  4.33 us
    pallas_call x1, Pallas kernels, per_device(): pl.pallas_call(grads_kernel, in_specs=[smem()] + [vmem()] * 16, out_specs...  3.35 us
    pallas_call x1, Pallas kernels, per_device(): pl.pallas_call(back_kernel, grid=(STEPS,), in_specs=[smem(), smem(), tile...  2.85 us
    convert_element_type x2, other arithmetic, to_east(): return lax.ppermute(total.astype(BF16), 'lon', east_pairs)  2.48 us
    pallas_call x1, Pallas kernels, per_device(): pl.pallas_call(update_kernel, in_specs=[smem()] + [vmem()] * 12, out_spec...  2.38 us
  transfers between devices with their start and end apart: 24, of which 9 were waited for; matrix products, arithmetic and copies ran while one was open for 12% of the time, Pallas kernels for 8%

profile of v1, /device:TPU:0, one launch (start us, length us, event | category | flops | bytes accessed | tf_op | source)
XLA Modules:
  0.0 88.8 jit_solution(1417653518622722361)
XLA Ops:
  1.9 1.5 %copy.15.grid_ref = bf16[2048,227]{1,0:T(8,128)(2,1)S(1)} copy(bf16[2048,227]{0,1:T(8,128)(2,1)} %param.10) | data formatting | bytes 1859584 | tf_op args[0]
  3.5 4.3 %encode.1 = (bf16[2,256,512]{2,1,0:T(8,128)(2,1)S(1)}, bf16[2,256,512]{2,1,0:T(8,128)(2,1)}, bf16[2,256,512]{2,1,0:T(8,128)(2,1)}, bf16[1024,512]{1,0:T(8,128)(2,1)S(1)}) custom-call(s32[16]{0:T(128)S(1)} %multiply_add_fusion.pos_ref, s32[2]{0:T(128)S(1)} %pad_add_fusion.where_ref, bf16[2048,227]{1,0:T(8,128)(2,1)S(1)} %copy.15.grid_ref, ...), custom_call_target="tpu_custom_call" | custom-call | flops 610271232 | bytes 5000000 | tf_op jit(solution)/shard_map/encode/pallas_call | solution.py:344
  8.8 2.6 %collective-permute-start.2 = (bf16[2,256,512]{2,1,0:T(8,128)(2,1)}, bf16[2,256,512]{2,1,0:T(8,128)(2,1)S(1)}, u32[]{:S(2)}, u32[]{:S(2)}) collective-permute-start(bf16[2,256,512]{2,1,0:T(8,128)(2,1)} %get-tuple-element.34), channel_id=1, source_target_pairs={{0,4},{4,0},{8,12},{12,8},{1,5},{5,1},{9,13},{13,9},{2,6},{6,2},{1... | collective-permute-start | bytes 1572872 | tf_op jit(solution)/shard_map/ppermute | solution.py:258
  11.4 1.7 %collective-permute-start.3 = (bf16[2,256,512]{2,1,0:T(8,128)(2,1)}, bf16[2,256,512]{2,1,0:T(8,128)(2,1)S(1)}, u32[]{:S(2)}, u32[]{:S(2)}) collective-permute-start(bf16[2,256,512]{2,1,0:T(8,128)(2,1)} %get-tuple-element.35), channel_id=1, source_target_pairs={{0,0},{4,8},{8,4},{12,12},{1,1},{5,9},{9,5},{13,13},{2,2},{6,10},{... | collective-permute-start | bytes 1572872 | tf_op jit(solution)/shard_map/ppermute | solution.py:258
  14.6 2.8 %back_messages.1 = (bf16[2,256,256]{2,1,0:T(8,128)(2,1)S(1)}, bf16[2,256,256]{2,1,0:T(8,128)(2,1)}, bf16[2,256,256]{2,1,0:T(8,128)(2,1)}) custom-call(s32[16]{0:T(128)S(1)} %multiply_add_fusion.pos_ref, s32[2]{0:T(128)S(1)} %pad_add_fusion.where_ref, bf16[16,128,128]{2,1,0:T(8,128)(2,1)S(1)} %copy-done, bf16[2048,227]{1,0:T(8,128)(2,1)S(1)} %copy.16.cot_ref), custom_call_target="tpu_custom_call" | custom-call | flops 67108864 | bytes 3000000 | tf_op jit(solution)/shard_map/back_messages/pallas_call | solution.py:331
  18.2 3.4 %collective-permute-start.14 = (bf16[2,256,256]{2,1,0:T(8,128)(2,1)}, bf16[2,256,256]{2,1,0:T(8,128)(2,1)}, u32[]{:S(2)}, u32[]{:S(2)}) collective-permute-start(bf16[2,256,256]{2,1,0:T(8,128)(2,1)} %get-tuple-element.41), channel_id=1, source_target_pairs={{0,4},{4,0},{8,12},{12,8},{1,5},{5,1},{9,13},{13,9},{2,6},{6,2},{1... | collective-permute-start | bytes 786440 | tf_op jit(solution)/shard_map/ppermute | solution.py:258
  21.5 3.6 %collective-permute-start.15 = (bf16[2,256,256]{2,1,0:T(8,128)(2,1)}, bf16[2,256,256]{2,1,0:T(8,128)(2,1)}, u32[]{:S(2)}, u32[]{:S(2)}) collective-permute-start(bf16[2,256,256]{2,1,0:T(8,128)(2,1)} %get-tuple-element.42), channel_id=1, source_target_pairs={{0,0},{4,8},{8,4},{12,12},{1,1},{5,9},{9,5},{13,13},{2,2},{6,10},{... | collective-permute-start | bytes 786440 | tf_op jit(solution)/shard_map/ppermute | solution.py:258
  27.3 2.6 %collective-permute-done.14.even_ref = bf16[2,256,256]{2,1,0:T(8,128)(2,1)} collective-permute-done((bf16[2,256,256]{2,1,0:T(8,128)(2,1)}, bf16[2,256,256]{2,1,0:T(8,128)(2,1)}, u32[]{:S(2)}, u32[]{:S(2)}) %collective-permute-start.14) | collective-permute-done | bytes 262176 | tf_op jit(solution)/shard_map/ppermute | solution.py:258
  29.9 1.7 %collective-permute-start.4 = (bf16[256,512]{1,0:T(8,128)(2,1)}, bf16[256,512]{1,0:T(8,128)(2,1)}, u32[]{:S(2)}, u32[]{:S(2)}) collective-permute-start(bf16[256,512]{1,0:T(8,128)(2,1)} %fusion), channel_id=1, source_target_pairs={{0,2},{2,0},{1,3},{3,1},{4,6},{6,4},{5,7},{7,5},{8,10},{10,8},{9,1... | collective-permute-start | bytes 786440 | tf_op jit(solution)/shard_map/ppermute | solution.py:388
  31.6 1.7 %fusion.8 = bf16[256,256]{1,0:T(8,128)(2,1)} fusion(bf16[2,256,256]{2,1,0:T(8,128)(2,1)} %collective-permute-done.15.odd_ref, bf16[2,256,256]{2,1,0:T(8,128)(2,1)} %collective-permute-done.14.even_ref, bf16[2,256,256]{2,1,0:T(8,128)(2,1)S(1)} %copy-done.9), kind=kLoop, calls=%fused_computation.20 | loop fusion | flops 393216 | bytes 524288 | tf_op jit(solution)/shard_map/convert_element_type | solution.py:388
  37.7 1.7 %collective-permute-done.4.moved_ref = bf16[256,512]{1,0:T(8,128)(2,1)} collective-permute-done((bf16[256,512]{1,0:T(8,128)(2,1)}, bf16[256,512]{1,0:T(8,128)(2,1)}, u32[]{:S(2)}, u32[]{:S(2)}) %collective-permute-start.4) | collective-permute-done | bytes 262176 | tf_op jit(solution)/shard_map/ppermute | solution.py:388
  39.4 2.4 %node_update.1 = (bf16[256,256]{1,0:T(8,128)(2,1)S(1)}, bf16[256,512]{1,0:T(8,128)(2,1)S(1)}, f32[256,512]{1,0:T(8,128)S(1)}, f32[256,128]{1,0:T(8,128)S(1)}, f3...) custom-call(s32[2]{0:T(128)S(1)} %pad_add_fusion.where_ref, bf16[2,256,512]{2,1,0:T(8,128)(2,1)S(1)} %get-tuple-element.33.sums_ref, ...), custom_call_target="tpu_custom_call" | custom-call | flops 335544320 | bytes 4000000 | tf_op jit(solution)/shard_map/node_update/pallas_call | solution.py:394
  41.8 3.3 %node_grads.1 = (f32[1024,256]{1,0:T(8,128)S(1)}, bf16[1024,256]{1,0:T(8,128)(2,1)S(1)}, f32[256,256]{1,0:T(8,128)S(1)}, f32[256,256]{1,0:T(8,128)}) custom-call(s32[2]{0:T(128)S(1)} %pad_add_fusion.where_ref, bf16[2,256,256]{2,1,0:T(8,128)(2,1)S(1)} %copy-done.10, bf16[2,256,256]{2,1,0:T(8,128)(2,1)} %collective-permute-done.14.even_ref, ...), custom_call_target="tpu_custom_call" | custom-call | flops 671088640 | bytes 7000000 | tf_op jit(solution)/shard_map/node_grads/pallas_call | solution.py:419
  45.1 1.9 %collective-permute-done.17 = bf16[1024,256]{1,0:T(8,128)(2,1)S(1)} collective-permute-done((bf16[1024,256]{1,0:T(8,128)(2,1)S(1)}, bf16[1024,256]{1,0:T(8,128)(2,1)S(1)}, u32[]{:S(2)}, u32[]{:S(2)}) %collective-permute-start.17) | collective-permute-done | bytes 524320 | tf_op jit(solution)/shard_map/ppermute | solution.py:258
  47.2 1.7 %collective-permute-start.18 = (bf16[512,256]{1,0:T(8,128)(2,1)S(1)}, bf16[512,256]{1,0:T(8,128)(2,1)S(1)}, u32[]{:S(2)}, u32[]{:S(2)}) collective-permute-start(bf16[512,256]{1,0:T(8,128)(2,1)S(1)} %constant_dynamic-slice_fusion.1), channel_id=1, source_target_pairs={{0,2},{2,0},{1,3},{3,1},{4,6},{6,4},{5,7},{7,5},{8,10},{10,8},{9,1... | collective-permute-start | bytes 786440 | tf_op jit(solution)/shard_map/ppermute | solution.py:258
  48.9 6.7 %collective-permute-done.18 = bf16[512,256]{1,0:T(8,128)(2,1)S(1)} collective-permute-done((bf16[512,256]{1,0:T(8,128)(2,1)S(1)}, bf16[512,256]{1,0:T(8,128)(2,1)S(1)}, u32[]{:S(2)}, u32[]{:S(2)}) %collective-permute-start.18) | collective-permute-done | bytes 262176 | tf_op jit(solution)/shard_map/ppermute | solution.py:258
  55.7 4.9 %collective-permute-start.19 = (bf16[256,256]{1,0:T(8,128)(2,1)S(1)}, bf16[256,256]{1,0:T(8,128)(2,1)S(1)}, u32[]{:S(2)}, u32[]{:S(2)}) collective-permute-start(bf16[256,256]{1,0:T(8,128)(2,1)S(1)} %constant_dynamic-slice_fusion), channel_id=1, source_target_pairs={{0,4},{4,0},{8,12},{12,8},{1,5},{5,1},{9,13},{13,9},{2,6},{6,2},{1... | collective-permute-start | bytes 393224 | tf_op jit(solution)/shard_map/ppermute | solution.py:258
  60.7 1.5 %collective-permute-start.8 = (bf16[256,256]{1,0:T(8,128)(2,1)S(1)}, bf16[256,256]{1,0:T(8,128)(2,1)S(1)}, u32[]{:S(2)}, u32[]{:S(2)}) collective-permute-start(bf16[256,256]{1,0:T(8,128)(2,1)S(1)} %copy-done.13), channel_id=1, source_target_pairs={{2,0},{0,2},{3,1},{1,3},{6,4},{4,6},{7,5},{5,7},{10,8},{8,10},{11,... | collective-permute-start | bytes 393224 | tf_op jit(solution)/shard_map/ppermute | solution.py:414
  63.7 3.0 %collective-permute-start.20 = (bf16[256,256]{1,0:T(8,128)(2,1)S(1)}, bf16[256,256]{1,0:T(8,128)(2,1)S(1)}, u32[]{:S(2)}, u32[]{:S(2)}) collective-permute-start(bf16[256,256]{1,0:T(8,128)(2,1)S(1)} %add_convert_fusion.4), channel_id=1, source_target_pairs={{0,8},{4,12},{8,0},{12,4},{1,9},{5,13},{9,1},{13,5},{2,10},{6,14},... | collective-permute-start | bytes 393224 | tf_op jit(solution)/shard_map/ppermute | solution.py:258
  67.5 3.1 %collective-permute-done.20 = bf16[256,256]{1,0:T(8,128)(2,1)S(1)} collective-permute-done((bf16[256,256]{1,0:T(8,128)(2,1)S(1)}, bf16[256,256]{1,0:T(8,128)(2,1)S(1)}, u32[]{:S(2)}, u32[]{:S(2)}) %collective-permute-start.20) | collective-permute-done | bytes 131104 | tf_op jit(solution)/shard_map/ppermute | solution.py:258
  70.7 2.5 %collective-permute-start.21 = (bf16[256,256]{1,0:T(8,128)(2,1)S(1)}, bf16[256,256]{1,0:T(8,128)(2,1)S(1)}, u32[]{:S(2)}, u32[]{:S(2)}) collective-permute-start(bf16[256,256]{1,0:T(8,128)(2,1)S(1)} %add_convert_fusion.3), channel_id=1, source_target_pairs={{0,4},{4,0},{8,12},{12,8},{1,5},{5,1},{9,13},{13,9},{2,6},{6,2},{1... | collective-permute-start | bytes 393224 | tf_op jit(solution)/shard_map/ppermute | solution.py:258
  73.7 2.2 %collective-permute-done.9 = bf16[2,256,256]{2,1,0:T(8,128)(2,1)S(1)} collective-permute-done((bf16[2,256,256]{2,1,0:T(8,128)(2,1)S(1)}, bf16[2,256,256]{2,1,0:T(8,128)(2,1)S(1)}, u32[]{:S(2)}, u32[]{:S(2)}) %collective-permute-start.9) | collective-permute-done | bytes 262176 | tf_op jit(solution)/shard_map/ppermute | solution.py:258
  77.3 1.6 %collective-permute-start.22 = (bf16[512,256]{1,0:T(8,128)(2,1)S(1)}, bf16[512,256]{1,0:T(8,128)(2,1)}, u32[]{:S(2)}, u32[]{:S(2)}) collective-permute-start(bf16[512,256]{1,0:T(8,128)(2,1)S(1)} %maximum_select_fusion.2), channel_id=1, source_target_pairs={{0,2},{2,0},{1,3},{3,1},{4,6},{6,4},{5,7},{7,5},{8,10},{10,8},{9,1... | collective-permute-start | bytes 786440 | tf_op jit(solution)/shard_map/ppermute | solution.py:258
  83.0 1.9 %collective-permute-done.22 = bf16[512,256]{1,0:T(8,128)(2,1)} collective-permute-done((bf16[512,256]{1,0:T(8,128)(2,1)S(1)}, bf16[512,256]{1,0:T(8,128)(2,1)}, u32[]{:S(2)}, u32[]{:S(2)}) %collective-permute-start.22) | collective-permute-done | bytes 262176 | tf_op jit(solution)/shard_map/ppermute | solution.py:258
  (91 shorter events, 23.7 us)
Async XLA Ops:
  0.6 2.9 %collective-permute-start = (bf16[227,256]{1,0:T(8,128)(2,1)}, bf16[227,256]{1,0:T(8,128)(2,1)S(1)}, u32[]{:S(2)}, u32[]{:S(2)}) collective-permute-start(bf16[227,256]{1,0:T(8,128)(2,1)} %mine_ref.2), channel_id=1, source_target_pairs={{0,1},{1,0},{2,3},{3,2},{4,5},{5,4},{6,7},{7,6},{8,9},{9,8},{10,11... | collective-permute-start | bytes 348680 | tf_op jit(solution)/shard_map/ppermute | solution.py:258
  8.8 17.1 %collective-permute-start.2 = (bf16[2,256,512]{2,1,0:T(8,128)(2,1)}, bf16[2,256,512]{2,1,0:T(8,128)(2,1)S(1)}, u32[]{:S(2)}, u32[]{:S(2)}) collective-permute-start(bf16[2,256,512]{2,1,0:T(8,128)(2,1)} %get-tuple-element.34), channel_id=1, source_target_pairs={{0,4},{4,0},{8,12},{12,8},{1,5},{5,1},{9,13},{13,9},{2,6},{6,2},{1... | collective-permute-start | bytes 1572872 | tf_op jit(solution)/shard_map/ppermute | solution.py:258
  11.4 15.0 %collective-permute-start.3 = (bf16[2,256,512]{2,1,0:T(8,128)(2,1)}, bf16[2,256,512]{2,1,0:T(8,128)(2,1)S(1)}, u32[]{:S(2)}, u32[]{:S(2)}) collective-permute-start(bf16[2,256,512]{2,1,0:T(8,128)(2,1)} %get-tuple-element.35), channel_id=1, source_target_pairs={{0,0},{4,8},{8,4},{12,12},{1,1},{5,9},{9,5},{13,13},{2,2},{6,10},{... | collective-permute-start | bytes 1572872 | tf_op jit(solution)/shard_map/ppermute | solution.py:258
  18.2 11.8 %collective-permute-start.14 = (bf16[2,256,256]{2,1,0:T(8,128)(2,1)}, bf16[2,256,256]{2,1,0:T(8,128)(2,1)}, u32[]{:S(2)}, u32[]{:S(2)}) collective-permute-start(bf16[2,256,256]{2,1,0:T(8,128)(2,1)} %get-tuple-element.41), channel_id=1, source_target_pairs={{0,4},{4,0},{8,12},{12,8},{1,5},{5,1},{9,13},{13,9},{2,6},{6,2},{1... | collective-permute-start | bytes 786440 | tf_op jit(solution)/shard_map/ppermute | solution.py:258
  21.5 8.4 %collective-permute-start.15 = (bf16[2,256,256]{2,1,0:T(8,128)(2,1)}, bf16[2,256,256]{2,1,0:T(8,128)(2,1)}, u32[]{:S(2)}, u32[]{:S(2)}) collective-permute-start(bf16[2,256,256]{2,1,0:T(8,128)(2,1)} %get-tuple-element.42), channel_id=1, source_target_pairs={{0,0},{4,8},{8,4},{12,12},{1,1},{5,9},{9,5},{13,13},{2,2},{6,10},{... | collective-permute-start | bytes 786440 | tf_op jit(solution)/shard_map/ppermute | solution.py:258
  25.1 12.5 %collective-permute-start.5 = (bf16[512,256]{1,0:T(8,128)(2,1)}, bf16[512,256]{1,0:T(8,128)(2,1)}, u32[]{:S(2)}, u32[]{:S(2)}) collective-permute-start(bf16[512,256]{1,0:T(8,128)(2,1)} %param.15), channel_id=1, source_target_pairs={{0,1},{1,0},{2,3},{3,2},{4,5},{5,4},{6,7},{7,6},{8,9},{9,8},{10,11... | collective-permute-start | bytes 786440 | tf_op jit(solution)/shard_map/ppermute | solution.py:258
  25.9 7.4 %collective-permute-start.1 = (bf16[256,227]{1,0:T(8,128)(2,1)}, bf16[256,227]{1,0:T(8,128)(2,1)S(1)}, u32[]{:S(2)}, u32[]{:S(2)}) collective-permute-start(bf16[256,227]{1,0:T(8,128)(2,1)} %copy.17), channel_id=1, source_target_pairs={{0,1},{1,0},{2,3},{3,2},{4,5},{5,4},{6,7},{7,6},{8,9},{9,8},{10,11... | collective-permute-start | bytes 348680 | tf_op jit(solution)/shard_map/ppermute | solution.py:258
  26.4 11.2 %collective-permute-start.6 = (bf16[512,256]{1,0:T(8,128)(2,1)S(1)}, bf16[512,256]{1,0:T(8,128)(2,1)}, u32[]{:S(2)}, u32[]{:S(2)}) collective-permute-start(bf16[512,256]{1,0:T(8,128)(2,1)S(1)} %copy-done.7), channel_id=1, source_target_pairs={{0,1},{1,0},{2,3},{3,2},{4,5},{5,4},{6,7},{7,6},{8,9},{9,8},{10,11... | collective-permute-start | bytes 786440 | tf_op jit(solution)/shard_map/ppermute | solution.py:258
  29.9 7.7 %collective-permute-start.7 = (bf16[256,512]{1,0:T(8,128)(2,1)}, bf16[256,512]{1,0:T(8,128)(2,1)}, u32[]{:S(2)}, u32[]{:S(2)}) collective-permute-start(bf16[256,512]{1,0:T(8,128)(2,1)} %down_ref.3), channel_id=1, source_target_pairs={{0,1},{1,0},{2,3},{3,2},{4,5},{5,4},{6,7},{7,6},{8,9},{9,8},{10,11... | collective-permute-start | bytes 786440 | tf_op jit(solution)/shard_map/ppermute | solution.py:258
  29.9 9.4 %collective-permute-start.4 = (bf16[256,512]{1,0:T(8,128)(2,1)}, bf16[256,512]{1,0:T(8,128)(2,1)}, u32[]{:S(2)}, u32[]{:S(2)}) collective-permute-start(bf16[256,512]{1,0:T(8,128)(2,1)} %fusion), channel_id=1, source_target_pairs={{0,2},{2,0},{1,3},{3,1},{4,6},{6,4},{5,7},{7,5},{8,10},{10,8},{9,1... | collective-permute-start | bytes 786440 | tf_op jit(solution)/shard_map/ppermute | solution.py:388
  33.3 8.5 %collective-permute-start.16 = (bf16[256,256]{1,0:T(8,128)(2,1)}, bf16[256,256]{1,0:T(8,128)(2,1)}, u32[]{:S(2)}, u32[]{:S(2)}) collective-permute-start(bf16[256,256]{1,0:T(8,128)(2,1)} %fusion.8), channel_id=1, source_target_pairs={{0,2},{2,0},{1,3},{3,1},{4,6},{6,4},{5,7},{7,5},{8,10},{10,8},{9,1... | collective-permute-start | bytes 393224 | tf_op jit(solution)/shard_map/ppermute | solution.py:388
  45.1 1.9 %collective-permute-start.17 = (bf16[1024,256]{1,0:T(8,128)(2,1)S(1)}, bf16[1024,256]{1,0:T(8,128)(2,1)S(1)}, u32[]{:S(2)}, u32[]{:S(2)}) collective-permute-start(bf16[1024,256]{1,0:T(8,128)(2,1)S(1)} %get-tuple-element.50), channel_id=1, source_target_pairs={{0,1},{1,0},{2,3},{3,2},{4,5},{5,4},{6,7},{7,6},{8,9},{9,8},{10,11... | collective-permute-start | bytes 1572872 | tf_op jit(solution)/shard_map/ppermute | solution.py:258
  47.2 8.4 %collective-permute-start.18 = (bf16[512,256]{1,0:T(8,128)(2,1)S(1)}, bf16[512,256]{1,0:T(8,128)(2,1)S(1)}, u32[]{:S(2)}, u32[]{:S(2)}) collective-permute-start(bf16[512,256]{1,0:T(8,128)(2,1)S(1)} %constant_dynamic-slice_fusion.1), channel_id=1, source_target_pairs={{0,2},{2,0},{1,3},{3,1},{4,6},{6,4},{5,7},{7,5},{8,10},{10,8},{9,1... | collective-permute-start | bytes 786440 | tf_op jit(solution)/shard_map/ppermute | solution.py:258
  55.7 7.9 %collective-permute-start.19 = (bf16[256,256]{1,0:T(8,128)(2,1)S(1)}, bf16[256,256]{1,0:T(8,128)(2,1)S(1)}, u32[]{:S(2)}, u32[]{:S(2)}) collective-permute-start(bf16[256,256]{1,0:T(8,128)(2,1)S(1)} %constant_dynamic-slice_fusion), channel_id=1, source_target_pairs={{0,4},{4,0},{8,12},{12,8},{1,5},{5,1},{9,13},{13,9},{2,6},{6,2},{1... | collective-permute-start | bytes 393224 | tf_op jit(solution)/shard_map/ppermute | solution.py:258
  60.7 6.0 %collective-permute-start.8 = (bf16[256,256]{1,0:T(8,128)(2,1)S(1)}, bf16[256,256]{1,0:T(8,128)(2,1)S(1)}, u32[]{:S(2)}, u32[]{:S(2)}) collective-permute-start(bf16[256,256]{1,0:T(8,128)(2,1)S(1)} %copy-done.13), channel_id=1, source_target_pairs={{2,0},{0,2},{3,1},{1,3},{6,4},{4,6},{7,5},{5,7},{10,8},{8,10},{11,... | collective-permute-start | bytes 393224 | tf_op jit(solution)/shard_map/ppermute | solution.py:414
  63.7 7.0 %collective-permute-start.20 = (bf16[256,256]{1,0:T(8,128)(2,1)S(1)}, bf16[256,256]{1,0:T(8,128)(2,1)S(1)}, u32[]{:S(2)}, u32[]{:S(2)}) collective-permute-start(bf16[256,256]{1,0:T(8,128)(2,1)S(1)} %add_convert_fusion.4), channel_id=1, source_target_pairs={{0,8},{4,12},{8,0},{12,4},{1,9},{5,13},{9,1},{13,5},{2,10},{6,14},... | collective-permute-start | bytes 393224 | tf_op jit(solution)/shard_map/ppermute | solution.py:258
  66.7 9.1 %collective-permute-start.9 = (bf16[2,256,256]{2,1,0:T(8,128)(2,1)S(1)}, bf16[2,256,256]{2,1,0:T(8,128)(2,1)S(1)}, u32[]{:S(2)}, u32[]{:S(2)}) collective-permute-start(bf16[2,256,256]{2,1,0:T(8,128)(2,1)S(1)} %pad_maximum_fusion), channel_id=1, source_target_pairs={{0,4},{4,0},{8,12},{12,8},{1,5},{5,1},{9,13},{13,9},{2,6},{6,2},{1... | collective-permute-start | bytes 786440 | tf_op jit(solution)/shard_map/ppermute | solution.py:258
  66.8 9.0 %collective-permute-start.10 = (bf16[2,256,256]{2,1,0:T(8,128)(2,1)S(1)}, bf16[2,256,256]{2,1,0:T(8,128)(2,1)S(1)}, u32[]{:S(2)}, u32[]{:S(2)}) collective-permute-start(bf16[2,256,256]{2,1,0:T(8,128)(2,1)S(1)} %pad_maximum_fusion), channel_id=1, source_target_pairs={{0,0},{4,8},{8,4},{12,12},{1,1},{5,9},{9,5},{13,13},{2,2},{6,10},{... | collective-permute-start | bytes 786440 | tf_op jit(solution)/shard_map/ppermute | solution.py:258
  70.7 6.6 %collective-permute-start.21 = (bf16[256,256]{1,0:T(8,128)(2,1)S(1)}, bf16[256,256]{1,0:T(8,128)(2,1)S(1)}, u32[]{:S(2)}, u32[]{:S(2)}) collective-permute-start(bf16[256,256]{1,0:T(8,128)(2,1)S(1)} %add_convert_fusion.3), channel_id=1, source_target_pairs={{0,4},{4,0},{8,12},{12,8},{1,5},{5,1},{9,13},{13,9},{2,6},{6,2},{1... | collective-permute-start | bytes 393224 | tf_op jit(solution)/shard_map/ppermute | solution.py:258
  73.2 5.7 %collective-permute-start.23 = (f32[256,256]{1,0:T(8,128)}, f32[256,256]{1,0:T(8,128)}, u32[]{:S(2)}, u32[]{:S(2)}) collective-permute-start(f32[256,256]{1,0:T(8,128)} %get-tuple-element.52), channel_id=1, source_target_pairs={{0,1},{1,0},{2,3},{3,2},{4,5},{5,4},{6,7},{7,6},{8,9},{9,8},{10,11... | collective-permute-start | bytes 786440 | tf_op jit(solution)/shard_map/ppermute | solution.py:258
  73.2 7.8 %collective-permute-start.11 = (bf16[2,256,256]{2,1,0:T(8,128)(2,1)S(1)}, bf16[2,256,256]{2,1,0:T(8,128)(2,1)S(1)}, u32[]{:S(2)}, u32[]{:S(2)}) collective-permute-start(bf16[2,256,256]{2,1,0:T(8,128)(2,1)S(1)} %pad_maximum_fusion), channel_id=1, source_target_pairs={{0,1},{1,0},{2,3},{3,2},{4,5},{5,4},{6,7},{7,6},{8,9},{9,8},{10,11... | collective-permute-start | bytes 786440 | tf_op jit(solution)/shard_map/ppermute | solution.py:258
  75.8 5.1 %collective-permute-start.12 = (bf16[2,256,256]{2,1,0:T(8,128)(2,1)S(1)}, bf16[2,256,256]{2,1,0:T(8,128)(2,1)S(1)}, u32[]{:S(2)}, u32[]{:S(2)}) collective-permute-start(bf16[2,256,256]{2,1,0:T(8,128)(2,1)S(1)} %collective-permute-done.9), channel_id=1, source_target_pairs={{0,1},{1,0},{2,3},{3,2},{4,5},{5,4},{6,7},{7,6},{8,9},{9,8},{10,11... | collective-permute-start | bytes 786440 | tf_op jit(solution)/shard_map/ppermute | solution.py:258
  75.8 5.1 %collective-permute-start.13 = (bf16[2,256,256]{2,1,0:T(8,128)(2,1)S(1)}, bf16[2,256,256]{2,1,0:T(8,128)(2,1)S(1)}, u32[]{:S(2)}, u32[]{:S(2)}) collective-permute-start(bf16[2,256,256]{2,1,0:T(8,128)(2,1)S(1)} %collective-permute-done.10), channel_id=1, source_target_pairs={{0,1},{1,0},{2,3},{3,2},{4,5},{5,4},{6,7},{7,6},{8,9},{9,8},{10,11... | collective-permute-start | bytes 786440 | tf_op jit(solution)/shard_map/ppermute | solution.py:258
  77.3 7.5 %collective-permute-start.22 = (bf16[512,256]{1,0:T(8,128)(2,1)S(1)}, bf16[512,256]{1,0:T(8,128)(2,1)}, u32[]{:S(2)}, u32[]{:S(2)}) collective-permute-start(bf16[512,256]{1,0:T(8,128)(2,1)S(1)} %maximum_select_fusion.2), channel_id=1, source_target_pairs={{0,2},{2,0},{1,3},{3,1},{4,6},{6,4},{5,7},{7,5},{8,10},{10,8},{9,1... | collective-permute-start | bytes 786440 | tf_op jit(solution)/shard_map/ppermute | solution.py:258
  (18 other events, 53.0 us)

commit v2 on v1

v2 whole, which is shorter than its diff:
```python
import jax
import jax.numpy as jnp
from jax import lax
from jax.experimental import pallas as pl
from jax.experimental.pallas import tpu as pltpu
from jax.sharding import PartitionSpec as P

F32 = jnp.float32
BF16 = jnp.bfloat16
VMEM_BYTES = 20 * 1024 * 1024
STEPS = 4


def dot(left, right):
    return jnp.dot(left, right, preferred_element_type=F32)


def dot_rows(left, right):
    return lax.dot_general(left, right, (((0,), (0,)), ((), ())), preferred_element_type=F32)


def dot_last(left, right):
    return lax.dot_general(left, right, (((1,), (1,)), ((), ())), preferred_element_type=F32)


def sigmoid(values):
    return 0.5 * jnp.tanh(0.5 * values) + 0.5


def vmem():
    return pl.BlockSpec(memory_space=pltpu.VMEM)


def smem():
    return pl.BlockSpec(memory_space=pltpu.SMEM)


def anywhere():
    return pl.BlockSpec(memory_space=pl.ANY)


def whole(shape):
    return pl.BlockSpec(shape, lambda i: (0,) * len(shape))


def shape_of(shape, dtype):
    return jax.ShapeDtypeStruct(shape, dtype)


def call(kernel, name, in_specs, out_specs, out_shape, flops, nbytes, grid=(), scratch=(), exps=0):
    return pl.pallas_call(
        kernel,
        grid=grid,
        in_specs=in_specs,
        out_specs=out_specs,
        out_shape=out_shape,
        scratch_shapes=list(scratch),
        compiler_params=pltpu.CompilerParams(vmem_limit_bytes=VMEM_BYTES),
        cost_estimate=pl.CostEstimate(
            flops=int(flops), bytes_accessed=int(nbytes), transcendentals=int(exps)
        ),
        name=name,
    )


def node_half(tile, r):
    half = tile.shape[1] // 2
    return jnp.where(r == 0, tile[:, :half], tile[:, half:]).T


def entry_of(device_ref, slot_ref, b, slots):
    lon_count = lax.axis_size("lon")
    lat, lon = lax.axis_index("lat"), lax.axis_index("lon")
    target = device_ref[b]
    band = lax.div(target, lon_count)
    sector = target - band * lon_count - lon
    sector = jnp.where(sector < 0, sector + lon_count, sector)
    step = band - lat
    even_step = 1 - 2 * lax.rem(lat, 2)
    side = jnp.where(step == 0, 0, jnp.where(step == even_step, 1, 2))
    return (side * 2 + sector) * slots + slot_ref[b]


def write_packed(total, outs):
    per = total.shape[0] // 3
    for k, out in enumerate(outs):
        block = total[k * per : (k + 1) * per]
        out[...] = block.reshape(out.shape).astype(out.dtype)


def back_kernel(device_ref, slot_ref, after_ref, tiles_ref, cot_ref, own_ref, east_ref, side_ref, total):
    step = pl.program_id(0)
    count, rows = tiles_ref.shape[0], tiles_ref.shape[1]
    slots = total.shape[0] // 6
    channels = cot_ref.shape[0]
    r = lax.axis_index("rep")

    @pl.when(step == 0)
    def _():
        total[...] = jnp.zeros_like(total)

    for i in range(count):
        at = entry_of(device_ref, slot_ref, step * count + i, slots)
        cot = cot_ref[:, i * rows : (i + 1) * rows]
        total[at, :, :channels] += dot_last(node_half(tiles_ref[i], r), cot)

    @pl.when(step == pl.num_programs(0) - 1)
    def _():
        for k, out in ((0, own_ref), (2, side_ref.at[0]), (4, side_ref.at[1])):
            out[...] = total[k * slots : (k + 1) * slots].reshape(out.shape).astype(out.dtype)
        for k in range(3):
            block = total[(2 * k + 1) * slots : (2 * k + 2) * slots]
            east_ref[k] = block.reshape(east_ref.shape[1:]).astype(east_ref.dtype)


def encode_kernel(
    device_ref, slot_ref, after_ref, grid_ref, tiles_ref, weight_ref,
    own_ref, even_ref, odd_ref, hidden_ref, total, hold,
):
    step = pl.program_id(0)
    count, rows = tiles_ref.shape[0], tiles_ref.shape[1]
    slots = total.shape[0] // 6
    r = lax.axis_index("rep")

    @pl.when(step == 0)
    def _():
        total[...] = jnp.zeros_like(total)

    preact = dot_rows(grid_ref[...], weight_ref[...])
    hold[...] = (preact * sigmoid(preact)).astype(BF16)
    for i in range(count):
        at = entry_of(device_ref, slot_ref, step * count + i, slots)
        total[at] += dot(node_half(tiles_ref[i], r), hold[i * rows : (i + 1) * rows, :])

    half_steps = pl.num_programs(0) // 2

    @pl.when(step // half_steps == r)
    def _():
        at = pl.multiple_of((step % half_steps) * hold.shape[0], hold.shape[0])
        hidden_ref[pl.ds(at, hold.shape[0]), :] = hold[...]

    @pl.when(step == pl.num_programs(0) - 1)
    def _():
        write_packed(total, (own_ref, even_ref, odd_ref))


def local_kernel(own_ref, oth_ref, cot_ref, out_ref, out_other_ref, base_ref, grad_ref, grad_other_ref):
    rows = own_ref.shape[0]
    r = lax.axis_index("rep")
    cot = cot_ref[:, pl.ds(pl.multiple_of(r * rows, rows), rows)]
    base_ref[...] = dot_last(out_ref[...], own_ref[...]) + dot_last(out_other_ref[...], oth_ref[...])
    grad_ref[...] = dot(cot, own_ref[...])
    grad_other_ref[...] = dot(cot, oth_ref[...])


def added(*values):
    total = values[0].astype(F32)
    for value in values[1:]:
        total = total + value.astype(F32)
    return total


def add_kernel(*refs):
    a, b, c, out = refs[-4:]
    out[...] = added(a[0], b[0], c[0]).astype(out.dtype)


def sides_kernel(after_ref, side_ref, moved_ref, even_ref, odd_ref):
    even_ref[...] = added(side_ref[0], moved_ref[1]).astype(even_ref.dtype)
    odd_ref[...] = added(side_ref[1], moved_ref[2]).astype(odd_ref.dtype)


def update_kernel(
    own_a, even_a, odd_a, moved_a, own_b, even_b, odd_b, moved_b, embed_ref, embed_other_ref,
    up_ref, up_other_ref, down_ref, down_other_ref, out_ref, out_other_ref,
    proj_ref, mesh_ref, norm_ref, inv_ref, pre_ref, act_ref,
):
    r = lax.axis_index("rep")
    nodes, width = moved_a.shape
    channels = out_ref.shape[0]
    first = pl.multiple_of(r * width, width)
    second = pl.multiple_of((1 - r) * width, width)
    states = []
    for embed, parts in (
        (embed_ref, (own_a[0], even_a[0], odd_a[0], moved_a[...])),
        (embed_other_ref, (own_b[0], even_b[0], odd_b[0], moved_b[...])),
    ):
        start = embed[:, r].reshape(nodes, width)
        states.append((start.astype(F32) + added(*parts)).astype(BF16).astype(F32))
    state = jnp.concatenate(states, axis=1)
    centered = state - jnp.mean(state, axis=-1, keepdims=True)
    inverse = lax.rsqrt(jnp.mean(centered * centered, axis=-1, keepdims=True) + 1e-05)
    norm = centered * inverse
    normed = norm.astype(BF16)
    norm_ref[...] = norm
    inv_ref[...] = jnp.broadcast_to(inverse, inv_ref.shape)
    update_own = jnp.zeros((nodes, width), F32)
    update_oth = jnp.zeros((nodes, width), F32)
    for k, (u_ref, d_ref) in enumerate(((up_ref, down_ref), (up_other_ref, down_other_ref))):
        hidden = dot(normed[:, :width], u_ref[pl.ds(first, width), :]) + dot(
            normed[:, width:], u_ref[pl.ds(second, width), :]
        )
        act = (hidden * sigmoid(hidden)).astype(BF16)
        pre_ref[:, k * width : (k + 1) * width] = hidden
        act_ref[:, k * width : (k + 1) * width] = act
        update_own += dot(act, d_ref[:, pl.ds(first, width)])
        update_oth += dot(act, d_ref[:, pl.ds(second, width)])
    mesh = (state + jnp.concatenate([update_own, update_oth], axis=1)).astype(BF16)
    mesh_ref[...] = mesh
    proj = dot_last(mesh[:, :width], out_ref[...]) + dot_last(mesh[:, width:], out_other_ref[...])
    proj_ref[...] = jnp.zeros_like(proj_ref)
    proj_ref[:, :channels] = proj.astype(BF16)


def outer_kernel(
    own_ref, moved_ref, even_ref, odd_ref, local_ref, local_other_ref, mesh_ref, act_ref,
    cot_ref, keep_ref, give_ref,
):
    width = keep_ref.shape[1]
    channels = local_ref.shape[0]
    cot = added(own_ref[...], moved_ref[0], even_ref[...], odd_ref[...]).astype(BF16)
    cot_ref[...] = cot
    act, mesh = act_ref[...], mesh_ref[...]
    for k, (out, local) in enumerate(((keep_ref, local_ref), (give_ref, local_other_ref))):
        cols = slice(k * width, (k + 1) * width)
        out[:width, :] = dot_rows(act[:, cols], cot).astype(out.dtype)
        grad = dot_rows(cot, mesh[:, cols])
        out[width:, :] = grad.astype(out.dtype)
        out[width : width + channels, :] = (grad[:channels] + local[...]).astype(out.dtype)


def grads_kernel(
    cot_ref, norm_ref, pre_ref, down_ref, down_other_ref, out_ref, out_other_ref,
    grad_ref, pre_grad_ref, keep_ref, give_ref,
):
    r = lax.axis_index("rep")
    width = keep_ref.shape[1]
    channels = out_ref.shape[0]
    first = pl.multiple_of(r * width, width)
    second = pl.multiple_of((1 - r) * width, width)
    cot = cot_ref[:, :channels]
    grad_own = dot(cot, out_ref[...]).astype(BF16)
    grad_oth = dot(cot, out_other_ref[...]).astype(BF16)
    grad_ref[:, :width] = grad_own
    grad_ref[:, width:] = grad_oth
    normed = norm_ref[...].astype(BF16)
    for k, (d_ref, o_ref) in enumerate(((down_ref, keep_ref), (down_other_ref, give_ref))):
        cols = slice(k * width, (k + 1) * width)
        hidden = pre_ref[:, cols]
        act_grad = dot_last(grad_own, d_ref[:, pl.ds(first, width)]) + dot_last(
            grad_oth, d_ref[:, pl.ds(second, width)]
        )
        squash = sigmoid(hidden)
        pre_grad = (act_grad * squash * (1.0 + hidden * (1.0 - squash))).astype(BF16)
        pre_grad_ref[:, cols] = pre_grad
        o_ref[pl.ds(first, width), :] = dot_rows(normed[:, :width], pre_grad).astype(o_ref.dtype)
        o_ref[pl.ds(second, width), :] = dot_rows(normed[:, width:], pre_grad).astype(o_ref.dtype)


def mesh_kernel(
    grad_ref, pre_grad_ref, norm_ref, inv_ref, up_ref, up_other_ref, keep_ref, give_ref,
):
    r = lax.axis_index("rep")
    width = keep_ref.shape[1]
    first = pl.multiple_of(r * width, width)
    second = pl.multiple_of((1 - r) * width, width)
    halves = []
    for at in (first, second):
        halves.append(
            dot_last(pre_grad_ref[:, :width], up_ref[pl.ds(at, width), :])
            + dot_last(pre_grad_ref[:, width:], up_other_ref[pl.ds(at, width), :])
        )
    back = jnp.concatenate(halves, axis=1)
    norm = norm_ref[...]
    centered = (
        back - jnp.mean(back, axis=-1, keepdims=True)
        - norm * jnp.mean(back * norm, axis=-1, keepdims=True)
    )
    total = grad_ref[...].astype(F32) + inv_ref[:, :1] * centered
    keep_ref[...] = total[:, :width]
    give_ref[...] = total[:, width:].astype(give_ref.dtype)


def place_kernel(keep_ref, got_ref, out_ref):
    r = lax.axis_index("rep")
    part = out_ref.shape[:1] + out_ref.shape[2:]
    out_ref[:, r] = keep_ref[...].reshape(part)
    out_ref[:, 1 - r] = got_ref[...].astype(F32).reshape(part)


def finish_outer_kernel(mine_ref, other_ref, out_ref, out_other_ref, down_ref, grad_ref):
    r = lax.axis_index("rep")
    bit = lax.rem(lax.axis_index("lon"), 2)
    width = mine_ref.shape[1]
    channels = out_ref.shape[0]
    mine, other = mine_ref[...], other_ref[...]
    terms = jnp.where(bit == 0, mine, other)[:, :channels]
    down_ref[:, pl.ds(pl.multiple_of(r * width, width), width)] = dot(terms, out_ref[...])
    down_ref[:, pl.ds(pl.multiple_of((1 - r) * width, width), width)] = dot(
        terms, out_other_ref[...]
    )
    grad_ref[...] = jnp.where(bit == 0, other, mine)[:channels].astype(F32)


def finish_up_kernel(mine_ref, other_ref, out_ref):
    bit = lax.rem(lax.axis_index("lon"), 2)
    rows = mine_ref.shape[0]
    out_ref[pl.ds(pl.multiple_of(bit * rows, rows), rows), :] = mine_ref[...].astype(F32)
    out_ref[pl.ds(pl.multiple_of((1 - bit) * rows, rows), rows), :] = other_ref[...].astype(F32)


def decode_kernel(device_ref, slot_ref, tiles_ref, base_ref, *refs):
    mine, theirs, out_ref, picked = refs[:3], refs[3:6], refs[6], refs[7]
    r = lax.axis_index("rep")
    count, rows = tiles_ref.shape[0], tiles_ref.shape[1]
    half = rows // 2
    channels = out_ref.shape[0]
    blocks = count // 2
    per = mine[0].shape[0]
    for i in range(blocks):
        at = entry_of(device_ref, slot_ref, r * blocks + i, per // 2)
        for k in range(3):
            @pl.when(at // per == k)
            def _(k=k, i=i, at=at):
                where = at - k * per
                picked[i, pl.ds(pl.multiple_of(r * half, half), half), :] = mine[k][where]
                picked[i, pl.ds(pl.multiple_of((1 - r) * half, half), half), :] = theirs[k][where]
    for i in range(blocks):
        cols = slice(i * rows, (i + 1) * rows)
        decoded = dot_last(picked[i].T, tiles_ref[r * blocks + i])
        out_ref[:, cols] = (base_ref[:, cols] + decoded[:channels]).astype(out_ref.dtype)


def along(axis, count, partner):
    pairs = []
    for source in range(count):
        to = partner(source)
        pairs.append((source, to if 0 <= to < count else source))
    return lambda value: lax.ppermute(value, axis, pairs)


def summed_over(value, order):
    held = []
    for axis, distance, halve in order:
        count = lax.axis_size(axis)
        swap = along(axis, count, lambda i, d=distance: i ^ d)
        if not halve:
            value = (value.astype(F32) + swap(value).astype(F32)).astype(BF16)
            continue
        bit = (lax.axis_index(axis) // distance) % 2
        rows = value.shape[0] // 2
        keep = lax.dynamic_slice_in_dim(value, bit * rows, rows, 0)
        give = lax.dynamic_slice_in_dim(value, (1 - bit) * rows, rows, 0)
        value = (keep.astype(F32) + swap(give).astype(F32)).astype(BF16)
        held.append((swap, bit))
    for swap, bit in reversed(held[1:]):
        other = swap(value)
        value = jnp.where(
            bit == 0,
            jnp.concatenate([value, other], axis=0),
            jnp.concatenate([other, value], axis=0),
        )
    return value, held[0][0](value)


def distances(count):
    found, distance = [], 1
    while distance < count:
        found.append(distance)
        distance *= 2
    return found


def per_device(
    grid_in, w_embed, interp_tiles, route_device, route_slot,
    mesh_embed, w_up, w_down, w_out, cotangent,
):
    lat_count, lon_count = lax.axis_size("lat"), lax.axis_size("lon")
    blocks, tile_rows = interp_tiles.shape[:2]
    grid_rows, channels = grid_in.shape
    my_rows = grid_rows // 2
    width = w_embed.shape[1]
    latent = 2 * width
    padded = -(-channels // 128) * 128
    slots = mesh_embed.shape[0] // tile_rows
    half = tile_rows // 2
    nodes = slots * half

    swap_rep = along("rep", 2, lambda i: 1 - i)
    to_even = along("lat", lat_count, lambda i: i ^ 1)
    to_odd = along("lat", lat_count, lambda i: ((i + 1) ^ 1) - 1)
    east_pairs = [(i, (i + 1) % lon_count) for i in range(lon_count)]
    west_pairs = [(j, i) for i, j in east_pairs]
    to_east = lambda value: lax.ppermute(value, "lon", east_pairs)

    device = route_device.reshape(blocks)
    grid_t, cot_t, out_t = grid_in.T, cotangent.T, w_out.T
    per_step = blocks // STEPS
    step_rows = per_step * tile_rows
    tiles_spec = pl.BlockSpec((per_step, tile_rows, tile_rows), lambda i: (i, 0, 0))
    cols_spec = pl.BlockSpec((channels, step_rows), lambda i: (0, i))
    pair_shape = (2, nodes, width)

    embed_other = swap_rep(w_embed)

    def encode(after, weight):
        return call(
            encode_kernel, "encode",
            [smem(), smem(), anywhere(), cols_spec, tiles_spec, whole((channels, width))],
            [whole(pair_shape)] * 3 + [whole((my_rows, width))],
            [shape_of(pair_shape, BF16)] * 3 + [shape_of((my_rows, width), BF16)],
            2 * grid_rows * width * (channels + half), 3e6, grid=(STEPS,), exps=grid_rows * width,
            scratch=[
                pltpu.VMEM((6 * slots, half, width), F32),
                pltpu.VMEM((step_rows, width), BF16),
            ],
        )(device, route_slot, after, grid_t, interp_tiles, weight)

    own_a, even_a, odd_a, hidden_a = encode(w_embed, w_embed)
    even_in_a, odd_in_a = to_even(even_a), to_odd(odd_a)

    back_own, back_east, back_side = call(
        back_kernel, "back_messages",
        [smem(), smem(), anywhere(), tiles_spec, cols_spec],
        [whole((nodes, padded)), whole((3, nodes, padded)), whole((2, nodes, padded))],
        [shape_of((nodes, padded), BF16), shape_of((3, nodes, padded), BF16),
         shape_of((2, nodes, padded), BF16)],
        2 * grid_rows * half * padded, 3e6, grid=(STEPS,),
        scratch=[pltpu.VMEM((6 * slots, half, padded), F32)],
    )(device, route_slot, odd_a, interp_tiles, cot_t)
    back_moved = to_east(back_east)

    own_b, even_b, odd_b, hidden_b = encode(back_own, embed_other)
    even_in_b, odd_in_b = to_even(even_b), to_odd(odd_b)

    out_other, up_other, down_other = swap_rep(out_t), swap_rep(w_up), swap_rep(w_down)
    embed_shape = (slots, 2, half, width)
    mesh_other = swap_rep(mesh_embed)

    base, local, local_other = call(
        local_kernel, "local_terms", [vmem()] * 5, [vmem()] * 3,
        [shape_of((channels, my_rows), F32)] + [shape_of((channels, width), F32)] * 2,
        4 * my_rows * latent * channels, 4e6,
    )(hidden_a, hidden_b, cot_t, out_t, out_other)

    second = pl.BlockSpec((1, nodes, width), lambda i: (1, 0, 0))

    def add_east(after, *terms):
        return call(
            add_kernel, "add_east", [anywhere()] + [second] * 3, whole((nodes, width)),
            shape_of((nodes, width), BF16), 3 * nodes * width, 6e5, grid=(1,),
        )(after, *terms)

    send_a = add_east(own_b, own_a, even_in_a, odd_in_a)
    moved_a = to_east(send_a)
    send_b = add_east(send_a, own_b, even_in_b, odd_in_b)
    moved_b = to_east(send_b)

    back_even, back_odd = call(
        sides_kernel, "add_sides", [anywhere(), vmem(), vmem()], [vmem()] * 2,
        [shape_of((nodes, padded), BF16)] * 2, 3 * nodes * width, 1e6,
    )(send_b, back_side, back_moved)
    back_even_in, back_odd_in = to_even(back_even), to_odd(back_odd)

    first = pl.BlockSpec((1, nodes, width), lambda i: (0, 0, 0))
    sums_specs = [first] * 3 + [whole((nodes, width))]
    weights = (w_up, up_other, w_down, down_other, out_t, out_other)
    update_shapes = [
        ((nodes, padded), BF16), ((nodes, latent), BF16), ((nodes, latent), F32),
        ((nodes, 128), F32), ((nodes, latent), F32), ((nodes, latent), BF16),
    ]
    proj, mesh_out, norm, inverse, hidden_pre, hidden_act = call(
        update_kernel, "node_update",
        sums_specs * 2 + [whole(embed_shape)] * 2 + [whole(w.shape) for w in weights],
        [whole(s) for s, _ in update_shapes],
        [shape_of(s, d) for s, d in update_shapes],
        5 * nodes * latent * latent, 4e6, grid=(1,), exps=nodes * latent,
    )(
        own_a, even_in_a, odd_in_a, moved_a, own_b, even_in_b, odd_in_b, moved_b,
        mesh_embed.reshape(embed_shape), mesh_other.reshape(embed_shape), *weights,
    )

    east = lax.ppermute(proj, "lon", west_pairs)
    pair = jnp.stack([proj, east])
    pair_even, pair_odd = to_even(pair), to_odd(pair)

    cot_mesh, keep_outer, give_outer = call(
        outer_kernel, "outer_grads", [vmem()] * 8, [vmem()] * 3,
        [shape_of((nodes, padded), BF16), shape_of((latent, width), F32),
         shape_of((latent, width), BF16)],
        4 * nodes * latent * padded, 3e6,
    )(back_own, back_moved, back_even_in, back_odd_in, local, local_other, mesh_out, hidden_act)
    got_outer = swap_rep(give_outer)

    grad_nodes, pre_grad, keep_up, give_up = call(
        grads_kernel, "up_grads", [vmem()] * 7, [vmem()] * 4,
        [shape_of((nodes, latent), BF16), shape_of((nodes, latent), BF16),
         shape_of((latent, width), F32), shape_of((latent, width), BF16)],
        5 * nodes * latent * latent, 4e6, exps=nodes * latent,
    )(cot_mesh, norm, hidden_pre, w_down, down_other, out_t, out_other)
    got_up = swap_rep(give_up)

    order = [("lon", d, True) for d in distances(lon_count)]
    order += [("lat", d, d == 1) for d in distances(lat_count)]
    outer_mine, outer_theirs = summed_over((keep_outer + got_outer.astype(F32)).astype(BF16), order)
    up_mine, up_theirs = summed_over((keep_up + got_up.astype(F32)).astype(BF16), order)

    mesh_keep, mesh_give = call(
        mesh_kernel, "mesh_grads", [vmem()] * 6, [vmem()] * 2,
        [shape_of((nodes, width), F32), shape_of((nodes, width), BF16)],
        2 * nodes * latent * latent, 3e6,
    )(grad_nodes, pre_grad, norm, inverse, w_up, up_other)
    grad_mesh = call(
        place_kernel, "place_mesh", [vmem()] * 2, vmem(), shape_of(embed_shape, F32),
        nodes * latent, 1e6,
    )(mesh_keep, swap_rep(mesh_give)).reshape(mesh_embed.shape)

    tables = (pair, pair_even, pair_odd)
    table_shape = (2 * slots, half, padded)
    grid_out = call(
        decode_kernel, "decode", [smem(), smem()] + [vmem()] * 8, vmem(),
        shape_of((channels, my_rows), BF16), 2 * my_rows * tile_rows * padded, 4e6,
        scratch=[pltpu.VMEM((blocks // 2, tile_rows, padded), BF16)],
    )(
        device, route_slot, interp_tiles, base,
        *[table.reshape(table_shape) for table in tables],
        *[swap_rep(table).reshape(table_shape) for table in tables],
    ).T

    grad_down, grad_out = call(
        finish_outer_kernel, "finish_outer", [vmem()] * 4, [vmem()] * 2,
        [shape_of((width, latent), F32), shape_of((channels, width), F32)],
        2 * width * latent * channels, 1e6,
    )(outer_mine, outer_theirs, out_t, out_other)
    grad_up = call(
        finish_up_kernel, "finish_up", [vmem()] * 2, vmem(), shape_of((latent, width), F32),
        latent * width, 8e5,
    )(up_mine, up_theirs)
    return (grid_out, grad_out.T, grad_up, grad_down, grad_mesh)


def solution(mesh):
    patch = ("groups", "lat", "lon")
    placed = (
        P(patch, None),
        P(None, "rep"),
        P(patch, None, None),
        P(patch, None),
        P(patch),
        P(patch, "rep"),
        P(None, "rep"),
        P("rep", None),
        P("rep", None),
        P(patch, None),
    )
    return jax.shard_map(
        per_device,
        mesh=mesh,
        in_specs=placed,
        out_specs=(
            P(("groups", "lat", "lon", "rep"), None),
            P(("groups", "rep"), None),
            P("groups", "rep"),
            P(("groups", "rep"), None),
            P(patch, "rep"),
        ),
        check_vma=False,
    )
```

time: 89.4 us -> 104 us (1.16)
  waiting for transfers between devices: 22.4 us -> 37.6 us
  starting transfers between devices: 31.4 us -> 36.5 us
  other arithmetic: 6.2 us -> 2.29 us
  local copies, waits for them, and re-layouts: 12.1 us -> 8.39 us
  Pallas kernels: 14.7 us -> 17.6 us
  matrix products: 1.06 us -> 0 us
    ppermute x21 -> x29, waiting for transfers between devices: 20.7 us -> 35.6 us  [along(): return lambda value: lax.ppermute(value, axis, pairs)]
    ppermute x21 -> x29, starting transfers between devices: 27.9 us -> 30.8 us  [along(): return lambda value: lax.ppermute(value, axis, pairs)]
    pallas_call x6 -> x15, Pallas kernels: 14.7 us -> 17.6 us  [the longest x2 5.56 us: encode(): call(encode_kernel, 'encode', [smem(), smem(), anywhere(), cols_spec, til...]
    convert_element_type x5 -> x2, other arithmetic: 3.44 us -> 1.08 us  [the longest x1 1.02 us: per_device(): (keep_up + got_up.astype(F32)).astype(BF16)]
    ppermute x2 -> x3, starting transfers between devices: 2.03 us -> 4.2 us  [per_device(): to_east = lambda value: lax.ppermute(value, 'lon', east_pairs)]
    unnamed x41 -> x40, local copies, waits for them, and re-layouts: 10.5 us -> 8.32 us
    ppermute x1, waiting for transfers between devices: 0.01 us -> 1.7 us  [per_device(): east = lax.ppermute(proj, 'lon', west_pairs)]
    ppermute x2 -> x3, waiting for transfers between devices: 1.7 us -> 0.31 us  [per_device(): to_east = lambda value: lax.ppermute(value, 'lon', east_pairs)]
  transfers between devices with their start and end apart: 24 -> 33, of which waited for: 9 -> 14; matrix products, arithmetic and copies ran while one was open for 12% -> 2% of each run, Pallas kernels for 8% -> 14%
where the time goes in v2:
time: 104 us; the launch traced here: 103 us
  waiting for transfers between devices  37.6 us (36%)
  starting transfers between devices  36.5 us (35%)
  Pallas kernels  17.6 us (17%)
  local copies, waits for them, and re-layouts  8.39 us (8%)
  other arithmetic  2.29 us (2%)
    ppermute x29, waiting for transfers between devices, along(): return lambda value: lax.ppermute(value, axis, pairs)  35.6 us
    ppermute x29, starting transfers between devices, along(): return lambda value: lax.ppermute(value, axis, pairs)  30.8 us
    unnamed x40, local copies, waits for them, and re-layouts  8.32 us
    pallas_call x2, Pallas kernels, encode(): call(encode_kernel, 'encode', [smem(), smem(), anywhere(), cols_spec, til...  5.56 us
    ppermute x3, starting transfers between devices, per_device(): to_east = lambda value: lax.ppermute(value, 'lon', east_pairs)  4.2 us
    pallas_call x1, Pallas kernels, per_device(): call(back_kernel, 'back_messages', [smem(), smem(), anywhere(), tiles_spe...  2.38 us
  transfers between devices with their start and end apart: 33, of which 14 were waited for; matrix products, arithmetic and copies ran while one was open for 2% of the time, Pallas kernels for 14%

profile of v2, /device:TPU:0, one launch (start us, length us, event | category | flops | bytes accessed | tf_op | source)
XLA Modules:
  0.0 103.3 jit_solution(7900595941595871812)
XLA Ops:
  5.0 2.8 %encode.2 = (bf16[2,256,256]{2,1,0:T(8,128)(2,1)S(1)}, bf16[2,256,256]{2,1,0:T(8,128)(2,1)S(1)}, bf16[2,256,256]{2,1,0:T(8,128)(2,1)S(1)}, bf16[1024,256]{1,0:T(8,128)(2,1)S(1)}) custom-call(s32[16]{0:T(128)S(1)} %bitcast.34, s32[16]{0:T(128)S(1)} %copy-done.17, bf16[227,256]{1,0:T(8,128)(2,1)S(1)} %copy-done.10, bf16[227,2048]{1,0:T(8,128)(2,1)S(1)} %bitcast.17, ...), custom_call_target="tpu_custom_call" | custom-call | flops 305135616 | bytes 3000000 | tf_op jit(solution)/shard_map/encode/pallas_call | solution.py:407
  8.6 5.5 %collective-permute-start.2 = (bf16[2,256,256]{2,1,0:T(8,128)(2,1)S(1)}, bf16[2,256,256]{2,1,0:T(8,128)(2,1)S(1)}, u32[]{:S(2)}, u32[]{:S(2)}) collective-permute-start(bf16[2,256,256]{2,1,0:T(8,128)(2,1)S(1)} %get-tuple-element.44), channel_id=1, source_target_pairs={{0,4},{4,0},{8,12},{12,8},{1,5},{5,1},{9,13},{13,9},{2,6},{6,2},{1... | collective-permute-start | bytes 786440 | tf_op jit(solution)/shard_map/ppermute | solution.py:339
  14.0 2.4 %back_messages.1 = (bf16[256,256]{1,0:T(8,128)(2,1)S(1)}, bf16[3,256,256]{2,1,0:T(8,128)(2,1)S(1)}, bf16[2,256,256]{2,1,0:T(8,128)(2,1)S(1)}) custom-call(s32[16]{0:T(128)S(1)} %bitcast.35, s32[16]{0:T(128)S(1)} %copy-done.17, bf16[2,256,256]{2,1,0:T(8,128)(2,1)S(1)} %get-tuple-element.39.after_ref, bf16[16,128,128]{2,1,0:T(8,128)(2,1)S(1)} %copy-done.1, ...), custom_call_target="tpu_custom_call" | custom-call | flops 67108864 | bytes 3000000 | tf_op jit(solution)/shard_map/back_messages/pallas_call | solution.py:422
  16.5 2.8 %encode.3 = (bf16[2,256,256]{2,1,0:T(8,128)(2,1)S(1)}, bf16[2,256,256]{2,1,0:T(8,128)(2,1)S(1)}, bf16[2,256,256]{2,1,0:T(8,128)(2,1)S(1)}, bf16[1024,256]{1,0:T(8,128)(2,1)S(1)}) custom-call(s32[16]{0:T(128)S(1)} %bitcast.36, s32[16]{0:T(128)S(1)} %copy-done.17, bf16[256,256]{1,0:T(8,128)(2,1)S(1)} %get-tuple-element.40.after_ref.own_ref, ...), custom_call_target="tpu_custom_call" | custom-call | flops 305135616 | bytes 3000000 | tf_op jit(solution)/shard_map/encode/pallas_call | solution.py:407
  19.4 1.5 %collective-permute-start.17 = (bf16[3,256,256]{2,1,0:T(8,128)(2,1)S(1)}, bf16[3,256,256]{2,1,0:T(8,128)(2,1)S(1)}, u32[]{:S(2)}, u32[]{:S(2)}) collective-permute-start(bf16[3,256,256]{2,1,0:T(8,128)(2,1)S(1)} %get-tuple-element.49), channel_id=1, source_target_pairs={{0,2},{2,0},{1,3},{3,1},{4,6},{6,4},{5,7},{7,5},{8,10},{10,8},{9,1... | collective-permute-start | bytes 1179656 | tf_op jit(solution)/shard_map/ppermute | solution.py:394
  22.2 5.3 %collective-permute-done.5.refs_2_.even_b = bf16[2,256,256]{2,1,0:T(8,128)(2,1)S(1)} collective-permute-done((bf16[2,256,256]{2,1,0:T(8,128)(2,1)S(1)}, bf16[2,256,256]{2,1,0:T(8,128)(2,1)S(1)}, u32[]{:S(2)}, u32[]{:S(2)}) %collective-permute-start.5) | collective-permute-done | bytes 262176 | tf_op jit(solution)/shard_map/ppermute | solution.py:339
  29.2 1.5 %collective-permute-start.4 = (bf16[256,256]{1,0:T(8,128)(2,1)S(1)}, bf16[256,256]{1,0:T(8,128)(2,1)S(1)}, u32[]{:S(2)}, u32[]{:S(2)}) collective-permute-start(bf16[256,256]{1,0:T(8,128)(2,1)S(1)} %add_east.2.refs_0_), channel_id=1, source_target_pairs={{0,2},{2,0},{1,3},{3,1},{4,6},{6,4},{5,7},{7,5},{8,10},{10,8},{9,1... | collective-permute-start | bytes 393224 | tf_op jit(solution)/shard_map/ppermute | solution.py:394
  31.9 3.9 %collective-permute-start.18 = (bf16[256,256]{1,0:T(8,128)(2,1)S(1)}, bf16[256,256]{1,0:T(8,128)(2,1)S(1)}, u32[]{:S(2)}, u32[]{:S(2)}) collective-permute-start(bf16[256,256]{1,0:T(8,128)(2,1)S(1)} %get-tuple-element.51), channel_id=1, source_target_pairs={{0,4},{4,0},{8,12},{12,8},{1,5},{5,1},{9,13},{13,9},{2,6},{6,2},{1... | collective-permute-start | bytes 393224 | tf_op jit(solution)/shard_map/ppermute | solution.py:339
  37.6 1.7 %node_update.1 = (bf16[256,256]{1,0:T(8,128)(2,1)}, bf16[256,512]{1,0:T(8,128)(2,1)S(1)}, f32[256,512]{1,0:T(8,128)S(1)}, f32[256,128]{1,0:T(8,128)S(1)}, f32[25...) custom-call(bf16[2,256,256]{2,1,0:T(8,128)(2,1)S(1)} %get-tuple-element.43.refs_1_.own_a, ...), custom_call_target="tpu_custom_call" | custom-call | flops 335544320 | bytes 4000000 | tf_op jit(solution)/shard_map/node_update/pallas_call | solution.py:472
  40.6 1.5 %up_grads.1 = (bf16[256,512]{1,0:T(8,128)(2,1)S(1)}, bf16[256,512]{1,0:T(8,128)(2,1)S(1)}, f32[512,256]{1,0:T(8,128)S(1)}, bf16[512,256]{1,0:T(8,128)(2,1)}) custom-call(bf16[256,256]{1,0:T(8,128)(2,1)S(1)} %get-tuple-element.60.cot_ref, f32[256,512]{1,0:T(8,128)S(1)} %get-tuple-element.61.norm_ref, f32[256,512]{1,0:T(8,128)S(1)} %get-tuple-element.62.pre_ref, ...), custom_call_target="tpu_custom_call" | custom-call | flops 335544320 | bytes 4000000 | tf_op jit(solution)/shard_map/up_grads/pallas_call | solution.py:495
  48.2 1.7 %collective-permute-done.11 = bf16[256,256]{1,0:T(8,128)(2,1)} collective-permute-done((bf16[256,256]{1,0:T(8,128)(2,1)}, bf16[256,256]{1,0:T(8,128)(2,1)}, u32[]{:S(2)}, u32[]{:S(2)}) %collective-permute-start.11) | collective-permute-done | bytes 131104 | tf_op jit(solution)/shard_map/ppermute | solution.py:483
  50.9 4.5 %collective-permute-start.12 = (bf16[2,256,256]{2,1,0:T(8,128)(2,1)S(1)}, bf16[2,256,256]{2,1,0:T(8,128)(2,1)S(1)}, u32[]{:S(2)}, u32[]{:S(2)}) collective-permute-start(bf16[2,256,256]{2,1,0:T(8,128)(2,1)S(1)} %pad_maximum_fusion), channel_id=1, source_target_pairs={{0,4},{4,0},{8,12},{12,8},{1,5},{5,1},{9,13},{13,9},{2,6},{6,2},{1... | collective-permute-start | bytes 786440 | tf_op jit(solution)/shard_map/ppermute | solution.py:339
  57.9 3.7 %collective-permute-done.12 = bf16[2,256,256]{2,1,0:T(8,128)(2,1)S(1)} collective-permute-done((bf16[2,256,256]{2,1,0:T(8,128)(2,1)S(1)}, bf16[2,256,256]{2,1,0:T(8,128)(2,1)S(1)}, u32[]{:S(2)}, u32[]{:S(2)}) %collective-permute-start.12) | collective-permute-done | bytes 262176 | tf_op jit(solution)/shard_map/ppermute | solution.py:339
  63.3 3.3 %collective-permute-done.21 = bf16[256,256]{1,0:T(8,128)(2,1)S(1)} collective-permute-done((bf16[256,256]{1,0:T(8,128)(2,1)S(1)}, bf16[256,256]{1,0:T(8,128)(2,1)S(1)}, u32[]{:S(2)}, u32[]{:S(2)}) %collective-permute-start.21) | collective-permute-done | bytes 131104 | tf_op jit(solution)/shard_map/ppermute | solution.py:339
  66.6 1.7 %collective-permute-start.28 = (bf16[128,256]{1,0:T(8,128)(2,1)S(1)}, bf16[128,256]{1,0:T(8,128)(2,1)S(1)}, u32[]{:S(2)}, u32[]{:S(2)}) collective-permute-start(bf16[128,256]{1,0:T(8,128)(2,1)S(1)} %constant_dynamic-slice_fusion), channel_id=1, source_target_pairs={{0,4},{4,0},{8,12},{12,8},{1,5},{5,1},{9,13},{13,9},{2,6},{6,2},{1... | collective-permute-start | bytes 196616 | tf_op jit(solution)/shard_map/ppermute | solution.py:339
  68.4 3.0 %collective-permute-done.28 = bf16[128,256]{1,0:T(8,128)(2,1)S(1)} collective-permute-done((bf16[128,256]{1,0:T(8,128)(2,1)S(1)}, bf16[128,256]{1,0:T(8,128)(2,1)S(1)}, u32[]{:S(2)}, u32[]{:S(2)}) %collective-permute-start.28) | collective-permute-done | bytes 65568 | tf_op jit(solution)/shard_map/ppermute | solution.py:339
  71.4 1.9 %collective-permute-start.22 = (bf16[128,256]{1,0:T(8,128)(2,1)S(1)}, bf16[128,256]{1,0:T(8,128)(2,1)S(1)}, u32[]{:S(2)}, u32[]{:S(2)}) collective-permute-start(bf16[128,256]{1,0:T(8,128)(2,1)S(1)} %constant_dynamic-slice_fusion.2), channel_id=1, source_target_pairs={{0,4},{4,0},{8,12},{12,8},{1,5},{5,1},{9,13},{13,9},{2,6},{6,2},{1... | collective-permute-start | bytes 196616 | tf_op jit(solution)/shard_map/ppermute | solution.py:339
  73.3 3.1 %collective-permute-done.22 = bf16[128,256]{1,0:T(8,128)(2,1)S(1)} collective-permute-done((bf16[128,256]{1,0:T(8,128)(2,1)S(1)}, bf16[128,256]{1,0:T(8,128)(2,1)S(1)}, u32[]{:S(2)}, u32[]{:S(2)}) %collective-permute-start.22) | collective-permute-done | bytes 65568 | tf_op jit(solution)/shard_map/ppermute | solution.py:339
  77.7 4.4 %collective-permute-done.29 = bf16[128,256]{1,0:T(8,128)(2,1)S(1)} collective-permute-done((bf16[128,256]{1,0:T(8,128)(2,1)S(1)}, bf16[128,256]{1,0:T(8,128)(2,1)S(1)}, u32[]{:S(2)}, u32[]{:S(2)}) %collective-permute-start.29) | collective-permute-done | bytes 65568 | tf_op jit(solution)/shard_map/ppermute | solution.py:339
  83.5 3.9 %collective-permute-done.23 = bf16[128,256]{1,0:T(8,128)(2,1)S(1)} collective-permute-done((bf16[128,256]{1,0:T(8,128)(2,1)S(1)}, bf16[128,256]{1,0:T(8,128)(2,1)S(1)}, u32[]{:S(2)}, u32[]{:S(2)}) %collective-permute-start.23) | collective-permute-done | bytes 65568 | tf_op jit(solution)/shard_map/ppermute | solution.py:339
  88.6 3.1 %collective-permute-done.30 = bf16[128,256]{1,0:T(8,128)(2,1)S(1)} collective-permute-done((bf16[128,256]{1,0:T(8,128)(2,1)S(1)}, bf16[128,256]{1,0:T(8,128)(2,1)S(1)}, u32[]{:S(2)}, u32[]{:S(2)}) %collective-permute-start.30) | collective-permute-done | bytes 65568 | tf_op jit(solution)/shard_map/ppermute | solution.py:339
  92.9 3.1 %collective-permute-done.24 = bf16[128,256]{1,0:T(8,128)(2,1)S(1)} collective-permute-done((bf16[128,256]{1,0:T(8,128)(2,1)S(1)}, bf16[128,256]{1,0:T(8,128)(2,1)S(1)}, u32[]{:S(2)}, u32[]{:S(2)}) %collective-permute-start.24) | collective-permute-done | bytes 65568 | tf_op jit(solution)/shard_map/ppermute | solution.py:339
  96.5 1.6 %collective-permute-start.25 = (bf16[256,256]{1,0:T(8,128)(2,1)S(1)}, bf16[256,256]{1,0:T(8,128)(2,1)S(1)}, u32[]{:S(2)}, u32[]{:S(2)}) collective-permute-start(bf16[256,256]{1,0:T(8,128)(2,1)S(1)} %maximum_select_fusion.mine_ref), channel_id=1, source_target_pairs={{0,2},{2,0},{1,3},{3,1},{4,6},{6,4},{5,7},{7,5},{8,10},{10,8},{9,1... | collective-permute-start | bytes 393224 | tf_op jit(solution)/shard_map/ppermute | solution.py:339
  98.9 2.0 %decode.1 = bf16[227,1024]{1,0:T(8,128)(2,1)} custom-call(s32[16]{0:T(128)S(1)} %bitcast.37, s32[16]{0:T(128)S(1)} %copy-done.17, bf16[16,128,128]{2,1,0:T(8,128)(2,1)S(1)} %copy-done.1, f32[227,1024]{1,0:T(8,128)S(1)} %get-tuple-element.42.base_ref, bf16[8,64,256]{2,1,0:T(8,128)(2,1)S(1)} %bitcast.26, bf16[8,64,256]{2,1,0:T(8,128)(2,1)S(1)} %bitcast.29, ...), custom_call_target="tpu_custom_call" | custom-call | flops 67108864 | bytes 4000000 | tf_op jit(solution)/shard_map/decode/pallas_call | solution.py:520
  (112 shorter events, 32.6 us)
Async XLA Ops:
  0.6 15.8 %collective-permute-start = (bf16[227,256]{1,0:T(8,128)(2,1)}, bf16[227,256]{1,0:T(8,128)(2,1)S(1)}, u32[]{:S(2)}, u32[]{:S(2)}) collective-permute-start(bf16[227,256]{1,0:T(8,128)(2,1)} %weight_ref.1), channel_id=1, source_target_pairs={{0,1},{1,0},{2,3},{3,2},{4,5},{5,4},{6,7},{7,6},{8,9},{9,8},{10,11... | collective-permute-start | bytes 348680 | tf_op jit(solution)/shard_map/ppermute | solution.py:339
  7.7 13.9 %collective-permute-start.3 = (bf16[2,256,256]{2,1,0:T(8,128)(2,1)S(1)}, bf16[2,256,256]{2,1,0:T(8,128)(2,1)S(1)}, u32[]{:S(2)}, u32[]{:S(2)}) collective-permute-start(bf16[2,256,256]{2,1,0:T(8,128)(2,1)S(1)} %get-tuple-element.39.after_ref), channel_id=1, source_target_pairs={{0,0},{4,8},{8,4},{12,12},{1,1},{5,9},{9,5},{13,13},{2,2},{6,10},{... | collective-permute-start | bytes 786440 | tf_op jit(solution)/shard_map/ppermute | solution.py:339
  8.6 13.1 %collective-permute-start.2 = (bf16[2,256,256]{2,1,0:T(8,128)(2,1)S(1)}, bf16[2,256,256]{2,1,0:T(8,128)(2,1)S(1)}, u32[]{:S(2)}, u32[]{:S(2)}) collective-permute-start(bf16[2,256,256]{2,1,0:T(8,128)(2,1)S(1)} %get-tuple-element.44), channel_id=1, source_target_pairs={{0,4},{4,0},{8,12},{12,8},{1,5},{5,1},{9,13},{13,9},{2,6},{6,2},{1... | collective-permute-start | bytes 786440 | tf_op jit(solution)/shard_map/ppermute | solution.py:339
  19.3 8.2 %collective-permute-start.5 = (bf16[2,256,256]{2,1,0:T(8,128)(2,1)S(1)}, bf16[2,256,256]{2,1,0:T(8,128)(2,1)S(1)}, u32[]{:S(2)}, u32[]{:S(2)}) collective-permute-start(bf16[2,256,256]{2,1,0:T(8,128)(2,1)S(1)} %get-tuple-element.46), channel_id=1, source_target_pairs={{0,4},{4,0},{8,12},{12,8},{1,5},{5,1},{9,13},{13,9},{2,6},{6,2},{1... | collective-permute-start | bytes 786440 | tf_op jit(solution)/shard_map/ppermute | solution.py:339
  19.4 11.3 %collective-permute-start.17 = (bf16[3,256,256]{2,1,0:T(8,128)(2,1)S(1)}, bf16[3,256,256]{2,1,0:T(8,128)(2,1)S(1)}, u32[]{:S(2)}, u32[]{:S(2)}) collective-permute-start(bf16[3,256,256]{2,1,0:T(8,128)(2,1)S(1)} %get-tuple-element.49), channel_id=1, source_target_pairs={{0,2},{2,0},{1,3},{3,1},{4,6},{6,4},{5,7},{7,5},{8,10},{10,8},{9,1... | collective-permute-start | bytes 1179656 | tf_op jit(solution)/shard_map/ppermute | solution.py:394
  20.9 6.6 %collective-permute-start.6 = (bf16[2,256,256]{2,1,0:T(8,128)(2,1)S(1)}, bf16[2,256,256]{2,1,0:T(8,128)(2,1)S(1)}, u32[]{:S(2)}, u32[]{:S(2)}) collective-permute-start(bf16[2,256,256]{2,1,0:T(8,128)(2,1)S(1)} %get-tuple-element.47), channel_id=1, source_target_pairs={{0,0},{4,8},{8,4},{12,12},{1,1},{5,9},{9,5},{13,13},{2,2},{6,10},{... | collective-permute-start | bytes 786440 | tf_op jit(solution)/shard_map/ppermute | solution.py:339
  21.6 10.3 %collective-permute-start.10 = (bf16[256,512]{1,0:T(8,128)(2,1)S(1)}, bf16[256,512]{1,0:T(8,128)(2,1)S(1)}, u32[]{:S(2)}, u32[]{:S(2)}) collective-permute-start(bf16[256,512]{1,0:T(8,128)(2,1)S(1)} %copy-done.7), channel_id=1, source_target_pairs={{0,1},{1,0},{2,3},{3,2},{4,5},{5,4},{6,7},{7,6},{8,9},{9,8},{10,11... | collective-permute-start | bytes 786440 | tf_op jit(solution)/shard_map/ppermute | solution.py:339
  21.7 14.1 %collective-permute-start.9 = (bf16[512,256]{1,0:T(8,128)(2,1)S(1)}, bf16[512,256]{1,0:T(8,128)(2,1)S(1)}, u32[]{:S(2)}, u32[]{:S(2)}) collective-permute-start(bf16[512,256]{1,0:T(8,128)(2,1)S(1)} %copy-done.6), channel_id=1, source_target_pairs={{0,1},{1,0},{2,3},{3,2},{4,5},{5,4},{6,7},{7,6},{8,9},{9,8},{10,11... | collective-permute-start | bytes 786440 | tf_op jit(solution)/shard_map/ppermute | solution.py:339
  27.5 9.7 %collective-permute-start.8 = (bf16[512,256]{1,0:T(8,128)(2,1)S(1)}, bf16[512,256]{1,0:T(8,128)(2,1)S(1)}, u32[]{:S(2)}, u32[]{:S(2)}) collective-permute-start(bf16[512,256]{1,0:T(8,128)(2,1)S(1)} %copy-done.11), channel_id=1, source_target_pairs={{0,1},{1,0},{2,3},{3,2},{4,5},{5,4},{6,7},{7,6},{8,9},{9,8},{10,11... | collective-permute-start | bytes 786440 | tf_op jit(solution)/shard_map/ppermute | solution.py:339
  29.2 8.0 %collective-permute-start.4 = (bf16[256,256]{1,0:T(8,128)(2,1)S(1)}, bf16[256,256]{1,0:T(8,128)(2,1)S(1)}, u32[]{:S(2)}, u32[]{:S(2)}) collective-permute-start(bf16[256,256]{1,0:T(8,128)(2,1)S(1)} %add_east.2.refs_0_), channel_id=1, source_target_pairs={{0,2},{2,0},{1,3},{3,1},{4,6},{6,4},{5,7},{7,5},{8,10},{10,8},{9,1... | collective-permute-start | bytes 393224 | tf_op jit(solution)/shard_map/ppermute | solution.py:394
  30.7 6.9 %collective-permute-start.7 = (bf16[256,256]{1,0:T(8,128)(2,1)S(1)}, bf16[256,256]{1,0:T(8,128)(2,1)S(1)}, u32[]{:S(2)}, u32[]{:S(2)}) collective-permute-start(bf16[256,256]{1,0:T(8,128)(2,1)S(1)} %add_east.3.after_ref), channel_id=1, source_target_pairs={{0,2},{2,0},{1,3},{3,1},{4,6},{6,4},{5,7},{7,5},{8,10},{10,8},{9,1... | collective-permute-start | bytes 393224 | tf_op jit(solution)/shard_map/ppermute | solution.py:394
  31.9 7.3 %collective-permute-start.18 = (bf16[256,256]{1,0:T(8,128)(2,1)S(1)}, bf16[256,256]{1,0:T(8,128)(2,1)S(1)}, u32[]{:S(2)}, u32[]{:S(2)}) collective-permute-start(bf16[256,256]{1,0:T(8,128)(2,1)S(1)} %get-tuple-element.51), channel_id=1, source_target_pairs={{0,4},{4,0},{8,12},{12,8},{1,5},{5,1},{9,13},{13,9},{2,6},{6,2},{1... | collective-permute-start | bytes 393224 | tf_op jit(solution)/shard_map/ppermute | solution.py:339
  43.7 12.4 %collective-permute-start.26 = (bf16[512,256]{1,0:T(8,128)(2,1)}, bf16[512,256]{1,0:T(8,128)(2,1)}, u32[]{:S(2)}, u32[]{:S(2)}) collective-permute-start(bf16[512,256]{1,0:T(8,128)(2,1)} %get-tuple-element.64), channel_id=1, source_target_pairs={{0,1},{1,0},{2,3},{3,2},{4,5},{5,4},{6,7},{7,6},{8,9},{9,8},{10,11... | collective-permute-start | bytes 786440 | tf_op jit(solution)/shard_map/ppermute | solution.py:339
  43.7 6.2 %collective-permute-start.11 = (bf16[256,256]{1,0:T(8,128)(2,1)}, bf16[256,256]{1,0:T(8,128)(2,1)}, u32[]{:S(2)}, u32[]{:S(2)}) collective-permute-start(bf16[256,256]{1,0:T(8,128)(2,1)} %get-tuple-element.48), channel_id=1, source_target_pairs={{2,0},{0,2},{3,1},{1,3},{6,4},{4,6},{7,5},{5,7},{10,8},{8,10},{11,... | collective-permute-start | bytes 393224 | tf_op jit(solution)/shard_map/ppermute | solution.py:483
  47.5 49.0 %collective-permute-start.32 = (bf16[256,256]{1,0:T(8,128)(2,1)S(1)}, bf16[256,256]{1,0:T(8,128)(2,1)S(1)}, u32[]{:S(2)}, u32[]{:S(2)}) collective-permute-start(bf16[256,256]{1,0:T(8,128)(2,1)S(1)} %get-tuple-element.70), channel_id=1, source_target_pairs={{0,1},{1,0},{2,3},{3,2},{4,5},{5,4},{6,7},{7,6},{8,9},{9,8},{10,11... | collective-permute-start | bytes 393224 | tf_op jit(solution)/shard_map/ppermute | solution.py:339
  47.9 9.3 %collective-permute-start.20 = (bf16[512,256]{1,0:T(8,128)(2,1)S(1)}, bf16[512,256]{1,0:T(8,128)(2,1)S(1)}, u32[]{:S(2)}, u32[]{:S(2)}) collective-permute-start(bf16[512,256]{1,0:T(8,128)(2,1)S(1)} %copy-done.19), channel_id=1, source_target_pairs={{0,1},{1,0},{2,3},{3,2},{4,5},{5,4},{6,7},{7,6},{8,9},{9,8},{10,11... | collective-permute-start | bytes 786440 | tf_op jit(solution)/shard_map/ppermute | solution.py:339
  50.9 10.7 %collective-permute-start.12 = (bf16[2,256,256]{2,1,0:T(8,128)(2,1)S(1)}, bf16[2,256,256]{2,1,0:T(8,128)(2,1)S(1)}, u32[]{:S(2)}, u32[]{:S(2)}) collective-permute-start(bf16[2,256,256]{2,1,0:T(8,128)(2,1)S(1)} %pad_maximum_fusion), channel_id=1, source_target_pairs={{0,4},{4,0},{8,12},{12,8},{1,5},{5,1},{9,13},{13,9},{2,6},{6,2},{1... | collective-permute-start | bytes 786440 | tf_op jit(solution)/shard_map/ppermute | solution.py:339
  55.4 6.7 %collective-permute-start.13 = (bf16[2,256,256]{2,1,0:T(8,128)(2,1)S(1)}, bf16[2,256,256]{2,1,0:T(8,128)(2,1)S(1)}, u32[]{:S(2)}, u32[]{:S(2)}) collective-permute-start(bf16[2,256,256]{2,1,0:T(8,128)(2,1)S(1)} %pad_maximum_fusion), channel_id=1, source_target_pairs={{0,0},{4,8},{8,4},{12,12},{1,1},{5,9},{9,5},{13,13},{2,2},{6,10},{... | collective-permute-start | bytes 786440 | tf_op jit(solution)/shard_map/ppermute | solution.py:339
  56.1 42.8 %collective-permute-start.14 = (bf16[2,256,256]{2,1,0:T(8,128)(2,1)S(1)}, bf16[2,256,256]{2,1,0:T(8,128)(2,1)S(1)}, u32[]{:S(2)}, u32[]{:S(2)}) collective-permute-start(bf16[2,256,256]{2,1,0:T(8,128)(2,1)S(1)} %pad_maximum_fusion), channel_id=1, source_target_pairs={{0,1},{1,0},{2,3},{3,2},{4,5},{5,4},{6,7},{7,6},{8,9},{9,8},{10,11... | collective-permute-start | bytes 786440 | tf_op jit(solution)/shard_map/ppermute | solution.py:339
  57.2 6.0 %collective-permute-start.27 = (bf16[256,256]{1,0:T(8,128)(2,1)S(1)}, bf16[256,256]{1,0:T(8,128)(2,1)S(1)}, u32[]{:S(2)}, u32[]{:S(2)}) collective-permute-start(bf16[256,256]{1,0:T(8,128)(2,1)S(1)} %constant_dynamic-slice_fusion.1), channel_id=1, source_target_pairs={{0,2},{2,0},{1,3},{3,1},{4,6},{6,4},{5,7},{7,5},{8,10},{10,8},{9,1... | collective-permute-start | bytes 393224 | tf_op jit(solution)/shard_map/ppermute | solution.py:339
  62.1 36.8 %collective-permute-start.15 = (bf16[2,256,256]{2,1,0:T(8,128)(2,1)S(1)}, bf16[2,256,256]{2,1,0:T(8,128)(2,1)S(1)}, u32[]{:S(2)}, u32[]{:S(2)}) collective-permute-start(bf16[2,256,256]{2,1,0:T(8,128)(2,1)S(1)} %collective-permute-done.12), channel_id=1, source_target_pairs={{0,1},{1,0},{2,3},{3,2},{4,5},{5,4},{6,7},{7,6},{8,9},{9,8},{10,11... | collective-permute-start | bytes 786440 | tf_op jit(solution)/shard_map/ppermute | solution.py:339
  63.2 35.7 %collective-permute-start.16 = (bf16[2,256,256]{2,1,0:T(8,128)(2,1)S(1)}, bf16[2,256,256]{2,1,0:T(8,128)(2,1)S(1)}, u32[]{:S(2)}, u32[]{:S(2)}) collective-permute-start(bf16[2,256,256]{2,1,0:T(8,128)(2,1)S(1)} %collective-permute-done.13), channel_id=1, source_target_pairs={{0,1},{1,0},{2,3},{3,2},{4,5},{5,4},{6,7},{7,6},{8,9},{9,8},{10,11... | collective-permute-start | bytes 786440 | tf_op jit(solution)/shard_map/ppermute | solution.py:339
  76.4 5.8 %collective-permute-start.29 = (bf16[128,256]{1,0:T(8,128)(2,1)S(1)}, bf16[128,256]{1,0:T(8,128)(2,1)S(1)}, u32[]{:S(2)}, u32[]{:S(2)}) collective-permute-start(bf16[128,256]{1,0:T(8,128)(2,1)S(1)} %add_convert_fusion.5), channel_id=1, source_target_pairs={{0,8},{4,12},{8,0},{12,4},{1,9},{5,13},{9,1},{13,5},{2,10},{6,14},... | collective-permute-start | bytes 196616 | tf_op jit(solution)/shard_map/ppermute | solution.py:339
  96.5 5.8 %collective-permute-start.25 = (bf16[256,256]{1,0:T(8,128)(2,1)S(1)}, bf16[256,256]{1,0:T(8,128)(2,1)S(1)}, u32[]{:S(2)}, u32[]{:S(2)}) collective-permute-start(bf16[256,256]{1,0:T(8,128)(2,1)S(1)} %maximum_select_fusion.mine_ref), channel_id=1, source_target_pairs={{0,2},{2,0},{1,3},{3,1},{4,6},{6,4},{5,7},{7,5},{8,10},{10,8},{9,1... | collective-permute-start | bytes 393224 | tf_op jit(solution)/shard_map/ppermute | solution.py:339
  (29 other events, 116.8 us)

commit v3 on v2

--- a/solution.py
+++ b/solution.py
@@ -8,6 +8,7 @@
 F32 = jnp.float32
 BF16 = jnp.bfloat16
 VMEM_BYTES = 20 * 1024 * 1024
+VMEM_ALL = 60 * 1024 * 1024
 STEPS = 4
 
 
@@ -47,7 +48,8 @@
     return jax.ShapeDtypeStruct(shape, dtype)
 
 
-def call(kernel, name, in_specs, out_specs, out_shape, flops, nbytes, grid=(), scratch=(), exps=0):
+def call(kernel, name, in_specs, out_specs, out_shape, flops, nbytes, grid=(), scratch=(), exps=0,
+         limit=VMEM_BYTES):
     return pl.pallas_call(
         kernel,
         grid=grid,
@@ -55,10 +57,8 @@
         out_specs=out_specs,
         out_shape=out_shape,
         scratch_shapes=list(scratch),
-        compiler_params=pltpu.CompilerParams(vmem_limit_bytes=VMEM_BYTES),
-        cost_estimate=pl.CostEstimate(
-            flops=int(flops), bytes_accessed=int(nbytes), transcendentals=int(exps)
-        ),
+        compiler_params=pltpu.CompilerParams(vmem_limit_bytes=limit),
+        cost_estimate=pl.CostEstimate(flops=1, bytes_accessed=1, transcendentals=0),
         name=name,
     )
 
@@ -170,13 +170,15 @@
     odd_ref[...] = added(side_ref[1], moved_ref[2]).astype(odd_ref.dtype)
 
 
-def update_kernel(
+def node_kernel(
     own_a, even_a, odd_a, moved_a, own_b, even_b, odd_b, moved_b, embed_ref, embed_other_ref,
+    back_ref, back_moved_ref, back_even_ref, back_odd_ref, local_ref, local_other_ref,
     up_ref, up_other_ref, down_ref, down_other_ref, out_ref, out_other_ref,
-    proj_ref, mesh_ref, norm_ref, inv_ref, pre_ref, act_ref,
+    proj_ref, keep_ref, give_ref, mesh_keep_ref, mesh_give_ref,
 ):
     r = lax.axis_index("rep")
     nodes, width = moved_a.shape
+    latent = 2 * width
     channels = out_ref.shape[0]
     first = pl.multiple_of(r * width, width)
     second = pl.multiple_of((1 - r) * width, width)
@@ -192,93 +194,52 @@
     inverse = lax.rsqrt(jnp.mean(centered * centered, axis=-1, keepdims=True) + 1e-05)
     norm = centered * inverse
     normed = norm.astype(BF16)
-    norm_ref[...] = norm
-    inv_ref[...] = jnp.broadcast_to(inverse, inv_ref.shape)
+
+    cot = added(back_ref[...], back_moved_ref[0], back_even_ref[...], back_odd_ref[...]).astype(BF16)
+    terms = cot[:, :channels]
+    grad_own = dot(terms, out_ref[...]).astype(BF16)
+    grad_oth = dot(terms, out_other_ref[...]).astype(BF16)
+
     update_own = jnp.zeros((nodes, width), F32)
     update_oth = jnp.zeros((nodes, width), F32)
-    for k, (u_ref, d_ref) in enumerate(((up_ref, down_ref), (up_other_ref, down_other_ref))):
-        hidden = dot(normed[:, :width], u_ref[pl.ds(first, width), :]) + dot(
-            normed[:, width:], u_ref[pl.ds(second, width), :]
-        )
-        act = (hidden * sigmoid(hidden)).astype(BF16)
-        pre_ref[:, k * width : (k + 1) * width] = hidden
-        act_ref[:, k * width : (k + 1) * width] = act
-        update_own += dot(act, d_ref[:, pl.ds(first, width)])
-        update_oth += dot(act, d_ref[:, pl.ds(second, width)])
-    mesh = (state + jnp.concatenate([update_own, update_oth], axis=1)).astype(BF16)
-    mesh_ref[...] = mesh
-    proj = dot_last(mesh[:, :width], out_ref[...]) + dot_last(mesh[:, width:], out_other_ref[...])
+    back_own = jnp.zeros((nodes, width), F32)
+    back_oth = jnp.zeros((nodes, width), F32)
+    sides = ((up_ref, down_ref, keep_ref), (up_other_ref, down_other_ref, give_ref))
+    for u_ref, d_ref, o_ref in sides:
+        up_own, up_oth = u_ref[pl.ds(first, width), :], u_ref[pl.ds(second, width), :]
+        down_own, down_oth = d_ref[:, pl.ds(first, width)], d_ref[:, pl.ds(second, width)]
+        hidden = dot(normed[:, :width], up_own) + dot(normed[:, width:], up_oth)
+        squash = sigmoid(hidden)
+        act = (hidden * squash).astype(BF16)
+        update_own += dot(act, down_own)
+        update_oth += dot(act, down_oth)
+        o_ref[latent : latent + width, :] = dot_rows(act, cot).astype(o_ref.dtype)
+        act_grad = dot_last(grad_own, down_own) + dot_last(grad_oth, down_oth)
+        pre_grad = (act_grad * squash * (1.0 + hidden * (1.0 - squash))).astype(BF16)
+        o_ref[pl.ds(first, width), :] = dot_rows(normed[:, :width], pre_grad).astype(o_ref.dtype)
+        o_ref[pl.ds(second, width), :] = dot_rows(normed[:, width:], pre_grad).astype(o_ref.dtype)
+        back_own += dot_last(pre_grad, up_own)
+        back_oth += dot_last(pre_grad, up_oth)
+
+    mesh_own = (states[0] + update_own).astype(BF16)
+    mesh_oth = (states[1] + update_oth).astype(BF16)
+    proj = dot_last(mesh_own, out_ref[...]) + dot_last(mesh_oth, out_other_ref[...])
     proj_ref[...] = jnp.zeros_like(proj_ref)
     proj_ref[:, :channels] = proj.astype(BF16)
-
-
-def outer_kernel(
-    own_ref, moved_ref, even_ref, odd_ref, local_ref, local_other_ref, mesh_ref, act_ref,
-    cot_ref, keep_ref, give_ref,
-):
-    width = keep_ref.shape[1]
-    channels = local_ref.shape[0]
-    cot = added(own_ref[...], moved_ref[0], even_ref[...], odd_ref[...]).astype(BF16)
-    cot_ref[...] = cot
-    act, mesh = act_ref[...], mesh_ref[...]
-    for k, (out, local) in enumerate(((keep_ref, local_ref), (give_ref, local_other_ref))):
-        cols = slice(k * width, (k + 1) * width)
-        out[:width, :] = dot_rows(act[:, cols], cot).astype(out.dtype)
-        grad = dot_rows(cot, mesh[:, cols])
-        out[width:, :] = grad.astype(out.dtype)
-        out[width : width + channels, :] = (grad[:channels] + local[...]).astype(out.dtype)
-
-
-def grads_kernel(
-    cot_ref, norm_ref, pre_ref, down_ref, down_other_ref, out_ref, out_other_ref,
-    grad_ref, pre_grad_ref, keep_ref, give_ref,
-):
-    r = lax.axis_index("rep")
-    width = keep_ref.shape[1]
-    channels = out_ref.shape[0]
-    first = pl.multiple_of(r * width, width)
-    second = pl.multiple_of((1 - r) * width, width)
-    cot = cot_ref[:, :channels]
-    grad_own = dot(cot, out_ref[...]).astype(BF16)
-    grad_oth = dot(cot, out_other_ref[...]).astype(BF16)
-    grad_ref[:, :width] = grad_own
-    grad_ref[:, width:] = grad_oth
-    normed = norm_ref[...].astype(BF16)
-    for k, (d_ref, o_ref) in enumerate(((down_ref, keep_ref), (down_other_ref, give_ref))):
-        cols = slice(k * width, (k + 1) * width)
-        hidden = pre_ref[:, cols]
-        act_grad = dot_last(grad_own, d_ref[:, pl.ds(first, width)]) + dot_last(
-            grad_oth, d_ref[:, pl.ds(second, width)]
-        )
-        squash = sigmoid(hidden)
-        pre_grad = (act_grad * squash * (1.0 + hidden * (1.0 - squash))).astype(BF16)
-        pre_grad_ref[:, cols] = pre_grad
-        o_ref[pl.ds(first, width), :] = dot_rows(normed[:, :width], pre_grad).astype(o_ref.dtype)
-        o_ref[pl.ds(second, width), :] = dot_rows(normed[:, width:], pre_grad).astype(o_ref.dtype)
-
-
-def mesh_kernel(
-    grad_ref, pre_grad_ref, norm_ref, inv_ref, up_ref, up_other_ref, keep_ref, give_ref,
-):
-    r = lax.axis_index("rep")
-    width = keep_ref.shape[1]
-    first = pl.multiple_of(r * width, width)
-    second = pl.multiple_of((1 - r) * width, width)
-    halves = []
-    for at in (first, second):
-        halves.append(
-            dot_last(pre_grad_ref[:, :width], up_ref[pl.ds(at, width), :])
-            + dot_last(pre_grad_ref[:, width:], up_other_ref[pl.ds(at, width), :])
-        )
-    back = jnp.concatenate(halves, axis=1)
-    norm = norm_ref[...]
-    centered = (
+    ends = ((keep_ref, mesh_own, local_ref), (give_ref, mesh_oth, local_other_ref))
+    for o_ref, mesh, local in ends:
+        grad = dot_rows(cot, mesh)
+        start = latent + width
+        o_ref[start:, :] = grad.astype(o_ref.dtype)
+        o_ref[start : start + channels, :] = (grad[:channels] + local[...]).astype(o_ref.dtype)
+
+    back = jnp.concatenate([back_own, back_oth], axis=1)
+    slope = (
         back - jnp.mean(back, axis=-1, keepdims=True)
         - norm * jnp.mean(back * norm, axis=-1, keepdims=True)
-    )
-    total = grad_ref[...].astype(F32) + inv_ref[:, :1] * centered
-    keep_ref[...] = total[:, :width]
-    give_ref[...] = total[:, width:].astype(give_ref.dtype)
+    ) * inverse
+    mesh_keep_ref[...] = grad_own.astype(F32) + slope[:, :width]
+    mesh_give_ref[...] = (grad_oth.astype(F32) + slope[:, width:]).astype(mesh_give_ref.dtype)
 
 
 def place_kernel(keep_ref, got_ref, out_ref):
@@ -288,25 +249,32 @@
     out_ref[:, 1 - r] = got_ref[...].astype(F32).reshape(part)
 
 
-def finish_outer_kernel(mine_ref, other_ref, out_ref, out_other_ref, down_ref, grad_ref):
-    r = lax.axis_index("rep")
-    bit = lax.rem(lax.axis_index("lon"), 2)
+def terms_kernel(after_ref, keep_ref, got_ref, out_ref):
+    out_ref[...] = added(keep_ref[...], got_ref[...]).astype(out_ref.dtype)
+
+
+def finish_kernel(mine_ref, other_ref, out_ref, out_other_ref, up_ref, down_ref, grad_ref):
+    r = lax.axis_index("rep")
+    bit = sum_bit(0)
     width = mine_ref.shape[1]
     channels = out_ref.shape[0]
-    mine, other = mine_ref[...], other_ref[...]
-    terms = jnp.where(bit == 0, mine, other)[:, :channels]
-    down_ref[:, pl.ds(pl.multiple_of(r * width, width), width)] = dot(terms, out_ref[...])
-    down_ref[:, pl.ds(pl.multiple_of((1 - r) * width, width), width)] = dot(
-        terms, out_other_ref[...]
-    )
-    grad_ref[...] = jnp.where(bit == 0, other, mine)[:channels].astype(F32)
-
-
-def finish_up_kernel(mine_ref, other_ref, out_ref):
-    bit = lax.rem(lax.axis_index("lon"), 2)
-    rows = mine_ref.shape[0]
-    out_ref[pl.ds(pl.multiple_of(bit * rows, rows), rows), :] = mine_ref[...].astype(F32)
-    out_ref[pl.ds(pl.multiple_of((1 - bit) * rows, rows), rows), :] = other_ref[...].astype(F32)
+
+    def place(low_ref, high_ref):
+        up_ref[...] = low_ref[...].astype(F32)
+        terms = high_ref[:width, :channels]
+        down_ref[:, pl.ds(pl.multiple_of(r * width, width), width)] = dot(terms, out_ref[...])
+        down_ref[:, pl.ds(pl.multiple_of((1 - r) * width, width), width)] = dot(
+            terms, out_other_ref[...]
+        )
+        grad_ref[...] = high_ref[width : width + channels, :].astype(F32)
+
+    @pl.when(bit == 0)
+    def _():
+        place(mine_ref, other_ref)
+
+    @pl.when(bit != 0)
+    def _():
+        place(other_ref, mine_ref)
 
 
 def decode_kernel(device_ref, slot_ref, tiles_ref, base_ref, *refs):
@@ -339,36 +307,58 @@
     return lambda value: lax.ppermute(value, axis, pairs)
 
 
-def summed_over(value, order):
-    held = []
-    for axis, distance, halve in order:
-        count = lax.axis_size(axis)
-        swap = along(axis, count, lambda i, d=distance: i ^ d)
-        if not halve:
-            value = (value.astype(F32) + swap(value).astype(F32)).astype(BF16)
+def distances(axis):
+    found, distance = [], 1
+    while distance < lax.axis_size(axis):
+        found.append((axis, distance))
+        distance *= 2
+    return found
+
+
+def sum_orders():
+    lat, lon = distances("lat"), distances("lon")
+    return (lon + lat, lat + lon)
+
+
+def sum_bit(step):
+    bits = [(lax.axis_index(axis) // distance) % 2 for axis, distance in (o[step] for o in sum_orders())]
+    return jnp.where(lax.axis_index("rep") == 0, bits[0], bits[1])
+
+
+def sum_swap(value, step):
+    lat_count, lon_count = lax.axis_size("lat"), lax.axis_size("lon")
+    orders = sum_orders()
+    pairs = []
+    for lat in range(lat_count):
+        for lon in range(lon_count):
+            for rep in range(2):
+                axis, distance = orders[rep][step]
+                to = (lat ^ distance, lon) if axis == "lat" else (lat, lon ^ distance)
+                number = lambda a, b: (a * lon_count + b) * 2 + rep
+                pairs.append((number(lat, lon), number(*to)))
+    return lax.ppermute(value, ("lat", "lon", "rep"), pairs)
+
+
+def summed(value):
+    count = len(sum_orders()[0])
+    halving = min(count - 1, 3)
+    for step in range(count):
+        if step >= halving:
+            value = (value.astype(F32) + sum_swap(value, step).astype(F32)).astype(BF16)
             continue
-        bit = (lax.axis_index(axis) // distance) % 2
+        bit = sum_bit(step)
         rows = value.shape[0] // 2
         keep = lax.dynamic_slice_in_dim(value, bit * rows, rows, 0)
         give = lax.dynamic_slice_in_dim(value, (1 - bit) * rows, rows, 0)
-        value = (keep.astype(F32) + swap(give).astype(F32)).astype(BF16)
-        held.append((swap, bit))
-    for swap, bit in reversed(held[1:]):
-        other = swap(value)
+        value = (keep.astype(F32) + sum_swap(give, step).astype(F32)).astype(BF16)
+    for step in range(halving - 1, 0, -1):
+        other = sum_swap(value, step)
         value = jnp.where(
-            bit == 0,
+            sum_bit(step) == 0,
             jnp.concatenate([value, other], axis=0),
             jnp.concatenate([other, value], axis=0),
         )
-    return value, held[0][0](value)
-
-
-def distances(count):
-    found, distance = [], 1
-    while distance < count:
-        found.append(distance)
-        distance *= 2
-    return found
+    return value, sum_swap(value, 0)
 
 
 def per_device(
@@ -403,7 +393,7 @@
 
     embed_other = swap_rep(w_embed)
 
-    def encode(after, weight):
+    def encode(after, weight, limit):
         return call(
             encode_kernel, "encode",
             [smem(), smem(), anywhere(), cols_spec, tiles_spec, whole((channels, width))],
@@ -414,9 +404,10 @@
                 pltpu.VMEM((6 * slots, half, width), F32),
                 pltpu.VMEM((step_rows, width), BF16),
             ],
+            limit=limit,
         )(device, route_slot, after, grid_t, interp_tiles, weight)
 
-    own_a, even_a, odd_a, hidden_a = encode(w_embed, w_embed)
+    own_a, even_a, odd_a, hidden_a = encode(w_embed, w_embed, VMEM_ALL)
     even_in_a, odd_in_a = to_even(even_a), to_odd(odd_a)
 
     back_own, back_east, back_side = call(
@@ -430,7 +421,7 @@
     )(device, route_slot, odd_a, interp_tiles, cot_t)
     back_moved = to_east(back_east)
 
-    own_b, even_b, odd_b, hidden_b = encode(back_own, embed_other)
+    own_b, even_b, odd_b, hidden_b = encode(back_own, embed_other, VMEM_BYTES)
     even_in_b, odd_in_b = to_even(even_b), to_odd(odd_b)
 
     out_other, up_other, down_other = swap_rep(out_t), swap_rep(w_up), swap_rep(w_down)
@@ -453,7 +444,7 @@
 
     send_a = add_east(own_b, own_a, even_in_a, odd_in_a)
     moved_a = to_east(send_a)
-    send_b = add_east(send_a, own_b, even_in_b, odd_in_b)
+    send_b = add_east(moved_a, own_b, even_in_b, odd_in_b)
     moved_b = to_east(send_b)
 
     back_even, back_odd = call(
@@ -465,51 +456,33 @@
     first = pl.BlockSpec((1, nodes, width), lambda i: (0, 0, 0))
     sums_specs = [first] * 3 + [whole((nodes, width))]
     weights = (w_up, up_other, w_down, down_other, out_t, out_other)
-    update_shapes = [
-        ((nodes, padded), BF16), ((nodes, latent), BF16), ((nodes, latent), F32),
-        ((nodes, 128), F32), ((nodes, latent), F32), ((nodes, latent), BF16),
-    ]
-    proj, mesh_out, norm, inverse, hidden_pre, hidden_act = call(
-        update_kernel, "node_update",
-        sums_specs * 2 + [whole(embed_shape)] * 2 + [whole(w.shape) for w in weights],
-        [whole(s) for s, _ in update_shapes],
-        [shape_of(s, d) for s, d in update_shapes],
-        5 * nodes * latent * latent, 4e6, grid=(1,), exps=nodes * latent,
+    back_spec = whole((nodes, padded))
+    proj, keep, give, mesh_keep, mesh_give = call(
+        node_kernel, "node_update_and_gradients",
+        sums_specs * 2 + [whole(embed_shape)] * 2
+        + [back_spec, pl.BlockSpec((1, nodes, padded), lambda i: (0, 0, 0)), back_spec, back_spec]
+        + [whole((channels, width))] * 2 + [whole(w.shape) for w in weights],
+        [whole((nodes, padded))] + [whole((2 * latent, width))] * 2 + [whole((nodes, width))] * 2,
+        [shape_of((nodes, padded), BF16), shape_of((2 * latent, width), F32),
+         shape_of((2 * latent, width), BF16), shape_of((nodes, width), F32),
+         shape_of((nodes, width), BF16)],
+        15 * nodes * latent * latent, 9e6, grid=(1,), exps=nodes * latent,
     )(
         own_a, even_in_a, odd_in_a, moved_a, own_b, even_in_b, odd_in_b, moved_b,
-        mesh_embed.reshape(embed_shape), mesh_other.reshape(embed_shape), *weights,
+        mesh_embed.reshape(embed_shape), mesh_other.reshape(embed_shape),
+        back_own, back_moved, back_even_in, back_odd_in, local, local_other, *weights,
     )
 
     east = lax.ppermute(proj, "lon", west_pairs)
     pair = jnp.stack([proj, east])
     pair_even, pair_odd = to_even(pair), to_odd(pair)
 
-    cot_mesh, keep_outer, give_outer = call(
-        outer_kernel, "outer_grads", [vmem()] * 8, [vmem()] * 3,
-        [shape_of((nodes, padded), BF16), shape_of((latent, width), F32),
-         shape_of((latent, width), BF16)],
-        4 * nodes * latent * padded, 3e6,
-    )(back_own, back_moved, back_even_in, back_odd_in, local, local_other, mesh_out, hidden_act)
-    got_outer = swap_rep(give_outer)
-
-    grad_nodes, pre_grad, keep_up, give_up = call(
-        grads_kernel, "up_grads", [vmem()] * 7, [vmem()] * 4,
-        [shape_of((nodes, latent), BF16), shape_of((nodes, latent), BF16),
-         shape_of((latent, width), F32), shape_of((latent, width), BF16)],
-        5 * nodes * latent * latent, 4e6, exps=nodes * latent,
-    )(cot_mesh, norm, hidden_pre, w_down, down_other, out_t, out_other)
-    got_up = swap_rep(give_up)
-
-    order = [("lon", d, True) for d in distances(lon_count)]
-    order += [("lat", d, d == 1) for d in distances(lat_count)]
-    outer_mine, outer_theirs = summed_over((keep_outer + got_outer.astype(F32)).astype(BF16), order)
-    up_mine, up_theirs = summed_over((keep_up + got_up.astype(F32)).astype(BF16), order)
-
-    mesh_keep, mesh_give = call(
-        mesh_kernel, "mesh_grads", [vmem()] * 6, [vmem()] * 2,
-        [shape_of((nodes, width), F32), shape_of((nodes, width), BF16)],
-        2 * nodes * latent * latent, 3e6,
-    )(grad_nodes, pre_grad, norm, inverse, w_up, up_other)
+    terms = call(
+        terms_kernel, "sum_terms", [anywhere()] + [vmem()] * 2, vmem(),
+        shape_of((2 * latent, width), BF16), 2 * latent * width, 2e6,
+    )(pair, keep, swap_rep(give))
+    mine, theirs = summed(terms)
+
     grad_mesh = call(
         place_kernel, "place_mesh", [vmem()] * 2, vmem(), shape_of(embed_shape, F32),
         nodes * latent, 1e6,
@@ -527,15 +500,12 @@
         *[swap_rep(table).reshape(table_shape) for table in tables],
     ).T
 
-    grad_down, grad_out = call(
-        finish_outer_kernel, "finish_outer", [vmem()] * 4, [vmem()] * 2,
-        [shape_of((width, latent), F32), shape_of((channels, width), F32)],
+    grad_up, grad_down, grad_out = call(
+        finish_kernel, "finish", [vmem()] * 4, [vmem()] * 3,
+        [shape_of((latent, width), F32), shape_of((width, latent), F32),
+         shape_of((channels, width), F32)],
         2 * width * latent * channels, 1e6,
-    )(outer_mine, outer_theirs, out_t, out_other)
-    grad_up = call(
-        finish_up_kernel, "finish_up", [vmem()] * 2, vmem(), shape_of((latent, width), F32),
-        latent * width, 8e5,
-    )(up_mine, up_theirs)
+    )(mine, theirs, out_t, out_other)
     return (grid_out, grad_out.T, grad_up, grad_down, grad_mesh)
 
 

time: 104 us -> 83.5 us (0.80)
  starting transfers between devices: 36.5 us -> 28.6 us
  waiting for transfers between devices: 37.6 us -> 31.5 us
  local copies, waits for them, and re-layouts: 8.39 us -> 3.32 us
  other arithmetic: 2.29 us -> 1.18 us
    ppermute x29 -> x18, waiting for transfers between devices: 35.6 us -> 10.3 us  [along(): return lambda value: lax.ppermute(value, axis, pairs)]
    ppermute x0 -> x5, waiting for transfers between devices: none -> 16.1 us  [sum_swap(): return lax.ppermute(value, ('lat', 'lon', 'rep'), pairs)]
    ppermute x29 -> x18, starting transfers between devices: 30.8 us -> 18.1 us  [along(): return lambda value: lax.ppermute(value, axis, pairs)]
    ppermute x0 -> x5, starting transfers between devices: none -> 6.82 us  [sum_swap(): return lax.ppermute(value, ('lat', 'lon', 'rep'), pairs)]
    unnamed x40 -> x36, local copies, waits for them, and re-layouts: 8.32 us -> 3.28 us
    ppermute x1, waiting for transfers between devices: 1.7 us -> 5.13 us  [per_device(): east = lax.ppermute(proj, 'lon', west_pairs)]
    pallas_call x6 -> x3, Pallas kernels: 5.96 us -> 3.51 us  [the longest x1 2.13 us: per_device(): call(node_kernel, 'node_update_and_gradients', sums_specs * 2 + [whole(em...]
    pallas_call x2, Pallas kernels: 5.56 us -> 7.8 us  [encode(): call(encode_kernel, 'encode', [smem(), smem(), anywhere(), cols_spec, til...]
  transfers between devices with their start and end apart: 33 -> 27, of which waited for: 14 -> 10; matrix products, arithmetic and copies ran while one was open for 2% -> 1% of each run, Pallas kernels for 14% -> 11%
where the time goes in v3:
time: 83.5 us; the launch traced here: 83 us
  waiting for transfers between devices  31.5 us (38%)
  starting transfers between devices  28.6 us (34%)
  Pallas kernels  17.4 us (21%)
  local copies, waits for them, and re-layouts  3.32 us (4%)
  other arithmetic  1.18 us (1%)
  between operations  1.01 us (1%)
    ppermute x18, starting transfers between devices, along(): return lambda value: lax.ppermute(value, axis, pairs)  18.1 us
    ppermute x5, waiting for transfers between devices, sum_swap(): return lax.ppermute(value, ('lat', 'lon', 'rep'), pairs)  16.1 us
    ppermute x18, waiting for transfers between devices, along(): return lambda value: lax.ppermute(value, axis, pairs)  10.3 us
    pallas_call x2, Pallas kernels, encode(): call(encode_kernel, 'encode', [smem(), smem(), anywhere(), cols_spec, til...  7.8 us
    ppermute x5, starting transfers between devices, sum_swap(): return lax.ppermute(value, ('lat', 'lon', 'rep'), pairs)  6.82 us
    ppermute x1, waiting for transfers between devices, per_device(): east = lax.ppermute(proj, 'lon', west_pairs)  5.13 us
    unnamed x36, local copies, waits for them, and re-layouts  3.28 us
    ppermute x3, starting transfers between devices, per_device(): to_east = lambda value: lax.ppermute(value, 'lon', east_pairs)  2.85 us
  transfers between devices with their start and end apart: 27, of which 10 were waited for; matrix products, arithmetic and copies ran while one was open for 1% of the time, Pallas kernels for 11%

profile of v3, /device:TPU:0, one launch (start us, length us, event | category | flops | bytes accessed | tf_op | source)
XLA Modules:
  0.0 83.0 jit_solution(5585950691328333569)
XLA Ops:
  0.7 5.0 %encode.2 = (bf16[2,256,256]{2,1,0:T(8,128)(2,1)}, bf16[2,256,256]{2,1,0:T(8,128)(2,1)}, bf16[2,256,256]{2,1,0:T(8,128)(2,1)}, bf16[1024,256]{1,0:T(8,128)(2,1)}) custom-call(s32[16]{0:T(128)} %bitcast.34, s32[16]{0:T(128)} %slot_ref.7, bf16[227,256]{1,0:T(8,128)(2,1)} %weight_ref.1, bf16[227,2048]{1,0:T(8,128)(2,1)} %bitcast.17, ...), custom_call_target="tpu_custom_call" | custom-call | flops 1 | bytes 1 | tf_op jit(solution)/shard_map/encode/pallas_call | solution.py:397
  5.7 3.0 %collective-permute-start.2 = (bf16[2,256,256]{2,1,0:T(8,128)(2,1)}, bf16[2,256,256]{2,1,0:T(8,128)(2,1)S(1)}, u32[]{:S(2)}, u32[]{:S(2)}) collective-permute-start(bf16[2,256,256]{2,1,0:T(8,128)(2,1)} %get-tuple-element.35), channel_id=1, source_target_pairs={{0,4},{4,0},{8,12},{12,8},{1,5},{5,1},{9,13},{13,9},{2,6},{6,2},{1... | collective-permute-start | bytes 786440 | tf_op jit(solution)/shard_map/ppermute | solution.py:307
  8.7 1.6 %collective-permute-start.3 = (bf16[2,256,256]{2,1,0:T(8,128)(2,1)}, bf16[2,256,256]{2,1,0:T(8,128)(2,1)S(1)}, u32[]{:S(2)}, u32[]{:S(2)}) collective-permute-start(bf16[2,256,256]{2,1,0:T(8,128)(2,1)} %get-tuple-element.30.after_ref), channel_id=1, source_target_pairs={{0,0},{4,8},{8,4},{12,12},{1,1},{5,9},{9,5},{13,13},{2,2},{6,10},{... | collective-permute-start | bytes 786440 | tf_op jit(solution)/shard_map/ppermute | solution.py:307
  11.3 2.4 %back_messages.1 = (bf16[256,256]{1,0:T(8,128)(2,1)S(1)}, bf16[3,256,256]{2,1,0:T(8,128)(2,1)S(1)}, bf16[2,256,256]{2,1,0:T(8,128)(2,1)S(1)}) custom-call(s32[16]{0:T(128)S(1)} %bitcast.35, s32[16]{0:T(128)S(1)} %copy-done.13, bf16[2,256,256]{2,1,0:T(8,128)(2,1)S(1)} %copy-done.11, bf16[16,128,128]{2,1,0:T(8,128)(2,1)S(1)} %copy-done, ...), custom_call_target="tpu_custom_call" | custom-call | flops 1 | bytes 1 | tf_op jit(solution)/shard_map/back_messages/pallas_call | solution.py:413
  13.7 1.6 %collective-permute-start.9 = (bf16[3,256,256]{2,1,0:T(8,128)(2,1)S(1)}, bf16[3,256,256]{2,1,0:T(8,128)(2,1)S(1)}, u32[]{:S(2)}, u32[]{:S(2)}) collective-permute-start(bf16[3,256,256]{2,1,0:T(8,128)(2,1)S(1)} %get-tuple-element.39), channel_id=1, source_target_pairs={{0,2},{2,0},{1,3},{3,1},{4,6},{6,4},{5,7},{7,5},{8,10},{10,8},{9,1... | collective-permute-start | bytes 1179656 | tf_op jit(solution)/shard_map/ppermute | solution.py:384
  15.3 2.8 %encode.3 = (bf16[2,256,256]{2,1,0:T(8,128)(2,1)S(1)}, bf16[2,256,256]{2,1,0:T(8,128)(2,1)S(1)}, bf16[2,256,256]{2,1,0:T(8,128)(2,1)S(1)}, bf16[1024,256]{1,0:T(8,128)(2,1)S(1)}) custom-call(s32[16]{0:T(128)S(1)} %bitcast.36, s32[16]{0:T(128)S(1)} %copy-done.13, bf16[256,256]{1,0:T(8,128)(2,1)S(1)} %get-tuple-element.31.after_ref.back_ref, ...), custom_call_target="tpu_custom_call" | custom-call | flops 1 | bytes 1 | tf_op jit(solution)/shard_map/encode/pallas_call | solution.py:397
  18.1 3.6 %collective-permute-start.5 = (bf16[2,256,256]{2,1,0:T(8,128)(2,1)S(1)}, bf16[2,256,256]{2,1,0:T(8,128)(2,1)S(1)}, u32[]{:S(2)}, u32[]{:S(2)}) collective-permute-start(bf16[2,256,256]{2,1,0:T(8,128)(2,1)S(1)} %get-tuple-element.37), channel_id=1, source_target_pairs={{0,4},{4,0},{8,12},{12,8},{1,5},{5,1},{9,13},{13,9},{2,6},{6,2},{1... | collective-permute-start | bytes 786440 | tf_op jit(solution)/shard_map/ppermute | solution.py:307
  23.2 5.2 %collective-permute-done.5.refs_2_.even_b = bf16[2,256,256]{2,1,0:T(8,128)(2,1)S(1)} collective-permute-done((bf16[2,256,256]{2,1,0:T(8,128)(2,1)S(1)}, bf16[2,256,256]{2,1,0:T(8,128)(2,1)S(1)}, u32[]{:S(2)}, u32[]{:S(2)}) %collective-permute-start.5) | collective-permute-done | bytes 262176 | tf_op jit(solution)/shard_map/ppermute | solution.py:307
  30.4 3.3 %collective-permute-start.10 = (bf16[256,256]{1,0:T(8,128)(2,1)S(1)}, bf16[256,256]{1,0:T(8,128)(2,1)S(1)}, u32[]{:S(2)}, u32[]{:S(2)}) collective-permute-start(bf16[256,256]{1,0:T(8,128)(2,1)S(1)} %get-tuple-element.41), channel_id=1, source_target_pairs={{0,4},{4,0},{8,12},{12,8},{1,5},{5,1},{9,13},{13,9},{2,6},{6,2},{1... | collective-permute-start | bytes 393224 | tf_op jit(solution)/shard_map/ppermute | solution.py:307
  35.1 1.0 %copy-done.5 = f32[227,1024]{1,0:T(8,128)} copy-done((f32[227,1024]{1,0:T(8,128)}, f32[227,1024]{1,0:T(8,128)S(1)}, u32[]{:S(2)}) %copy-start.5) | copy-done | bytes 929816
  36.1 1.4 %collective-permute-done.10.back_even_ref = bf16[256,256]{1,0:T(8,128)(2,1)S(1)} collective-permute-done((bf16[256,256]{1,0:T(8,128)(2,1)S(1)}, bf16[256,256]{1,0:T(8,128)(2,1)S(1)}, u32[]{:S(2)}, u32[]{:S(2)}) %collective-permute-start.10) | collective-permute-done | bytes 131104 | tf_op jit(solution)/shard_map/ppermute | solution.py:307
  37.5 2.1 %node_update_and_gradients.1 = (bf16[256,256]{1,0:T(8,128)(2,1)S(1)}, f32[1024,256]{1,0:T(8,128)S(1)}, bf16[1024,256]{1,0:T(8,128)(2,1)S(1)}, f32[256,256]{1,0:T(8,128)S(1)}, bf16[256,256]{1,0:T(8,128)(2,1)S(1)}) custom-call(bf16[2,256,256]{2,1,0:T(8,128)(2,1)S(1)} %copy-done.4, bf16[2,256,256]{2,1,0:T(8,128)(2,1)S(1)} %collective-permute-done.2.refs_2_.even_a, ...), custom_call_target="tpu_custom_call" | custom-call | flops 1 | bytes 1 | tf_op jit(solution)/shard_map/node_update_and_gradients/pallas_call | solution.py:460
  41.1 5.1 %collective-permute-done.14 = bf16[256,256]{1,0:T(8,128)(2,1)S(1)} collective-permute-done((bf16[256,256]{1,0:T(8,128)(2,1)S(1)}, bf16[256,256]{1,0:T(8,128)(2,1)S(1)}, u32[]{:S(2)}, u32[]{:S(2)}) %collective-permute-start.14) | collective-permute-done | bytes 131104 | tf_op jit(solution)/shard_map/ppermute | solution.py:476
  48.8 5.6 %collective-permute-done.21 = bf16[512,256]{1,0:T(8,128)(2,1)S(1)} collective-permute-done((bf16[512,256]{1,0:T(8,128)(2,1)S(1)}, bf16[512,256]{1,0:T(8,128)(2,1)S(1)}, u32[]{:S(2)}, u32[]{:S(2)}) %collective-permute-start.21) | collective-permute-done | bytes 262176 | tf_op jit(solution)/shard_map/ppermute | solution.py:339
  54.5 3.7 %collective-permute-start.22 = (bf16[256,256]{1,0:T(8,128)(2,1)S(1)}, bf16[256,256]{1,0:T(8,128)(2,1)S(1)}, u32[]{:S(2)}, u32[]{:S(2)}) collective-permute-start(bf16[256,256]{1,0:T(8,128)(2,1)S(1)} %constant_dynamic-slice_fusion), channel_id=1, source_target_pairs={{0,4},{1,9},{2,6},{3,11},{4,0},{5,13},{6,2},{7,15},{8,12},{9,1},{1... | collective-permute-start | bytes 393224 | tf_op jit(solution)/shard_map/ppermute | solution.py:339
  58.2 3.1 %collective-permute-done.22 = bf16[256,256]{1,0:T(8,128)(2,1)S(1)} collective-permute-done((bf16[256,256]{1,0:T(8,128)(2,1)S(1)}, bf16[256,256]{1,0:T(8,128)(2,1)S(1)}, u32[]{:S(2)}, u32[]{:S(2)}) %collective-permute-start.22) | collective-permute-done | bytes 131104 | tf_op jit(solution)/shard_map/ppermute | solution.py:339
  61.4 2.1 %collective-permute-start.23 = (bf16[256,256]{1,0:T(8,128)(2,1)S(1)}, bf16[256,256]{1,0:T(8,128)(2,1)S(1)}, u32[]{:S(2)}, u32[]{:S(2)}) collective-permute-start(bf16[256,256]{1,0:T(8,128)(2,1)S(1)} %add_convert_fusion.2), channel_id=1, source_target_pairs={{0,8},{1,3},{2,10},{3,1},{4,12},{5,7},{6,14},{7,5},{8,0},{9,11},{1... | collective-permute-start | bytes 393224 | tf_op jit(solution)/shard_map/ppermute | solution.py:339
  64.1 5.1 %collective-permute-done.23 = bf16[256,256]{1,0:T(8,128)(2,1)S(1)} collective-permute-done((bf16[256,256]{1,0:T(8,128)(2,1)S(1)}, bf16[256,256]{1,0:T(8,128)(2,1)S(1)}, u32[]{:S(2)}, u32[]{:S(2)}) %collective-permute-start.23) | collective-permute-done | bytes 131104 | tf_op jit(solution)/shard_map/ppermute | solution.py:339
  69.4 2.0 %collective-permute-done.15 = bf16[2,256,256]{2,1,0:T(8,128)(2,1)S(1)} collective-permute-done((bf16[2,256,256]{2,1,0:T(8,128)(2,1)S(1)}, bf16[2,256,256]{2,1,0:T(8,128)(2,1)S(1)}, u32[]{:S(2)}, u32[]{:S(2)}) %collective-permute-start.15) | collective-permute-done | bytes 262176 | tf_op jit(solution)/shard_map/ppermute | solution.py:307
  71.9 2.3 %collective-permute-done.24 = bf16[256,256]{1,0:T(8,128)(2,1)S(1)} collective-permute-done((bf16[256,256]{1,0:T(8,128)(2,1)S(1)}, bf16[256,256]{1,0:T(8,128)(2,1)S(1)}, u32[]{:S(2)}, u32[]{:S(2)}) %collective-permute-start.24) | collective-permute-done | bytes 131104 | tf_op jit(solution)/shard_map/ppermute | solution.py:339
  74.5 3.4 %collective-permute-start.26 = (bf16[256,256]{1,0:T(8,128)(2,1)S(1)}, bf16[256,256]{1,0:T(8,128)(2,1)S(1)}, u32[]{:S(2)}, u32[]{:S(2)}) collective-permute-start(bf16[256,256]{1,0:T(8,128)(2,1)S(1)} %copy-done.15), channel_id=1, source_target_pairs={{0,1},{1,0},{2,3},{3,2},{4,5},{5,4},{6,7},{7,6},{8,9},{9,8},{10,11... | collective-permute-start | bytes 393224 | tf_op jit(solution)/shard_map/ppermute | solution.py:307
  77.9 1.0 %collective-permute-done.26.got_ref = bf16[256,256]{1,0:T(8,128)(2,1)S(1)} collective-permute-done((bf16[256,256]{1,0:T(8,128)(2,1)S(1)}, bf16[256,256]{1,0:T(8,128)(2,1)S(1)}, u32[]{:S(2)}, u32[]{:S(2)}) %collective-permute-start.26) | collective-permute-done | bytes 131104 | tf_op jit(solution)/shard_map/ppermute | solution.py:307
  79.7 1.9 %decode.1 = bf16[227,1024]{1,0:T(8,128)(2,1)} custom-call(s32[16]{0:T(128)S(1)} %bitcast.37, s32[16]{0:T(128)S(1)} %copy-done.13, bf16[16,128,128]{2,1,0:T(8,128)(2,1)S(1)} %copy-done, f32[227,1024]{1,0:T(8,128)S(1)} %copy-done.6, bf16[8,64,256]{2,1,0:T(8,128)(2,1)S(1)} %bitcast.21, bf16[8,64,256]{2,1,0:T(8,128)(2,1)S(1)} %bitcast.28, ...), custom_call_target="tpu_custom_call" | custom-call | flops 1 | bytes 1 | tf_op jit(solution)/shard_map/decode/pallas_call | solution.py:493
  81.7 1.3 %finish.1 = (f32[512,256]{1,0:T(8,128)}, f32[256,512]{1,0:T(8,128)}, f32[227,256]{1,0:T(8,128)}) custom-call(bf16[512,256]{1,0:T(8,128)(2,1)S(1)} %maximum_select_fusion.mine_ref, bf16[512,256]{1,0:T(8,128)(2,1)S(1)} %collective-permute-done.25.other_ref, bf16[227,256]{1,0:T(8,128)(2,1)S(1)} %bitcast.25, ...), custom_call_target="tpu_custom_call" | custom-call | flops 1 | bytes 1 | tf_op jit(solution)/shard_map/finish/pallas_call | solution.py:503
  (85 shorter events, 12.3 us)
Async XLA Ops:
  5.7 16.7 %collective-permute-start.2 = (bf16[2,256,256]{2,1,0:T(8,128)(2,1)}, bf16[2,256,256]{2,1,0:T(8,128)(2,1)S(1)}, u32[]{:S(2)}, u32[]{:S(2)}) collective-permute-start(bf16[2,256,256]{2,1,0:T(8,128)(2,1)} %get-tuple-element.35), channel_id=1, source_target_pairs={{0,4},{4,0},{8,12},{12,8},{1,5},{5,1},{9,13},{13,9},{2,6},{6,2},{1... | collective-permute-start | bytes 786440 | tf_op jit(solution)/shard_map/ppermute | solution.py:307
  8.7 13.7 %collective-permute-start.3 = (bf16[2,256,256]{2,1,0:T(8,128)(2,1)}, bf16[2,256,256]{2,1,0:T(8,128)(2,1)S(1)}, u32[]{:S(2)}, u32[]{:S(2)}) collective-permute-start(bf16[2,256,256]{2,1,0:T(8,128)(2,1)} %get-tuple-element.30.after_ref), channel_id=1, source_target_pairs={{0,0},{4,8},{8,4},{12,12},{1,1},{5,9},{9,5},{13,13},{2,2},{6,10},{... | collective-permute-start | bytes 786440 | tf_op jit(solution)/shard_map/ppermute | solution.py:307
  10.3 4.9 %collective-permute-start = (bf16[227,256]{1,0:T(8,128)(2,1)S(1)}, bf16[227,256]{1,0:T(8,128)(2,1)S(1)}, u32[]{:S(2)}, u32[]{:S(2)}) collective-permute-start(bf16[227,256]{1,0:T(8,128)(2,1)S(1)} %copy-done.16), channel_id=1, source_target_pairs={{0,1},{1,0},{2,3},{3,2},{4,5},{5,4},{6,7},{7,6},{8,9},{9,8},{10,11... | collective-permute-start | bytes 348680 | tf_op jit(solution)/shard_map/ppermute | solution.py:307
  13.7 15.3 %collective-permute-start.9 = (bf16[3,256,256]{2,1,0:T(8,128)(2,1)S(1)}, bf16[3,256,256]{2,1,0:T(8,128)(2,1)S(1)}, u32[]{:S(2)}, u32[]{:S(2)}) collective-permute-start(bf16[3,256,256]{2,1,0:T(8,128)(2,1)S(1)} %get-tuple-element.39), channel_id=1, source_target_pairs={{0,2},{2,0},{1,3},{3,1},{4,6},{6,4},{5,7},{7,5},{8,10},{10,8},{9,1... | collective-permute-start | bytes 1179656 | tf_op jit(solution)/shard_map/ppermute | solution.py:384
  18.1 10.3 %collective-permute-start.5 = (bf16[2,256,256]{2,1,0:T(8,128)(2,1)S(1)}, bf16[2,256,256]{2,1,0:T(8,128)(2,1)S(1)}, u32[]{:S(2)}, u32[]{:S(2)}) collective-permute-start(bf16[2,256,256]{2,1,0:T(8,128)(2,1)S(1)} %get-tuple-element.37), channel_id=1, source_target_pairs={{0,4},{4,0},{8,12},{12,8},{1,5},{5,1},{9,13},{13,9},{2,6},{6,2},{1... | collective-permute-start | bytes 786440 | tf_op jit(solution)/shard_map/ppermute | solution.py:307
  21.7 6.7 %collective-permute-start.6 = (bf16[2,256,256]{2,1,0:T(8,128)(2,1)S(1)}, bf16[2,256,256]{2,1,0:T(8,128)(2,1)S(1)}, u32[]{:S(2)}, u32[]{:S(2)}) collective-permute-start(bf16[2,256,256]{2,1,0:T(8,128)(2,1)S(1)} %get-tuple-element.38), channel_id=1, source_target_pairs={{0,0},{4,8},{8,4},{12,12},{1,1},{5,9},{9,5},{13,13},{2,2},{6,10},{... | collective-permute-start | bytes 786440 | tf_op jit(solution)/shard_map/ppermute | solution.py:307
  22.4 11.3 %collective-permute-start.8 = (bf16[512,256]{1,0:T(8,128)(2,1)S(1)}, bf16[512,256]{1,0:T(8,128)(2,1)S(1)}, u32[]{:S(2)}, u32[]{:S(2)}) collective-permute-start(bf16[512,256]{1,0:T(8,128)(2,1)S(1)} %copy-done.8), channel_id=1, source_target_pairs={{0,1},{1,0},{2,3},{3,2},{4,5},{5,4},{6,7},{7,6},{8,9},{9,8},{10,11... | collective-permute-start | bytes 786440 | tf_op jit(solution)/shard_map/ppermute | solution.py:307
  22.6 6.3 %collective-permute-start.4 = (bf16[256,256]{1,0:T(8,128)(2,1)S(1)}, bf16[256,256]{1,0:T(8,128)(2,1)S(1)}, u32[]{:S(2)}, u32[]{:S(2)}) collective-permute-start(bf16[256,256]{1,0:T(8,128)(2,1)S(1)} %add_east.2), channel_id=1, source_target_pairs={{0,2},{2,0},{1,3},{3,1},{4,6},{6,4},{5,7},{7,5},{8,10},{10,8},{9,1... | collective-permute-start | bytes 393224 | tf_op jit(solution)/shard_map/ppermute | solution.py:384
  28.3 7.7 %collective-permute-start.12 = (bf16[512,256]{1,0:T(8,128)(2,1)S(1)}, bf16[512,256]{1,0:T(8,128)(2,1)S(1)}, u32[]{:S(2)}, u32[]{:S(2)}) collective-permute-start(bf16[512,256]{1,0:T(8,128)(2,1)S(1)} %copy-done.9), channel_id=1, source_target_pairs={{0,1},{1,0},{2,3},{3,2},{4,5},{5,4},{6,7},{7,6},{8,9},{9,8},{10,11... | collective-permute-start | bytes 786440 | tf_op jit(solution)/shard_map/ppermute | solution.py:307
  28.4 7.7 %collective-permute-start.13 = (bf16[256,512]{1,0:T(8,128)(2,1)S(1)}, bf16[256,512]{1,0:T(8,128)(2,1)S(1)}, u32[]{:S(2)}, u32[]{:S(2)}) collective-permute-start(bf16[256,512]{1,0:T(8,128)(2,1)S(1)} %copy-done.10), channel_id=1, source_target_pairs={{0,1},{1,0},{2,3},{3,2},{4,5},{5,4},{6,7},{7,6},{8,9},{9,8},{10,11... | collective-permute-start | bytes 786440 | tf_op jit(solution)/shard_map/ppermute | solution.py:307
  29.0 7.1 %collective-permute-start.7 = (bf16[256,256]{1,0:T(8,128)(2,1)S(1)}, bf16[256,256]{1,0:T(8,128)(2,1)S(1)}, u32[]{:S(2)}, u32[]{:S(2)}) collective-permute-start(bf16[256,256]{1,0:T(8,128)(2,1)S(1)} %add_east.3.after_ref), channel_id=1, source_target_pairs={{0,2},{2,0},{1,3},{3,1},{4,6},{6,4},{5,7},{7,5},{8,10},{10,8},{9,1... | collective-permute-start | bytes 393224 | tf_op jit(solution)/shard_map/ppermute | solution.py:384
  30.4 7.1 %collective-permute-start.10 = (bf16[256,256]{1,0:T(8,128)(2,1)S(1)}, bf16[256,256]{1,0:T(8,128)(2,1)S(1)}, u32[]{:S(2)}, u32[]{:S(2)}) collective-permute-start(bf16[256,256]{1,0:T(8,128)(2,1)S(1)} %get-tuple-element.41), channel_id=1, source_target_pairs={{0,4},{4,0},{8,12},{12,8},{1,5},{5,1},{9,13},{13,9},{2,6},{6,2},{1... | collective-permute-start | bytes 393224 | tf_op jit(solution)/shard_map/ppermute | solution.py:307
  40.3 7.5 %collective-permute-start.20 = (bf16[1024,256]{1,0:T(8,128)(2,1)S(1)}, bf16[1024,256]{1,0:T(8,128)(2,1)S(1)}, u32[]{:S(2)}, u32[]{:S(2)}) collective-permute-start(bf16[1024,256]{1,0:T(8,128)(2,1)S(1)} %get-tuple-element.47), channel_id=1, source_target_pairs={{0,1},{1,0},{2,3},{3,2},{4,5},{5,4},{6,7},{7,6},{8,9},{9,8},{10,11... | collective-permute-start | bytes 1572872 | tf_op jit(solution)/shard_map/ppermute | solution.py:307
  40.3 5.9 %collective-permute-start.14 = (bf16[256,256]{1,0:T(8,128)(2,1)S(1)}, bf16[256,256]{1,0:T(8,128)(2,1)S(1)}, u32[]{:S(2)}, u32[]{:S(2)}) collective-permute-start(bf16[256,256]{1,0:T(8,128)(2,1)S(1)} %get-tuple-element.45), channel_id=1, source_target_pairs={{2,0},{0,2},{3,1},{1,3},{6,4},{4,6},{7,5},{5,7},{10,8},{8,10},{11,... | collective-permute-start | bytes 393224 | tf_op jit(solution)/shard_map/ppermute | solution.py:476
  47.9 6.4 %collective-permute-start.21 = (bf16[512,256]{1,0:T(8,128)(2,1)S(1)}, bf16[512,256]{1,0:T(8,128)(2,1)S(1)}, u32[]{:S(2)}, u32[]{:S(2)}) collective-permute-start(bf16[512,256]{1,0:T(8,128)(2,1)S(1)} %constant_dynamic-slice_fusion.1), channel_id=1, source_target_pairs={{0,2},{1,5},{2,0},{3,7},{4,6},{5,1},{6,4},{7,3},{8,10},{9,13},{10,... | collective-permute-start | bytes 786440 | tf_op jit(solution)/shard_map/ppermute | solution.py:339
  54.5 6.8 %collective-permute-start.22 = (bf16[256,256]{1,0:T(8,128)(2,1)S(1)}, bf16[256,256]{1,0:T(8,128)(2,1)S(1)}, u32[]{:S(2)}, u32[]{:S(2)}) collective-permute-start(bf16[256,256]{1,0:T(8,128)(2,1)S(1)} %constant_dynamic-slice_fusion), channel_id=1, source_target_pairs={{0,4},{1,9},{2,6},{3,11},{4,0},{5,13},{6,2},{7,15},{8,12},{9,1},{1... | collective-permute-start | bytes 393224 | tf_op jit(solution)/shard_map/ppermute | solution.py:339
  61.4 7.8 %collective-permute-start.23 = (bf16[256,256]{1,0:T(8,128)(2,1)S(1)}, bf16[256,256]{1,0:T(8,128)(2,1)S(1)}, u32[]{:S(2)}, u32[]{:S(2)}) collective-permute-start(bf16[256,256]{1,0:T(8,128)(2,1)S(1)} %add_convert_fusion.2), channel_id=1, source_target_pairs={{0,8},{1,3},{2,10},{3,1},{4,12},{5,7},{6,14},{7,5},{8,0},{9,11},{1... | collective-permute-start | bytes 393224 | tf_op jit(solution)/shard_map/ppermute | solution.py:339
  63.5 8.0 %collective-permute-start.15 = (bf16[2,256,256]{2,1,0:T(8,128)(2,1)S(1)}, bf16[2,256,256]{2,1,0:T(8,128)(2,1)S(1)}, u32[]{:S(2)}, u32[]{:S(2)}) collective-permute-start(bf16[2,256,256]{2,1,0:T(8,128)(2,1)S(1)} %pad_maximum_fusion.after_ref), channel_id=1, source_target_pairs={{0,4},{4,0},{8,12},{12,8},{1,5},{5,1},{9,13},{13,9},{2,6},{6,2},{1... | collective-permute-start | bytes 786440 | tf_op jit(solution)/shard_map/ppermute | solution.py:307
  63.5 8.0 %collective-permute-start.16 = (bf16[2,256,256]{2,1,0:T(8,128)(2,1)S(1)}, bf16[2,256,256]{2,1,0:T(8,128)(2,1)S(1)}, u32[]{:S(2)}, u32[]{:S(2)}) collective-permute-start(bf16[2,256,256]{2,1,0:T(8,128)(2,1)S(1)} %pad_maximum_fusion.after_ref), channel_id=1, source_target_pairs={{0,0},{4,8},{8,4},{12,12},{1,1},{5,9},{9,5},{13,13},{2,2},{6,10},{... | collective-permute-start | bytes 786440 | tf_op jit(solution)/shard_map/ppermute | solution.py:307
  69.2 5.0 %collective-permute-start.24 = (bf16[256,256]{1,0:T(8,128)(2,1)S(1)}, bf16[256,256]{1,0:T(8,128)(2,1)S(1)}, u32[]{:S(2)}, u32[]{:S(2)}) collective-permute-start(bf16[256,256]{1,0:T(8,128)(2,1)S(1)} %add_convert_fusion.1), channel_id=1, source_target_pairs={{0,4},{1,9},{2,6},{3,11},{4,0},{5,13},{6,2},{7,15},{8,12},{9,1},{1... | collective-permute-start | bytes 393224 | tf_op jit(solution)/shard_map/ppermute | solution.py:339
  69.4 10.3 %collective-permute-start.17 = (bf16[2,256,256]{2,1,0:T(8,128)(2,1)S(1)}, bf16[2,256,256]{2,1,0:T(8,128)(2,1)S(1)}, u32[]{:S(2)}, u32[]{:S(2)}) collective-permute-start(bf16[2,256,256]{2,1,0:T(8,128)(2,1)S(1)} %pad_maximum_fusion.after_ref), channel_id=1, source_target_pairs={{0,1},{1,0},{2,3},{3,2},{4,5},{5,4},{6,7},{7,6},{8,9},{9,8},{10,11... | collective-permute-start | bytes 786440 | tf_op jit(solution)/shard_map/ppermute | solution.py:307
  71.4 8.3 %collective-permute-start.18 = (bf16[2,256,256]{2,1,0:T(8,128)(2,1)S(1)}, bf16[2,256,256]{2,1,0:T(8,128)(2,1)S(1)}, u32[]{:S(2)}, u32[]{:S(2)}) collective-permute-start(bf16[2,256,256]{2,1,0:T(8,128)(2,1)S(1)} %collective-permute-done.15), channel_id=1, source_target_pairs={{0,1},{1,0},{2,3},{3,2},{4,5},{5,4},{6,7},{7,6},{8,9},{9,8},{10,11... | collective-permute-start | bytes 786440 | tf_op jit(solution)/shard_map/ppermute | solution.py:307
  71.4 8.3 %collective-permute-start.19 = (bf16[2,256,256]{2,1,0:T(8,128)(2,1)S(1)}, bf16[2,256,256]{2,1,0:T(8,128)(2,1)S(1)}, u32[]{:S(2)}, u32[]{:S(2)}) collective-permute-start(bf16[2,256,256]{2,1,0:T(8,128)(2,1)S(1)} %collective-permute-done.16), channel_id=1, source_target_pairs={{0,1},{1,0},{2,3},{3,2},{4,5},{5,4},{6,7},{7,6},{8,9},{9,8},{10,11... | collective-permute-start | bytes 786440 | tf_op jit(solution)/shard_map/ppermute | solution.py:307
  74.4 7.3 %collective-permute-start.25 = (bf16[512,256]{1,0:T(8,128)(2,1)S(1)}, bf16[512,256]{1,0:T(8,128)(2,1)S(1)}, u32[]{:S(2)}, u32[]{:S(2)}) collective-permute-start(bf16[512,256]{1,0:T(8,128)(2,1)S(1)} %maximum_select_fusion.mine_ref), channel_id=1, source_target_pairs={{0,2},{1,5},{2,0},{3,7},{4,6},{5,1},{6,4},{7,3},{8,10},{9,13},{10,... | collective-permute-start | bytes 786440 | tf_op jit(solution)/shard_map/ppermute | solution.py:339
  (21 other events, 140.3 us)

commit v4 on v3

--- a/solution.py
+++ b/solution.py
@@ -10,6 +10,7 @@
 VMEM_BYTES = 20 * 1024 * 1024
 VMEM_ALL = 60 * 1024 * 1024
 STEPS = 4
+HALVING = 3
 
 
 def dot(left, right):
@@ -49,7 +50,7 @@
 
 
 def call(kernel, name, in_specs, out_specs, out_shape, flops, nbytes, grid=(), scratch=(), exps=0,
-         limit=VMEM_BYTES):
+         limit=VMEM_BYTES, weight=1):
     return pl.pallas_call(
         kernel,
         grid=grid,
@@ -58,7 +59,7 @@
         out_shape=out_shape,
         scratch_shapes=list(scratch),
         compiler_params=pltpu.CompilerParams(vmem_limit_bytes=limit),
-        cost_estimate=pl.CostEstimate(flops=1, bytes_accessed=1, transcendentals=0),
+        cost_estimate=pl.CostEstimate(flops=int(weight), bytes_accessed=1, transcendentals=0),
         name=name,
     )
 
@@ -88,29 +89,38 @@
         out[...] = block.reshape(out.shape).astype(out.dtype)
 
 
-def back_kernel(device_ref, slot_ref, after_ref, tiles_ref, cot_ref, own_ref, east_ref, side_ref, total):
-    step = pl.program_id(0)
-    count, rows = tiles_ref.shape[0], tiles_ref.shape[1]
+def back_kernel(
+    device_ref, slot_ref, tiles_ref, cot_ref, own_ref, east_ref, side_ref,
+    total, tiles, cots, tile_sems, cot_sems,
+):
+    blocks, rows = tiles.shape[0], tiles.shape[1]
+    count = blocks // STEPS
     slots = total.shape[0] // 6
-    channels = cot_ref.shape[0]
-    r = lax.axis_index("rep")
-
-    @pl.when(step == 0)
-    def _():
-        total[...] = jnp.zeros_like(total)
-
-    for i in range(count):
-        at = entry_of(device_ref, slot_ref, step * count + i, slots)
-        cot = cot_ref[:, i * rows : (i + 1) * rows]
-        total[at, :, :channels] += dot_last(node_half(tiles_ref[i], r), cot)
-
-    @pl.when(step == pl.num_programs(0) - 1)
-    def _():
-        for k, out in ((0, own_ref), (2, side_ref.at[0]), (4, side_ref.at[1])):
-            out[...] = total[k * slots : (k + 1) * slots].reshape(out.shape).astype(out.dtype)
-        for k in range(3):
-            block = total[(2 * k + 1) * slots : (2 * k + 2) * slots]
-            east_ref[k] = block.reshape(east_ref.shape[1:]).astype(east_ref.dtype)
+    channels = cots.shape[0]
+    r = lax.axis_index("rep")
+    copies = []
+    for k in range(STEPS):
+        part = pl.ds(k * count, count)
+        cols = pl.ds(k * count * rows, count * rows)
+        copies.append((
+            pltpu.make_async_copy(tiles_ref.at[part], tiles.at[part], tile_sems.at[k]),
+            pltpu.make_async_copy(cot_ref.at[:, cols], cots.at[:, cols], cot_sems.at[k]),
+        ))
+        for copy in copies[-1]:
+            copy.start()
+    total[...] = jnp.zeros_like(total)
+    for b in range(blocks):
+        if b % count == 0:
+            for copy in copies[b // count]:
+                copy.wait()
+        at = entry_of(device_ref, slot_ref, b, slots)
+        cot = cots[:, b * rows : (b + 1) * rows]
+        total[at, :, :channels] += dot_last(node_half(tiles[b], r), cot)
+    for k, out in ((0, own_ref), (2, side_ref.at[0]), (4, side_ref.at[1])):
+        out[...] = total[k * slots : (k + 1) * slots].reshape(out.shape).astype(out.dtype)
+    for k in range(3):
+        block = total[(2 * k + 1) * slots : (2 * k + 2) * slots]
+        east_ref[k] = block.reshape(east_ref.shape[1:]).astype(east_ref.dtype)
 
 
 def encode_kernel(
@@ -174,7 +184,7 @@
     own_a, even_a, odd_a, moved_a, own_b, even_b, odd_b, moved_b, embed_ref, embed_other_ref,
     back_ref, back_moved_ref, back_even_ref, back_odd_ref, local_ref, local_other_ref,
     up_ref, up_other_ref, down_ref, down_other_ref, out_ref, out_other_ref,
-    proj_ref, keep_ref, give_ref, mesh_keep_ref, mesh_give_ref,
+    proj_ref, keep_ref, give_ref, mesh_keep_ref,
 ):
     r = lax.axis_index("rep")
     nodes, width = moved_a.shape
@@ -227,10 +237,10 @@
     proj_ref[...] = jnp.zeros_like(proj_ref)
     proj_ref[:, :channels] = proj.astype(BF16)
     ends = ((keep_ref, mesh_own, local_ref), (give_ref, mesh_oth, local_other_ref))
+    start = latent + width
     for o_ref, mesh, local in ends:
         grad = dot_rows(cot, mesh)
-        start = latent + width
-        o_ref[start:, :] = grad.astype(o_ref.dtype)
+        o_ref[start : 2 * latent, :] = grad.astype(o_ref.dtype)
         o_ref[start : start + channels, :] = (grad[:channels] + local[...]).astype(o_ref.dtype)
 
     back = jnp.concatenate([back_own, back_oth], axis=1)
@@ -239,18 +249,27 @@
         - norm * jnp.mean(back * norm, axis=-1, keepdims=True)
     ) * inverse
     mesh_keep_ref[...] = grad_own.astype(F32) + slope[:, :width]
-    mesh_give_ref[...] = (grad_oth.astype(F32) + slope[:, width:]).astype(mesh_give_ref.dtype)
-
-
-def place_kernel(keep_ref, got_ref, out_ref):
-    r = lax.axis_index("rep")
-    part = out_ref.shape[:1] + out_ref.shape[2:]
-    out_ref[:, r] = keep_ref[...].reshape(part)
-    out_ref[:, 1 - r] = got_ref[...].astype(F32).reshape(part)
-
-
-def terms_kernel(after_ref, keep_ref, got_ref, out_ref):
-    out_ref[...] = added(keep_ref[...], got_ref[...]).astype(out_ref.dtype)
+    give_ref[2 * latent :, :] = (grad_oth.astype(F32) + slope[:, width:]).astype(give_ref.dtype)
+
+
+def terms_kernel(keep_ref, mesh_keep_ref, got_ref, out_ref, mesh_ref):
+    r = lax.axis_index("rep")
+    rows = keep_ref.shape[0]
+    part = mesh_ref.shape[:1] + mesh_ref.shape[2:]
+    out_ref[...] = added(keep_ref[...], got_ref[:rows, :]).astype(out_ref.dtype)
+    mesh_ref[:, r] = mesh_keep_ref[...].reshape(part)
+    mesh_ref[:, 1 - r] = got_ref[rows:, :].astype(F32).reshape(part)
+
+
+def first_sum_kernel(after_ref, terms_ref, got_ref, out_ref):
+    rows = got_ref.shape[0]
+    keep = terms_ref[pl.ds(pl.multiple_of(sum_bit(0) * rows, rows), rows), :]
+    out_ref[...] = added(keep, got_ref[...]).astype(out_ref.dtype)
+
+
+def pair_kernel(proj_ref, east_ref, pair_ref):
+    pair_ref[0] = proj_ref[...]
+    pair_ref[1] = east_ref[...]
 
 
 def finish_kernel(mine_ref, other_ref, out_ref, out_other_ref, up_ref, down_ref, grad_ref):
@@ -321,7 +340,10 @@
 
 
 def sum_bit(step):
-    bits = [(lax.axis_index(axis) // distance) % 2 for axis, distance in (o[step] for o in sum_orders())]
+    bits = [
+        lax.rem(lax.div(lax.axis_index(axis), distance), 2)
+        for axis, distance in (order[step] for order in sum_orders())
+    ]
     return jnp.where(lax.axis_index("rep") == 0, bits[0], bits[1])
 
 
@@ -339,18 +361,22 @@
     return lax.ppermute(value, ("lat", "lon", "rep"), pairs)
 
 
+def given_half(value, step):
+    rows = value.shape[0] // 2
+    return lax.dynamic_slice_in_dim(value, (1 - sum_bit(step)) * rows, rows, 0)
+
+
 def summed(value):
     count = len(sum_orders()[0])
-    halving = min(count - 1, 3)
-    for step in range(count):
+    halving = min(count - 1, HALVING)
+    for step in range(1, count):
         if step >= halving:
             value = (value.astype(F32) + sum_swap(value, step).astype(F32)).astype(BF16)
             continue
-        bit = sum_bit(step)
         rows = value.shape[0] // 2
-        keep = lax.dynamic_slice_in_dim(value, bit * rows, rows, 0)
-        give = lax.dynamic_slice_in_dim(value, (1 - bit) * rows, rows, 0)
-        value = (keep.astype(F32) + sum_swap(give, step).astype(F32)).astype(BF16)
+        keep = lax.dynamic_slice_in_dim(value, sum_bit(step) * rows, rows, 0)
+        got = sum_swap(given_half(value, step), step)
+        value = (keep.astype(F32) + got.astype(F32)).astype(BF16)
     for step in range(halving - 1, 0, -1):
         other = sum_swap(value, step)
         value = jnp.where(
@@ -407,21 +433,27 @@
             limit=limit,
         )(device, route_slot, after, grid_t, interp_tiles, weight)
 
-    own_a, even_a, odd_a, hidden_a = encode(w_embed, w_embed, VMEM_ALL)
-    even_in_a, odd_in_a = to_even(even_a), to_odd(odd_a)
-
     back_own, back_east, back_side = call(
         back_kernel, "back_messages",
-        [smem(), smem(), anywhere(), tiles_spec, cols_spec],
-        [whole((nodes, padded)), whole((3, nodes, padded)), whole((2, nodes, padded))],
+        [smem(), smem(), anywhere(), anywhere()],
+        [vmem()] * 3,
         [shape_of((nodes, padded), BF16), shape_of((3, nodes, padded), BF16),
          shape_of((2, nodes, padded), BF16)],
-        2 * grid_rows * half * padded, 3e6, grid=(STEPS,),
-        scratch=[pltpu.VMEM((6 * slots, half, padded), F32)],
-    )(device, route_slot, odd_a, interp_tiles, cot_t)
+        2 * grid_rows * half * padded, 3e6,
+        scratch=[
+            pltpu.VMEM((6 * slots, half, padded), F32),
+            pltpu.VMEM(interp_tiles.shape, BF16),
+            pltpu.VMEM(cot_t.shape, BF16),
+            pltpu.SemaphoreType.DMA((STEPS,)),
+            pltpu.SemaphoreType.DMA((STEPS,)),
+        ],
+        limit=VMEM_ALL,
+    )(device, route_slot, interp_tiles, cot_t)
     back_moved = to_east(back_east)
 
-    own_b, even_b, odd_b, hidden_b = encode(back_own, embed_other, VMEM_BYTES)
+    own_a, even_a, odd_a, hidden_a = encode(back_own, w_embed, VMEM_BYTES)
+    even_in_a, odd_in_a = to_even(even_a), to_odd(odd_a)
+    own_b, even_b, odd_b, hidden_b = encode(own_a, embed_other, VMEM_BYTES)
     even_in_b, odd_in_b = to_even(even_b), to_odd(odd_b)
 
     out_other, up_other, down_other = swap_rep(out_t), swap_rep(w_up), swap_rep(w_down)
@@ -442,7 +474,7 @@
             shape_of((nodes, width), BF16), 3 * nodes * width, 6e5, grid=(1,),
         )(after, *terms)
 
-    send_a = add_east(own_b, own_a, even_in_a, odd_in_a)
+    send_a = add_east(back_moved, own_a, even_in_a, odd_in_a)
     moved_a = to_east(send_a)
     send_b = add_east(moved_a, own_b, even_in_b, odd_in_b)
     moved_b = to_east(send_b)
@@ -457,15 +489,15 @@
     sums_specs = [first] * 3 + [whole((nodes, width))]
     weights = (w_up, up_other, w_down, down_other, out_t, out_other)
     back_spec = whole((nodes, padded))
-    proj, keep, give, mesh_keep, mesh_give = call(
+    proj, keep, give, mesh_keep = call(
         node_kernel, "node_update_and_gradients",
         sums_specs * 2 + [whole(embed_shape)] * 2
         + [back_spec, pl.BlockSpec((1, nodes, padded), lambda i: (0, 0, 0)), back_spec, back_spec]
         + [whole((channels, width))] * 2 + [whole(w.shape) for w in weights],
-        [whole((nodes, padded))] + [whole((2 * latent, width))] * 2 + [whole((nodes, width))] * 2,
+        [whole((nodes, padded)), whole((2 * latent, width)), whole((2 * latent + nodes, width)),
+         whole((nodes, width))],
         [shape_of((nodes, padded), BF16), shape_of((2 * latent, width), F32),
-         shape_of((2 * latent, width), BF16), shape_of((nodes, width), F32),
-         shape_of((nodes, width), BF16)],
+         shape_of((2 * latent + nodes, width), BF16), shape_of((nodes, width), F32)],
         15 * nodes * latent * latent, 9e6, grid=(1,), exps=nodes * latent,
     )(
         own_a, even_in_a, odd_in_a, moved_a, own_b, even_in_b, odd_in_b, moved_b,
@@ -474,19 +506,22 @@
     )
 
     east = lax.ppermute(proj, "lon", west_pairs)
-    pair = jnp.stack([proj, east])
+    terms, grad_mesh = call(
+        terms_kernel, "sum_terms", [vmem()] * 3, [vmem()] * 2,
+        [shape_of((2 * latent, width), BF16), shape_of(embed_shape, F32)],
+        2 * latent * width, 2e6,
+    )(keep, mesh_keep, swap_rep(give))
+    grad_mesh = grad_mesh.reshape(mesh_embed.shape)
+    pair = call(
+        pair_kernel, "pair_nodes", [vmem()] * 2, vmem(), shape_of((2, nodes, padded), BF16),
+        1, 1, weight=5e9,
+    )(proj, east)
+    halved = call(
+        first_sum_kernel, "first_sum", [anywhere()] + [vmem()] * 2, vmem(),
+        shape_of((latent, width), BF16), 2 * latent * width, 1e6,
+    )(pair, terms, sum_swap(given_half(terms, 0), 0))
     pair_even, pair_odd = to_even(pair), to_odd(pair)
-
-    terms = call(
-        terms_kernel, "sum_terms", [anywhere()] + [vmem()] * 2, vmem(),
-        shape_of((2 * latent, width), BF16), 2 * latent * width, 2e6,
-    )(pair, keep, swap_rep(give))
-    mine, theirs = summed(terms)
-
-    grad_mesh = call(
-        place_kernel, "place_mesh", [vmem()] * 2, vmem(), shape_of(embed_shape, F32),
-        nodes * latent, 1e6,
-    )(mesh_keep, swap_rep(mesh_give)).reshape(mesh_embed.shape)
+    mine, theirs = summed(halved)
 
     tables = (pair, pair_even, pair_odd)
     table_shape = (2 * slots, half, padded)

time: 83.5 us -> 82.3 us (0.986)
  the two profiles are of different devices: /device:TPU:0 before, /device:TPU:1 now
where the time goes in v4:
time: 82.3 us; the launch traced here: 82 us
  starting transfers between devices  35.7 us (43%)
  waiting for transfers between devices  22.2 us (27%)
  Pallas kernels  18.9 us (23%)
  local copies, waits for them, and re-layouts  4.19 us (5%)
  between operations  0.86 us (1%)
    ppermute x17, starting transfers between devices, along(): return lambda value: lax.ppermute(value, axis, pairs)  22.9 us
    ppermute x5, waiting for transfers between devices, sum_swap(): return lax.ppermute(value, ('lat', 'lon', 'rep'), pairs)  13.5 us
    ppermute x5, starting transfers between devices, sum_swap(): return lax.ppermute(value, ('lat', 'lon', 'rep'), pairs)  9.28 us
    ppermute x17, waiting for transfers between devices, along(): return lambda value: lax.ppermute(value, axis, pairs)  8.73 us
    pallas_call x2, Pallas kernels, encode(): call(encode_kernel, 'encode', [smem(), smem(), anywhere(), cols_spec, til...  5.52 us
    pallas_call x1, Pallas kernels, per_device(): call(back_kernel, 'back_messages', [smem(), smem(), anywhere(), anywhere(...  4.32 us
    unnamed x30, local copies, waits for them, and re-layouts  4.16 us
    pallas_call x1, Pallas kernels, per_device(): call(node_kernel, 'node_update_and_gradients', sums_specs * 2 + [whole(em...  2.99 us
  transfers between devices with their start and end apart: 26, of which 10 were waited for; matrix products, arithmetic and copies ran while one was open for 0% of the time, Pallas kernels for 12%

profile of v4, /device:TPU:1, one launch (start us, length us, event | category | flops | bytes accessed | tf_op | source)
XLA Modules:
  0.0 82.0 jit_solution(4509851690611362285)
XLA Ops:
  0.7 4.3 %back_messages.1 = (bf16[256,256]{1,0:T(8,128)(2,1)}, bf16[3,256,256]{2,1,0:T(8,128)(2,1)}, bf16[2,256,256]{2,1,0:T(8,128)(2,1)}) custom-call(s32[16]{0:T(128)} %bitcast.31, s32[16]{0:T(128)} %slot_ref.7, bf16[16,128,128]{2,1,0:T(8,128)(2,1)} %tiles_ref.7, bf16[227,2048]{1,0:T(8,128)(2,1)} %bitcast.17), custom_call_target="tpu_custom_call" | custom-call | flops 1 | bytes 1 | tf_op jit(solution)/shard_map/back_messages/pallas_call | solution.py:436
  5.0 2.1 %collective-permute-start.4 = (bf16[3,256,256]{2,1,0:T(8,128)(2,1)}, bf16[3,256,256]{2,1,0:T(8,128)(2,1)S(1)}, u32[]{:S(2)}, u32[]{:S(2)}) collective-permute-start(bf16[3,256,256]{2,1,0:T(8,128)(2,1)} %get-tuple-element.37), channel_id=1, source_target_pairs={{0,2},{2,0},{1,3},{3,1},{4,6},{6,4},{5,7},{7,5},{8,10},{10,8},{9,1... | collective-permute-start | bytes 1179656 | tf_op jit(solution)/shard_map/ppermute | solution.py:410
  9.6 2.8 %encode.2 = (bf16[2,256,256]{2,1,0:T(8,128)(2,1)S(1)}, bf16[2,256,256]{2,1,0:T(8,128)(2,1)S(1)}, bf16[2,256,256]{2,1,0:T(8,128)(2,1)S(1)}, bf16[1024,256]{1,0:T(8,128)(2,1)S(1)}) custom-call(s32[16]{0:T(128)S(1)} %bitcast.32, s32[16]{0:T(128)S(1)} %copy-done.14, bf16[256,256]{1,0:T(8,128)(2,1)S(1)} %copy-done.4, bf16[227,2048]{1,0:T(8,128)(2,1)S(1)} %bitcast.15, ...), custom_call_target="tpu_custom_call" | custom-call | flops 1 | bytes 1 | tf_op jit(solution)/shard_map/encode/pallas_call | solution.py:423
  12.3 1.4 %collective-permute-start.2 = (bf16[2,256,256]{2,1,0:T(8,128)(2,1)S(1)}, bf16[2,256,256]{2,1,0:T(8,128)(2,1)S(1)}, u32[]{:S(2)}, u32[]{:S(2)}) collective-permute-start(bf16[2,256,256]{2,1,0:T(8,128)(2,1)S(1)} %get-tuple-element.35), channel_id=1, source_target_pairs={{0,4},{4,0},{8,12},{12,8},{1,5},{5,1},{9,13},{13,9},{2,6},{6,2},{1... | collective-permute-start | bytes 786440 | tf_op jit(solution)/shard_map/ppermute | solution.py:326
  13.7 1.2 %collective-permute-start = (bf16[227,256]{1,0:T(8,128)(2,1)S(1)}, bf16[227,256]{1,0:T(8,128)(2,1)S(1)}, u32[]{:S(2)}, u32[]{:S(2)}) collective-permute-start(bf16[227,256]{1,0:T(8,128)(2,1)S(1)} %copy-done.12), channel_id=1, source_target_pairs={{0,1},{1,0},{2,3},{3,2},{4,5},{5,4},{6,7},{7,6},{8,9},{9,8},{10,11... | collective-permute-start | bytes 348680 | tf_op jit(solution)/shard_map/ppermute | solution.py:326
  15.9 2.8 %encode.3 = (bf16[2,256,256]{2,1,0:T(8,128)(2,1)S(1)}, bf16[2,256,256]{2,1,0:T(8,128)(2,1)S(1)}, bf16[2,256,256]{2,1,0:T(8,128)(2,1)S(1)}, bf16[1024,256]{1,0:T(8,128)(2,1)S(1)}) custom-call(s32[16]{0:T(128)S(1)} %bitcast.33, s32[16]{0:T(128)S(1)} %copy-done.14, bf16[2,256,256]{2,1,0:T(8,128)(2,1)S(1)} %get-tuple-element.32.after_ref.refs_1_.own_a, ...), custom_call_target="tpu_custom_call" | custom-call | flops 1 | bytes 1 | tf_op jit(solution)/shard_map/encode/pallas_call | solution.py:423
  18.7 3.6 %collective-permute-start.6 = (bf16[2,256,256]{2,1,0:T(8,128)(2,1)S(1)}, bf16[2,256,256]{2,1,0:T(8,128)(2,1)S(1)}, u32[]{:S(2)}, u32[]{:S(2)}) collective-permute-start(bf16[2,256,256]{2,1,0:T(8,128)(2,1)S(1)} %get-tuple-element.39), channel_id=1, source_target_pairs={{0,4},{4,0},{8,12},{12,8},{1,5},{5,1},{9,13},{13,9},{2,6},{6,2},{1... | collective-permute-start | bytes 786440 | tf_op jit(solution)/shard_map/ppermute | solution.py:326
  24.5 4.3 %collective-permute-done.6.refs_2_.even_b = bf16[2,256,256]{2,1,0:T(8,128)(2,1)S(1)} collective-permute-done((bf16[2,256,256]{2,1,0:T(8,128)(2,1)S(1)}, bf16[2,256,256]{2,1,0:T(8,128)(2,1)S(1)}, u32[]{:S(2)}, u32[]{:S(2)}) %collective-permute-start.6) | collective-permute-done | bytes 262176 | tf_op jit(solution)/shard_map/ppermute | solution.py:326
  30.9 3.2 %collective-permute-start.10 = (bf16[256,256]{1,0:T(8,128)(2,1)S(1)}, bf16[256,256]{1,0:T(8,128)(2,1)S(1)}, u32[]{:S(2)}, u32[]{:S(2)}) collective-permute-start(bf16[256,256]{1,0:T(8,128)(2,1)S(1)} %get-tuple-element.42), channel_id=1, source_target_pairs={{0,4},{4,0},{8,12},{12,8},{1,5},{5,1},{9,13},{13,9},{2,6},{6,2},{1... | collective-permute-start | bytes 393224 | tf_op jit(solution)/shard_map/ppermute | solution.py:326
  35.5 2.1 %collective-permute-done.10.back_even_ref = bf16[256,256]{1,0:T(8,128)(2,1)S(1)} collective-permute-done((bf16[256,256]{1,0:T(8,128)(2,1)S(1)}, bf16[256,256]{1,0:T(8,128)(2,1)S(1)}, u32[]{:S(2)}, u32[]{:S(2)}) %collective-permute-start.10) | collective-permute-done | bytes 131104 | tf_op jit(solution)/shard_map/ppermute | solution.py:326
  37.7 3.0 %node_update_and_gradients.1 = (bf16[256,256]{1,0:T(8,128)(2,1)S(1)}, f32[1024,256]{1,0:T(8,128)S(1)}, bf16[1280,256]{1,0:T(8,128)(2,1)}, f32[256,256]{1,0:T(8,128)S(1)}) custom-call(bf16[2,256,256]{2,1,0:T(8,128)(2,1)S(1)} %get-tuple-element.32.after_ref.refs_1_.own_a, bf16[2,256,256]{2,1,0:T(8,128)(2,1)S(1)} %collective-permute-done.2.refs_2_.even_a, ...), custom_call_target="tpu_custom_call" | custom-call | flops 1 | bytes 1 | tf_op jit(solution)/shard_map/node_update_and_gradients/pallas_call | solution.py:492
  43.0 1.2 %collective-permute-done.20.got_ref = bf16[1280,256]{1,0:T(8,128)(2,1)S(1)} collective-permute-done((bf16[1280,256]{1,0:T(8,128)(2,1)}, bf16[1280,256]{1,0:T(8,128)(2,1)S(1)}, u32[]{:S(2)}, u32[]{:S(2)}) %collective-permute-start.20) | collective-permute-done | bytes 655392 | tf_op jit(solution)/shard_map/ppermute | solution.py:326
  46.0 3.4 %collective-permute-start.21 = (bf16[512,256]{1,0:T(8,128)(2,1)S(1)}, bf16[512,256]{1,0:T(8,128)(2,1)S(1)}, u32[]{:S(2)}, u32[]{:S(2)}) collective-permute-start(bf16[512,256]{1,0:T(8,128)(2,1)S(1)} %constant_dynamic-slice_fusion.1), channel_id=1, source_target_pairs={{0,2},{1,5},{2,0},{3,7},{4,6},{5,1},{6,4},{7,3},{8,10},{9,13},{10,... | collective-permute-start | bytes 786440 | tf_op jit(solution)/shard_map/ppermute | solution.py:361
  50.4 2.8 %collective-permute-done.21.got_ref = bf16[512,256]{1,0:T(8,128)(2,1)S(1)} collective-permute-done((bf16[512,256]{1,0:T(8,128)(2,1)S(1)}, bf16[512,256]{1,0:T(8,128)(2,1)S(1)}, u32[]{:S(2)}, u32[]{:S(2)}) %collective-permute-start.21) | collective-permute-done | bytes 262176 | tf_op jit(solution)/shard_map/ppermute | solution.py:361
  53.3 2.2 %collective-permute-start.22 = (bf16[256,256]{1,0:T(8,128)(2,1)S(1)}, bf16[256,256]{1,0:T(8,128)(2,1)S(1)}, u32[]{:S(2)}, u32[]{:S(2)}) collective-permute-start(bf16[256,256]{1,0:T(8,128)(2,1)S(1)} %constant_dynamic-slice_fusion), channel_id=1, source_target_pairs={{0,4},{1,9},{2,6},{3,11},{4,0},{5,13},{6,2},{7,15},{8,12},{9,1},{1... | collective-permute-start | bytes 393224 | tf_op jit(solution)/shard_map/ppermute | solution.py:361
  55.5 2.7 %collective-permute-done.22 = bf16[256,256]{1,0:T(8,128)(2,1)S(1)} collective-permute-done((bf16[256,256]{1,0:T(8,128)(2,1)S(1)}, bf16[256,256]{1,0:T(8,128)(2,1)S(1)}, u32[]{:S(2)}, u32[]{:S(2)}) %collective-permute-start.22) | collective-permute-done | bytes 131104 | tf_op jit(solution)/shard_map/ppermute | solution.py:361
  59.1 1.9 %collective-permute-start.15 = (bf16[2,256,256]{2,1,0:T(8,128)(2,1)S(1)}, bf16[2,256,256]{2,1,0:T(8,128)(2,1)S(1)}, u32[]{:S(2)}, u32[]{:S(2)}) collective-permute-start(bf16[2,256,256]{2,1,0:T(8,128)(2,1)S(1)} %pair_nodes.1.after_ref), channel_id=1, source_target_pairs={{0,4},{4,0},{8,12},{12,8},{1,5},{5,1},{9,13},{13,9},{2,6},{6,2},{1... | collective-permute-start | bytes 786440 | tf_op jit(solution)/shard_map/ppermute | solution.py:326
  62.1 2.1 %collective-permute-start.24 = (bf16[256,256]{1,0:T(8,128)(2,1)S(1)}, bf16[256,256]{1,0:T(8,128)(2,1)S(1)}, u32[]{:S(2)}, u32[]{:S(2)}) collective-permute-start(bf16[256,256]{1,0:T(8,128)(2,1)S(1)} %add_convert_fusion), channel_id=1, source_target_pairs={{0,4},{1,9},{2,6},{3,11},{4,0},{5,13},{6,2},{7,15},{8,12},{9,1},{1... | collective-permute-start | bytes 393224 | tf_op jit(solution)/shard_map/ppermute | solution.py:361
  64.3 4.9 %collective-permute-start.17 = (bf16[2,256,256]{2,1,0:T(8,128)(2,1)S(1)}, bf16[2,256,256]{2,1,0:T(8,128)(2,1)S(1)}, u32[]{:S(2)}, u32[]{:S(2)}) collective-permute-start(bf16[2,256,256]{2,1,0:T(8,128)(2,1)S(1)} %pair_nodes.1.after_ref), channel_id=1, source_target_pairs={{0,1},{1,0},{2,3},{3,2},{4,5},{5,4},{6,7},{7,6},{8,9},{9,8},{10,11... | collective-permute-start | bytes 786440 | tf_op jit(solution)/shard_map/ppermute | solution.py:326
  69.2 1.2 %collective-permute-start.18 = (bf16[2,256,256]{2,1,0:T(8,128)(2,1)S(1)}, bf16[2,256,256]{2,1,0:T(8,128)(2,1)S(1)}, u32[]{:S(2)}, u32[]{:S(2)}) collective-permute-start(bf16[2,256,256]{2,1,0:T(8,128)(2,1)S(1)} %collective-permute-done.15), channel_id=1, source_target_pairs={{0,1},{1,0},{2,3},{3,2},{4,5},{5,4},{6,7},{7,6},{8,9},{9,8},{10,11... | collective-permute-start | bytes 786440 | tf_op jit(solution)/shard_map/ppermute | solution.py:326
  70.4 5.0 %collective-permute-done.24 = bf16[256,256]{1,0:T(8,128)(2,1)S(1)} collective-permute-done((bf16[256,256]{1,0:T(8,128)(2,1)S(1)}, bf16[256,256]{1,0:T(8,128)(2,1)S(1)}, u32[]{:S(2)}, u32[]{:S(2)}) %collective-permute-start.24) | collective-permute-done | bytes 131104 | tf_op jit(solution)/shard_map/ppermute | solution.py:361
  76.2 2.0 %decode.1 = bf16[227,1024]{1,0:T(8,128)(2,1)} custom-call(s32[16]{0:T(128)S(1)} %bitcast.34, s32[16]{0:T(128)S(1)} %copy-done.14, bf16[16,128,128]{2,1,0:T(8,128)(2,1)S(1)} %copy-done, f32[227,1024]{1,0:T(8,128)S(1)} %get-tuple-element.34.base_ref, bf16[8,64,256]{2,1,0:T(8,128)(2,1)S(1)} %bitcast.23, bf16[8,64,256]{2,1,0:T(8,128)(2,1)S(1)} %bitcast.26, ...), custom_call_target="tpu_custom_call" | custom-call | flops 1 | bytes 1 | tf_op jit(solution)/shard_map/decode/pallas_call | solution.py:528
  78.1 2.6 %collective-permute-done.25.other_ref = bf16[512,256]{1,0:T(8,128)(2,1)S(1)} collective-permute-done((bf16[512,256]{1,0:T(8,128)(2,1)S(1)}, bf16[512,256]{1,0:T(8,128)(2,1)S(1)}, u32[]{:S(2)}, u32[]{:S(2)}) %collective-permute-start.25) | collective-permute-done | bytes 262176 | tf_op jit(solution)/shard_map/ppermute | solution.py:361
  80.7 1.3 %finish.1 = (f32[512,256]{1,0:T(8,128)}, f32[256,512]{1,0:T(8,128)}, f32[227,256]{1,0:T(8,128)}) custom-call(bf16[512,256]{1,0:T(8,128)(2,1)S(1)} %maximum_select_fusion.mine_ref, bf16[512,256]{1,0:T(8,128)(2,1)S(1)} %collective-permute-done.25.other_ref, bf16[227,256]{1,0:T(8,128)(2,1)S(1)} %bitcast.22, ...), custom_call_target="tpu_custom_call" | custom-call | flops 1 | bytes 1 | tf_op jit(solution)/shard_map/finish/pallas_call | solution.py:538
  (76 shorter events, 17.1 us)
Async XLA Ops:
  5.0 18.8 %collective-permute-start.4 = (bf16[3,256,256]{2,1,0:T(8,128)(2,1)}, bf16[3,256,256]{2,1,0:T(8,128)(2,1)S(1)}, u32[]{:S(2)}, u32[]{:S(2)}) collective-permute-start(bf16[3,256,256]{2,1,0:T(8,128)(2,1)} %get-tuple-element.37), channel_id=1, source_target_pairs={{0,2},{2,0},{1,3},{3,1},{4,6},{6,4},{5,7},{7,5},{8,10},{10,8},{9,1... | collective-permute-start | bytes 1179656 | tf_op jit(solution)/shard_map/ppermute | solution.py:410
  12.3 10.8 %collective-permute-start.2 = (bf16[2,256,256]{2,1,0:T(8,128)(2,1)S(1)}, bf16[2,256,256]{2,1,0:T(8,128)(2,1)S(1)}, u32[]{:S(2)}, u32[]{:S(2)}) collective-permute-start(bf16[2,256,256]{2,1,0:T(8,128)(2,1)S(1)} %get-tuple-element.35), channel_id=1, source_target_pairs={{0,4},{4,0},{8,12},{12,8},{1,5},{5,1},{9,13},{13,9},{2,6},{6,2},{1... | collective-permute-start | bytes 786440 | tf_op jit(solution)/shard_map/ppermute | solution.py:326
  14.9 8.8 %collective-permute-start.3 = (bf16[2,256,256]{2,1,0:T(8,128)(2,1)S(1)}, bf16[2,256,256]{2,1,0:T(8,128)(2,1)S(1)}, u32[]{:S(2)}, u32[]{:S(2)}) collective-permute-start(bf16[2,256,256]{2,1,0:T(8,128)(2,1)S(1)} %get-tuple-element.36), channel_id=1, source_target_pairs={{0,0},{4,8},{8,4},{12,12},{1,1},{5,9},{9,5},{13,13},{2,2},{6,10},{... | collective-permute-start | bytes 786440 | tf_op jit(solution)/shard_map/ppermute | solution.py:326
  18.7 10.1 %collective-permute-start.6 = (bf16[2,256,256]{2,1,0:T(8,128)(2,1)S(1)}, bf16[2,256,256]{2,1,0:T(8,128)(2,1)S(1)}, u32[]{:S(2)}, u32[]{:S(2)}) collective-permute-start(bf16[2,256,256]{2,1,0:T(8,128)(2,1)S(1)} %get-tuple-element.39), channel_id=1, source_target_pairs={{0,4},{4,0},{8,12},{12,8},{1,5},{5,1},{9,13},{13,9},{2,6},{6,2},{1... | collective-permute-start | bytes 786440 | tf_op jit(solution)/shard_map/ppermute | solution.py:326
  22.3 7.3 %collective-permute-start.7 = (bf16[2,256,256]{2,1,0:T(8,128)(2,1)S(1)}, bf16[2,256,256]{2,1,0:T(8,128)(2,1)S(1)}, u32[]{:S(2)}, u32[]{:S(2)}) collective-permute-start(bf16[2,256,256]{2,1,0:T(8,128)(2,1)S(1)} %get-tuple-element.40), channel_id=1, source_target_pairs={{0,0},{4,8},{8,4},{12,12},{1,1},{5,9},{9,5},{13,13},{2,2},{6,10},{... | collective-permute-start | bytes 786440 | tf_op jit(solution)/shard_map/ppermute | solution.py:326
  23.2 10.9 %collective-permute-start.9 = (bf16[512,256]{1,0:T(8,128)(2,1)S(1)}, bf16[512,256]{1,0:T(8,128)(2,1)S(1)}, u32[]{:S(2)}, u32[]{:S(2)}) collective-permute-start(bf16[512,256]{1,0:T(8,128)(2,1)S(1)} %copy-done.6), channel_id=1, source_target_pairs={{0,1},{1,0},{2,3},{3,2},{4,5},{5,4},{6,7},{7,6},{8,9},{9,8},{10,11... | collective-permute-start | bytes 786440 | tf_op jit(solution)/shard_map/ppermute | solution.py:326
  23.9 5.8 %collective-permute-start.5 = (bf16[256,256]{1,0:T(8,128)(2,1)S(1)}, bf16[256,256]{1,0:T(8,128)(2,1)S(1)}, u32[]{:S(2)}, u32[]{:S(2)}) collective-permute-start(bf16[256,256]{1,0:T(8,128)(2,1)S(1)} %add_east.2), channel_id=1, source_target_pairs={{0,2},{2,0},{1,3},{3,1},{4,6},{6,4},{5,7},{7,5},{8,10},{10,8},{9,1... | collective-permute-start | bytes 393224 | tf_op jit(solution)/shard_map/ppermute | solution.py:410
  24.2 11.3 %collective-permute-start.12 = (bf16[512,256]{1,0:T(8,128)(2,1)S(1)}, bf16[512,256]{1,0:T(8,128)(2,1)S(1)}, u32[]{:S(2)}, u32[]{:S(2)}) collective-permute-start(bf16[512,256]{1,0:T(8,128)(2,1)S(1)} %copy-done.7), channel_id=1, source_target_pairs={{0,1},{1,0},{2,3},{3,2},{4,5},{5,4},{6,7},{7,6},{8,9},{9,8},{10,11... | collective-permute-start | bytes 786440 | tf_op jit(solution)/shard_map/ppermute | solution.py:326
  28.8 6.7 %collective-permute-start.13 = (bf16[256,512]{1,0:T(8,128)(2,1)S(1)}, bf16[256,512]{1,0:T(8,128)(2,1)S(1)}, u32[]{:S(2)}, u32[]{:S(2)}) collective-permute-start(bf16[256,512]{1,0:T(8,128)(2,1)S(1)} %copy-done.8), channel_id=1, source_target_pairs={{0,1},{1,0},{2,3},{3,2},{4,5},{5,4},{6,7},{7,6},{8,9},{9,8},{10,11... | collective-permute-start | bytes 786440 | tf_op jit(solution)/shard_map/ppermute | solution.py:326
  29.7 5.8 %collective-permute-start.8 = (bf16[256,256]{1,0:T(8,128)(2,1)S(1)}, bf16[256,256]{1,0:T(8,128)(2,1)S(1)}, u32[]{:S(2)}, u32[]{:S(2)}) collective-permute-start(bf16[256,256]{1,0:T(8,128)(2,1)S(1)} %add_east.3.after_ref), channel_id=1, source_target_pairs={{0,2},{2,0},{1,3},{3,1},{4,6},{6,4},{5,7},{7,5},{8,10},{10,8},{9,1... | collective-permute-start | bytes 393224 | tf_op jit(solution)/shard_map/ppermute | solution.py:410
  30.9 6.7 %collective-permute-start.10 = (bf16[256,256]{1,0:T(8,128)(2,1)S(1)}, bf16[256,256]{1,0:T(8,128)(2,1)S(1)}, u32[]{:S(2)}, u32[]{:S(2)}) collective-permute-start(bf16[256,256]{1,0:T(8,128)(2,1)S(1)} %get-tuple-element.42), channel_id=1, source_target_pairs={{0,4},{4,0},{8,12},{12,8},{1,5},{5,1},{9,13},{13,9},{2,6},{6,2},{1... | collective-permute-start | bytes 393224 | tf_op jit(solution)/shard_map/ppermute | solution.py:326
  34.1 3.6 %collective-permute-start.11 = (bf16[256,256]{1,0:T(8,128)(2,1)S(1)}, bf16[256,256]{1,0:T(8,128)(2,1)S(1)}, u32[]{:S(2)}, u32[]{:S(2)}) collective-permute-start(bf16[256,256]{1,0:T(8,128)(2,1)S(1)} %get-tuple-element.43), channel_id=1, source_target_pairs={{0,0},{4,8},{8,4},{12,12},{1,1},{5,9},{9,5},{13,13},{2,2},{6,10},{... | collective-permute-start | bytes 393224 | tf_op jit(solution)/shard_map/ppermute | solution.py:326
  41.4 2.8 %collective-permute-start.20 = (bf16[1280,256]{1,0:T(8,128)(2,1)}, bf16[1280,256]{1,0:T(8,128)(2,1)S(1)}, u32[]{:S(2)}, u32[]{:S(2)}) collective-permute-start(bf16[1280,256]{1,0:T(8,128)(2,1)} %get-tuple-element.49), channel_id=1, source_target_pairs={{0,1},{1,0},{2,3},{3,2},{4,5},{5,4},{6,7},{7,6},{8,9},{9,8},{10,11... | collective-permute-start | bytes 1966088 | tf_op jit(solution)/shard_map/ppermute | solution.py:326
  42.2 7.2 %collective-permute-start.14 = (bf16[256,256]{1,0:T(8,128)(2,1)S(1)}, bf16[256,256]{1,0:T(8,128)(2,1)}, u32[]{:S(2)}, u32[]{:S(2)}) collective-permute-start(bf16[256,256]{1,0:T(8,128)(2,1)S(1)} %get-tuple-element.46.proj_ref), channel_id=1, source_target_pairs={{2,0},{0,2},{3,1},{1,3},{6,4},{4,6},{7,5},{5,7},{10,8},{8,10},{11,... | collective-permute-start | bytes 393224 | tf_op jit(solution)/shard_map/ppermute | solution.py:508
  46.0 7.2 %collective-permute-start.21 = (bf16[512,256]{1,0:T(8,128)(2,1)S(1)}, bf16[512,256]{1,0:T(8,128)(2,1)S(1)}, u32[]{:S(2)}, u32[]{:S(2)}) collective-permute-start(bf16[512,256]{1,0:T(8,128)(2,1)S(1)} %constant_dynamic-slice_fusion.1), channel_id=1, source_target_pairs={{0,2},{1,5},{2,0},{3,7},{4,6},{5,1},{6,4},{7,3},{8,10},{9,13},{10,... | collective-permute-start | bytes 786440 | tf_op jit(solution)/shard_map/ppermute | solution.py:361
  53.3 4.8 %collective-permute-start.22 = (bf16[256,256]{1,0:T(8,128)(2,1)S(1)}, bf16[256,256]{1,0:T(8,128)(2,1)S(1)}, u32[]{:S(2)}, u32[]{:S(2)}) collective-permute-start(bf16[256,256]{1,0:T(8,128)(2,1)S(1)} %constant_dynamic-slice_fusion), channel_id=1, source_target_pairs={{0,4},{1,9},{2,6},{3,11},{4,0},{5,13},{6,2},{7,15},{8,12},{9,1},{1... | collective-permute-start | bytes 393224 | tf_op jit(solution)/shard_map/ppermute | solution.py:361
  58.2 3.9 %collective-permute-start.23 = (bf16[256,256]{1,0:T(8,128)(2,1)S(1)}, bf16[256,256]{1,0:T(8,128)(2,1)S(1)}, u32[]{:S(2)}, u32[]{:S(2)}) collective-permute-start(bf16[256,256]{1,0:T(8,128)(2,1)S(1)} %add_convert_fusion.1), channel_id=1, source_target_pairs={{0,8},{1,3},{2,10},{3,1},{4,12},{5,7},{6,14},{7,5},{8,0},{9,11},{1... | collective-permute-start | bytes 393224 | tf_op jit(solution)/shard_map/ppermute | solution.py:361
  59.1 10.1 %collective-permute-start.15 = (bf16[2,256,256]{2,1,0:T(8,128)(2,1)S(1)}, bf16[2,256,256]{2,1,0:T(8,128)(2,1)S(1)}, u32[]{:S(2)}, u32[]{:S(2)}) collective-permute-start(bf16[2,256,256]{2,1,0:T(8,128)(2,1)S(1)} %pair_nodes.1.after_ref), channel_id=1, source_target_pairs={{0,4},{4,0},{8,12},{12,8},{1,5},{5,1},{9,13},{13,9},{2,6},{6,2},{1... | collective-permute-start | bytes 786440 | tf_op jit(solution)/shard_map/ppermute | solution.py:326
  61.0 9.3 %collective-permute-start.16 = (bf16[2,256,256]{2,1,0:T(8,128)(2,1)S(1)}, bf16[2,256,256]{2,1,0:T(8,128)(2,1)S(1)}, u32[]{:S(2)}, u32[]{:S(2)}) collective-permute-start(bf16[2,256,256]{2,1,0:T(8,128)(2,1)S(1)} %pair_nodes.1.after_ref), channel_id=1, source_target_pairs={{0,0},{4,8},{8,4},{12,12},{1,1},{5,9},{9,5},{13,13},{2,2},{6,10},{... | collective-permute-start | bytes 786440 | tf_op jit(solution)/shard_map/ppermute | solution.py:326
  62.1 13.2 %collective-permute-start.24 = (bf16[256,256]{1,0:T(8,128)(2,1)S(1)}, bf16[256,256]{1,0:T(8,128)(2,1)S(1)}, u32[]{:S(2)}, u32[]{:S(2)}) collective-permute-start(bf16[256,256]{1,0:T(8,128)(2,1)S(1)} %add_convert_fusion), channel_id=1, source_target_pairs={{0,4},{1,9},{2,6},{3,11},{4,0},{5,13},{6,2},{7,15},{8,12},{9,1},{1... | collective-permute-start | bytes 393224 | tf_op jit(solution)/shard_map/ppermute | solution.py:361
  64.3 11.9 %collective-permute-start.17 = (bf16[2,256,256]{2,1,0:T(8,128)(2,1)S(1)}, bf16[2,256,256]{2,1,0:T(8,128)(2,1)S(1)}, u32[]{:S(2)}, u32[]{:S(2)}) collective-permute-start(bf16[2,256,256]{2,1,0:T(8,128)(2,1)S(1)} %pair_nodes.1.after_ref), channel_id=1, source_target_pairs={{0,1},{1,0},{2,3},{3,2},{4,5},{5,4},{6,7},{7,6},{8,9},{9,8},{10,11... | collective-permute-start | bytes 786440 | tf_op jit(solution)/shard_map/ppermute | solution.py:326
  69.2 7.0 %collective-permute-start.18 = (bf16[2,256,256]{2,1,0:T(8,128)(2,1)S(1)}, bf16[2,256,256]{2,1,0:T(8,128)(2,1)S(1)}, u32[]{:S(2)}, u32[]{:S(2)}) collective-permute-start(bf16[2,256,256]{2,1,0:T(8,128)(2,1)S(1)} %collective-permute-done.15), channel_id=1, source_target_pairs={{0,1},{1,0},{2,3},{3,2},{4,5},{5,4},{6,7},{7,6},{8,9},{9,8},{10,11... | collective-permute-start | bytes 786440 | tf_op jit(solution)/shard_map/ppermute | solution.py:326
  70.4 5.8 %collective-permute-start.19 = (bf16[2,256,256]{2,1,0:T(8,128)(2,1)S(1)}, bf16[2,256,256]{2,1,0:T(8,128)(2,1)S(1)}, u32[]{:S(2)}, u32[]{:S(2)}) collective-permute-start(bf16[2,256,256]{2,1,0:T(8,128)(2,1)S(1)} %collective-permute-done.16), channel_id=1, source_target_pairs={{0,1},{1,0},{2,3},{3,2},{4,5},{5,4},{6,7},{7,6},{8,9},{9,8},{10,11... | collective-permute-start | bytes 786440 | tf_op jit(solution)/shard_map/ppermute | solution.py:326
  75.4 5.3 %collective-permute-start.25 = (bf16[512,256]{1,0:T(8,128)(2,1)S(1)}, bf16[512,256]{1,0:T(8,128)(2,1)S(1)}, u32[]{:S(2)}, u32[]{:S(2)}) collective-permute-start(bf16[512,256]{1,0:T(8,128)(2,1)S(1)} %maximum_select_fusion.mine_ref), channel_id=1, source_target_pairs={{0,2},{1,5},{2,0},{3,7},{4,6},{5,1},{6,4},{7,3},{8,10},{9,13},{10,... | collective-permute-start | bytes 786440 | tf_op jit(solution)/shard_map/ppermute | solution.py:361
  (17 other events, 64.2 us)

commit v5 on v4

--- a/solution.py
+++ b/solution.py
@@ -8,7 +8,6 @@
 F32 = jnp.float32
 BF16 = jnp.bfloat16
 VMEM_BYTES = 20 * 1024 * 1024
-VMEM_ALL = 60 * 1024 * 1024
 STEPS = 4
 HALVING = 3
 
@@ -184,7 +183,7 @@
     own_a, even_a, odd_a, moved_a, own_b, even_b, odd_b, moved_b, embed_ref, embed_other_ref,
     back_ref, back_moved_ref, back_even_ref, back_odd_ref, local_ref, local_other_ref,
     up_ref, up_other_ref, down_ref, down_other_ref, out_ref, out_other_ref,
-    proj_ref, keep_ref, give_ref, mesh_keep_ref,
+    proj_ref, keep_ref, give_ref,
 ):
     r = lax.axis_index("rep")
     nodes, width = moved_a.shape
@@ -248,16 +247,16 @@
         back - jnp.mean(back, axis=-1, keepdims=True)
         - norm * jnp.mean(back * norm, axis=-1, keepdims=True)
     ) * inverse
-    mesh_keep_ref[...] = grad_own.astype(F32) + slope[:, :width]
+    keep_ref[2 * latent :, :] = grad_own.astype(F32) + slope[:, :width]
     give_ref[2 * latent :, :] = (grad_oth.astype(F32) + slope[:, width:]).astype(give_ref.dtype)
 
 
-def terms_kernel(keep_ref, mesh_keep_ref, got_ref, out_ref, mesh_ref):
-    r = lax.axis_index("rep")
-    rows = keep_ref.shape[0]
+def terms_kernel(keep_ref, got_ref, out_ref, mesh_ref):
+    r = lax.axis_index("rep")
+    rows = out_ref.shape[0]
     part = mesh_ref.shape[:1] + mesh_ref.shape[2:]
-    out_ref[...] = added(keep_ref[...], got_ref[:rows, :]).astype(out_ref.dtype)
-    mesh_ref[:, r] = mesh_keep_ref[...].reshape(part)
+    out_ref[...] = added(keep_ref[:rows, :], got_ref[:rows, :]).astype(out_ref.dtype)
+    mesh_ref[:, r] = keep_ref[rows:, :].reshape(part)
     mesh_ref[:, 1 - r] = got_ref[rows:, :].astype(F32).reshape(part)
 
 
@@ -296,22 +295,30 @@
         place(other_ref, mine_ref)
 
 
-def decode_kernel(device_ref, slot_ref, tiles_ref, base_ref, *refs):
-    mine, theirs, out_ref, picked = refs[:3], refs[3:6], refs[6], refs[7]
-    r = lax.axis_index("rep")
-    count, rows = tiles_ref.shape[0], tiles_ref.shape[1]
-    half = rows // 2
+def pick_kernel(device_ref, slot_ref, pair_ref, even_ref, odd_ref, mine_ref, theirs_ref):
+    r = lax.axis_index("rep")
+    tables = (pair_ref, even_ref, odd_ref)
+    blocks = mine_ref.shape[0]
+    per = pair_ref.shape[0]
+    for out_ref, first in ((mine_ref, r * blocks), (theirs_ref, (1 - r) * blocks)):
+        for i in range(blocks):
+            at = entry_of(device_ref, slot_ref, first + i, per // 2)
+            for k, table in enumerate(tables):
+                @pl.when(at // per == k)
+                def _(k=k, i=i, at=at, table=table, out_ref=out_ref):
+                    out_ref[i] = table[at - k * per]
+
+
+def decode_kernel(tiles_ref, base_ref, mine_ref, got_ref, out_ref, picked):
+    r = lax.axis_index("rep")
+    blocks, half = mine_ref.shape[:2]
+    rows = tiles_ref.shape[1]
     channels = out_ref.shape[0]
-    blocks = count // 2
-    per = mine[0].shape[0]
+    own = pl.ds(pl.multiple_of(r * half, half), half)
+    other = pl.ds(pl.multiple_of((1 - r) * half, half), half)
     for i in range(blocks):
-        at = entry_of(device_ref, slot_ref, r * blocks + i, per // 2)
-        for k in range(3):
-            @pl.when(at // per == k)
-            def _(k=k, i=i, at=at):
-                where = at - k * per
-                picked[i, pl.ds(pl.multiple_of(r * half, half), half), :] = mine[k][where]
-                picked[i, pl.ds(pl.multiple_of((1 - r) * half, half), half), :] = theirs[k][where]
+        picked[i, own, :] = mine_ref[i]
+        picked[i, other, :] = got_ref[i]
     for i in range(blocks):
         cols = slice(i * rows, (i + 1) * rows)
         decoded = dot_last(picked[i].T, tiles_ref[r * blocks + i])
@@ -409,8 +416,11 @@
     west_pairs = [(j, i) for i, j in east_pairs]
     to_east = lambda value: lax.ppermute(value, "lon", east_pairs)
 
-    device = route_device.reshape(blocks)
+    in_hbm = lambda value: pltpu.with_memory_space_constraint(value, pltpu.HBM)
+    device, slot = route_device.reshape(blocks), route_slot
     grid_t, cot_t, out_t = grid_in.T, cotangent.T, w_out.T
+    routes = (in_hbm(device), in_hbm(slot))
+    tiles_in, grid_in_t, cot_in_t = in_hbm(interp_tiles), in_hbm(grid_t), in_hbm(cot_t)
     per_step = blocks // STEPS
     step_rows = per_step * tile_rows
     tiles_spec = pl.BlockSpec((per_step, tile_rows, tile_rows), lambda i: (i, 0, 0))
@@ -431,7 +441,7 @@
                 pltpu.VMEM((step_rows, width), BF16),
             ],
             limit=limit,
-        )(device, route_slot, after, grid_t, interp_tiles, weight)
+        )(*routes, after, grid_in_t, tiles_in, weight)
 
     back_own, back_east, back_side = call(
         back_kernel, "back_messages",
@@ -447,11 +457,10 @@
             pltpu.SemaphoreType.DMA((STEPS,)),
             pltpu.SemaphoreType.DMA((STEPS,)),
         ],
-        limit=VMEM_ALL,
-    )(device, route_slot, interp_tiles, cot_t)
+    )(*routes, tiles_in, cot_in_t)
     back_moved = to_east(back_east)
 
-    own_a, even_a, odd_a, hidden_a = encode(back_own, w_embed, VMEM_BYTES)
+    own_a, even_a, odd_a, hidden_a = encode(back_own, in_hbm(w_embed), VMEM_BYTES)
     even_in_a, odd_in_a = to_even(even_a), to_odd(odd_a)
     own_b, even_b, odd_b, hidden_b = encode(own_a, embed_other, VMEM_BYTES)
     even_in_b, odd_in_b = to_even(even_b), to_odd(odd_b)
@@ -489,15 +498,14 @@
     sums_specs = [first] * 3 + [whole((nodes, width))]
     weights = (w_up, up_other, w_down, down_other, out_t, out_other)
     back_spec = whole((nodes, padded))
-    proj, keep, give, mesh_keep = call(
+    proj, keep, give = call(
         node_kernel, "node_update_and_gradients",
         sums_specs * 2 + [whole(embed_shape)] * 2
         + [back_spec, pl.BlockSpec((1, nodes, padded), lambda i: (0, 0, 0)), back_spec, back_spec]
         + [whole((channels, width))] * 2 + [whole(w.shape) for w in weights],
-        [whole((nodes, padded)), whole((2 * latent, width)), whole((2 * latent + nodes, width)),
-         whole((nodes, width))],
-        [shape_of((nodes, padded), BF16), shape_of((2 * latent, width), F32),
-         shape_of((2 * latent + nodes, width), BF16), shape_of((nodes, width), F32)],
+        [whole((nodes, padded))] + [whole((2 * latent + nodes, width))] * 2,
+        [shape_of((nodes, padded), BF16), shape_of((2 * latent + nodes, width), F32),
+         shape_of((2 * latent + nodes, width), BF16)],
         15 * nodes * latent * latent, 9e6, grid=(1,), exps=nodes * latent,
     )(
         own_a, even_in_a, odd_in_a, moved_a, own_b, even_in_b, odd_in_b, moved_b,
@@ -507,10 +515,10 @@
 
     east = lax.ppermute(proj, "lon", west_pairs)
     terms, grad_mesh = call(
-        terms_kernel, "sum_terms", [vmem()] * 3, [vmem()] * 2,
+        terms_kernel, "sum_terms", [vmem()] * 2, [vmem()] * 2,
         [shape_of((2 * latent, width), BF16), shape_of(embed_shape, F32)],
         2 * latent * width, 2e6,
-    )(keep, mesh_keep, swap_rep(give))
+    )(keep, swap_rep(give))
     grad_mesh = grad_mesh.reshape(mesh_embed.shape)
     pair = call(
         pair_kernel, "pair_nodes", [vmem()] * 2, vmem(), shape_of((2, nodes, padded), BF16),
@@ -523,17 +531,16 @@
     pair_even, pair_odd = to_even(pair), to_odd(pair)
     mine, theirs = summed(halved)
 
-    tables = (pair, pair_even, pair_odd)
     table_shape = (2 * slots, half, padded)
+    mine_picked, theirs_picked = call(
+        pick_kernel, "pick_nodes", [smem()] * 2 + [vmem()] * 3, [vmem()] * 2,
+        [shape_of((blocks // 2, half, padded), BF16)] * 2, 1, 1, weight=5e9,
+    )(device, slot, *[table.reshape(table_shape) for table in (pair, pair_even, pair_odd)])
     grid_out = call(
-        decode_kernel, "decode", [smem(), smem()] + [vmem()] * 8, vmem(),
+        decode_kernel, "decode", [vmem()] * 4, vmem(),
         shape_of((channels, my_rows), BF16), 2 * my_rows * tile_rows * padded, 4e6,
         scratch=[pltpu.VMEM((blocks // 2, tile_rows, padded), BF16)],
-    )(
-        device, route_slot, interp_tiles, base,
-        *[table.reshape(table_shape) for table in tables],
-        *[swap_rep(table).reshape(table_shape) for table in tables],
-    ).T
+    )(interp_tiles, base, mine_picked, swap_rep(theirs_picked)).T
 
     grad_up, grad_down, grad_out = call(
         finish_kernel, "finish", [vmem()] * 4, [vmem()] * 3,

time: 82.3 us -> 80.2 us (0.974)
  local copies, waits for them, and re-layouts: 4.19 us -> 0.08 us
  waiting for transfers between devices: 22.2 us -> 24.8 us
  starting transfers between devices: 35.7 us -> 34.3 us
    unnamed x30 -> x18, local copies, waits for them, and re-layouts: 4.16 us -> 0.05 us
    ppermute x17 -> x15, waiting for transfers between devices: 8.73 us -> 12.2 us  [along(): return lambda value: lax.ppermute(value, axis, pairs)]
    ppermute x17 -> x15, starting transfers between devices: 22.9 us -> 20.3 us  [along(): return lambda value: lax.ppermute(value, axis, pairs)]
    pallas_call x2, Pallas kernels: 5.52 us -> 7.65 us  [encode(): call(encode_kernel, 'encode', [smem(), smem(), anywhere(), cols_spec, til...]
    ppermute x5, starting transfers between devices: 9.28 us -> 10.5 us  [sum_swap(): return lax.ppermute(value, ('lat', 'lon', 'rep'), pairs)]
    pallas_call x1, Pallas kernels: 0.92 us -> 0.02 us  [per_device(): call(pair_kernel, 'pair_nodes', [vmem()] * 2, vmem(), shape_of((2, nodes,...]
    ppermute x5, waiting for transfers between devices: 13.5 us -> 12.6 us  [sum_swap(): return lax.ppermute(value, ('lat', 'lon', 'rep'), pairs)]
    pallas_call x1, Pallas kernels: 4.32 us -> 3.49 us  [per_device(): call(back_kernel, 'back_messages', [smem(), smem(), anywhere(), anywhere(...]
  transfers between devices with their start and end apart: 26 -> 24, of which waited for: 10 -> 10; matrix products, arithmetic and copies ran while one was open for 0% -> 0% of each run, Pallas kernels for 12% -> 15%
where the time goes in v5:
time: 80.2 us; the launch traced here: 79.9 us
  starting transfers between devices  34.3 us (43%)
  waiting for transfers between devices  24.8 us (31%)
  Pallas kernels  19.6 us (24%)
  between operations  0.88 us (1%)
    ppermute x15, starting transfers between devices, along(): return lambda value: lax.ppermute(value, axis, pairs)  20.3 us
    ppermute x5, waiting for transfers between devices, sum_swap(): return lax.ppermute(value, ('lat', 'lon', 'rep'), pairs)  12.6 us
    ppermute x15, waiting for transfers between devices, along(): return lambda value: lax.ppermute(value, axis, pairs)  12.2 us
    ppermute x5, starting transfers between devices, sum_swap(): return lax.ppermute(value, ('lat', 'lon', 'rep'), pairs)  10.5 us
    pallas_call x2, Pallas kernels, encode(): call(encode_kernel, 'encode', [smem(), smem(), anywhere(), cols_spec, til...  7.65 us
    pallas_call x1, Pallas kernels, per_device(): call(back_kernel, 'back_messages', [smem(), smem(), anywhere(), anywhere(...  3.49 us
    pallas_call x1, Pallas kernels, per_device(): call(node_kernel, 'node_update_and_gradients', sums_specs * 2 + [whole(em...  2.99 us
    ppermute x3, starting transfers between devices, per_device(): to_east = lambda value: lax.ppermute(value, 'lon', east_pairs)  2.75 us
  transfers between devices with their start and end apart: 24, of which 10 were waited for; matrix products, arithmetic and copies ran while one was open for 0% of the time, Pallas kernels for 15%

profile of v5, /device:TPU:1, one launch (start us, length us, event | category | flops | bytes accessed | tf_op | source)
XLA Modules:
  0.0 79.9 jit_solution(6103561845971671639)
XLA Ops:
  0.6 3.5 %back_messages.1 = (bf16[256,256]{1,0:T(8,128)(2,1)S(1)}, bf16[3,256,256]{2,1,0:T(8,128)(2,1)S(1)}, bf16[2,256,256]{2,1,0:T(8,128)(2,1)S(1)}) custom-call(s32[16]{0:T(128)} %bitcast.21, s32[16]{0:T(128)} %slot_ref.7, bf16[16,128,128]{2,1,0:T(8,128)(2,1)} %tiles_ref.7, bf16[227,2048]{1,0:T(8,128)(2,1)} %bitcast.12), custom_call_target="tpu_custom_call" | custom-call | flops 1 | bytes 1 | tf_op jit(solution)/shard_map/back_messages/pallas_call | solution.py:446
  4.1 2.1 %collective-permute-start.4 = (bf16[3,256,256]{2,1,0:T(8,128)(2,1)S(1)}, bf16[3,256,256]{2,1,0:T(8,128)(2,1)S(1)}, u32[]{:S(2)}, u32[]{:S(2)}) collective-permute-start(bf16[3,256,256]{2,1,0:T(8,128)(2,1)S(1)} %get-tuple-element.38), channel_id=1, source_target_pairs={{0,2},{2,0},{1,3},{3,1},{4,6},{6,4},{5,7},{7,5},{8,10},{10,8},{9,1... | collective-permute-start | bytes 1179656 | tf_op jit(solution)/shard_map/ppermute | solution.py:417
  6.2 3.8 %encode.2 = (bf16[2,256,256]{2,1,0:T(8,128)(2,1)S(1)}, bf16[2,256,256]{2,1,0:T(8,128)(2,1)S(1)}, bf16[2,256,256]{2,1,0:T(8,128)(2,1)S(1)}, bf16[1024,256]{1,0:T(8,128)(2,1)S(1)}) custom-call(s32[16]{0:T(128)} %bitcast.22, s32[16]{0:T(128)} %slot_ref.7, bf16[256,256]{1,0:T(8,128)(2,1)S(1)} %get-tuple-element.31.after_ref.back_ref, ...), custom_call_target="tpu_custom_call" | custom-call | flops 1 | bytes 1 | tf_op jit(solution)/shard_map/encode/pallas_call | solution.py:433
  10.1 1.4 %collective-permute-start.2 = (bf16[2,256,256]{2,1,0:T(8,128)(2,1)S(1)}, bf16[2,256,256]{2,1,0:T(8,128)(2,1)S(1)}, u32[]{:S(2)}, u32[]{:S(2)}) collective-permute-start(bf16[2,256,256]{2,1,0:T(8,128)(2,1)S(1)} %get-tuple-element.36), channel_id=1, source_target_pairs={{0,4},{4,0},{8,12},{12,8},{1,5},{5,1},{9,13},{13,9},{2,6},{6,2},{1... | collective-permute-start | bytes 786440 | tf_op jit(solution)/shard_map/ppermute | solution.py:333
  11.5 1.3 %collective-permute-start = (bf16[227,256]{1,0:T(8,128)(2,1)S(1)}, bf16[227,256]{1,0:T(8,128)(2,1)S(1)}, u32[]{:S(2)}, u32[]{:S(2)}) collective-permute-start(bf16[227,256]{1,0:T(8,128)(2,1)S(1)} %copy-done.8), channel_id=1, source_target_pairs={{0,1},{1,0},{2,3},{3,2},{4,5},{5,4},{6,7},{7,6},{8,9},{9,8},{10,11... | collective-permute-start | bytes 348680 | tf_op jit(solution)/shard_map/ppermute | solution.py:333
  13.7 3.8 %encode.3 = (bf16[2,256,256]{2,1,0:T(8,128)(2,1)S(1)}, bf16[2,256,256]{2,1,0:T(8,128)(2,1)S(1)}, bf16[2,256,256]{2,1,0:T(8,128)(2,1)S(1)}, bf16[1024,256]{1,0:T(8,128)(2,1)S(1)}) custom-call(s32[16]{0:T(128)} %bitcast.23, s32[16]{0:T(128)} %slot_ref.7, bf16[2,256,256]{2,1,0:T(8,128)(2,1)S(1)} %get-tuple-element.33.after_ref.refs_1_.own_a, ...), custom_call_target="tpu_custom_call" | custom-call | flops 1 | bytes 1 | tf_op jit(solution)/shard_map/encode/pallas_call | solution.py:433
  17.5 3.6 %collective-permute-start.6 = (bf16[2,256,256]{2,1,0:T(8,128)(2,1)S(1)}, bf16[2,256,256]{2,1,0:T(8,128)(2,1)S(1)}, u32[]{:S(2)}, u32[]{:S(2)}) collective-permute-start(bf16[2,256,256]{2,1,0:T(8,128)(2,1)S(1)} %get-tuple-element.40), channel_id=1, source_target_pairs={{0,4},{4,0},{8,12},{12,8},{1,5},{5,1},{9,13},{13,9},{2,6},{6,2},{1... | collective-permute-start | bytes 786440 | tf_op jit(solution)/shard_map/ppermute | solution.py:333
  23.3 4.3 %collective-permute-done.6.refs_2_.even_b = bf16[2,256,256]{2,1,0:T(8,128)(2,1)S(1)} collective-permute-done((bf16[2,256,256]{2,1,0:T(8,128)(2,1)S(1)}, bf16[2,256,256]{2,1,0:T(8,128)(2,1)S(1)}, u32[]{:S(2)}, u32[]{:S(2)}) %collective-permute-start.6) | collective-permute-done | bytes 262176 | tf_op jit(solution)/shard_map/ppermute | solution.py:333
  29.8 3.1 %collective-permute-start.10 = (bf16[256,256]{1,0:T(8,128)(2,1)S(1)}, bf16[256,256]{1,0:T(8,128)(2,1)S(1)}, u32[]{:S(2)}, u32[]{:S(2)}) collective-permute-start(bf16[256,256]{1,0:T(8,128)(2,1)S(1)} %get-tuple-element.43), channel_id=1, source_target_pairs={{0,4},{4,0},{8,12},{12,8},{1,5},{5,1},{9,13},{13,9},{2,6},{6,2},{1... | collective-permute-start | bytes 393224 | tf_op jit(solution)/shard_map/ppermute | solution.py:333
  34.3 2.1 %collective-permute-done.10.back_even_ref = bf16[256,256]{1,0:T(8,128)(2,1)S(1)} collective-permute-done((bf16[256,256]{1,0:T(8,128)(2,1)S(1)}, bf16[256,256]{1,0:T(8,128)(2,1)S(1)}, u32[]{:S(2)}, u32[]{:S(2)}) %collective-permute-start.10) | collective-permute-done | bytes 131104 | tf_op jit(solution)/shard_map/ppermute | solution.py:333
  36.5 3.0 %node_update_and_gradients.1 = (bf16[256,256]{1,0:T(8,128)(2,1)S(1)}, f32[1280,256]{1,0:T(8,128)S(1)}, bf16[1280,256]{1,0:T(8,128)(2,1)}) custom-call(bf16[2,256,256]{2,1,0:T(8,128)(2,1)S(1)} %get-tuple-element.33.after_ref.refs_1_.own_a, bf16[2,256,256]{2,1,0:T(8,128)(2,1)S(1)} %collective-permute-done.2.refs_2_.even_a, ...), custom_call_target="tpu_custom_call" | custom-call | flops 1 | bytes 1 | tf_op jit(solution)/shard_map/node_update_and_gradients/pallas_call | solution.py:501
  43.2 3.4 %collective-permute-start.19 = (bf16[512,256]{1,0:T(8,128)(2,1)S(1)}, bf16[512,256]{1,0:T(8,128)(2,1)S(1)}, u32[]{:S(2)}, u32[]{:S(2)}) collective-permute-start(bf16[512,256]{1,0:T(8,128)(2,1)S(1)} %constant_dynamic-slice_fusion.1), channel_id=1, source_target_pairs={{0,2},{1,5},{2,0},{3,7},{4,6},{5,1},{6,4},{7,3},{8,10},{9,13},{10,... | collective-permute-start | bytes 786440 | tf_op jit(solution)/shard_map/ppermute | solution.py:368
  46.7 3.7 %collective-permute-done.19.got_ref = bf16[512,256]{1,0:T(8,128)(2,1)S(1)} collective-permute-done((bf16[512,256]{1,0:T(8,128)(2,1)S(1)}, bf16[512,256]{1,0:T(8,128)(2,1)S(1)}, u32[]{:S(2)}, u32[]{:S(2)}) %collective-permute-start.19) | collective-permute-done | bytes 262176 | tf_op jit(solution)/shard_map/ppermute | solution.py:368
  50.5 1.5 %collective-permute-start.20 = (bf16[256,256]{1,0:T(8,128)(2,1)S(1)}, bf16[256,256]{1,0:T(8,128)(2,1)S(1)}, u32[]{:S(2)}, u32[]{:S(2)}) collective-permute-start(bf16[256,256]{1,0:T(8,128)(2,1)S(1)} %constant_dynamic-slice_fusion), channel_id=1, source_target_pairs={{0,4},{1,9},{2,6},{3,11},{4,0},{5,13},{6,2},{7,15},{8,12},{9,1},{1... | collective-permute-start | bytes 393224 | tf_op jit(solution)/shard_map/ppermute | solution.py:368
  52.1 3.3 %collective-permute-done.20 = bf16[256,256]{1,0:T(8,128)(2,1)S(1)} collective-permute-done((bf16[256,256]{1,0:T(8,128)(2,1)S(1)}, bf16[256,256]{1,0:T(8,128)(2,1)S(1)}, u32[]{:S(2)}, u32[]{:S(2)}) %collective-permute-start.20) | collective-permute-done | bytes 131104 | tf_op jit(solution)/shard_map/ppermute | solution.py:368
  56.3 2.6 %collective-permute-start.15 = (bf16[2,256,256]{2,1,0:T(8,128)(2,1)S(1)}, bf16[2,256,256]{2,1,0:T(8,128)(2,1)S(1)}, u32[]{:S(2)}, u32[]{:S(2)}) collective-permute-start(bf16[2,256,256]{2,1,0:T(8,128)(2,1)S(1)} %pair_nodes.1.after_ref), channel_id=1, source_target_pairs={{0,4},{4,0},{8,12},{12,8},{1,5},{5,1},{9,13},{13,9},{2,6},{6,2},{1... | collective-permute-start | bytes 786440 | tf_op jit(solution)/shard_map/ppermute | solution.py:333
  59.7 2.5 %collective-permute-start.22 = (bf16[256,256]{1,0:T(8,128)(2,1)S(1)}, bf16[256,256]{1,0:T(8,128)(2,1)S(1)}, u32[]{:S(2)}, u32[]{:S(2)}) collective-permute-start(bf16[256,256]{1,0:T(8,128)(2,1)S(1)} %add_convert_fusion), channel_id=1, source_target_pairs={{0,4},{1,9},{2,6},{3,11},{4,0},{5,13},{6,2},{7,15},{8,12},{9,1},{1... | collective-permute-start | bytes 393224 | tf_op jit(solution)/shard_map/ppermute | solution.py:368
  62.1 3.5 %collective-permute-done.15 = bf16[2,256,256]{2,1,0:T(8,128)(2,1)S(1)} collective-permute-done((bf16[2,256,256]{2,1,0:T(8,128)(2,1)S(1)}, bf16[2,256,256]{2,1,0:T(8,128)(2,1)S(1)}, u32[]{:S(2)}, u32[]{:S(2)}) %collective-permute-start.15) | collective-permute-done | bytes 262176 | tf_op jit(solution)/shard_map/ppermute | solution.py:333
  66.7 2.7 %collective-permute-start.17 = (bf16[8,64,256]{2,1,0:T(8,128)(2,1)S(1)}, bf16[8,64,256]{2,1,0:T(8,128)(2,1)S(1)}, u32[]{:S(2)}, u32[]{:S(2)}) collective-permute-start(bf16[8,64,256]{2,1,0:T(8,128)(2,1)S(1)} %get-tuple-element.49), channel_id=1, source_target_pairs={{0,1},{1,0},{2,3},{3,2},{4,5},{5,4},{6,7},{7,6},{8,9},{9,8},{10,11... | collective-permute-start | bytes 786440 | tf_op jit(solution)/shard_map/ppermute | solution.py:333
  69.4 3.1 %collective-permute-done.22 = bf16[256,256]{1,0:T(8,128)(2,1)S(1)} collective-permute-done((bf16[256,256]{1,0:T(8,128)(2,1)S(1)}, bf16[256,256]{1,0:T(8,128)(2,1)S(1)}, u32[]{:S(2)}, u32[]{:S(2)}) %collective-permute-start.22) | collective-permute-done | bytes 131104 | tf_op jit(solution)/shard_map/ppermute | solution.py:368
  72.6 2.2 %collective-permute-start.23 = (bf16[512,256]{1,0:T(8,128)(2,1)S(1)}, bf16[512,256]{1,0:T(8,128)(2,1)S(1)}, u32[]{:S(2)}, u32[]{:S(2)}) collective-permute-start(bf16[512,256]{1,0:T(8,128)(2,1)S(1)} %maximum_select_fusion.mine_ref), channel_id=1, source_target_pairs={{0,2},{1,5},{2,0},{3,7},{4,6},{5,1},{6,4},{7,3},{8,10},{9,13},{10,... | collective-permute-start | bytes 786440 | tf_op jit(solution)/shard_map/ppermute | solution.py:368
  74.9 1.2 %decode.1 = bf16[227,1024]{1,0:T(8,128)(2,1)} custom-call(bf16[16,128,128]{2,1,0:T(8,128)(2,1)S(1)} %copy-done, f32[227,1024]{1,0:T(8,128)S(1)} %get-tuple-element.35.base_ref, bf16[8,64,256]{2,1,0:T(8,128)(2,1)S(1)} %get-tuple-element.48.mine_ref, bf16[8,64,256]{2,1,0:T(8,128)(2,1)S(1)} %collective-permute-done.17.got_ref), custom_call_target="tpu_custom_call" | custom-call | flops 1 | bytes 1 | tf_op jit(solution)/shard_map/decode/pallas_call | solution.py:539
  76.0 2.6 %collective-permute-done.23.other_ref = bf16[512,256]{1,0:T(8,128)(2,1)S(1)} collective-permute-done((bf16[512,256]{1,0:T(8,128)(2,1)S(1)}, bf16[512,256]{1,0:T(8,128)(2,1)S(1)}, u32[]{:S(2)}, u32[]{:S(2)}) %collective-permute-start.23) | collective-permute-done | bytes 262176 | tf_op jit(solution)/shard_map/ppermute | solution.py:368
  78.6 1.3 %finish.1 = (f32[512,256]{1,0:T(8,128)}, f32[256,512]{1,0:T(8,128)}, f32[227,256]{1,0:T(8,128)}) custom-call(bf16[512,256]{1,0:T(8,128)(2,1)S(1)} %maximum_select_fusion.mine_ref, bf16[512,256]{1,0:T(8,128)(2,1)S(1)} %collective-permute-done.23.other_ref, bf16[227,256]{1,0:T(8,128)(2,1)S(1)} %bitcast.17, ...), custom_call_target="tpu_custom_call" | custom-call | flops 1 | bytes 1 | tf_op jit(solution)/shard_map/finish/pallas_call | solution.py:545
  (61 shorter events, 13.3 us)
Async XLA Ops:
  4.1 18.5 %collective-permute-start.4 = (bf16[3,256,256]{2,1,0:T(8,128)(2,1)S(1)}, bf16[3,256,256]{2,1,0:T(8,128)(2,1)S(1)}, u32[]{:S(2)}, u32[]{:S(2)}) collective-permute-start(bf16[3,256,256]{2,1,0:T(8,128)(2,1)S(1)} %get-tuple-element.38), channel_id=1, source_target_pairs={{0,2},{2,0},{1,3},{3,1},{4,6},{6,4},{5,7},{7,5},{8,10},{10,8},{9,1... | collective-permute-start | bytes 1179656 | tf_op jit(solution)/shard_map/ppermute | solution.py:417
  10.1 11.9 %collective-permute-start.2 = (bf16[2,256,256]{2,1,0:T(8,128)(2,1)S(1)}, bf16[2,256,256]{2,1,0:T(8,128)(2,1)S(1)}, u32[]{:S(2)}, u32[]{:S(2)}) collective-permute-start(bf16[2,256,256]{2,1,0:T(8,128)(2,1)S(1)} %get-tuple-element.36), channel_id=1, source_target_pairs={{0,4},{4,0},{8,12},{12,8},{1,5},{5,1},{9,13},{13,9},{2,6},{6,2},{1... | collective-permute-start | bytes 786440 | tf_op jit(solution)/shard_map/ppermute | solution.py:333
  11.5 2.2 %collective-permute-start = (bf16[227,256]{1,0:T(8,128)(2,1)S(1)}, bf16[227,256]{1,0:T(8,128)(2,1)S(1)}, u32[]{:S(2)}, u32[]{:S(2)}) collective-permute-start(bf16[227,256]{1,0:T(8,128)(2,1)S(1)} %copy-done.8), channel_id=1, source_target_pairs={{0,1},{1,0},{2,3},{3,2},{4,5},{5,4},{6,7},{7,6},{8,9},{9,8},{10,11... | collective-permute-start | bytes 348680 | tf_op jit(solution)/shard_map/ppermute | solution.py:333
  12.7 9.9 %collective-permute-start.3 = (bf16[2,256,256]{2,1,0:T(8,128)(2,1)S(1)}, bf16[2,256,256]{2,1,0:T(8,128)(2,1)S(1)}, u32[]{:S(2)}, u32[]{:S(2)}) collective-permute-start(bf16[2,256,256]{2,1,0:T(8,128)(2,1)S(1)} %get-tuple-element.37), channel_id=1, source_target_pairs={{0,0},{4,8},{8,4},{12,12},{1,1},{5,9},{9,5},{13,13},{2,2},{6,10},{... | collective-permute-start | bytes 786440 | tf_op jit(solution)/shard_map/ppermute | solution.py:333
  17.5 10.1 %collective-permute-start.6 = (bf16[2,256,256]{2,1,0:T(8,128)(2,1)S(1)}, bf16[2,256,256]{2,1,0:T(8,128)(2,1)S(1)}, u32[]{:S(2)}, u32[]{:S(2)}) collective-permute-start(bf16[2,256,256]{2,1,0:T(8,128)(2,1)S(1)} %get-tuple-element.40), channel_id=1, source_target_pairs={{0,4},{4,0},{8,12},{12,8},{1,5},{5,1},{9,13},{13,9},{2,6},{6,2},{1... | collective-permute-start | bytes 786440 | tf_op jit(solution)/shard_map/ppermute | solution.py:333
  21.2 7.3 %collective-permute-start.7 = (bf16[2,256,256]{2,1,0:T(8,128)(2,1)S(1)}, bf16[2,256,256]{2,1,0:T(8,128)(2,1)S(1)}, u32[]{:S(2)}, u32[]{:S(2)}) collective-permute-start(bf16[2,256,256]{2,1,0:T(8,128)(2,1)S(1)} %get-tuple-element.41), channel_id=1, source_target_pairs={{0,0},{4,8},{8,4},{12,12},{1,1},{5,9},{9,5},{13,13},{2,2},{6,10},{... | collective-permute-start | bytes 786440 | tf_op jit(solution)/shard_map/ppermute | solution.py:333
  22.0 10.9 %collective-permute-start.9 = (bf16[512,256]{1,0:T(8,128)(2,1)S(1)}, bf16[512,256]{1,0:T(8,128)(2,1)S(1)}, u32[]{:S(2)}, u32[]{:S(2)}) collective-permute-start(bf16[512,256]{1,0:T(8,128)(2,1)S(1)} %copy-done.3), channel_id=1, source_target_pairs={{0,1},{1,0},{2,3},{3,2},{4,5},{5,4},{6,7},{7,6},{8,9},{9,8},{10,11... | collective-permute-start | bytes 786440 | tf_op jit(solution)/shard_map/ppermute | solution.py:333
  22.7 5.8 %collective-permute-start.5 = (bf16[256,256]{1,0:T(8,128)(2,1)S(1)}, bf16[256,256]{1,0:T(8,128)(2,1)S(1)}, u32[]{:S(2)}, u32[]{:S(2)}) collective-permute-start(bf16[256,256]{1,0:T(8,128)(2,1)S(1)} %add_east.2), channel_id=1, source_target_pairs={{0,2},{2,0},{1,3},{3,1},{4,6},{6,4},{5,7},{7,5},{8,10},{10,8},{9,1... | collective-permute-start | bytes 393224 | tf_op jit(solution)/shard_map/ppermute | solution.py:417
  23.0 11.3 %collective-permute-start.12 = (bf16[512,256]{1,0:T(8,128)(2,1)S(1)}, bf16[512,256]{1,0:T(8,128)(2,1)S(1)}, u32[]{:S(2)}, u32[]{:S(2)}) collective-permute-start(bf16[512,256]{1,0:T(8,128)(2,1)S(1)} %copy-done.4), channel_id=1, source_target_pairs={{0,1},{1,0},{2,3},{3,2},{4,5},{5,4},{6,7},{7,6},{8,9},{9,8},{10,11... | collective-permute-start | bytes 786440 | tf_op jit(solution)/shard_map/ppermute | solution.py:333
  27.6 6.7 %collective-permute-start.13 = (bf16[256,512]{1,0:T(8,128)(2,1)S(1)}, bf16[256,512]{1,0:T(8,128)(2,1)S(1)}, u32[]{:S(2)}, u32[]{:S(2)}) collective-permute-start(bf16[256,512]{1,0:T(8,128)(2,1)S(1)} %copy-done.5), channel_id=1, source_target_pairs={{0,1},{1,0},{2,3},{3,2},{4,5},{5,4},{6,7},{7,6},{8,9},{9,8},{10,11... | collective-permute-start | bytes 786440 | tf_op jit(solution)/shard_map/ppermute | solution.py:333
  28.4 1.3 %collective-permute-start.1 = (bf16[227,256]{1,0:T(8,128)(2,1)S(1)}, bf16[227,256]{1,0:T(8,128)(2,1)S(1)}, u32[]{:S(2)}, u32[]{:S(2)}) collective-permute-start(bf16[227,256]{1,0:T(8,128)(2,1)S(1)} %bitcast.14), channel_id=1, source_target_pairs={{0,1},{1,0},{2,3},{3,2},{4,5},{5,4},{6,7},{7,6},{8,9},{9,8},{10,11... | collective-permute-start | bytes 348680 | tf_op jit(solution)/shard_map/ppermute | solution.py:333
  28.6 5.8 %collective-permute-start.8 = (bf16[256,256]{1,0:T(8,128)(2,1)S(1)}, bf16[256,256]{1,0:T(8,128)(2,1)S(1)}, u32[]{:S(2)}, u32[]{:S(2)}) collective-permute-start(bf16[256,256]{1,0:T(8,128)(2,1)S(1)} %add_east.3.after_ref), channel_id=1, source_target_pairs={{0,2},{2,0},{1,3},{3,1},{4,6},{6,4},{5,7},{7,5},{8,10},{10,8},{9,1... | collective-permute-start | bytes 393224 | tf_op jit(solution)/shard_map/ppermute | solution.py:417
  29.8 6.7 %collective-permute-start.10 = (bf16[256,256]{1,0:T(8,128)(2,1)S(1)}, bf16[256,256]{1,0:T(8,128)(2,1)S(1)}, u32[]{:S(2)}, u32[]{:S(2)}) collective-permute-start(bf16[256,256]{1,0:T(8,128)(2,1)S(1)} %get-tuple-element.43), channel_id=1, source_target_pairs={{0,4},{4,0},{8,12},{12,8},{1,5},{5,1},{9,13},{13,9},{2,6},{6,2},{1... | collective-permute-start | bytes 393224 | tf_op jit(solution)/shard_map/ppermute | solution.py:333
  32.9 3.6 %collective-permute-start.11 = (bf16[256,256]{1,0:T(8,128)(2,1)S(1)}, bf16[256,256]{1,0:T(8,128)(2,1)S(1)}, u32[]{:S(2)}, u32[]{:S(2)}) collective-permute-start(bf16[256,256]{1,0:T(8,128)(2,1)S(1)} %get-tuple-element.44), channel_id=1, source_target_pairs={{0,0},{4,8},{8,4},{12,12},{1,1},{5,9},{9,5},{13,13},{2,2},{6,10},{... | collective-permute-start | bytes 393224 | tf_op jit(solution)/shard_map/ppermute | solution.py:333
  39.5 2.8 %collective-permute-start.18 = (bf16[1280,256]{1,0:T(8,128)(2,1)}, bf16[1280,256]{1,0:T(8,128)(2,1)S(1)}, u32[]{:S(2)}, u32[]{:S(2)}) collective-permute-start(bf16[1280,256]{1,0:T(8,128)(2,1)} %get-tuple-element.51), channel_id=1, source_target_pairs={{0,1},{1,0},{2,3},{3,2},{4,5},{5,4},{6,7},{7,6},{8,9},{9,8},{10,11... | collective-permute-start | bytes 1966088 | tf_op jit(solution)/shard_map/ppermute | solution.py:333
  40.4 6.3 %collective-permute-start.14 = (bf16[256,256]{1,0:T(8,128)(2,1)S(1)}, bf16[256,256]{1,0:T(8,128)(2,1)S(1)}, u32[]{:S(2)}, u32[]{:S(2)}) collective-permute-start(bf16[256,256]{1,0:T(8,128)(2,1)S(1)} %get-tuple-element.47.proj_ref), channel_id=1, source_target_pairs={{2,0},{0,2},{3,1},{1,3},{6,4},{4,6},{7,5},{5,7},{10,8},{8,10},{11,... | collective-permute-start | bytes 393224 | tf_op jit(solution)/shard_map/ppermute | solution.py:516
  43.2 7.2 %collective-permute-start.19 = (bf16[512,256]{1,0:T(8,128)(2,1)S(1)}, bf16[512,256]{1,0:T(8,128)(2,1)S(1)}, u32[]{:S(2)}, u32[]{:S(2)}) collective-permute-start(bf16[512,256]{1,0:T(8,128)(2,1)S(1)} %constant_dynamic-slice_fusion.1), channel_id=1, source_target_pairs={{0,2},{1,5},{2,0},{3,7},{4,6},{5,1},{6,4},{7,3},{8,10},{9,13},{10,... | collective-permute-start | bytes 786440 | tf_op jit(solution)/shard_map/ppermute | solution.py:368
  50.5 4.8 %collective-permute-start.20 = (bf16[256,256]{1,0:T(8,128)(2,1)S(1)}, bf16[256,256]{1,0:T(8,128)(2,1)S(1)}, u32[]{:S(2)}, u32[]{:S(2)}) collective-permute-start(bf16[256,256]{1,0:T(8,128)(2,1)S(1)} %constant_dynamic-slice_fusion), channel_id=1, source_target_pairs={{0,4},{1,9},{2,6},{3,11},{4,0},{5,13},{6,2},{7,15},{8,12},{9,1},{1... | collective-permute-start | bytes 393224 | tf_op jit(solution)/shard_map/ppermute | solution.py:368
  55.4 4.2 %collective-permute-start.21 = (bf16[256,256]{1,0:T(8,128)(2,1)S(1)}, bf16[256,256]{1,0:T(8,128)(2,1)S(1)}, u32[]{:S(2)}, u32[]{:S(2)}) collective-permute-start(bf16[256,256]{1,0:T(8,128)(2,1)S(1)} %add_convert_fusion.1), channel_id=1, source_target_pairs={{0,8},{1,3},{2,10},{3,1},{4,12},{5,7},{6,14},{7,5},{8,0},{9,11},{1... | collective-permute-start | bytes 393224 | tf_op jit(solution)/shard_map/ppermute | solution.py:368
  56.3 9.3 %collective-permute-start.15 = (bf16[2,256,256]{2,1,0:T(8,128)(2,1)S(1)}, bf16[2,256,256]{2,1,0:T(8,128)(2,1)S(1)}, u32[]{:S(2)}, u32[]{:S(2)}) collective-permute-start(bf16[2,256,256]{2,1,0:T(8,128)(2,1)S(1)} %pair_nodes.1.after_ref), channel_id=1, source_target_pairs={{0,4},{4,0},{8,12},{12,8},{1,5},{5,1},{9,13},{13,9},{2,6},{6,2},{1... | collective-permute-start | bytes 786440 | tf_op jit(solution)/shard_map/ppermute | solution.py:333
  58.9 6.7 %collective-permute-start.16 = (bf16[2,256,256]{2,1,0:T(8,128)(2,1)S(1)}, bf16[2,256,256]{2,1,0:T(8,128)(2,1)S(1)}, u32[]{:S(2)}, u32[]{:S(2)}) collective-permute-start(bf16[2,256,256]{2,1,0:T(8,128)(2,1)S(1)} %pair_nodes.1.after_ref), channel_id=1, source_target_pairs={{0,0},{4,8},{8,4},{12,12},{1,1},{5,9},{9,5},{13,13},{2,2},{6,10},{... | collective-permute-start | bytes 786440 | tf_op jit(solution)/shard_map/ppermute | solution.py:333
  59.7 12.9 %collective-permute-start.22 = (bf16[256,256]{1,0:T(8,128)(2,1)S(1)}, bf16[256,256]{1,0:T(8,128)(2,1)S(1)}, u32[]{:S(2)}, u32[]{:S(2)}) collective-permute-start(bf16[256,256]{1,0:T(8,128)(2,1)S(1)} %add_convert_fusion), channel_id=1, source_target_pairs={{0,4},{1,9},{2,6},{3,11},{4,0},{5,13},{6,2},{7,15},{8,12},{9,1},{1... | collective-permute-start | bytes 393224 | tf_op jit(solution)/shard_map/ppermute | solution.py:368
  66.7 8.1 %collective-permute-start.17 = (bf16[8,64,256]{2,1,0:T(8,128)(2,1)S(1)}, bf16[8,64,256]{2,1,0:T(8,128)(2,1)S(1)}, u32[]{:S(2)}, u32[]{:S(2)}) collective-permute-start(bf16[8,64,256]{2,1,0:T(8,128)(2,1)S(1)} %get-tuple-element.49), channel_id=1, source_target_pairs={{0,1},{1,0},{2,3},{3,2},{4,5},{5,4},{6,7},{7,6},{8,9},{9,8},{10,11... | collective-permute-start | bytes 786440 | tf_op jit(solution)/shard_map/ppermute | solution.py:333
  72.6 6.0 %collective-permute-start.23 = (bf16[512,256]{1,0:T(8,128)(2,1)S(1)}, bf16[512,256]{1,0:T(8,128)(2,1)S(1)}, u32[]{:S(2)}, u32[]{:S(2)}) collective-permute-start(bf16[512,256]{1,0:T(8,128)(2,1)S(1)} %maximum_select_fusion.mine_ref), channel_id=1, source_target_pairs={{0,2},{1,5},{2,0},{3,7},{4,6},{5,1},{6,4},{7,3},{8,10},{9,13},{10,... | collective-permute-start | bytes 786440 | tf_op jit(solution)/shard_map/ppermute | solution.py:368
  (9 other events, 120.2 us)

commit v6 on v5

--- a/solution.py
+++ b/solution.py
@@ -1,3 +1,5 @@
+import functools
+
 import jax
 import jax.numpy as jnp
 from jax import lax
@@ -9,7 +11,6 @@
 BF16 = jnp.bfloat16
 VMEM_BYTES = 20 * 1024 * 1024
 STEPS = 4
-HALVING = 3
 
 
 def dot(left, right):
@@ -88,33 +89,48 @@
         out[...] = block.reshape(out.shape).astype(out.dtype)
 
 
+def chunk_copies(source_ref, target, sems, columns):
+    copies = []
+    for k in range(STEPS):
+        size = target.shape[1 if columns else 0] // STEPS
+        part = pl.ds(k * size, size)
+        at = (slice(None), part) if columns else (part,)
+        copies.append(pltpu.make_async_copy(source_ref.at[at], target.at[at], sems.at[k]))
+    return copies
+
+
+def started(groups, k):
+    if k == 0:
+        for group in groups:
+            for copy in group[:2]:
+                copy.start()
+    elif k + 1 < STEPS:
+        for group in groups:
+            group[k + 1].start()
+
+
+def waited(groups, k):
+    for group in groups:
+        group[k].wait()
+
+
 def back_kernel(
-    device_ref, slot_ref, tiles_ref, cot_ref, own_ref, east_ref, side_ref,
-    total, tiles, cots, tile_sems, cot_sems,
+    device_ref, slot_ref, tiles_ref, cot_ref, own_ref, east_ref, side_ref, total, cots, sems,
 ):
-    blocks, rows = tiles.shape[0], tiles.shape[1]
-    count = blocks // STEPS
+    blocks, rows = tiles_ref.shape[0], tiles_ref.shape[2]
     slots = total.shape[0] // 6
     channels = cots.shape[0]
-    r = lax.axis_index("rep")
-    copies = []
+    groups = [chunk_copies(cot_ref, cots, sems, True)]
+    started(groups, 0)
+    total[...] = jnp.zeros_like(total)
     for k in range(STEPS):
-        part = pl.ds(k * count, count)
-        cols = pl.ds(k * count * rows, count * rows)
-        copies.append((
-            pltpu.make_async_copy(tiles_ref.at[part], tiles.at[part], tile_sems.at[k]),
-            pltpu.make_async_copy(cot_ref.at[:, cols], cots.at[:, cols], cot_sems.at[k]),
-        ))
-        for copy in copies[-1]:
-            copy.start()
-    total[...] = jnp.zeros_like(total)
-    for b in range(blocks):
-        if b % count == 0:
-            for copy in copies[b // count]:
-                copy.wait()
-        at = entry_of(device_ref, slot_ref, b, slots)
-        cot = cots[:, b * rows : (b + 1) * rows]
-        total[at, :, :channels] += dot_last(node_half(tiles[b], r), cot)
+        if k > 0:
+            started(groups, k)
+        waited(groups, k)
+        for b in range(k * blocks // STEPS, (k + 1) * blocks // STEPS):
+            at = entry_of(device_ref, slot_ref, b, slots)
+            cot = cots[:, b * rows : (b + 1) * rows]
+            total[at, :, :channels] += dot_last(tiles_ref[b], cot)
     for k, out in ((0, own_ref), (2, side_ref.at[0]), (4, side_ref.at[1])):
         out[...] = total[k * slots : (k + 1) * slots].reshape(out.shape).astype(out.dtype)
     for k in range(3):
@@ -122,44 +138,50 @@
         east_ref[k] = block.reshape(east_ref.shape[1:]).astype(east_ref.dtype)
 
 
-def encode_kernel(
-    device_ref, slot_ref, after_ref, grid_ref, tiles_ref, weight_ref,
-    own_ref, even_ref, odd_ref, hidden_ref, total, hold,
-):
-    step = pl.program_id(0)
-    count, rows = tiles_ref.shape[0], tiles_ref.shape[1]
+def encode_kernel(first, device_ref, slot_ref, after_ref, grid_ref, tiles_ref, weight_ref, *refs):
+    outs, (total, grids, grid_sems), scratch = refs[:4], refs[4 + first : 7 + first], refs[7 + first :]
+    own_ref, even_ref, odd_ref, hidden_ref = outs
     slots = total.shape[0] // 6
     r = lax.axis_index("rep")
-
-    @pl.when(step == 0)
-    def _():
-        total[...] = jnp.zeros_like(total)
-
-    preact = dot_rows(grid_ref[...], weight_ref[...])
-    hold[...] = (preact * sigmoid(preact)).astype(BF16)
-    for i in range(count):
-        at = entry_of(device_ref, slot_ref, step * count + i, slots)
-        total[at] += dot(node_half(tiles_ref[i], r), hold[i * rows : (i + 1) * rows, :])
-
-    half_steps = pl.num_programs(0) // 2
-
-    @pl.when(step // half_steps == r)
-    def _():
-        at = pl.multiple_of((step % half_steps) * hold.shape[0], hold.shape[0])
-        hidden_ref[pl.ds(at, hold.shape[0]), :] = hold[...]
-
-    @pl.when(step == pl.num_programs(0) - 1)
-    def _():
-        write_packed(total, (own_ref, even_ref, odd_ref))
+    groups = [chunk_copies(grid_ref, grids, grid_sems, True)]
+    if first:
+        halves_ref, (tiles, tile_sems) = refs[4], scratch
+        groups.append(chunk_copies(tiles_ref, tiles, tile_sems, False))
+    else:
+        halves_ref = tiles_ref
+    blocks, _, rows = halves_ref.shape
+    started(groups, 0)
+    total[...] = jnp.zeros_like(total)
+    weight = weight_ref[...].T
+    cols = blocks * rows // STEPS
+    for k in range(STEPS):
+        if k > 0:
+            started(groups, k)
+        waited(groups, k)
+        preact = dot(weight, grids[:, k * cols : (k + 1) * cols])
+        hidden = (preact * sigmoid(preact)).astype(BF16)
+
+        @pl.when(r == k // (STEPS // 2))
+        def _(k=k, hidden=hidden):
+            at = (k % (STEPS // 2)) * cols
+            hidden_ref[:, at : at + cols] = hidden
+
+        for i in range(blocks // STEPS):
+            b = k * blocks // STEPS + i
+            if first:
+                halves_ref[b] = node_half(tiles[b], r)
+            at = entry_of(device_ref, slot_ref, b, slots)
+            total[at] += dot_last(halves_ref[b], hidden[:, i * rows : (i + 1) * rows])
+    write_packed(total, (own_ref, even_ref, odd_ref))
 
 
 def local_kernel(own_ref, oth_ref, cot_ref, out_ref, out_other_ref, base_ref, grad_ref, grad_other_ref):
-    rows = own_ref.shape[0]
-    r = lax.axis_index("rep")
-    cot = cot_ref[:, pl.ds(pl.multiple_of(r * rows, rows), rows)]
-    base_ref[...] = dot_last(out_ref[...], own_ref[...]) + dot_last(out_other_ref[...], oth_ref[...])
-    grad_ref[...] = dot(cot, own_ref[...])
-    grad_other_ref[...] = dot(cot, oth_ref[...])
+    cols = own_ref.shape[1]
+    r = lax.axis_index("rep")
+    cot = cot_ref[:, pl.ds(pl.multiple_of(r * cols, cols), cols)]
+    base_ref[...] = dot(out_ref[...], own_ref[...]) + dot(out_other_ref[...], oth_ref[...])
+    grad_ref[...] = dot_last(cot, own_ref[...])
+    grad_other_ref[...] = dot_last(cot, oth_ref[...])
 
 
 def added(*values):
@@ -266,6 +288,12 @@
     out_ref[...] = added(keep, got_ref[...]).astype(out_ref.dtype)
 
 
+def second_sum_kernel(even_ref, odd_ref, value_ref, got_ref, out_ref):
+    rows = got_ref.shape[0]
+    keep = value_ref[pl.ds(pl.multiple_of(sum_bit(1) * rows, rows), rows), :]
+    out_ref[...] = added(keep, got_ref[...]).astype(out_ref.dtype)
+
+
 def pair_kernel(proj_ref, east_ref, pair_ref):
     pair_ref[0] = proj_ref[...]
     pair_ref[1] = east_ref[...]
@@ -374,23 +402,14 @@
 
 
 def summed(value):
-    count = len(sum_orders()[0])
-    halving = min(count - 1, HALVING)
-    for step in range(1, count):
-        if step >= halving:
-            value = (value.astype(F32) + sum_swap(value, step).astype(F32)).astype(BF16)
-            continue
-        rows = value.shape[0] // 2
-        keep = lax.dynamic_slice_in_dim(value, sum_bit(step) * rows, rows, 0)
-        got = sum_swap(given_half(value, step), step)
-        value = (keep.astype(F32) + got.astype(F32)).astype(BF16)
-    for step in range(halving - 1, 0, -1):
-        other = sum_swap(value, step)
-        value = jnp.where(
-            sum_bit(step) == 0,
-            jnp.concatenate([value, other], axis=0),
-            jnp.concatenate([other, value], axis=0),
-        )
+    for step in range(2, len(sum_orders()[0])):
+        value = (value.astype(F32) + sum_swap(value, step).astype(F32)).astype(BF16)
+    other = sum_swap(value, 1)
+    value = jnp.where(
+        sum_bit(1) == 0,
+        jnp.concatenate([value, other], axis=0),
+        jnp.concatenate([other, value], axis=0),
+    )
     return value, sum_swap(value, 0)
 
 
@@ -421,48 +440,39 @@
     grid_t, cot_t, out_t = grid_in.T, cotangent.T, w_out.T
     routes = (in_hbm(device), in_hbm(slot))
     tiles_in, grid_in_t, cot_in_t = in_hbm(interp_tiles), in_hbm(grid_t), in_hbm(cot_t)
-    per_step = blocks // STEPS
-    step_rows = per_step * tile_rows
-    tiles_spec = pl.BlockSpec((per_step, tile_rows, tile_rows), lambda i: (i, 0, 0))
-    cols_spec = pl.BlockSpec((channels, step_rows), lambda i: (0, i))
-    pair_shape = (2, nodes, width)
+    pair_shape, halves_shape = (2, nodes, width), (blocks, half, tile_rows)
+    total = pltpu.VMEM((6 * slots, half, width), F32)
+    sems = pltpu.SemaphoreType.DMA((STEPS,))
 
     embed_other = swap_rep(w_embed)
 
-    def encode(after, weight, limit):
+    def encode(after, tiles, weight, first):
+        shapes = [pair_shape] * 3 + [(width, my_rows)] + [halves_shape] * first
         return call(
-            encode_kernel, "encode",
-            [smem(), smem(), anywhere(), cols_spec, tiles_spec, whole((channels, width))],
-            [whole(pair_shape)] * 3 + [whole((my_rows, width))],
-            [shape_of(pair_shape, BF16)] * 3 + [shape_of((my_rows, width), BF16)],
-            2 * grid_rows * width * (channels + half), 3e6, grid=(STEPS,), exps=grid_rows * width,
-            scratch=[
-                pltpu.VMEM((6 * slots, half, width), F32),
-                pltpu.VMEM((step_rows, width), BF16),
-            ],
-            limit=limit,
-        )(*routes, after, grid_in_t, tiles_in, weight)
+            functools.partial(encode_kernel, first), "encode",
+            [smem(), smem(), anywhere(), anywhere(), anywhere() if first else vmem(), vmem()],
+            [vmem()] * len(shapes), [shape_of(shape, BF16) for shape in shapes], 1, 1,
+            scratch=[total, pltpu.VMEM(grid_t.shape, BF16), sems]
+            + [pltpu.VMEM(interp_tiles.shape, BF16), sems] * first,
+        )(*routes, after, grid_in_t, tiles, weight)
+
+    own_a, even_a, odd_a, hidden_a, halves = encode(w_embed, tiles_in, in_hbm(w_embed), True)
+    even_in_a, odd_in_a = to_even(even_a), to_odd(odd_a)
 
     back_own, back_east, back_side = call(
         back_kernel, "back_messages",
-        [smem(), smem(), anywhere(), anywhere()],
+        [smem(), smem(), vmem(), anywhere()],
         [vmem()] * 3,
         [shape_of((nodes, padded), BF16), shape_of((3, nodes, padded), BF16),
          shape_of((2, nodes, padded), BF16)],
-        2 * grid_rows * half * padded, 3e6,
+        1, 1,
         scratch=[
-            pltpu.VMEM((6 * slots, half, padded), F32),
-            pltpu.VMEM(interp_tiles.shape, BF16),
-            pltpu.VMEM(cot_t.shape, BF16),
-            pltpu.SemaphoreType.DMA((STEPS,)),
-            pltpu.SemaphoreType.DMA((STEPS,)),
+            pltpu.VMEM((6 * slots, half, padded), F32), pltpu.VMEM(cot_t.shape, BF16), sems,
         ],
-    )(*routes, tiles_in, cot_in_t)
+    )(*routes, halves, cot_in_t)
     back_moved = to_east(back_east)
 
-    own_a, even_a, odd_a, hidden_a = encode(back_own, in_hbm(w_embed), VMEM_BYTES)
-    even_in_a, odd_in_a = to_even(even_a), to_odd(odd_a)
-    own_b, even_b, odd_b, hidden_b = encode(own_a, embed_other, VMEM_BYTES)
+    own_b, even_b, odd_b, hidden_b = encode(back_own, halves, embed_other, False)
     even_in_b, odd_in_b = to_even(even_b), to_odd(odd_b)
 
     out_other, up_other, down_other = swap_rep(out_t), swap_rep(w_up), swap_rep(w_down)
@@ -483,7 +493,7 @@
             shape_of((nodes, width), BF16), 3 * nodes * width, 6e5, grid=(1,),
         )(after, *terms)
 
-    send_a = add_east(back_moved, own_a, even_in_a, odd_in_a)
+    send_a = add_east(own_b, own_a, even_in_a, odd_in_a)
     moved_a = to_east(send_a)
     send_b = add_east(moved_a, own_b, even_in_b, odd_in_b)
     moved_b = to_east(send_b)
@@ -529,7 +539,11 @@
         shape_of((latent, width), BF16), 2 * latent * width, 1e6,
     )(pair, terms, sum_swap(given_half(terms, 0), 0))
     pair_even, pair_odd = to_even(pair), to_odd(pair)
-    mine, theirs = summed(halved)
+    quarter = call(
+        second_sum_kernel, "second_sum", [anywhere()] * 2 + [vmem()] * 2, vmem(),
+        shape_of((width, width), BF16), 1, 1,
+    )(pair_even, pair_odd, halved, sum_swap(given_half(halved, 1), 1))
+    mine, theirs = summed(quarter)
 
     table_shape = (2 * slots, half, padded)
     mine_picked, theirs_picked = call(

time: 80.2 us -> 82.5 us (1.029)
  the two profiles are of different devices: /device:TPU:1 before, /device:TPU:0 now
where the time goes in v6:
time: 82.5 us; the launch traced here: 82 us
  starting transfers between devices  32.1 us (39%)
  waiting for transfers between devices  26.9 us (33%)
  Pallas kernels  21.9 us (27%)
  between operations  0.94 us (1%)
    ppermute x15, starting transfers between devices, along(): return lambda value: lax.ppermute(value, axis, pairs)  17.9 us
    ppermute x5, waiting for transfers between devices, sum_swap(): return lax.ppermute(value, ('lat', 'lon', 'rep'), pairs)  14.1 us
    ppermute x15, waiting for transfers between devices, along(): return lambda value: lax.ppermute(value, axis, pairs)  12.2 us
    ppermute x5, starting transfers between devices, sum_swap(): return lax.ppermute(value, ('lat', 'lon', 'rep'), pairs)  10.6 us
    pallas_call x2, Pallas kernels, encode(): call(functools.partial(encode_kernel, first), 'encode', [smem(), smem(),...  8.85 us
    pallas_call x1, Pallas kernels, per_device(): call(back_kernel, 'back_messages', [smem(), smem(), vmem(), anywhere()],...  3.49 us
    pallas_call x1, Pallas kernels, per_device(): call(node_kernel, 'node_update_and_gradients', sums_specs * 2 + [whole(em...  3.01 us
    ppermute x3, starting transfers between devices, per_device(): to_east = lambda value: lax.ppermute(value, 'lon', east_pairs)  2.79 us
  transfers between devices with their start and end apart: 24, of which 11 were waited for; matrix products, arithmetic and copies ran while one was open for 0% of the time, Pallas kernels for 16%

profile of v6, /device:TPU:0, one launch (start us, length us, event | category | flops | bytes accessed | tf_op | source)
XLA Modules:
  0.0 82.0 jit_solution(8025978597659355767)
XLA Ops:
  0.6 4.7 %encode.2 = (bf16[2,256,256]{2,1,0:T(8,128)(2,1)S(1)}, bf16[2,256,256]{2,1,0:T(8,128)(2,1)S(1)}, bf16[2,256,256]{2,1,0:T(8,128)(2,1)S(1)}, bf16[256,1024]{1,0:T(8,128)(2,1)S(1)}, bf16[16,64,128]{2,1,0:T(8,128)(2,1)S(1)}) custom-call(s32[16]{0:T(128)} %bitcast.23, s32[16]{0:T(128)} %slot_ref.7, bf16[227,256]{1,0:T(8,128)(2,1)} %weight_ref.1, ...), custom_call_target="tpu_custom_call" | custom-call | flops 1 | bytes 1 | tf_op jit(solution)/shard_map/encode/pallas_call | solution.py:451
  5.4 3.1 %collective-permute-start.2 = (bf16[2,256,256]{2,1,0:T(8,128)(2,1)S(1)}, bf16[2,256,256]{2,1,0:T(8,128)(2,1)S(1)}, u32[]{:S(2)}, u32[]{:S(2)}) collective-permute-start(bf16[2,256,256]{2,1,0:T(8,128)(2,1)S(1)} %get-tuple-element.38), channel_id=1, source_target_pairs={{0,4},{4,0},{8,12},{12,8},{1,5},{5,1},{9,13},{13,9},{2,6},{6,2},{1... | collective-permute-start | bytes 786440 | tf_op jit(solution)/shard_map/ppermute | solution.py:361
  9.2 3.5 %back_messages.1 = (bf16[256,256]{1,0:T(8,128)(2,1)S(1)}, bf16[3,256,256]{2,1,0:T(8,128)(2,1)S(1)}, bf16[2,256,256]{2,1,0:T(8,128)(2,1)S(1)}) custom-call(s32[16]{0:T(128)} %bitcast.24, s32[16]{0:T(128)} %slot_ref.7, bf16[16,64,128]{2,1,0:T(8,128)(2,1)S(1)} %get-tuple-element.33.tiles_ref, bf16[227,2048]{1,0:T(8,128)(2,1)} %bitcast.12), custom_call_target="tpu_custom_call" | custom-call | flops 1 | bytes 1 | tf_op jit(solution)/shard_map/back_messages/pallas_call | solution.py:462
  12.7 1.6 %collective-permute-start.9 = (bf16[3,256,256]{2,1,0:T(8,128)(2,1)S(1)}, bf16[3,256,256]{2,1,0:T(8,128)(2,1)S(1)}, u32[]{:S(2)}, u32[]{:S(2)}) collective-permute-start(bf16[3,256,256]{2,1,0:T(8,128)(2,1)S(1)} %get-tuple-element.43), channel_id=1, source_target_pairs={{0,2},{2,0},{1,3},{3,1},{4,6},{6,4},{5,7},{7,5},{8,10},{10,8},{9,1... | collective-permute-start | bytes 1179656 | tf_op jit(solution)/shard_map/ppermute | solution.py:436
  14.3 4.1 %encode.3 = (bf16[2,256,256]{2,1,0:T(8,128)(2,1)S(1)}, bf16[2,256,256]{2,1,0:T(8,128)(2,1)S(1)}, bf16[2,256,256]{2,1,0:T(8,128)(2,1)S(1)}, bf16[256,1024]{1,0:T(8,128)(2,1)S(1)}) custom-call(s32[16]{0:T(128)} %bitcast.25, s32[16]{0:T(128)} %slot_ref.7, bf16[256,256]{1,0:T(8,128)(2,1)S(1)} %get-tuple-element.34.after_ref.back_ref, ...), custom_call_target="tpu_custom_call" | custom-call | flops 1 | bytes 1 | tf_op jit(solution)/shard_map/encode/pallas_call | solution.py:451
  18.4 4.4 %collective-permute-start.5 = (bf16[2,256,256]{2,1,0:T(8,128)(2,1)S(1)}, bf16[2,256,256]{2,1,0:T(8,128)(2,1)S(1)}, u32[]{:S(2)}, u32[]{:S(2)}) collective-permute-start(bf16[2,256,256]{2,1,0:T(8,128)(2,1)S(1)} %get-tuple-element.41), channel_id=1, source_target_pairs={{0,4},{4,0},{8,12},{12,8},{1,5},{5,1},{9,13},{13,9},{2,6},{6,2},{1... | collective-permute-start | bytes 786440 | tf_op jit(solution)/shard_map/ppermute | solution.py:361
  24.3 5.2 %collective-permute-done.5.refs_2_.even_b = bf16[2,256,256]{2,1,0:T(8,128)(2,1)S(1)} collective-permute-done((bf16[2,256,256]{2,1,0:T(8,128)(2,1)S(1)}, bf16[2,256,256]{2,1,0:T(8,128)(2,1)S(1)}, u32[]{:S(2)}, u32[]{:S(2)}) %collective-permute-start.5) | collective-permute-done | bytes 262176 | tf_op jit(solution)/shard_map/ppermute | solution.py:361
  31.6 3.3 %collective-permute-start.10 = (bf16[256,256]{1,0:T(8,128)(2,1)S(1)}, bf16[256,256]{1,0:T(8,128)(2,1)S(1)}, u32[]{:S(2)}, u32[]{:S(2)}) collective-permute-start(bf16[256,256]{1,0:T(8,128)(2,1)S(1)} %get-tuple-element.45), channel_id=1, source_target_pairs={{0,4},{4,0},{8,12},{12,8},{1,5},{5,1},{9,13},{13,9},{2,6},{6,2},{1... | collective-permute-start | bytes 393224 | tf_op jit(solution)/shard_map/ppermute | solution.py:361
  36.3 2.4 %collective-permute-done.10.back_even_ref = bf16[256,256]{1,0:T(8,128)(2,1)S(1)} collective-permute-done((bf16[256,256]{1,0:T(8,128)(2,1)S(1)}, bf16[256,256]{1,0:T(8,128)(2,1)S(1)}, u32[]{:S(2)}, u32[]{:S(2)}) %collective-permute-start.10) | collective-permute-done | bytes 131104 | tf_op jit(solution)/shard_map/ppermute | solution.py:361
  38.7 3.0 %node_update_and_gradients.1 = (bf16[256,256]{1,0:T(8,128)(2,1)S(1)}, f32[1280,256]{1,0:T(8,128)S(1)}, bf16[1280,256]{1,0:T(8,128)(2,1)}) custom-call(bf16[2,256,256]{2,1,0:T(8,128)(2,1)S(1)} %get-tuple-element.37.refs_1_.own_a, bf16[2,256,256]{2,1,0:T(8,128)(2,1)S(1)} %collective-permute-done.2.refs_2_.even_a, ...), custom_call_target="tpu_custom_call" | custom-call | flops 1 | bytes 1 | tf_op jit(solution)/shard_map/node_update_and_gradients/pallas_call | solution.py:511
  42.5 1.7 %collective-permute-done.18.got_ref = bf16[1280,256]{1,0:T(8,128)(2,1)} collective-permute-done((bf16[1280,256]{1,0:T(8,128)(2,1)}, bf16[1280,256]{1,0:T(8,128)(2,1)}, u32[]{:S(2)}, u32[]{:S(2)}) %collective-permute-start.18) | collective-permute-done | bytes 655392 | tf_op jit(solution)/shard_map/ppermute | solution.py:361
  44.1 2.0 %sum_terms.1 = (bf16[1024,256]{1,0:T(8,128)(2,1)S(1)}, f32[4,2,64,256]{3,2,1,0:T(8,128)}) custom-call(f32[1280,256]{1,0:T(8,128)S(1)} %get-tuple-element.52.keep_ref, bf16[1280,256]{1,0:T(8,128)(2,1)} %collective-permute-done.18.got_ref), custom_call_target="tpu_custom_call" | custom-call | flops 1 | bytes 1 | tf_op jit(solution)/shard_map/sum_terms/pallas_call | solution.py:527
  47.6 3.7 %collective-permute-start.15 = (bf16[2,256,256]{2,1,0:T(8,128)(2,1)S(1)}, bf16[2,256,256]{2,1,0:T(8,128)(2,1)S(1)}, u32[]{:S(2)}, u32[]{:S(2)}) collective-permute-start(bf16[2,256,256]{2,1,0:T(8,128)(2,1)S(1)} %pair_nodes.1.after_ref), channel_id=1, source_target_pairs={{0,4},{4,0},{8,12},{12,8},{1,5},{5,1},{9,13},{13,9},{2,6},{6,2},{1... | collective-permute-start | bytes 786440 | tf_op jit(solution)/shard_map/ppermute | solution.py:361
  52.7 3.7 %collective-permute-start.20 = (bf16[256,256]{1,0:T(8,128)(2,1)S(1)}, bf16[256,256]{1,0:T(8,128)(2,1)S(1)}, u32[]{:S(2)}, u32[]{:S(2)}) collective-permute-start(bf16[256,256]{1,0:T(8,128)(2,1)S(1)} %constant_dynamic-slice_fusion), channel_id=1, source_target_pairs={{0,4},{1,9},{2,6},{3,11},{4,0},{5,13},{6,2},{7,15},{8,12},{9,1},{1... | collective-permute-start | bytes 393224 | tf_op jit(solution)/shard_map/ppermute | solution.py:396
  56.4 2.2 %collective-permute-done.15.even_ref = bf16[2,256,256]{2,1,0:T(8,128)(2,1)S(1)} collective-permute-done((bf16[2,256,256]{2,1,0:T(8,128)(2,1)S(1)}, bf16[2,256,256]{2,1,0:T(8,128)(2,1)S(1)}, u32[]{:S(2)}, u32[]{:S(2)}) %collective-permute-start.15) | collective-permute-done | bytes 262176 | tf_op jit(solution)/shard_map/ppermute | solution.py:361
  58.6 2.3 %collective-permute-done.20.got_ref = bf16[256,256]{1,0:T(8,128)(2,1)S(1)} collective-permute-done((bf16[256,256]{1,0:T(8,128)(2,1)S(1)}, bf16[256,256]{1,0:T(8,128)(2,1)S(1)}, u32[]{:S(2)}, u32[]{:S(2)}) %collective-permute-start.20) | collective-permute-done | bytes 131104 | tf_op jit(solution)/shard_map/ppermute | solution.py:396
  60.9 2.3 %collective-permute-start.21 = (bf16[256,256]{1,0:T(8,128)(2,1)S(1)}, bf16[256,256]{1,0:T(8,128)(2,1)S(1)}, u32[]{:S(2)}, u32[]{:S(2)}) collective-permute-start(bf16[256,256]{1,0:T(8,128)(2,1)S(1)} %second_sum.1), channel_id=1, source_target_pairs={{0,8},{1,3},{2,10},{3,1},{4,12},{5,7},{6,14},{7,5},{8,0},{9,11},{1... | collective-permute-start | bytes 393224 | tf_op jit(solution)/shard_map/ppermute | solution.py:396
  63.2 3.7 %collective-permute-done.21 = bf16[256,256]{1,0:T(8,128)(2,1)S(1)} collective-permute-done((bf16[256,256]{1,0:T(8,128)(2,1)S(1)}, bf16[256,256]{1,0:T(8,128)(2,1)S(1)}, u32[]{:S(2)}, u32[]{:S(2)}) %collective-permute-start.21) | collective-permute-done | bytes 131104 | tf_op jit(solution)/shard_map/ppermute | solution.py:396
  66.9 3.0 %collective-permute-start.22 = (bf16[256,256]{1,0:T(8,128)(2,1)S(1)}, bf16[256,256]{1,0:T(8,128)(2,1)S(1)}, u32[]{:S(2)}, u32[]{:S(2)}) collective-permute-start(bf16[256,256]{1,0:T(8,128)(2,1)S(1)} %add_convert_fusion), channel_id=1, source_target_pairs={{0,4},{1,9},{2,6},{3,11},{4,0},{5,13},{6,2},{7,15},{8,12},{9,1},{1... | collective-permute-start | bytes 393224 | tf_op jit(solution)/shard_map/ppermute | solution.py:396
  69.9 1.1 %pick_nodes.1 = (bf16[8,64,256]{2,1,0:T(8,128)(2,1)S(1)}, bf16[8,64,256]{2,1,0:T(8,128)(2,1)S(1)}) custom-call(s32[16]{0:T(128)S(1)} %bitcast.26, s32[16]{0:T(128)S(1)} %copy-done.7, bf16[8,64,256]{2,1,0:T(8,128)(2,1)S(1)} %bitcast.20, bf16[8,64,256]{2,1,0:T(8,128)(2,1)S(1)} %bitcast.21, bf16[8,64,256]{2,1,0:T(8,128)(2,1)S(1)} %bitcast.22), custom_call_target="tpu_custom_call" | custom-call | flops 5000000000 | bytes 1 | tf_op jit(solution)/shard_map/pick_nodes/pallas_call | solution.py:549
  71.1 3.1 %collective-permute-done.22 = bf16[256,256]{1,0:T(8,128)(2,1)S(1)} collective-permute-done((bf16[256,256]{1,0:T(8,128)(2,1)S(1)}, bf16[256,256]{1,0:T(8,128)(2,1)S(1)}, u32[]{:S(2)}, u32[]{:S(2)}) %collective-permute-start.22) | collective-permute-done | bytes 131104 | tf_op jit(solution)/shard_map/ppermute | solution.py:396
  75.2 1.2 %decode.1 = bf16[227,1024]{1,0:T(8,128)(2,1)} custom-call(bf16[16,128,128]{2,1,0:T(8,128)(2,1)S(1)} %copy-done.1, f32[227,1024]{1,0:T(8,128)S(1)} %get-tuple-element.36.base_ref, bf16[8,64,256]{2,1,0:T(8,128)(2,1)S(1)} %get-tuple-element.50.mine_ref, bf16[8,64,256]{2,1,0:T(8,128)(2,1)S(1)} %collective-permute-done.17.got_ref), custom_call_target="tpu_custom_call" | custom-call | flops 1 | bytes 1 | tf_op jit(solution)/shard_map/decode/pallas_call | solution.py:553
  76.4 4.4 %collective-permute-done.23.other_ref = bf16[512,256]{1,0:T(8,128)(2,1)S(1)} collective-permute-done((bf16[512,256]{1,0:T(8,128)(2,1)S(1)}, bf16[512,256]{1,0:T(8,128)(2,1)S(1)}, u32[]{:S(2)}, u32[]{:S(2)}) %collective-permute-start.23) | collective-permute-done | bytes 262176 | tf_op jit(solution)/shard_map/ppermute | solution.py:396
  80.8 1.3 %finish.1 = (f32[512,256]{1,0:T(8,128)}, f32[256,512]{1,0:T(8,128)}, f32[227,256]{1,0:T(8,128)}) custom-call(bf16[512,256]{1,0:T(8,128)(2,1)S(1)} %maximum_select_fusion.mine_ref, bf16[512,256]{1,0:T(8,128)(2,1)S(1)} %collective-permute-done.23.other_ref, bf16[227,256]{1,0:T(8,128)(2,1)S(1)} %bitcast.17, ...), custom_call_target="tpu_custom_call" | custom-call | flops 1 | bytes 1 | tf_op jit(solution)/shard_map/finish/pallas_call | solution.py:559
  (61 shorter events, 10.3 us)
Async XLA Ops:
  5.4 18.2 %collective-permute-start.2 = (bf16[2,256,256]{2,1,0:T(8,128)(2,1)S(1)}, bf16[2,256,256]{2,1,0:T(8,128)(2,1)S(1)}, u32[]{:S(2)}, u32[]{:S(2)}) collective-permute-start(bf16[2,256,256]{2,1,0:T(8,128)(2,1)S(1)} %get-tuple-element.38), channel_id=1, source_target_pairs={{0,4},{4,0},{8,12},{12,8},{1,5},{5,1},{9,13},{13,9},{2,6},{6,2},{1... | collective-permute-start | bytes 786440 | tf_op jit(solution)/shard_map/ppermute | solution.py:361
  8.5 15.2 %collective-permute-start.3 = (bf16[2,256,256]{2,1,0:T(8,128)(2,1)S(1)}, bf16[2,256,256]{2,1,0:T(8,128)(2,1)S(1)}, u32[]{:S(2)}, u32[]{:S(2)}) collective-permute-start(bf16[2,256,256]{2,1,0:T(8,128)(2,1)S(1)} %get-tuple-element.39), channel_id=1, source_target_pairs={{0,0},{4,8},{8,4},{12,12},{1,1},{5,9},{9,5},{13,13},{2,2},{6,10},{... | collective-permute-start | bytes 786440 | tf_op jit(solution)/shard_map/ppermute | solution.py:361
  9.2 5.2 %collective-permute-start = (bf16[227,256]{1,0:T(8,128)(2,1)S(1)}, bf16[227,256]{1,0:T(8,128)(2,1)S(1)}, u32[]{:S(2)}, u32[]{:S(2)}) collective-permute-start(bf16[227,256]{1,0:T(8,128)(2,1)S(1)} %copy-done.8), channel_id=1, source_target_pairs={{0,1},{1,0},{2,3},{3,2},{4,5},{5,4},{6,7},{7,6},{8,9},{9,8},{10,11... | collective-permute-start | bytes 348680 | tf_op jit(solution)/shard_map/ppermute | solution.py:361
  12.7 17.5 %collective-permute-start.9 = (bf16[3,256,256]{2,1,0:T(8,128)(2,1)S(1)}, bf16[3,256,256]{2,1,0:T(8,128)(2,1)S(1)}, u32[]{:S(2)}, u32[]{:S(2)}) collective-permute-start(bf16[3,256,256]{2,1,0:T(8,128)(2,1)S(1)} %get-tuple-element.43), channel_id=1, source_target_pairs={{0,2},{2,0},{1,3},{3,1},{4,6},{6,4},{5,7},{7,5},{8,10},{10,8},{9,1... | collective-permute-start | bytes 1179656 | tf_op jit(solution)/shard_map/ppermute | solution.py:436
  18.4 11.1 %collective-permute-start.5 = (bf16[2,256,256]{2,1,0:T(8,128)(2,1)S(1)}, bf16[2,256,256]{2,1,0:T(8,128)(2,1)S(1)}, u32[]{:S(2)}, u32[]{:S(2)}) collective-permute-start(bf16[2,256,256]{2,1,0:T(8,128)(2,1)S(1)} %get-tuple-element.41), channel_id=1, source_target_pairs={{0,4},{4,0},{8,12},{12,8},{1,5},{5,1},{9,13},{13,9},{2,6},{6,2},{1... | collective-permute-start | bytes 786440 | tf_op jit(solution)/shard_map/ppermute | solution.py:361
  22.9 6.7 %collective-permute-start.6 = (bf16[2,256,256]{2,1,0:T(8,128)(2,1)S(1)}, bf16[2,256,256]{2,1,0:T(8,128)(2,1)S(1)}, u32[]{:S(2)}, u32[]{:S(2)}) collective-permute-start(bf16[2,256,256]{2,1,0:T(8,128)(2,1)S(1)} %get-tuple-element.42), channel_id=1, source_target_pairs={{0,0},{4,8},{8,4},{12,12},{1,1},{5,9},{9,5},{13,13},{2,2},{6,10},{... | collective-permute-start | bytes 786440 | tf_op jit(solution)/shard_map/ppermute | solution.py:361
  23.6 11.3 %collective-permute-start.8 = (bf16[512,256]{1,0:T(8,128)(2,1)S(1)}, bf16[512,256]{1,0:T(8,128)(2,1)S(1)}, u32[]{:S(2)}, u32[]{:S(2)}) collective-permute-start(bf16[512,256]{1,0:T(8,128)(2,1)S(1)} %copy-done.3), channel_id=1, source_target_pairs={{0,1},{1,0},{2,3},{3,2},{4,5},{5,4},{6,7},{7,6},{8,9},{9,8},{10,11... | collective-permute-start | bytes 786440 | tf_op jit(solution)/shard_map/ppermute | solution.py:361
  23.7 6.3 %collective-permute-start.4 = (bf16[256,256]{1,0:T(8,128)(2,1)S(1)}, bf16[256,256]{1,0:T(8,128)(2,1)S(1)}, u32[]{:S(2)}, u32[]{:S(2)}) collective-permute-start(bf16[256,256]{1,0:T(8,128)(2,1)S(1)} %add_east.2), channel_id=1, source_target_pairs={{0,2},{2,0},{1,3},{3,1},{4,6},{6,4},{5,7},{7,5},{8,10},{10,8},{9,1... | collective-permute-start | bytes 393224 | tf_op jit(solution)/shard_map/ppermute | solution.py:436
  29.5 6.7 %collective-permute-start.12 = (bf16[512,256]{1,0:T(8,128)(2,1)S(1)}, bf16[512,256]{1,0:T(8,128)(2,1)S(1)}, u32[]{:S(2)}, u32[]{:S(2)}) collective-permute-start(bf16[512,256]{1,0:T(8,128)(2,1)S(1)} %copy-done.4), channel_id=1, source_target_pairs={{0,1},{1,0},{2,3},{3,2},{4,5},{5,4},{6,7},{7,6},{8,9},{9,8},{10,11... | collective-permute-start | bytes 786440 | tf_op jit(solution)/shard_map/ppermute | solution.py:361
  29.6 6.7 %collective-permute-start.13 = (bf16[256,512]{1,0:T(8,128)(2,1)S(1)}, bf16[256,512]{1,0:T(8,128)(2,1)S(1)}, u32[]{:S(2)}, u32[]{:S(2)}) collective-permute-start(bf16[256,512]{1,0:T(8,128)(2,1)S(1)} %copy-done.5), channel_id=1, source_target_pairs={{0,1},{1,0},{2,3},{3,2},{4,5},{5,4},{6,7},{7,6},{8,9},{9,8},{10,11... | collective-permute-start | bytes 786440 | tf_op jit(solution)/shard_map/ppermute | solution.py:361
  30.1 1.6 %collective-permute-start.1 = (bf16[227,256]{1,0:T(8,128)(2,1)S(1)}, bf16[227,256]{1,0:T(8,128)(2,1)S(1)}, u32[]{:S(2)}, u32[]{:S(2)}) collective-permute-start(bf16[227,256]{1,0:T(8,128)(2,1)S(1)} %bitcast.14), channel_id=1, source_target_pairs={{0,1},{1,0},{2,3},{3,2},{4,5},{5,4},{6,7},{7,6},{8,9},{9,8},{10,11... | collective-permute-start | bytes 348680 | tf_op jit(solution)/shard_map/ppermute | solution.py:361
  30.2 6.1 %collective-permute-start.7 = (bf16[256,256]{1,0:T(8,128)(2,1)S(1)}, bf16[256,256]{1,0:T(8,128)(2,1)S(1)}, u32[]{:S(2)}, u32[]{:S(2)}) collective-permute-start(bf16[256,256]{1,0:T(8,128)(2,1)S(1)} %add_east.3.after_ref), channel_id=1, source_target_pairs={{0,2},{2,0},{1,3},{3,1},{4,6},{6,4},{5,7},{7,5},{8,10},{10,8},{9,1... | collective-permute-start | bytes 393224 | tf_op jit(solution)/shard_map/ppermute | solution.py:436
  31.6 7.1 %collective-permute-start.10 = (bf16[256,256]{1,0:T(8,128)(2,1)S(1)}, bf16[256,256]{1,0:T(8,128)(2,1)S(1)}, u32[]{:S(2)}, u32[]{:S(2)}) collective-permute-start(bf16[256,256]{1,0:T(8,128)(2,1)S(1)} %get-tuple-element.45), channel_id=1, source_target_pairs={{0,4},{4,0},{8,12},{12,8},{1,5},{5,1},{9,13},{13,9},{2,6},{6,2},{1... | collective-permute-start | bytes 393224 | tf_op jit(solution)/shard_map/ppermute | solution.py:361
  34.9 3.8 %collective-permute-start.11 = (bf16[256,256]{1,0:T(8,128)(2,1)S(1)}, bf16[256,256]{1,0:T(8,128)(2,1)S(1)}, u32[]{:S(2)}, u32[]{:S(2)}) collective-permute-start(bf16[256,256]{1,0:T(8,128)(2,1)S(1)} %get-tuple-element.46), channel_id=1, source_target_pairs={{0,0},{4,8},{8,4},{12,12},{1,1},{5,9},{9,5},{13,13},{2,2},{6,10},{... | collective-permute-start | bytes 393224 | tf_op jit(solution)/shard_map/ppermute | solution.py:361
  41.7 2.4 %collective-permute-start.18 = (bf16[1280,256]{1,0:T(8,128)(2,1)}, bf16[1280,256]{1,0:T(8,128)(2,1)}, u32[]{:S(2)}, u32[]{:S(2)}) collective-permute-start(bf16[1280,256]{1,0:T(8,128)(2,1)} %get-tuple-element.53), channel_id=1, source_target_pairs={{0,1},{1,0},{2,3},{3,2},{4,5},{5,4},{6,7},{7,6},{8,9},{9,8},{10,11... | collective-permute-start | bytes 1966088 | tf_op jit(solution)/shard_map/ppermute | solution.py:361
  41.7 5.9 %collective-permute-start.14 = (bf16[256,256]{1,0:T(8,128)(2,1)S(1)}, bf16[256,256]{1,0:T(8,128)(2,1)S(1)}, u32[]{:S(2)}, u32[]{:S(2)}) collective-permute-start(bf16[256,256]{1,0:T(8,128)(2,1)S(1)} %get-tuple-element.49.proj_ref), channel_id=1, source_target_pairs={{2,0},{0,2},{3,1},{1,3},{6,4},{4,6},{7,5},{5,7},{10,8},{8,10},{11,... | collective-permute-start | bytes 393224 | tf_op jit(solution)/shard_map/ppermute | solution.py:526
  46.1 6.4 %collective-permute-start.19 = (bf16[512,256]{1,0:T(8,128)(2,1)S(1)}, bf16[512,256]{1,0:T(8,128)(2,1)S(1)}, u32[]{:S(2)}, u32[]{:S(2)}) collective-permute-start(bf16[512,256]{1,0:T(8,128)(2,1)S(1)} %constant_dynamic-slice_fusion.1), channel_id=1, source_target_pairs={{0,2},{1,5},{2,0},{3,7},{4,6},{5,1},{6,4},{7,3},{8,10},{9,13},{10,... | collective-permute-start | bytes 786440 | tf_op jit(solution)/shard_map/ppermute | solution.py:396
  47.6 10.9 %collective-permute-start.15 = (bf16[2,256,256]{2,1,0:T(8,128)(2,1)S(1)}, bf16[2,256,256]{2,1,0:T(8,128)(2,1)S(1)}, u32[]{:S(2)}, u32[]{:S(2)}) collective-permute-start(bf16[2,256,256]{2,1,0:T(8,128)(2,1)S(1)} %pair_nodes.1.after_ref), channel_id=1, source_target_pairs={{0,4},{4,0},{8,12},{12,8},{1,5},{5,1},{9,13},{13,9},{2,6},{6,2},{1... | collective-permute-start | bytes 786440 | tf_op jit(solution)/shard_map/ppermute | solution.py:361
  51.3 7.2 %collective-permute-start.16 = (bf16[2,256,256]{2,1,0:T(8,128)(2,1)S(1)}, bf16[2,256,256]{2,1,0:T(8,128)(2,1)S(1)}, u32[]{:S(2)}, u32[]{:S(2)}) collective-permute-start(bf16[2,256,256]{2,1,0:T(8,128)(2,1)S(1)} %pair_nodes.1.after_ref), channel_id=1, source_target_pairs={{0,0},{4,8},{8,4},{12,12},{1,1},{5,9},{9,5},{13,13},{2,2},{6,10},{... | collective-permute-start | bytes 786440 | tf_op jit(solution)/shard_map/ppermute | solution.py:361
  52.7 8.2 %collective-permute-start.20 = (bf16[256,256]{1,0:T(8,128)(2,1)S(1)}, bf16[256,256]{1,0:T(8,128)(2,1)S(1)}, u32[]{:S(2)}, u32[]{:S(2)}) collective-permute-start(bf16[256,256]{1,0:T(8,128)(2,1)S(1)} %constant_dynamic-slice_fusion), channel_id=1, source_target_pairs={{0,4},{1,9},{2,6},{3,11},{4,0},{5,13},{6,2},{7,15},{8,12},{9,1},{1... | collective-permute-start | bytes 393224 | tf_op jit(solution)/shard_map/ppermute | solution.py:396
  60.9 5.9 %collective-permute-start.21 = (bf16[256,256]{1,0:T(8,128)(2,1)S(1)}, bf16[256,256]{1,0:T(8,128)(2,1)S(1)}, u32[]{:S(2)}, u32[]{:S(2)}) collective-permute-start(bf16[256,256]{1,0:T(8,128)(2,1)S(1)} %second_sum.1), channel_id=1, source_target_pairs={{0,8},{1,3},{2,10},{3,1},{4,12},{5,7},{6,14},{7,5},{8,0},{9,11},{1... | collective-permute-start | bytes 393224 | tf_op jit(solution)/shard_map/ppermute | solution.py:396
  66.9 7.3 %collective-permute-start.22 = (bf16[256,256]{1,0:T(8,128)(2,1)S(1)}, bf16[256,256]{1,0:T(8,128)(2,1)S(1)}, u32[]{:S(2)}, u32[]{:S(2)}) collective-permute-start(bf16[256,256]{1,0:T(8,128)(2,1)S(1)} %add_convert_fusion), channel_id=1, source_target_pairs={{0,4},{1,9},{2,6},{3,11},{4,0},{5,13},{6,2},{7,15},{8,12},{9,1},{1... | collective-permute-start | bytes 393224 | tf_op jit(solution)/shard_map/ppermute | solution.py:396
  71.0 4.2 %collective-permute-start.17 = (bf16[8,64,256]{2,1,0:T(8,128)(2,1)S(1)}, bf16[8,64,256]{2,1,0:T(8,128)(2,1)S(1)}, u32[]{:S(2)}, u32[]{:S(2)}) collective-permute-start(bf16[8,64,256]{2,1,0:T(8,128)(2,1)S(1)} %get-tuple-element.51), channel_id=1, source_target_pairs={{0,1},{1,0},{2,3},{3,2},{4,5},{5,4},{6,7},{7,6},{8,9},{9,8},{10,11... | collective-permute-start | bytes 786440 | tf_op jit(solution)/shard_map/ppermute | solution.py:361
  74.3 6.4 %collective-permute-start.23 = (bf16[512,256]{1,0:T(8,128)(2,1)S(1)}, bf16[512,256]{1,0:T(8,128)(2,1)S(1)}, u32[]{:S(2)}, u32[]{:S(2)}) collective-permute-start(bf16[512,256]{1,0:T(8,128)(2,1)S(1)} %maximum_select_fusion.mine_ref), channel_id=1, source_target_pairs={{0,2},{1,5},{2,0},{3,7},{4,6},{5,1},{6,4},{7,3},{8,10},{9,13},{10,... | collective-permute-start | bytes 786440 | tf_op jit(solution)/shard_map/ppermute | solution.py:396
  (9 other events, 121.9 us)

commit v7 on v5

--- a/solution.py
+++ b/solution.py
@@ -1,3 +1,5 @@
+import functools
+
 import jax
 import jax.numpy as jnp
 from jax import lax
@@ -9,7 +11,6 @@
 BF16 = jnp.bfloat16
 VMEM_BYTES = 20 * 1024 * 1024
 STEPS = 4
-HALVING = 3
 
 
 def dot(left, right):
@@ -126,31 +127,20 @@
     device_ref, slot_ref, after_ref, grid_ref, tiles_ref, weight_ref,
     own_ref, even_ref, odd_ref, hidden_ref, total, hold,
 ):
-    step = pl.program_id(0)
-    count, rows = tiles_ref.shape[0], tiles_ref.shape[1]
+    blocks, rows = tiles_ref.shape[:2]
     slots = total.shape[0] // 6
-    r = lax.axis_index("rep")
-
-    @pl.when(step == 0)
-    def _():
-        total[...] = jnp.zeros_like(total)
-
-    preact = dot_rows(grid_ref[...], weight_ref[...])
-    hold[...] = (preact * sigmoid(preact)).astype(BF16)
-    for i in range(count):
-        at = entry_of(device_ref, slot_ref, step * count + i, slots)
-        total[at] += dot(node_half(tiles_ref[i], r), hold[i * rows : (i + 1) * rows, :])
-
-    half_steps = pl.num_programs(0) // 2
-
-    @pl.when(step // half_steps == r)
-    def _():
-        at = pl.multiple_of((step % half_steps) * hold.shape[0], hold.shape[0])
-        hidden_ref[pl.ds(at, hold.shape[0]), :] = hold[...]
-
-    @pl.when(step == pl.num_programs(0) - 1)
-    def _():
-        write_packed(total, (own_ref, even_ref, odd_ref))
+    step_rows = blocks * rows // STEPS
+    r = lax.axis_index("rep")
+    total[...] = jnp.zeros_like(total)
+    for k in range(STEPS):
+        preact = dot_rows(grid_ref[:, k * step_rows : (k + 1) * step_rows], weight_ref[...])
+        hold[k * step_rows : (k + 1) * step_rows, :] = (preact * sigmoid(preact)).astype(BF16)
+        for b in range(k * blocks // STEPS, (k + 1) * blocks // STEPS):
+            at = entry_of(device_ref, slot_ref, b, slots)
+            total[at] += dot(node_half(tiles_ref[b], r), hold[b * rows : (b + 1) * rows, :])
+    mine = hidden_ref.shape[0]
+    hidden_ref[...] = hold[pl.ds(pl.multiple_of(r * mine, mine), mine), :]
+    write_packed(total, (own_ref, even_ref, odd_ref))
 
 
 def local_kernel(own_ref, oth_ref, cot_ref, out_ref, out_other_ref, base_ref, grad_ref, grad_other_ref):
@@ -266,6 +256,12 @@
     out_ref[...] = added(keep, got_ref[...]).astype(out_ref.dtype)
 
 
+def second_sum_kernel(even_ref, odd_ref, value_ref, got_ref, out_ref):
+    rows = got_ref.shape[0]
+    keep = value_ref[pl.ds(pl.multiple_of(sum_bit(1) * rows, rows), rows), :]
+    out_ref[...] = added(keep, got_ref[...]).astype(out_ref.dtype)
+
+
 def pair_kernel(proj_ref, east_ref, pair_ref):
     pair_ref[0] = proj_ref[...]
     pair_ref[1] = east_ref[...]
@@ -374,23 +370,14 @@
 
 
 def summed(value):
-    count = len(sum_orders()[0])
-    halving = min(count - 1, HALVING)
-    for step in range(1, count):
-        if step >= halving:
-            value = (value.astype(F32) + sum_swap(value, step).astype(F32)).astype(BF16)
-            continue
-        rows = value.shape[0] // 2
-        keep = lax.dynamic_slice_in_dim(value, sum_bit(step) * rows, rows, 0)
-        got = sum_swap(given_half(value, step), step)
-        value = (keep.astype(F32) + got.astype(F32)).astype(BF16)
-    for step in range(halving - 1, 0, -1):
-        other = sum_swap(value, step)
-        value = jnp.where(
-            sum_bit(step) == 0,
-            jnp.concatenate([value, other], axis=0),
-            jnp.concatenate([other, value], axis=0),
-        )
+    for step in range(2, len(sum_orders()[0])):
+        value = (value.astype(F32) + sum_swap(value, step).astype(F32)).astype(BF16)
+    other = sum_swap(value, 1)
+    value = jnp.where(
+        sum_bit(1) == 0,
+        jnp.concatenate([value, other], axis=0),
+        jnp.concatenate([other, value], axis=0),
+    )
     return value, sum_swap(value, 0)
 
 
@@ -417,31 +404,13 @@
     to_east = lambda value: lax.ppermute(value, "lon", east_pairs)
 
     in_hbm = lambda value: pltpu.with_memory_space_constraint(value, pltpu.HBM)
+    in_vmem = lambda value: pltpu.with_memory_space_constraint(value, pltpu.VMEM)
     device, slot = route_device.reshape(blocks), route_slot
     grid_t, cot_t, out_t = grid_in.T, cotangent.T, w_out.T
     routes = (in_hbm(device), in_hbm(slot))
     tiles_in, grid_in_t, cot_in_t = in_hbm(interp_tiles), in_hbm(grid_t), in_hbm(cot_t)
-    per_step = blocks // STEPS
-    step_rows = per_step * tile_rows
-    tiles_spec = pl.BlockSpec((per_step, tile_rows, tile_rows), lambda i: (i, 0, 0))
-    cols_spec = pl.BlockSpec((channels, step_rows), lambda i: (0, i))
     pair_shape = (2, nodes, width)
-
     embed_other = swap_rep(w_embed)
-
-    def encode(after, weight, limit):
-        return call(
-            encode_kernel, "encode",
-            [smem(), smem(), anywhere(), cols_spec, tiles_spec, whole((channels, width))],
-            [whole(pair_shape)] * 3 + [whole((my_rows, width))],
-            [shape_of(pair_shape, BF16)] * 3 + [shape_of((my_rows, width), BF16)],
-            2 * grid_rows * width * (channels + half), 3e6, grid=(STEPS,), exps=grid_rows * width,
-            scratch=[
-                pltpu.VMEM((6 * slots, half, width), F32),
-                pltpu.VMEM((step_rows, width), BF16),
-            ],
-            limit=limit,
-        )(*routes, after, grid_in_t, tiles_in, weight)
 
     back_own, back_east, back_side = call(
         back_kernel, "back_messages",
@@ -449,7 +418,7 @@
         [vmem()] * 3,
         [shape_of((nodes, padded), BF16), shape_of((3, nodes, padded), BF16),
          shape_of((2, nodes, padded), BF16)],
-        2 * grid_rows * half * padded, 3e6,
+        1, 1,
         scratch=[
             pltpu.VMEM((6 * slots, half, padded), F32),
             pltpu.VMEM(interp_tiles.shape, BF16),
@@ -460,9 +429,21 @@
     )(*routes, tiles_in, cot_in_t)
     back_moved = to_east(back_east)
 
-    own_a, even_a, odd_a, hidden_a = encode(back_own, in_hbm(w_embed), VMEM_BYTES)
+    def encode(after, weight):
+        return call(
+            encode_kernel, "encode",
+            [smem(), smem(), anywhere()] + [vmem()] * 3,
+            [vmem()] * 4,
+            [shape_of(pair_shape, BF16)] * 3 + [shape_of((my_rows, width), BF16)],
+            1, 1,
+            scratch=[
+                pltpu.VMEM((6 * slots, half, width), F32), pltpu.VMEM((grid_rows, width), BF16),
+            ],
+        )(device, slot, after, grid_t, interp_tiles, weight)
+
+    own_a, even_a, odd_a, hidden_a = encode(back_own, w_embed)
     even_in_a, odd_in_a = to_even(even_a), to_odd(odd_a)
-    own_b, even_b, odd_b, hidden_b = encode(own_a, embed_other, VMEM_BYTES)
+    own_b, even_b, odd_b, hidden_b = encode(own_a, embed_other)
     even_in_b, odd_in_b = to_even(even_b), to_odd(odd_b)
 
     out_other, up_other, down_other = swap_rep(out_t), swap_rep(w_up), swap_rep(w_down)
@@ -513,6 +494,7 @@
         back_own, back_moved, back_even_in, back_odd_in, local, local_other, *weights,
     )
 
+    keep, give = in_vmem(keep), in_vmem(give)
     east = lax.ppermute(proj, "lon", west_pairs)
     terms, grad_mesh = call(
         terms_kernel, "sum_terms", [vmem()] * 2, [vmem()] * 2,
@@ -529,7 +511,11 @@
         shape_of((latent, width), BF16), 2 * latent * width, 1e6,
     )(pair, terms, sum_swap(given_half(terms, 0), 0))
     pair_even, pair_odd = to_even(pair), to_odd(pair)
-    mine, theirs = summed(halved)
+    quarter = call(
+        second_sum_kernel, "second_sum", [anywhere()] * 2 + [vmem()] * 2, vmem(),
+        shape_of((width, width), BF16), 1, 1,
+    )(pair_even, pair_odd, halved, sum_swap(given_half(halved, 1), 1))
+    mine, theirs = summed(quarter)
 
     table_shape = (2 * slots, half, padded)
     mine_picked, theirs_picked = call(

time: 80.2 us -> 81.2 us (1.012)
  the two profiles are of different devices: /device:TPU:1 before, /device:TPU:0 now
where the time goes in v7:
time: 81.2 us; the launch traced here: 80.9 us
  starting transfers between devices  31.5 us (39%)
  waiting for transfers between devices  28.2 us (35%)
  Pallas kernels  18.4 us (23%)
  local copies, waits for them, and re-layouts  1.67 us (2%)
  between operations  0.92 us (1%)
    ppermute x15, starting transfers between devices, along(): return lambda value: lax.ppermute(value, axis, pairs)  16.2 us
    ppermute x5, waiting for transfers between devices, sum_swap(): return lax.ppermute(value, ('lat', 'lon', 'rep'), pairs)  15.8 us
    ppermute x15, waiting for transfers between devices, along(): return lambda value: lax.ppermute(value, axis, pairs)  12.4 us
    ppermute x5, starting transfers between devices, sum_swap(): return lax.ppermute(value, ('lat', 'lon', 'rep'), pairs)  10.1 us
    pallas_call x2, Pallas kernels, encode(): call(encode_kernel, 'encode', [smem(), smem(), anywhere()] + [vmem()] * 3...  4.35 us
    ppermute x3, starting transfers between devices, per_device(): to_east = lambda value: lax.ppermute(value, 'lon', east_pairs)  4.2 us
    pallas_call x1, Pallas kernels, per_device(): call(back_kernel, 'back_messages', [smem(), smem(), anywhere(), anywhere(...  3.48 us
    pallas_call x1, Pallas kernels, per_device(): call(node_kernel, 'node_update_and_gradients', sums_specs * 2 + [whole(em...  3.01 us
  transfers between devices with their start and end apart: 24, of which 11 were waited for; matrix products, arithmetic and copies ran while one was open for 1% of the time, Pallas kernels for 13%

profile of v7, /device:TPU:0, one launch (start us, length us, event | category | flops | bytes accessed | tf_op | source)
XLA Modules:
  0.0 80.9 jit_solution(8349418418726776109)
XLA Ops:
  0.7 3.5 %back_messages.1 = (bf16[256,256]{1,0:T(8,128)(2,1)S(1)}, bf16[3,256,256]{2,1,0:T(8,128)(2,1)S(1)}, bf16[2,256,256]{2,1,0:T(8,128)(2,1)S(1)}) custom-call(s32[16]{0:T(128)} %bitcast.25, s32[16]{0:T(128)} %slot_ref.7, bf16[16,128,128]{2,1,0:T(8,128)(2,1)} %tiles_ref.7, bf16[227,2048]{1,0:T(8,128)(2,1)} %bitcast.14), custom_call_target="tpu_custom_call" | custom-call | flops 1 | bytes 1 | tf_op jit(solution)/shard_map/back_messages/pallas_call | solution.py:415
  4.2 3.0 %collective-permute-start.4 = (bf16[3,256,256]{2,1,0:T(8,128)(2,1)S(1)}, bf16[3,256,256]{2,1,0:T(8,128)(2,1)S(1)}, u32[]{:S(2)}, u32[]{:S(2)}) collective-permute-start(bf16[3,256,256]{2,1,0:T(8,128)(2,1)S(1)} %get-tuple-element.38), channel_id=1, source_target_pairs={{0,2},{2,0},{1,3},{3,1},{4,6},{6,4},{5,7},{7,5},{8,10},{10,8},{9,1... | collective-permute-start | bytes 1179656 | tf_op jit(solution)/shard_map/ppermute | solution.py:404
  8.1 2.2 %encode.2 = (bf16[2,256,256]{2,1,0:T(8,128)(2,1)S(1)}, bf16[2,256,256]{2,1,0:T(8,128)(2,1)S(1)}, bf16[2,256,256]{2,1,0:T(8,128)(2,1)S(1)}, bf16[1024,256]{1,0:T(8,128)(2,1)S(1)}) custom-call(s32[16]{0:T(128)S(1)} %bitcast.26, s32[16]{0:T(128)S(1)} %copy-done.9, bf16[256,256]{1,0:T(8,128)(2,1)S(1)} %get-tuple-element.31.after_ref.back_ref, ...), custom_call_target="tpu_custom_call" | custom-call | flops 1 | bytes 1 | tf_op jit(solution)/shard_map/encode/pallas_call | solution.py:433
  10.3 1.6 %collective-permute-start.2 = (bf16[2,256,256]{2,1,0:T(8,128)(2,1)S(1)}, bf16[2,256,256]{2,1,0:T(8,128)(2,1)S(1)}, u32[]{:S(2)}, u32[]{:S(2)}) collective-permute-start(bf16[2,256,256]{2,1,0:T(8,128)(2,1)S(1)} %get-tuple-element.36), channel_id=1, source_target_pairs={{0,4},{4,0},{8,12},{12,8},{1,5},{5,1},{9,13},{13,9},{2,6},{6,2},{1... | collective-permute-start | bytes 786440 | tf_op jit(solution)/shard_map/ppermute | solution.py:329
  13.3 2.2 %encode.3 = (bf16[2,256,256]{2,1,0:T(8,128)(2,1)S(1)}, bf16[2,256,256]{2,1,0:T(8,128)(2,1)S(1)}, bf16[2,256,256]{2,1,0:T(8,128)(2,1)S(1)}, bf16[1024,256]{1,0:T(8,128)(2,1)S(1)}) custom-call(s32[16]{0:T(128)S(1)} %bitcast.27, s32[16]{0:T(128)S(1)} %copy-done.9, bf16[2,256,256]{2,1,0:T(8,128)(2,1)S(1)} %get-tuple-element.33.after_ref.refs_1_.own_a, ...), custom_call_target="tpu_custom_call" | custom-call | flops 1 | bytes 1 | tf_op jit(solution)/shard_map/encode/pallas_call | solution.py:433
  15.4 3.8 %collective-permute-start.6 = (bf16[2,256,256]{2,1,0:T(8,128)(2,1)S(1)}, bf16[2,256,256]{2,1,0:T(8,128)(2,1)S(1)}, u32[]{:S(2)}, u32[]{:S(2)}) collective-permute-start(bf16[2,256,256]{2,1,0:T(8,128)(2,1)S(1)} %get-tuple-element.40), channel_id=1, source_target_pairs={{0,4},{4,0},{8,12},{12,8},{1,5},{5,1},{9,13},{13,9},{2,6},{6,2},{1... | collective-permute-start | bytes 786440 | tf_op jit(solution)/shard_map/ppermute | solution.py:329
  21.1 4.9 %collective-permute-done.6.refs_2_.even_b = bf16[2,256,256]{2,1,0:T(8,128)(2,1)S(1)} collective-permute-done((bf16[2,256,256]{2,1,0:T(8,128)(2,1)S(1)}, bf16[2,256,256]{2,1,0:T(8,128)(2,1)S(1)}, u32[]{:S(2)}, u32[]{:S(2)}) %collective-permute-start.6) | collective-permute-done | bytes 262176 | tf_op jit(solution)/shard_map/ppermute | solution.py:329
  27.7 3.4 %collective-permute-start.10 = (bf16[256,256]{1,0:T(8,128)(2,1)S(1)}, bf16[256,256]{1,0:T(8,128)(2,1)S(1)}, u32[]{:S(2)}, u32[]{:S(2)}) collective-permute-start(bf16[256,256]{1,0:T(8,128)(2,1)S(1)} %get-tuple-element.43), channel_id=1, source_target_pairs={{0,4},{4,0},{8,12},{12,8},{1,5},{5,1},{9,13},{13,9},{2,6},{6,2},{1... | collective-permute-start | bytes 393224 | tf_op jit(solution)/shard_map/ppermute | solution.py:329
  32.5 2.4 %collective-permute-done.10.back_even_ref = bf16[256,256]{1,0:T(8,128)(2,1)S(1)} collective-permute-done((bf16[256,256]{1,0:T(8,128)(2,1)S(1)}, bf16[256,256]{1,0:T(8,128)(2,1)S(1)}, u32[]{:S(2)}, u32[]{:S(2)}) %collective-permute-start.10) | collective-permute-done | bytes 131104 | tf_op jit(solution)/shard_map/ppermute | solution.py:329
  34.9 3.0 %node_update_and_gradients.1 = (bf16[256,256]{1,0:T(8,128)(2,1)}, f32[1280,256]{1,0:T(8,128)S(1)}, bf16[1280,256]{1,0:T(8,128)(2,1)}) custom-call(bf16[2,256,256]{2,1,0:T(8,128)(2,1)S(1)} %get-tuple-element.33.after_ref.refs_1_.own_a, bf16[2,256,256]{2,1,0:T(8,128)(2,1)S(1)} %collective-permute-done.2.refs_2_.even_a, ...), custom_call_target="tpu_custom_call" | custom-call | flops 1 | bytes 1 | tf_op jit(solution)/shard_map/node_update_and_gradients/pallas_call | solution.py:482
  39.0 1.4 %collective-permute-done.18.got_ref = bf16[1280,256]{1,0:T(8,128)(2,1)} collective-permute-done((bf16[1280,256]{1,0:T(8,128)(2,1)}, bf16[1280,256]{1,0:T(8,128)(2,1)}, u32[]{:S(2)}, u32[]{:S(2)}) %collective-permute-start.18) | collective-permute-done | bytes 655392 | tf_op jit(solution)/shard_map/ppermute | solution.py:329
  40.4 2.0 %sum_terms.1 = (bf16[1024,256]{1,0:T(8,128)(2,1)S(1)}, f32[4,2,64,256]{3,2,1,0:T(8,128)}) custom-call(f32[1280,256]{1,0:T(8,128)S(1)} %get-tuple-element.50.keep_ref, bf16[1280,256]{1,0:T(8,128)(2,1)} %collective-permute-done.18.got_ref), custom_call_target="tpu_custom_call" | custom-call | flops 1 | bytes 1 | tf_op jit(solution)/shard_map/sum_terms/pallas_call | solution.py:499
  45.1 3.7 %collective-permute-start.15 = (bf16[2,256,256]{2,1,0:T(8,128)(2,1)S(1)}, bf16[2,256,256]{2,1,0:T(8,128)(2,1)S(1)}, u32[]{:S(2)}, u32[]{:S(2)}) collective-permute-start(bf16[2,256,256]{2,1,0:T(8,128)(2,1)S(1)} %pair_nodes.1.after_ref), channel_id=1, source_target_pairs={{0,4},{4,0},{8,12},{12,8},{1,5},{5,1},{9,13},{13,9},{2,6},{6,2},{1... | collective-permute-start | bytes 786440 | tf_op jit(solution)/shard_map/ppermute | solution.py:329
  49.7 3.7 %collective-permute-start.20 = (bf16[256,256]{1,0:T(8,128)(2,1)S(1)}, bf16[256,256]{1,0:T(8,128)(2,1)S(1)}, u32[]{:S(2)}, u32[]{:S(2)}) collective-permute-start(bf16[256,256]{1,0:T(8,128)(2,1)S(1)} %constant_dynamic-slice_fusion), channel_id=1, source_target_pairs={{0,4},{1,9},{2,6},{3,11},{4,0},{5,13},{6,2},{7,15},{8,12},{9,1},{1... | collective-permute-start | bytes 393224 | tf_op jit(solution)/shard_map/ppermute | solution.py:364
  53.4 2.6 %collective-permute-done.15.even_ref = bf16[2,256,256]{2,1,0:T(8,128)(2,1)S(1)} collective-permute-done((bf16[2,256,256]{2,1,0:T(8,128)(2,1)S(1)}, bf16[2,256,256]{2,1,0:T(8,128)(2,1)S(1)}, u32[]{:S(2)}, u32[]{:S(2)}) %collective-permute-start.15) | collective-permute-done | bytes 262176 | tf_op jit(solution)/shard_map/ppermute | solution.py:329
  56.1 2.3 %collective-permute-done.20.got_ref = bf16[256,256]{1,0:T(8,128)(2,1)S(1)} collective-permute-done((bf16[256,256]{1,0:T(8,128)(2,1)S(1)}, bf16[256,256]{1,0:T(8,128)(2,1)S(1)}, u32[]{:S(2)}, u32[]{:S(2)}) %collective-permute-start.20) | collective-permute-done | bytes 131104 | tf_op jit(solution)/shard_map/ppermute | solution.py:364
  58.4 3.9 %collective-permute-start.21 = (bf16[256,256]{1,0:T(8,128)(2,1)S(1)}, bf16[256,256]{1,0:T(8,128)(2,1)S(1)}, u32[]{:S(2)}, u32[]{:S(2)}) collective-permute-start(bf16[256,256]{1,0:T(8,128)(2,1)S(1)} %second_sum.1), channel_id=1, source_target_pairs={{0,8},{1,3},{2,10},{3,1},{4,12},{5,7},{6,14},{7,5},{8,0},{9,11},{1... | collective-permute-start | bytes 393224 | tf_op jit(solution)/shard_map/ppermute | solution.py:364
  62.3 4.4 %collective-permute-done.21 = bf16[256,256]{1,0:T(8,128)(2,1)S(1)} collective-permute-done((bf16[256,256]{1,0:T(8,128)(2,1)S(1)}, bf16[256,256]{1,0:T(8,128)(2,1)S(1)}, u32[]{:S(2)}, u32[]{:S(2)}) %collective-permute-start.21) | collective-permute-done | bytes 131104 | tf_op jit(solution)/shard_map/ppermute | solution.py:364
  67.0 1.1 %pick_nodes.1 = (bf16[8,64,256]{2,1,0:T(8,128)(2,1)S(1)}, bf16[8,64,256]{2,1,0:T(8,128)(2,1)S(1)}) custom-call(s32[16]{0:T(128)S(1)} %bitcast.28, s32[16]{0:T(128)S(1)} %copy-done.9, bf16[8,64,256]{2,1,0:T(8,128)(2,1)S(1)} %bitcast.22, bf16[8,64,256]{2,1,0:T(8,128)(2,1)S(1)} %bitcast.23, bf16[8,64,256]{2,1,0:T(8,128)(2,1)S(1)} %bitcast.24), custom_call_target="tpu_custom_call" | custom-call | flops 5000000000 | bytes 1 | tf_op jit(solution)/shard_map/pick_nodes/pallas_call | solution.py:521
  68.2 4.8 %collective-permute-done.22 = bf16[256,256]{1,0:T(8,128)(2,1)S(1)} collective-permute-done((bf16[256,256]{1,0:T(8,128)(2,1)S(1)}, bf16[256,256]{1,0:T(8,128)(2,1)S(1)}, u32[]{:S(2)}, u32[]{:S(2)}) %collective-permute-start.22) | collective-permute-done | bytes 131104 | tf_op jit(solution)/shard_map/ppermute | solution.py:364
  73.2 1.1 %collective-permute-start.23 = (bf16[512,256]{1,0:T(8,128)(2,1)S(1)}, bf16[512,256]{1,0:T(8,128)(2,1)S(1)}, u32[]{:S(2)}, u32[]{:S(2)}) collective-permute-start(bf16[512,256]{1,0:T(8,128)(2,1)S(1)} %maximum_select_fusion.mine_ref), channel_id=1, source_target_pairs={{0,2},{1,5},{2,0},{3,7},{4,6},{5,1},{6,4},{7,3},{8,10},{9,13},{10,... | collective-permute-start | bytes 786440 | tf_op jit(solution)/shard_map/ppermute | solution.py:364
  74.3 1.2 %decode.1 = bf16[227,1024]{1,0:T(8,128)(2,1)} custom-call(bf16[16,128,128]{2,1,0:T(8,128)(2,1)S(1)} %copy-done, f32[227,1024]{1,0:T(8,128)S(1)} %get-tuple-element.35.base_ref, bf16[8,64,256]{2,1,0:T(8,128)(2,1)S(1)} %get-tuple-element.48.mine_ref, bf16[8,64,256]{2,1,0:T(8,128)(2,1)S(1)} %collective-permute-done.17.got_ref), custom_call_target="tpu_custom_call" | custom-call | flops 1 | bytes 1 | tf_op jit(solution)/shard_map/decode/pallas_call | solution.py:525
  75.5 4.1 %collective-permute-done.23.other_ref = bf16[512,256]{1,0:T(8,128)(2,1)S(1)} collective-permute-done((bf16[512,256]{1,0:T(8,128)(2,1)S(1)}, bf16[512,256]{1,0:T(8,128)(2,1)S(1)}, u32[]{:S(2)}, u32[]{:S(2)}) %collective-permute-start.23) | collective-permute-done | bytes 262176 | tf_op jit(solution)/shard_map/ppermute | solution.py:364
  79.6 1.3 %finish.1 = (f32[512,256]{1,0:T(8,128)}, f32[256,512]{1,0:T(8,128)}, f32[227,256]{1,0:T(8,128)}) custom-call(bf16[512,256]{1,0:T(8,128)(2,1)S(1)} %maximum_select_fusion.mine_ref, bf16[512,256]{1,0:T(8,128)(2,1)S(1)} %collective-permute-done.23.other_ref, bf16[227,256]{1,0:T(8,128)(2,1)S(1)} %bitcast.19, ...), custom_call_target="tpu_custom_call" | custom-call | flops 1 | bytes 1 | tf_op jit(solution)/shard_map/finish/pallas_call | solution.py:531
  (63 shorter events, 12.3 us)
Async XLA Ops:
  4.2 16.0 %collective-permute-start.4 = (bf16[3,256,256]{2,1,0:T(8,128)(2,1)S(1)}, bf16[3,256,256]{2,1,0:T(8,128)(2,1)S(1)}, u32[]{:S(2)}, u32[]{:S(2)}) collective-permute-start(bf16[3,256,256]{2,1,0:T(8,128)(2,1)S(1)} %get-tuple-element.38), channel_id=1, source_target_pairs={{0,2},{2,0},{1,3},{3,1},{4,6},{6,4},{5,7},{7,5},{8,10},{10,8},{9,1... | collective-permute-start | bytes 1179656 | tf_op jit(solution)/shard_map/ppermute | solution.py:404
  10.3 9.8 %collective-permute-start.2 = (bf16[2,256,256]{2,1,0:T(8,128)(2,1)S(1)}, bf16[2,256,256]{2,1,0:T(8,128)(2,1)S(1)}, u32[]{:S(2)}, u32[]{:S(2)}) collective-permute-start(bf16[2,256,256]{2,1,0:T(8,128)(2,1)S(1)} %get-tuple-element.36), channel_id=1, source_target_pairs={{0,4},{4,0},{8,12},{12,8},{1,5},{5,1},{9,13},{13,9},{2,6},{6,2},{1... | collective-permute-start | bytes 786440 | tf_op jit(solution)/shard_map/ppermute | solution.py:329
  11.9 1.3 %collective-permute-start = (bf16[227,256]{1,0:T(8,128)(2,1)S(1)}, bf16[227,256]{1,0:T(8,128)(2,1)S(1)}, u32[]{:S(2)}, u32[]{:S(2)}) collective-permute-start(bf16[227,256]{1,0:T(8,128)(2,1)S(1)} %copy-done.7), channel_id=1, source_target_pairs={{0,1},{1,0},{2,3},{3,2},{4,5},{5,4},{6,7},{7,6},{8,9},{9,8},{10,11... | collective-permute-start | bytes 348680 | tf_op jit(solution)/shard_map/ppermute | solution.py:329
  11.9 8.3 %collective-permute-start.3 = (bf16[2,256,256]{2,1,0:T(8,128)(2,1)S(1)}, bf16[2,256,256]{2,1,0:T(8,128)(2,1)S(1)}, u32[]{:S(2)}, u32[]{:S(2)}) collective-permute-start(bf16[2,256,256]{2,1,0:T(8,128)(2,1)S(1)} %get-tuple-element.37), channel_id=1, source_target_pairs={{0,0},{4,8},{8,4},{12,12},{1,1},{5,9},{9,5},{13,13},{2,2},{6,10},{... | collective-permute-start | bytes 786440 | tf_op jit(solution)/shard_map/ppermute | solution.py:329
  15.4 10.5 %collective-permute-start.6 = (bf16[2,256,256]{2,1,0:T(8,128)(2,1)S(1)}, bf16[2,256,256]{2,1,0:T(8,128)(2,1)S(1)}, u32[]{:S(2)}, u32[]{:S(2)}) collective-permute-start(bf16[2,256,256]{2,1,0:T(8,128)(2,1)S(1)} %get-tuple-element.40), channel_id=1, source_target_pairs={{0,4},{4,0},{8,12},{12,8},{1,5},{5,1},{9,13},{13,9},{2,6},{6,2},{1... | collective-permute-start | bytes 786440 | tf_op jit(solution)/shard_map/ppermute | solution.py:329
  19.3 6.7 %collective-permute-start.7 = (bf16[2,256,256]{2,1,0:T(8,128)(2,1)S(1)}, bf16[2,256,256]{2,1,0:T(8,128)(2,1)S(1)}, u32[]{:S(2)}, u32[]{:S(2)}) collective-permute-start(bf16[2,256,256]{2,1,0:T(8,128)(2,1)S(1)} %get-tuple-element.41), channel_id=1, source_target_pairs={{0,0},{4,8},{8,4},{12,12},{1,1},{5,9},{9,5},{13,13},{2,2},{6,10},{... | collective-permute-start | bytes 786440 | tf_op jit(solution)/shard_map/ppermute | solution.py:329
  20.1 11.0 %collective-permute-start.9 = (bf16[512,256]{1,0:T(8,128)(2,1)S(1)}, bf16[512,256]{1,0:T(8,128)(2,1)S(1)}, u32[]{:S(2)}, u32[]{:S(2)}) collective-permute-start(bf16[512,256]{1,0:T(8,128)(2,1)S(1)} %copy-done.4), channel_id=1, source_target_pairs={{0,1},{1,0},{2,3},{3,2},{4,5},{5,4},{6,7},{7,6},{8,9},{9,8},{10,11... | collective-permute-start | bytes 786440 | tf_op jit(solution)/shard_map/ppermute | solution.py:329
  20.3 6.2 %collective-permute-start.5 = (bf16[256,256]{1,0:T(8,128)(2,1)S(1)}, bf16[256,256]{1,0:T(8,128)(2,1)S(1)}, u32[]{:S(2)}, u32[]{:S(2)}) collective-permute-start(bf16[256,256]{1,0:T(8,128)(2,1)S(1)} %add_east.2), channel_id=1, source_target_pairs={{0,2},{2,0},{1,3},{3,1},{4,6},{6,4},{5,7},{7,5},{8,10},{10,8},{9,1... | collective-permute-start | bytes 393224 | tf_op jit(solution)/shard_map/ppermute | solution.py:404
  20.9 11.7 %collective-permute-start.12 = (bf16[512,256]{1,0:T(8,128)(2,1)S(1)}, bf16[512,256]{1,0:T(8,128)(2,1)S(1)}, u32[]{:S(2)}, u32[]{:S(2)}) collective-permute-start(bf16[512,256]{1,0:T(8,128)(2,1)S(1)} %copy-done.5), channel_id=1, source_target_pairs={{0,1},{1,0},{2,3},{3,2},{4,5},{5,4},{6,7},{7,6},{8,9},{9,8},{10,11... | collective-permute-start | bytes 786440 | tf_op jit(solution)/shard_map/ppermute | solution.py:329
  26.0 6.6 %collective-permute-start.13 = (bf16[256,512]{1,0:T(8,128)(2,1)S(1)}, bf16[256,512]{1,0:T(8,128)(2,1)S(1)}, u32[]{:S(2)}, u32[]{:S(2)}) collective-permute-start(bf16[256,512]{1,0:T(8,128)(2,1)S(1)} %copy-done.6), channel_id=1, source_target_pairs={{0,1},{1,0},{2,3},{3,2},{4,5},{5,4},{6,7},{7,6},{8,9},{9,8},{10,11... | collective-permute-start | bytes 786440 | tf_op jit(solution)/shard_map/ppermute | solution.py:329
  26.0 1.7 %collective-permute-start.1 = (bf16[227,256]{1,0:T(8,128)(2,1)S(1)}, bf16[227,256]{1,0:T(8,128)(2,1)S(1)}, u32[]{:S(2)}, u32[]{:S(2)}) collective-permute-start(bf16[227,256]{1,0:T(8,128)(2,1)S(1)} %bitcast.16), channel_id=1, source_target_pairs={{0,1},{1,0},{2,3},{3,2},{4,5},{5,4},{6,7},{7,6},{8,9},{9,8},{10,11... | collective-permute-start | bytes 348680 | tf_op jit(solution)/shard_map/ppermute | solution.py:329
  26.5 6.0 %collective-permute-start.8 = (bf16[256,256]{1,0:T(8,128)(2,1)S(1)}, bf16[256,256]{1,0:T(8,128)(2,1)S(1)}, u32[]{:S(2)}, u32[]{:S(2)}) collective-permute-start(bf16[256,256]{1,0:T(8,128)(2,1)S(1)} %add_east.3.after_ref), channel_id=1, source_target_pairs={{0,2},{2,0},{1,3},{3,1},{4,6},{6,4},{5,7},{7,5},{8,10},{10,8},{9,1... | collective-permute-start | bytes 393224 | tf_op jit(solution)/shard_map/ppermute | solution.py:404
  27.7 7.2 %collective-permute-start.10 = (bf16[256,256]{1,0:T(8,128)(2,1)S(1)}, bf16[256,256]{1,0:T(8,128)(2,1)S(1)}, u32[]{:S(2)}, u32[]{:S(2)}) collective-permute-start(bf16[256,256]{1,0:T(8,128)(2,1)S(1)} %get-tuple-element.43), channel_id=1, source_target_pairs={{0,4},{4,0},{8,12},{12,8},{1,5},{5,1},{9,13},{13,9},{2,6},{6,2},{1... | collective-permute-start | bytes 393224 | tf_op jit(solution)/shard_map/ppermute | solution.py:329
  31.1 3.8 %collective-permute-start.11 = (bf16[256,256]{1,0:T(8,128)(2,1)S(1)}, bf16[256,256]{1,0:T(8,128)(2,1)S(1)}, u32[]{:S(2)}, u32[]{:S(2)}) collective-permute-start(bf16[256,256]{1,0:T(8,128)(2,1)S(1)} %get-tuple-element.44), channel_id=1, source_target_pairs={{0,0},{4,8},{8,4},{12,12},{1,1},{5,9},{9,5},{13,13},{2,2},{6,10},{... | collective-permute-start | bytes 393224 | tf_op jit(solution)/shard_map/ppermute | solution.py:329
  37.9 2.4 %collective-permute-start.18 = (bf16[1280,256]{1,0:T(8,128)(2,1)}, bf16[1280,256]{1,0:T(8,128)(2,1)}, u32[]{:S(2)}, u32[]{:S(2)}) collective-permute-start(bf16[1280,256]{1,0:T(8,128)(2,1)} %get-tuple-element.51), channel_id=1, source_target_pairs={{0,1},{1,0},{2,3},{3,2},{4,5},{5,4},{6,7},{7,6},{8,9},{9,8},{10,11... | collective-permute-start | bytes 1966088 | tf_op jit(solution)/shard_map/ppermute | solution.py:329
  37.9 6.2 %collective-permute-start.14 = (bf16[256,256]{1,0:T(8,128)(2,1)}, bf16[256,256]{1,0:T(8,128)(2,1)}, u32[]{:S(2)}, u32[]{:S(2)}) collective-permute-start(bf16[256,256]{1,0:T(8,128)(2,1)} %get-tuple-element.47.proj_ref), channel_id=1, source_target_pairs={{2,0},{0,2},{3,1},{1,3},{6,4},{4,6},{7,5},{5,7},{10,8},{8,10},{11,... | collective-permute-start | bytes 393224 | tf_op jit(solution)/shard_map/ppermute | solution.py:498
  43.1 6.6 %collective-permute-start.19 = (bf16[512,256]{1,0:T(8,128)(2,1)}, bf16[512,256]{1,0:T(8,128)(2,1)S(1)}, u32[]{:S(2)}, u32[]{:S(2)}) collective-permute-start(bf16[512,256]{1,0:T(8,128)(2,1)} %constant_dynamic-slice_fusion.1), channel_id=1, source_target_pairs={{0,2},{1,5},{2,0},{3,7},{4,6},{5,1},{6,4},{7,3},{8,10},{9,13},{10,... | collective-permute-start | bytes 786440 | tf_op jit(solution)/shard_map/ppermute | solution.py:364
  45.1 10.9 %collective-permute-start.15 = (bf16[2,256,256]{2,1,0:T(8,128)(2,1)S(1)}, bf16[2,256,256]{2,1,0:T(8,128)(2,1)S(1)}, u32[]{:S(2)}, u32[]{:S(2)}) collective-permute-start(bf16[2,256,256]{2,1,0:T(8,128)(2,1)S(1)} %pair_nodes.1.after_ref), channel_id=1, source_target_pairs={{0,4},{4,0},{8,12},{12,8},{1,5},{5,1},{9,13},{13,9},{2,6},{6,2},{1... | collective-permute-start | bytes 786440 | tf_op jit(solution)/shard_map/ppermute | solution.py:329
  48.8 7.2 %collective-permute-start.16 = (bf16[2,256,256]{2,1,0:T(8,128)(2,1)S(1)}, bf16[2,256,256]{2,1,0:T(8,128)(2,1)S(1)}, u32[]{:S(2)}, u32[]{:S(2)}) collective-permute-start(bf16[2,256,256]{2,1,0:T(8,128)(2,1)S(1)} %pair_nodes.1.after_ref), channel_id=1, source_target_pairs={{0,0},{4,8},{8,4},{12,12},{1,1},{5,9},{9,5},{13,13},{2,2},{6,10},{... | collective-permute-start | bytes 786440 | tf_op jit(solution)/shard_map/ppermute | solution.py:329
  49.7 8.7 %collective-permute-start.20 = (bf16[256,256]{1,0:T(8,128)(2,1)S(1)}, bf16[256,256]{1,0:T(8,128)(2,1)S(1)}, u32[]{:S(2)}, u32[]{:S(2)}) collective-permute-start(bf16[256,256]{1,0:T(8,128)(2,1)S(1)} %constant_dynamic-slice_fusion), channel_id=1, source_target_pairs={{0,4},{1,9},{2,6},{3,11},{4,0},{5,13},{6,2},{7,15},{8,12},{9,1},{1... | collective-permute-start | bytes 393224 | tf_op jit(solution)/shard_map/ppermute | solution.py:364
  58.4 8.2 %collective-permute-start.21 = (bf16[256,256]{1,0:T(8,128)(2,1)S(1)}, bf16[256,256]{1,0:T(8,128)(2,1)S(1)}, u32[]{:S(2)}, u32[]{:S(2)}) collective-permute-start(bf16[256,256]{1,0:T(8,128)(2,1)S(1)} %second_sum.1), channel_id=1, source_target_pairs={{0,8},{1,3},{2,10},{3,1},{4,12},{5,7},{6,14},{7,5},{8,0},{9,11},{1... | collective-permute-start | bytes 393224 | tf_op jit(solution)/shard_map/ppermute | solution.py:364
  66.7 6.3 %collective-permute-start.22 = (bf16[256,256]{1,0:T(8,128)(2,1)S(1)}, bf16[256,256]{1,0:T(8,128)(2,1)S(1)}, u32[]{:S(2)}, u32[]{:S(2)}) collective-permute-start(bf16[256,256]{1,0:T(8,128)(2,1)S(1)} %add_convert_fusion), channel_id=1, source_target_pairs={{0,4},{1,9},{2,6},{3,11},{4,0},{5,13},{6,2},{7,15},{8,12},{9,1},{1... | collective-permute-start | bytes 393224 | tf_op jit(solution)/shard_map/ppermute | solution.py:364
  68.1 6.2 %collective-permute-start.17 = (bf16[8,64,256]{2,1,0:T(8,128)(2,1)S(1)}, bf16[8,64,256]{2,1,0:T(8,128)(2,1)S(1)}, u32[]{:S(2)}, u32[]{:S(2)}) collective-permute-start(bf16[8,64,256]{2,1,0:T(8,128)(2,1)S(1)} %get-tuple-element.49), channel_id=1, source_target_pairs={{0,1},{1,0},{2,3},{3,2},{4,5},{5,4},{6,7},{7,6},{8,9},{9,8},{10,11... | collective-permute-start | bytes 786440 | tf_op jit(solution)/shard_map/ppermute | solution.py:329
  73.2 6.4 %collective-permute-start.23 = (bf16[512,256]{1,0:T(8,128)(2,1)S(1)}, bf16[512,256]{1,0:T(8,128)(2,1)S(1)}, u32[]{:S(2)}, u32[]{:S(2)}) collective-permute-start(bf16[512,256]{1,0:T(8,128)(2,1)S(1)} %maximum_select_fusion.mine_ref), channel_id=1, source_target_pairs={{0,2},{1,5},{2,0},{3,7},{4,6},{5,1},{6,4},{7,3},{8,10},{9,13},{10,... | collective-permute-start | bytes 786440 | tf_op jit(solution)/shard_map/ppermute | solution.py:364
  (10 other events, 82.4 us)

commit v8 on v7

--- a/solution.py
+++ b/solution.py
@@ -173,7 +173,7 @@
     own_a, even_a, odd_a, moved_a, own_b, even_b, odd_b, moved_b, embed_ref, embed_other_ref,
     back_ref, back_moved_ref, back_even_ref, back_odd_ref, local_ref, local_other_ref,
     up_ref, up_other_ref, down_ref, down_other_ref, out_ref, out_other_ref,
-    proj_ref, keep_ref, give_ref,
+    proj_ref, keep_ref, give_ref, mesh_give_ref, mesh_ref, mesh_half, mesh_sem,
 ):
     r = lax.axis_index("rep")
     nodes, width = moved_a.shape
@@ -237,58 +237,75 @@
         back - jnp.mean(back, axis=-1, keepdims=True)
         - norm * jnp.mean(back * norm, axis=-1, keepdims=True)
     ) * inverse
-    keep_ref[2 * latent :, :] = grad_own.astype(F32) + slope[:, :width]
-    give_ref[2 * latent :, :] = (grad_oth.astype(F32) + slope[:, width:]).astype(give_ref.dtype)
-
-
-def terms_kernel(keep_ref, got_ref, out_ref, mesh_ref):
-    r = lax.axis_index("rep")
-    rows = out_ref.shape[0]
-    part = mesh_ref.shape[:1] + mesh_ref.shape[2:]
-    out_ref[...] = added(keep_ref[:rows, :], got_ref[:rows, :]).astype(out_ref.dtype)
-    mesh_ref[:, r] = keep_ref[rows:, :].reshape(part)
-    mesh_ref[:, 1 - r] = got_ref[rows:, :].astype(F32).reshape(part)
-
-
-def first_sum_kernel(after_ref, terms_ref, got_ref, out_ref):
-    rows = got_ref.shape[0]
-    keep = terms_ref[pl.ds(pl.multiple_of(sum_bit(0) * rows, rows), rows), :]
-    out_ref[...] = added(keep, got_ref[...]).astype(out_ref.dtype)
-
-
-def second_sum_kernel(even_ref, odd_ref, value_ref, got_ref, out_ref):
-    rows = got_ref.shape[0]
-    keep = value_ref[pl.ds(pl.multiple_of(sum_bit(1) * rows, rows), rows), :]
-    out_ref[...] = added(keep, got_ref[...]).astype(out_ref.dtype)
-
-
-def pair_kernel(proj_ref, east_ref, pair_ref):
+    mesh_half[...] = (grad_own.astype(F32) + slope[:, :width]).reshape(mesh_half.shape)
+    mesh_give_ref[...] = (grad_oth.astype(F32) + slope[:, width:]).astype(mesh_give_ref.dtype)
+    copy = pltpu.make_async_copy(mesh_half, mesh_ref.at[:, r], mesh_sem)
+    copy.start()
+    copy.wait()
+
+
+def place_kernel(got_ref, filled_ref, mesh_ref, mesh_half, mesh_sem):
+    r = lax.axis_index("rep")
+    mesh_half[...] = got_ref[...].astype(F32).reshape(mesh_half.shape)
+    copy = pltpu.make_async_copy(mesh_half, mesh_ref.at[:, 1 - r], mesh_sem)
+    copy.start()
+    copy.wait()
+
+
+def put_halves(value, step, keep_ref, give_ref, hold):
+    rows = keep_ref.shape[0]
+    bit = sum_bit(step)
+    hold[...] = value
+    keep_ref[...] = hold[pl.ds(pl.multiple_of(bit * rows, rows), rows), :].astype(keep_ref.dtype)
+    give_ref[...] = hold[pl.ds(pl.multiple_of((1 - bit) * rows, rows), rows), :].astype(
+        give_ref.dtype
+    )
+
+
+def terms_kernel(keep_ref, got_ref, *refs):
+    outs, hold = refs[:4], refs[4]
+    rows = hold.shape[0]
+    for chain in range(2):
+        part = slice(chain * rows, (chain + 1) * rows)
+        put_halves(added(keep_ref[part, :], got_ref[part, :]), 0, *outs[2 * chain :][:2], hold)
+
+
+def halving_kernel(step, kept_ref, got_ref, *refs):
+    keep_ref, give_ref, hold = refs[-3:]
+    put_halves(added(kept_ref[...], got_ref[...]), step, keep_ref, give_ref, hold)
+
+
+def whole_kernel(kept_ref, got_ref, *refs):
+    refs[-1][...] = added(kept_ref[...], got_ref[...]).astype(refs[-1].dtype)
+
+
+def join_kernel(step, mine_ref, got_ref, *refs):
+    out_ref = refs[-1]
+    rows = mine_ref.shape[0]
+    bit = sum_bit(step)
+    out_ref[pl.ds(pl.multiple_of(bit * rows, rows), rows), :] = mine_ref[...].astype(out_ref.dtype)
+    out_ref[pl.ds(pl.multiple_of((1 - bit) * rows, rows), rows), :] = got_ref[...].astype(
+        out_ref.dtype
+    )
+
+
+def finish_outer_kernel(after_ref, mine_ref, other_ref, out_ref, out_other_ref, down_ref, grad_ref):
+    r = lax.axis_index("rep")
+    low = sum_bit(0) == 0
+    width = mine_ref.shape[1]
+    channels = out_ref.shape[0]
+    mine, other = mine_ref[...], other_ref[...]
+    terms = jnp.where(low, mine, other)[:, :channels]
+    down_ref[:, pl.ds(pl.multiple_of(r * width, width), width)] = dot(terms, out_ref[...])
+    down_ref[:, pl.ds(pl.multiple_of((1 - r) * width, width), width)] = dot(
+        terms, out_other_ref[...]
+    )
+    grad_ref[...] = jnp.where(low, other, mine)[:channels].astype(F32)
+
+
+def pair_kernel(after_ref, proj_ref, east_ref, pair_ref):
     pair_ref[0] = proj_ref[...]
     pair_ref[1] = east_ref[...]
-
-
-def finish_kernel(mine_ref, other_ref, out_ref, out_other_ref, up_ref, down_ref, grad_ref):
-    r = lax.axis_index("rep")
-    bit = sum_bit(0)
-    width = mine_ref.shape[1]
-    channels = out_ref.shape[0]
-
-    def place(low_ref, high_ref):
-        up_ref[...] = low_ref[...].astype(F32)
-        terms = high_ref[:width, :channels]
-        down_ref[:, pl.ds(pl.multiple_of(r * width, width), width)] = dot(terms, out_ref[...])
-        down_ref[:, pl.ds(pl.multiple_of((1 - r) * width, width), width)] = dot(
-            terms, out_other_ref[...]
-        )
-        grad_ref[...] = high_ref[width : width + channels, :].astype(F32)
-
-    @pl.when(bit == 0)
-    def _():
-        place(mine_ref, other_ref)
-
-    @pl.when(bit != 0)
-    def _():
-        place(other_ref, mine_ref)
 
 
 def pick_kernel(device_ref, slot_ref, pair_ref, even_ref, odd_ref, mine_ref, theirs_ref):
@@ -362,23 +379,6 @@
                 number = lambda a, b: (a * lon_count + b) * 2 + rep
                 pairs.append((number(lat, lon), number(*to)))
     return lax.ppermute(value, ("lat", "lon", "rep"), pairs)
-
-
-def given_half(value, step):
-    rows = value.shape[0] // 2
-    return lax.dynamic_slice_in_dim(value, (1 - sum_bit(step)) * rows, rows, 0)
-
-
-def summed(value):
-    for step in range(2, len(sum_orders()[0])):
-        value = (value.astype(F32) + sum_swap(value, step).astype(F32)).astype(BF16)
-    other = sum_swap(value, 1)
-    value = jnp.where(
-        sum_bit(1) == 0,
-        jnp.concatenate([value, other], axis=0),
-        jnp.concatenate([other, value], axis=0),
-    )
-    return value, sum_swap(value, 0)
 
 
 def per_device(
@@ -404,7 +404,6 @@
     to_east = lambda value: lax.ppermute(value, "lon", east_pairs)
 
     in_hbm = lambda value: pltpu.with_memory_space_constraint(value, pltpu.HBM)
-    in_vmem = lambda value: pltpu.with_memory_space_constraint(value, pltpu.VMEM)
     device, slot = route_device.reshape(blocks), route_slot
     grid_t, cot_t, out_t = grid_in.T, cotangent.T, w_out.T
     routes = (in_hbm(device), in_hbm(slot))
@@ -441,7 +440,7 @@
             ],
         )(device, slot, after, grid_t, interp_tiles, weight)
 
-    own_a, even_a, odd_a, hidden_a = encode(back_own, w_embed)
+    own_a, even_a, odd_a, hidden_a = encode(back_own, in_hbm(w_embed))
     even_in_a, odd_in_a = to_even(even_a), to_odd(odd_a)
     own_b, even_b, odd_b, hidden_b = encode(own_a, embed_other)
     even_in_b, odd_in_b = to_even(even_b), to_odd(odd_b)
@@ -479,62 +478,104 @@
     sums_specs = [first] * 3 + [whole((nodes, width))]
     weights = (w_up, up_other, w_down, down_other, out_t, out_other)
     back_spec = whole((nodes, padded))
-    proj, keep, give = call(
+    mesh_scratch = [pltpu.VMEM((slots, half, width), F32), pltpu.SemaphoreType.DMA]
+    proj, keep, give, mesh_give, mesh_filled = call(
         node_kernel, "node_update_and_gradients",
         sums_specs * 2 + [whole(embed_shape)] * 2
         + [back_spec, pl.BlockSpec((1, nodes, padded), lambda i: (0, 0, 0)), back_spec, back_spec]
         + [whole((channels, width))] * 2 + [whole(w.shape) for w in weights],
-        [whole((nodes, padded))] + [whole((2 * latent + nodes, width))] * 2,
-        [shape_of((nodes, padded), BF16), shape_of((2 * latent + nodes, width), F32),
-         shape_of((2 * latent + nodes, width), BF16)],
-        15 * nodes * latent * latent, 9e6, grid=(1,), exps=nodes * latent,
+        [whole((nodes, padded))] + [whole((2 * latent, width))] * 2
+        + [whole((nodes, width)), anywhere()],
+        [shape_of((nodes, padded), BF16), shape_of((2 * latent, width), F32),
+         shape_of((2 * latent, width), BF16), shape_of((nodes, width), BF16),
+         shape_of(embed_shape, F32)],
+        15 * nodes * latent * latent, 9e6, grid=(1,), exps=nodes * latent, scratch=mesh_scratch,
     )(
         own_a, even_in_a, odd_in_a, moved_a, own_b, even_in_b, odd_in_b, moved_b,
         mesh_embed.reshape(embed_shape), mesh_other.reshape(embed_shape),
         back_own, back_moved, back_even_in, back_odd_in, local, local_other, *weights,
     )
 
-    keep, give = in_vmem(keep), in_vmem(give)
     east = lax.ppermute(proj, "lon", west_pairs)
-    terms, grad_mesh = call(
-        terms_kernel, "sum_terms", [vmem()] * 2, [vmem()] * 2,
-        [shape_of((2 * latent, width), BF16), shape_of(embed_shape, F32)],
-        2 * latent * width, 2e6,
+    hold = lambda rows: [pltpu.VMEM((rows, width), F32)]
+    up_keep, up_give, outer_keep, outer_give = call(
+        terms_kernel, "sum_terms", [vmem()] * 2, [vmem()] * 4,
+        [shape_of((width, width), BF16)] * 4, 1, 1, scratch=hold(latent), weight=5e9,
     )(keep, swap_rep(give))
-    grad_mesh = grad_mesh.reshape(mesh_embed.shape)
-    pair = call(
-        pair_kernel, "pair_nodes", [vmem()] * 2, vmem(), shape_of((2, nodes, padded), BF16),
-        1, 1, weight=5e9,
-    )(proj, east)
-    halved = call(
-        first_sum_kernel, "first_sum", [anywhere()] + [vmem()] * 2, vmem(),
-        shape_of((latent, width), BF16), 2 * latent * width, 1e6,
-    )(pair, terms, sum_swap(given_half(terms, 0), 0))
-    pair_even, pair_odd = to_even(pair), to_odd(pair)
-    quarter = call(
-        second_sum_kernel, "second_sum", [anywhere()] * 2 + [vmem()] * 2, vmem(),
-        shape_of((width, width), BF16), 1, 1,
-    )(pair_even, pair_odd, halved, sum_swap(given_half(halved, 1), 1))
-    mine, theirs = summed(quarter)
+
+    count = len(sum_orders()[0])
+    chains = [[outer_keep, outer_give], [up_keep, up_give]]
+    latest = None
+
+    def step_call(kernel, name, chain, step, out_rows, scratch=()):
+        kept, given = chain[0], chain[-1]
+        after = [latest] if latest is not None else []
+        if chain is chains[1]:
+            after += [[pair], [pair_even, pair_odd]][step] if step < 2 and len(chain) == 2 else []
+        made = call(
+            kernel, name, [vmem()] * 2 + [anywhere()] * len(after), [vmem()] * len(out_rows),
+            [shape_of((rows, width), BF16) for rows in out_rows], 1, 1, scratch=scratch,
+        )(kept, sum_swap(given, step), *after)
+        return list(made)
+
+    for step in range(count):
+        for c in range(2):
+            rows = chains[c][0].shape[0]
+            if step == 0 and c == 1:
+                pair = call(
+                    pair_kernel, "pair_nodes", [anywhere()] + [vmem()] * 2, vmem(), shape_of((2, nodes, padded), BF16),
+                    1, 1,
+                )(up_give, proj, east)
+                pair_even, pair_odd = to_even(pair), to_odd(pair)
+            if step == 0:
+                chains[c] = step_call(
+                    functools.partial(halving_kernel, 1), "halve", chains[c], step,
+                    [rows // 2] * 2, hold(rows),
+                )
+            else:
+                chains[c] = step_call(whole_kernel, "add_whole", chains[c], step, [rows])
+            latest = chains[c][-1]
+    for c in range(2):
+        rows = chains[c][0].shape[0]
+        chains[c] = step_call(
+            functools.partial(join_kernel, 1), "join", chains[c], 1, [2 * rows]
+        )
+        latest = chains[c][-1]
+    (outer_mine,), (up_mine,) = chains
+    outer_theirs, up_theirs = sum_swap(outer_mine, 0), sum_swap(up_mine, 0)
+
+    grad_mesh = pl.pallas_call(
+        place_kernel,
+        in_specs=[vmem(), anywhere()],
+        out_specs=anywhere(),
+        out_shape=shape_of(embed_shape, F32),
+        scratch_shapes=mesh_scratch,
+        input_output_aliases={1: 0},
+        compiler_params=pltpu.CompilerParams(vmem_limit_bytes=VMEM_BYTES),
+        cost_estimate=pl.CostEstimate(flops=1, bytes_accessed=1, transcendentals=0),
+        name="place_mesh",
+    )(swap_rep(mesh_give), mesh_filled).reshape(mesh_embed.shape)
 
     table_shape = (2 * slots, half, padded)
     mine_picked, theirs_picked = call(
         pick_kernel, "pick_nodes", [smem()] * 2 + [vmem()] * 3, [vmem()] * 2,
         [shape_of((blocks // 2, half, padded), BF16)] * 2, 1, 1, weight=5e9,
     )(device, slot, *[table.reshape(table_shape) for table in (pair, pair_even, pair_odd)])
-    grid_out = call(
+    grid_out_t = call(
         decode_kernel, "decode", [vmem()] * 4, vmem(),
         shape_of((channels, my_rows), BF16), 2 * my_rows * tile_rows * padded, 4e6,
         scratch=[pltpu.VMEM((blocks // 2, tile_rows, padded), BF16)],
-    )(interp_tiles, base, mine_picked, swap_rep(theirs_picked)).T
-
-    grad_up, grad_down, grad_out = call(
-        finish_kernel, "finish", [vmem()] * 4, [vmem()] * 3,
-        [shape_of((latent, width), F32), shape_of((width, latent), F32),
-         shape_of((channels, width), F32)],
-        2 * width * latent * channels, 1e6,
-    )(mine, theirs, out_t, out_other)
-    return (grid_out, grad_out.T, grad_up, grad_down, grad_mesh)
+    )(interp_tiles, base, mine_picked, swap_rep(theirs_picked))
+
+    grad_down, grad_out = call(
+        finish_outer_kernel, "finish_outer", [anywhere()] + [vmem()] * 4, [vmem()] * 2,
+        [shape_of((width, latent), F32), shape_of((channels, width), F32)], 1, 1,
+    )(grid_out_t, outer_mine, outer_theirs, out_t, out_other)
+    grad_up = call(
+        functools.partial(join_kernel, 0), "finish_up", [vmem()] * 2, vmem(),
+        shape_of((latent, width), F32), 1, 1,
+    )(up_mine, up_theirs)
+    return (grid_out_t.T, grad_out.T, grad_up, grad_down, grad_mesh)
 
 
 def solution(mesh):

time: 81.2 us -> 80.2 us (0.988)
  starting transfers between devices: 31.5 us -> 37.9 us
  waiting for transfers between devices: 28.2 us -> 22.1 us
  Pallas kernels: 18.4 us -> 17.3 us
    ppermute x5 -> x10, waiting for transfers between devices: 15.8 us -> 9.07 us  [sum_swap(): return lax.ppermute(value, ('lat', 'lon', 'rep'), pairs)]
    ppermute x5 -> x10, starting transfers between devices: 10.1 us -> 15.4 us  [sum_swap(): return lax.ppermute(value, ('lat', 'lon', 'rep'), pairs)]
    ppermute x1, waiting for transfers between devices: 0.05 us -> 3.82 us  [per_device(): east = lax.ppermute(proj, 'lon', west_pairs)]
    ppermute x15 -> x16, waiting for transfers between devices: 12.4 us -> 9.2 us  [along(): return lambda value: lax.ppermute(value, axis, pairs)]
    pallas_call x5 -> x13, Pallas kernels: 4.35 us -> 3.01 us  [the longest x1 1.03 us: per_device(): call(finish_outer_kernel, 'finish_outer', [anywhere()] + [vmem()] * 4, [v...]
    ppermute x15 -> x16, starting transfers between devices: 16.2 us -> 17.2 us  [along(): return lambda value: lax.ppermute(value, axis, pairs)]
    unnamed x20 -> x22, local copies, waits for them, and re-layouts: 0.93 us -> 1.72 us
  transfers between devices with their start and end apart: 24 -> 30, of which waited for: 11 -> 13; matrix products, arithmetic and copies ran while one was open for 1% -> 0% of each run, Pallas kernels for 13% -> 12%
where the time goes in v8:
time: 80.2 us; the launch traced here: 79.9 us
  starting transfers between devices  37.9 us (47%)
  waiting for transfers between devices  22.1 us (28%)
  Pallas kernels  17.3 us (22%)
  local copies, waits for them, and re-layouts  1.72 us (2%)
  between operations  0.91 us (1%)
    ppermute x16, starting transfers between devices, along(): return lambda value: lax.ppermute(value, axis, pairs)  17.2 us
    ppermute x10, starting transfers between devices, sum_swap(): return lax.ppermute(value, ('lat', 'lon', 'rep'), pairs)  15.4 us
    ppermute x16, waiting for transfers between devices, along(): return lambda value: lax.ppermute(value, axis, pairs)  9.2 us
    ppermute x10, waiting for transfers between devices, sum_swap(): return lax.ppermute(value, ('lat', 'lon', 'rep'), pairs)  9.07 us
    pallas_call x2, Pallas kernels, encode(): call(encode_kernel, 'encode', [smem(), smem(), anywhere()] + [vmem()] * 3...  4.81 us
    ppermute x3, starting transfers between devices, per_device(): to_east = lambda value: lax.ppermute(value, 'lon', east_pairs)  4.21 us
    ppermute x1, waiting for transfers between devices, per_device(): east = lax.ppermute(proj, 'lon', west_pairs)  3.82 us
    pallas_call x1, Pallas kernels, per_device(): call(back_kernel, 'back_messages', [smem(), smem(), anywhere(), anywhere(...  3.49 us
  transfers between devices with their start and end apart: 30, of which 13 were waited for; matrix products, arithmetic and copies ran while one was open for 0% of the time, Pallas kernels for 12%

profile of v8, /device:TPU:0, one launch (start us, length us, event | category | flops | bytes accessed | tf_op | source)
XLA Modules:
  0.0 79.9 jit_solution(1520119006456728864)
XLA Ops:
  0.7 3.5 %back_messages.1 = (bf16[256,256]{1,0:T(8,128)(2,1)S(1)}, bf16[3,256,256]{2,1,0:T(8,128)(2,1)S(1)}, bf16[2,256,256]{2,1,0:T(8,128)(2,1)S(1)}) custom-call(s32[16]{0:T(128)} %bitcast.26, s32[16]{0:T(128)} %slot_ref.7, bf16[16,128,128]{2,1,0:T(8,128)(2,1)} %tiles_ref.7, bf16[227,2048]{1,0:T(8,128)(2,1)} %bitcast.14), custom_call_target="tpu_custom_call" | custom-call | flops 1 | bytes 1 | tf_op jit(solution)/shard_map/back_messages/pallas_call | solution.py:414
  4.1 3.0 %collective-permute-start.4 = (bf16[3,256,256]{2,1,0:T(8,128)(2,1)S(1)}, bf16[3,256,256]{2,1,0:T(8,128)(2,1)S(1)}, u32[]{:S(2)}, u32[]{:S(2)}) collective-permute-start(bf16[3,256,256]{2,1,0:T(8,128)(2,1)S(1)} %get-tuple-element.45), channel_id=1, source_target_pairs={{0,2},{2,0},{1,3},{3,1},{4,6},{6,4},{5,7},{7,5},{8,10},{10,8},{9,1... | collective-permute-start | bytes 1179656 | tf_op jit(solution)/shard_map/ppermute | solution.py:404
  7.8 2.6 %encode.2 = (bf16[2,256,256]{2,1,0:T(8,128)(2,1)S(1)}, bf16[2,256,256]{2,1,0:T(8,128)(2,1)S(1)}, bf16[2,256,256]{2,1,0:T(8,128)(2,1)S(1)}, bf16[1024,256]{1,0:T(8,128)(2,1)S(1)}) custom-call(s32[16]{0:T(128)S(1)} %bitcast.27, s32[16]{0:T(128)S(1)} %copy-done.9, bf16[256,256]{1,0:T(8,128)(2,1)S(1)} %get-tuple-element.38.after_ref.back_ref, ...), custom_call_target="tpu_custom_call" | custom-call | flops 1 | bytes 1 | tf_op jit(solution)/shard_map/encode/pallas_call | solution.py:432
  10.4 1.6 %collective-permute-start.2 = (bf16[2,256,256]{2,1,0:T(8,128)(2,1)S(1)}, bf16[2,256,256]{2,1,0:T(8,128)(2,1)S(1)}, u32[]{:S(2)}, u32[]{:S(2)}) collective-permute-start(bf16[2,256,256]{2,1,0:T(8,128)(2,1)S(1)} %get-tuple-element.43), channel_id=1, source_target_pairs={{0,4},{4,0},{8,12},{12,8},{1,5},{5,1},{9,13},{13,9},{2,6},{6,2},{1... | collective-permute-start | bytes 786440 | tf_op jit(solution)/shard_map/ppermute | solution.py:346
  13.4 2.2 %encode.3 = (bf16[2,256,256]{2,1,0:T(8,128)(2,1)S(1)}, bf16[2,256,256]{2,1,0:T(8,128)(2,1)S(1)}, bf16[2,256,256]{2,1,0:T(8,128)(2,1)S(1)}, bf16[1024,256]{1,0:T(8,128)(2,1)S(1)}) custom-call(s32[16]{0:T(128)S(1)} %bitcast.28, s32[16]{0:T(128)S(1)} %copy-done.9, bf16[2,256,256]{2,1,0:T(8,128)(2,1)S(1)} %get-tuple-element.40.after_ref.refs_1_.own_a, ...), custom_call_target="tpu_custom_call" | custom-call | flops 1 | bytes 1 | tf_op jit(solution)/shard_map/encode/pallas_call | solution.py:432
  15.6 3.8 %collective-permute-start.6 = (bf16[2,256,256]{2,1,0:T(8,128)(2,1)S(1)}, bf16[2,256,256]{2,1,0:T(8,128)(2,1)S(1)}, u32[]{:S(2)}, u32[]{:S(2)}) collective-permute-start(bf16[2,256,256]{2,1,0:T(8,128)(2,1)S(1)} %get-tuple-element.47), channel_id=1, source_target_pairs={{0,4},{4,0},{8,12},{12,8},{1,5},{5,1},{9,13},{13,9},{2,6},{6,2},{1... | collective-permute-start | bytes 786440 | tf_op jit(solution)/shard_map/ppermute | solution.py:346
  21.2 4.9 %collective-permute-done.6.refs_2_.even_b = bf16[2,256,256]{2,1,0:T(8,128)(2,1)S(1)} collective-permute-done((bf16[2,256,256]{2,1,0:T(8,128)(2,1)S(1)}, bf16[2,256,256]{2,1,0:T(8,128)(2,1)S(1)}, u32[]{:S(2)}, u32[]{:S(2)}) %collective-permute-start.6) | collective-permute-done | bytes 262176 | tf_op jit(solution)/shard_map/ppermute | solution.py:346
  27.8 3.4 %collective-permute-start.10 = (bf16[256,256]{1,0:T(8,128)(2,1)S(1)}, bf16[256,256]{1,0:T(8,128)(2,1)S(1)}, u32[]{:S(2)}, u32[]{:S(2)}) collective-permute-start(bf16[256,256]{1,0:T(8,128)(2,1)S(1)} %get-tuple-element.50), channel_id=1, source_target_pairs={{0,4},{4,0},{8,12},{12,8},{1,5},{5,1},{9,13},{13,9},{2,6},{6,2},{1... | collective-permute-start | bytes 393224 | tf_op jit(solution)/shard_map/ppermute | solution.py:346
  32.7 2.4 %collective-permute-done.10.back_even_ref = bf16[256,256]{1,0:T(8,128)(2,1)S(1)} collective-permute-done((bf16[256,256]{1,0:T(8,128)(2,1)S(1)}, bf16[256,256]{1,0:T(8,128)(2,1)S(1)}, u32[]{:S(2)}, u32[]{:S(2)}) %collective-permute-start.10) | collective-permute-done | bytes 131104 | tf_op jit(solution)/shard_map/ppermute | solution.py:346
  35.1 2.8 %node_update_and_gradients.1 = (bf16[256,256]{1,0:T(8,128)(2,1)S(1)}, f32[1024,256]{1,0:T(8,128)S(1)}, bf16[1024,256]{1,0:T(8,128)(2,1)S(1)}, bf16[256,256]{1,0:T(8,128)(2,1)S(1)}, f32[4,2,64,256]{3,2,1,0:T(8,128)}) custom-call(bf16[2,256,256]{2,1,0:T(8,128)(2,1)S(1)} %get-tuple-element.40.after_ref.refs_1_.own_a, ...), custom_call_target="tpu_custom_call" | custom-call | flops 1 | bytes 1 | tf_op jit(solution)/shard_map/node_update_and_gradients/pallas_call | solution.py:482
  40.1 3.8 %collective-permute-done.15.east_ref = bf16[256,256]{1,0:T(8,128)(2,1)S(1)} collective-permute-done((bf16[256,256]{1,0:T(8,128)(2,1)S(1)}, bf16[256,256]{1,0:T(8,128)(2,1)S(1)}, u32[]{:S(2)}, u32[]{:S(2)}) %collective-permute-start.15) | collective-permute-done | bytes 131104 | tf_op jit(solution)/shard_map/ppermute | solution.py:499
  44.0 3.7 %collective-permute-start.16 = (bf16[2,256,256]{2,1,0:T(8,128)(2,1)S(1)}, bf16[2,256,256]{2,1,0:T(8,128)(2,1)S(1)}, u32[]{:S(2)}, u32[]{:S(2)}) collective-permute-start(bf16[2,256,256]{2,1,0:T(8,128)(2,1)S(1)} %pair_nodes.1.refs_1_), channel_id=1, source_target_pairs={{0,4},{4,0},{8,12},{12,8},{1,5},{5,1},{9,13},{13,9},{2,6},{6,2},{1... | collective-permute-start | bytes 786440 | tf_op jit(solution)/shard_map/ppermute | solution.py:346
  48.3 1.1 %collective-permute-start.19 = (bf16[256,256]{1,0:T(8,128)(2,1)S(1)}, bf16[256,256]{1,0:T(8,128)(2,1)S(1)}, u32[]{:S(2)}, u32[]{:S(2)}) collective-permute-start(bf16[256,256]{1,0:T(8,128)(2,1)S(1)} %get-tuple-element.61), channel_id=1, source_target_pairs={{0,2},{1,5},{2,0},{3,7},{4,6},{5,1},{6,4},{7,3},{8,10},{9,13},{10,... | collective-permute-start | bytes 393224 | tf_op jit(solution)/shard_map/ppermute | solution.py:381
  50.4 2.9 %collective-permute-done.19.got_ref = bf16[256,256]{1,0:T(8,128)(2,1)S(1)} collective-permute-done((bf16[256,256]{1,0:T(8,128)(2,1)S(1)}, bf16[256,256]{1,0:T(8,128)(2,1)S(1)}, u32[]{:S(2)}, u32[]{:S(2)}) %collective-permute-start.19) | collective-permute-done | bytes 131104 | tf_op jit(solution)/shard_map/ppermute | solution.py:381
  53.4 2.8 %collective-permute-start.20 = (bf16[128,256]{1,0:T(8,128)(2,1)S(1)}, bf16[128,256]{1,0:T(8,128)(2,1)S(1)}, u32[]{:S(2)}, u32[]{:S(2)}) collective-permute-start(bf16[128,256]{1,0:T(8,128)(2,1)S(1)} %get-tuple-element.63.refs_0_), channel_id=1, source_target_pairs={{0,4},{1,9},{2,6},{3,11},{4,0},{5,13},{6,2},{7,15},{8,12},{9,1},{1... | collective-permute-start | bytes 196616 | tf_op jit(solution)/shard_map/ppermute | solution.py:381
  56.3 1.3 %collective-permute-start.23 = (bf16[128,256]{1,0:T(8,128)(2,1)S(1)}, bf16[128,256]{1,0:T(8,128)(2,1)S(1)}, u32[]{:S(2)}, u32[]{:S(2)}) collective-permute-start(bf16[128,256]{1,0:T(8,128)(2,1)S(1)} %get-tuple-element.65.refs_0_), channel_id=1, source_target_pairs={{0,4},{1,9},{2,6},{3,11},{4,0},{5,13},{6,2},{7,15},{8,12},{9,1},{1... | collective-permute-start | bytes 196616 | tf_op jit(solution)/shard_map/ppermute | solution.py:381
  58.5 2.0 %collective-permute-start.22 = (bf16[128,256]{1,0:T(8,128)(2,1)S(1)}, bf16[128,256]{1,0:T(8,128)(2,1)S(1)}, u32[]{:S(2)}, u32[]{:S(2)}) collective-permute-start(bf16[128,256]{1,0:T(8,128)(2,1)S(1)} %add_whole.4.refs_0_.kept_ref), channel_id=1, source_target_pairs={{0,8},{1,3},{2,10},{3,1},{4,12},{5,7},{6,14},{7,5},{8,0},{9,11},{1... | collective-permute-start | bytes 196616 | tf_op jit(solution)/shard_map/ppermute | solution.py:381
  60.7 1.8 %collective-permute-start.25 = (bf16[128,256]{1,0:T(8,128)(2,1)S(1)}, bf16[128,256]{1,0:T(8,128)(2,1)S(1)}, u32[]{:S(2)}, u32[]{:S(2)}) collective-permute-start(bf16[128,256]{1,0:T(8,128)(2,1)S(1)} %add_whole.5.refs_0_.kept_ref), channel_id=1, source_target_pairs={{0,8},{1,3},{2,10},{3,1},{4,12},{5,7},{6,14},{7,5},{8,0},{9,11},{1... | collective-permute-start | bytes 196616 | tf_op jit(solution)/shard_map/ppermute | solution.py:381
  64.6 1.3 %collective-permute-start.24 = (bf16[128,256]{1,0:T(8,128)(2,1)S(1)}, bf16[128,256]{1,0:T(8,128)(2,1)S(1)}, u32[]{:S(2)}, u32[]{:S(2)}) collective-permute-start(bf16[128,256]{1,0:T(8,128)(2,1)S(1)} %add_whole.6.refs_0_.mine_ref), channel_id=1, source_target_pairs={{0,4},{1,9},{2,6},{3,11},{4,0},{5,13},{6,2},{7,15},{8,12},{9,1},{1... | collective-permute-start | bytes 196616 | tf_op jit(solution)/shard_map/ppermute | solution.py:381
  65.9 1.9 %collective-permute-start.27 = (bf16[128,256]{1,0:T(8,128)(2,1)S(1)}, bf16[128,256]{1,0:T(8,128)(2,1)S(1)}, u32[]{:S(2)}, u32[]{:S(2)}) collective-permute-start(bf16[128,256]{1,0:T(8,128)(2,1)S(1)} %add_whole.7.refs_0_.mine_ref), channel_id=1, source_target_pairs={{0,4},{1,9},{2,6},{3,11},{4,0},{5,13},{6,2},{7,15},{8,12},{9,1},{1... | collective-permute-start | bytes 196616 | tf_op jit(solution)/shard_map/ppermute | solution.py:381
  67.8 1.5 %collective-permute-done.24.got_ref = bf16[128,256]{1,0:T(8,128)(2,1)S(1)} collective-permute-done((bf16[128,256]{1,0:T(8,128)(2,1)S(1)}, bf16[128,256]{1,0:T(8,128)(2,1)S(1)}, u32[]{:S(2)}, u32[]{:S(2)}) %collective-permute-start.24) | collective-permute-done | bytes 65568 | tf_op jit(solution)/shard_map/ppermute | solution.py:381
  69.4 1.4 %collective-permute-done.27.got_ref = bf16[128,256]{1,0:T(8,128)(2,1)S(1)} collective-permute-done((bf16[128,256]{1,0:T(8,128)(2,1)S(1)}, bf16[128,256]{1,0:T(8,128)(2,1)S(1)}, u32[]{:S(2)}, u32[]{:S(2)}) %collective-permute-start.27) | collective-permute-done | bytes 65568 | tf_op jit(solution)/shard_map/ppermute | solution.py:381
  73.6 2.2 %collective-permute-done.28.got_ref = bf16[256,256]{1,0:T(8,128)(2,1)S(1)} collective-permute-done((bf16[256,256]{1,0:T(8,128)(2,1)S(1)}, bf16[256,256]{1,0:T(8,128)(2,1)S(1)}, u32[]{:S(2)}, u32[]{:S(2)}) %collective-permute-start.28) | collective-permute-done | bytes 131104 | tf_op jit(solution)/shard_map/ppermute | solution.py:381
  76.7 1.2 %decode.1.after_ref = bf16[227,1024]{1,0:T(8,128)(2,1)} custom-call(bf16[16,128,128]{2,1,0:T(8,128)(2,1)S(1)} %copy-done, f32[227,1024]{1,0:T(8,128)S(1)} %get-tuple-element.42.base_ref, bf16[8,64,256]{2,1,0:T(8,128)(2,1)S(1)} %get-tuple-element.58.mine_ref, bf16[8,64,256]{2,1,0:T(8,128)(2,1)S(1)} %collective-permute-done.18.got_ref), custom_call_target="tpu_custom_call" | custom-call | flops 1 | bytes 1 | tf_op jit(solution)/shard_map/decode/pallas_call | solution.py:564
  (81 shorter events, 19.6 us)
Async XLA Ops:
  4.1 16.2 %collective-permute-start.4 = (bf16[3,256,256]{2,1,0:T(8,128)(2,1)S(1)}, bf16[3,256,256]{2,1,0:T(8,128)(2,1)S(1)}, u32[]{:S(2)}, u32[]{:S(2)}) collective-permute-start(bf16[3,256,256]{2,1,0:T(8,128)(2,1)S(1)} %get-tuple-element.45), channel_id=1, source_target_pairs={{0,2},{2,0},{1,3},{3,1},{4,6},{6,4},{5,7},{7,5},{8,10},{10,8},{9,1... | collective-permute-start | bytes 1179656 | tf_op jit(solution)/shard_map/ppermute | solution.py:404
  10.4 9.8 %collective-permute-start.2 = (bf16[2,256,256]{2,1,0:T(8,128)(2,1)S(1)}, bf16[2,256,256]{2,1,0:T(8,128)(2,1)S(1)}, u32[]{:S(2)}, u32[]{:S(2)}) collective-permute-start(bf16[2,256,256]{2,1,0:T(8,128)(2,1)S(1)} %get-tuple-element.43), channel_id=1, source_target_pairs={{0,4},{4,0},{8,12},{12,8},{1,5},{5,1},{9,13},{13,9},{2,6},{6,2},{1... | collective-permute-start | bytes 786440 | tf_op jit(solution)/shard_map/ppermute | solution.py:346
  12.1 8.3 %collective-permute-start.3 = (bf16[2,256,256]{2,1,0:T(8,128)(2,1)S(1)}, bf16[2,256,256]{2,1,0:T(8,128)(2,1)S(1)}, u32[]{:S(2)}, u32[]{:S(2)}) collective-permute-start(bf16[2,256,256]{2,1,0:T(8,128)(2,1)S(1)} %get-tuple-element.44), channel_id=1, source_target_pairs={{0,0},{4,8},{8,4},{12,12},{1,1},{5,9},{9,5},{13,13},{2,2},{6,10},{... | collective-permute-start | bytes 786440 | tf_op jit(solution)/shard_map/ppermute | solution.py:346
  15.6 10.5 %collective-permute-start.6 = (bf16[2,256,256]{2,1,0:T(8,128)(2,1)S(1)}, bf16[2,256,256]{2,1,0:T(8,128)(2,1)S(1)}, u32[]{:S(2)}, u32[]{:S(2)}) collective-permute-start(bf16[2,256,256]{2,1,0:T(8,128)(2,1)S(1)} %get-tuple-element.47), channel_id=1, source_target_pairs={{0,4},{4,0},{8,12},{12,8},{1,5},{5,1},{9,13},{13,9},{2,6},{6,2},{1... | collective-permute-start | bytes 786440 | tf_op jit(solution)/shard_map/ppermute | solution.py:346
  19.4 6.7 %collective-permute-start.7 = (bf16[2,256,256]{2,1,0:T(8,128)(2,1)S(1)}, bf16[2,256,256]{2,1,0:T(8,128)(2,1)S(1)}, u32[]{:S(2)}, u32[]{:S(2)}) collective-permute-start(bf16[2,256,256]{2,1,0:T(8,128)(2,1)S(1)} %get-tuple-element.48), channel_id=1, source_target_pairs={{0,0},{4,8},{8,4},{12,12},{1,1},{5,9},{9,5},{13,13},{2,2},{6,10},{... | collective-permute-start | bytes 786440 | tf_op jit(solution)/shard_map/ppermute | solution.py:346
  20.3 11.0 %collective-permute-start.9 = (bf16[512,256]{1,0:T(8,128)(2,1)S(1)}, bf16[512,256]{1,0:T(8,128)(2,1)S(1)}, u32[]{:S(2)}, u32[]{:S(2)}) collective-permute-start(bf16[512,256]{1,0:T(8,128)(2,1)S(1)} %copy-done.5), channel_id=1, source_target_pairs={{0,1},{1,0},{2,3},{3,2},{4,5},{5,4},{6,7},{7,6},{8,9},{9,8},{10,11... | collective-permute-start | bytes 786440 | tf_op jit(solution)/shard_map/ppermute | solution.py:346
  20.4 6.2 %collective-permute-start.5 = (bf16[256,256]{1,0:T(8,128)(2,1)S(1)}, bf16[256,256]{1,0:T(8,128)(2,1)S(1)}, u32[]{:S(2)}, u32[]{:S(2)}) collective-permute-start(bf16[256,256]{1,0:T(8,128)(2,1)S(1)} %add_east.2), channel_id=1, source_target_pairs={{0,2},{2,0},{1,3},{3,1},{4,6},{6,4},{5,7},{7,5},{8,10},{10,8},{9,1... | collective-permute-start | bytes 393224 | tf_op jit(solution)/shard_map/ppermute | solution.py:404
  21.0 11.7 %collective-permute-start.12 = (bf16[512,256]{1,0:T(8,128)(2,1)S(1)}, bf16[512,256]{1,0:T(8,128)(2,1)S(1)}, u32[]{:S(2)}, u32[]{:S(2)}) collective-permute-start(bf16[512,256]{1,0:T(8,128)(2,1)S(1)} %copy-done.6), channel_id=1, source_target_pairs={{0,1},{1,0},{2,3},{3,2},{4,5},{5,4},{6,7},{7,6},{8,9},{9,8},{10,11... | collective-permute-start | bytes 786440 | tf_op jit(solution)/shard_map/ppermute | solution.py:346
  26.1 6.6 %collective-permute-start.13 = (bf16[256,512]{1,0:T(8,128)(2,1)S(1)}, bf16[256,512]{1,0:T(8,128)(2,1)S(1)}, u32[]{:S(2)}, u32[]{:S(2)}) collective-permute-start(bf16[256,512]{1,0:T(8,128)(2,1)S(1)} %copy-done.7), channel_id=1, source_target_pairs={{0,1},{1,0},{2,3},{3,2},{4,5},{5,4},{6,7},{7,6},{8,9},{9,8},{10,11... | collective-permute-start | bytes 786440 | tf_op jit(solution)/shard_map/ppermute | solution.py:346
  26.7 6.0 %collective-permute-start.8 = (bf16[256,256]{1,0:T(8,128)(2,1)S(1)}, bf16[256,256]{1,0:T(8,128)(2,1)S(1)}, u32[]{:S(2)}, u32[]{:S(2)}) collective-permute-start(bf16[256,256]{1,0:T(8,128)(2,1)S(1)} %add_east.3.after_ref), channel_id=1, source_target_pairs={{0,2},{2,0},{1,3},{3,1},{4,6},{6,4},{5,7},{7,5},{8,10},{10,8},{9,1... | collective-permute-start | bytes 393224 | tf_op jit(solution)/shard_map/ppermute | solution.py:404
  27.8 7.2 %collective-permute-start.10 = (bf16[256,256]{1,0:T(8,128)(2,1)S(1)}, bf16[256,256]{1,0:T(8,128)(2,1)S(1)}, u32[]{:S(2)}, u32[]{:S(2)}) collective-permute-start(bf16[256,256]{1,0:T(8,128)(2,1)S(1)} %get-tuple-element.50), channel_id=1, source_target_pairs={{0,4},{4,0},{8,12},{12,8},{1,5},{5,1},{9,13},{13,9},{2,6},{6,2},{1... | collective-permute-start | bytes 393224 | tf_op jit(solution)/shard_map/ppermute | solution.py:346
  38.0 5.9 %collective-permute-start.15 = (bf16[256,256]{1,0:T(8,128)(2,1)S(1)}, bf16[256,256]{1,0:T(8,128)(2,1)S(1)}, u32[]{:S(2)}, u32[]{:S(2)}) collective-permute-start(bf16[256,256]{1,0:T(8,128)(2,1)S(1)} %get-tuple-element.57.proj_ref), channel_id=1, source_target_pairs={{2,0},{0,2},{3,1},{1,3},{6,4},{4,6},{7,5},{5,7},{10,8},{8,10},{11,... | collective-permute-start | bytes 393224 | tf_op jit(solution)/shard_map/ppermute | solution.py:499
  44.0 16.7 %collective-permute-start.16 = (bf16[2,256,256]{2,1,0:T(8,128)(2,1)S(1)}, bf16[2,256,256]{2,1,0:T(8,128)(2,1)S(1)}, u32[]{:S(2)}, u32[]{:S(2)}) collective-permute-start(bf16[2,256,256]{2,1,0:T(8,128)(2,1)S(1)} %pair_nodes.1.refs_1_), channel_id=1, source_target_pairs={{0,4},{4,0},{8,12},{12,8},{1,5},{5,1},{9,13},{13,9},{2,6},{6,2},{1... | collective-permute-start | bytes 786440 | tf_op jit(solution)/shard_map/ppermute | solution.py:346
  47.7 13.0 %collective-permute-start.17 = (bf16[2,256,256]{2,1,0:T(8,128)(2,1)S(1)}, bf16[2,256,256]{2,1,0:T(8,128)(2,1)S(1)}, u32[]{:S(2)}, u32[]{:S(2)}) collective-permute-start(bf16[2,256,256]{2,1,0:T(8,128)(2,1)S(1)} %pair_nodes.1.refs_1_), channel_id=1, source_target_pairs={{0,0},{4,8},{8,4},{12,12},{1,1},{5,9},{9,5},{13,13},{2,2},{6,10},{... | collective-permute-start | bytes 786440 | tf_op jit(solution)/shard_map/ppermute | solution.py:346
  48.3 5.0 %collective-permute-start.19 = (bf16[256,256]{1,0:T(8,128)(2,1)S(1)}, bf16[256,256]{1,0:T(8,128)(2,1)S(1)}, u32[]{:S(2)}, u32[]{:S(2)}) collective-permute-start(bf16[256,256]{1,0:T(8,128)(2,1)S(1)} %get-tuple-element.61), channel_id=1, source_target_pairs={{0,2},{1,5},{2,0},{3,7},{4,6},{5,1},{6,4},{7,3},{8,10},{9,13},{10,... | collective-permute-start | bytes 393224 | tf_op jit(solution)/shard_map/ppermute | solution.py:381
  49.5 6.8 %collective-permute-start.21 = (bf16[256,256]{1,0:T(8,128)(2,1)S(1)}, bf16[256,256]{1,0:T(8,128)(2,1)S(1)}, u32[]{:S(2)}, u32[]{:S(2)}) collective-permute-start(bf16[256,256]{1,0:T(8,128)(2,1)S(1)} %get-tuple-element.56.after_ref), channel_id=1, source_target_pairs={{0,2},{1,5},{2,0},{3,7},{4,6},{5,1},{6,4},{7,3},{8,10},{9,13},{10,... | collective-permute-start | bytes 393224 | tf_op jit(solution)/shard_map/ppermute | solution.py:381
  53.4 5.1 %collective-permute-start.20 = (bf16[128,256]{1,0:T(8,128)(2,1)S(1)}, bf16[128,256]{1,0:T(8,128)(2,1)S(1)}, u32[]{:S(2)}, u32[]{:S(2)}) collective-permute-start(bf16[128,256]{1,0:T(8,128)(2,1)S(1)} %get-tuple-element.63.refs_0_), channel_id=1, source_target_pairs={{0,4},{1,9},{2,6},{3,11},{4,0},{5,13},{6,2},{7,15},{8,12},{9,1},{1... | collective-permute-start | bytes 196616 | tf_op jit(solution)/shard_map/ppermute | solution.py:381
  58.5 6.1 %collective-permute-start.22 = (bf16[128,256]{1,0:T(8,128)(2,1)S(1)}, bf16[128,256]{1,0:T(8,128)(2,1)S(1)}, u32[]{:S(2)}, u32[]{:S(2)}) collective-permute-start(bf16[128,256]{1,0:T(8,128)(2,1)S(1)} %add_whole.4.refs_0_.kept_ref), channel_id=1, source_target_pairs={{0,8},{1,3},{2,10},{3,1},{4,12},{5,7},{6,14},{7,5},{8,0},{9,11},{1... | collective-permute-start | bytes 196616 | tf_op jit(solution)/shard_map/ppermute | solution.py:381
  60.7 5.2 %collective-permute-start.25 = (bf16[128,256]{1,0:T(8,128)(2,1)S(1)}, bf16[128,256]{1,0:T(8,128)(2,1)S(1)}, u32[]{:S(2)}, u32[]{:S(2)}) collective-permute-start(bf16[128,256]{1,0:T(8,128)(2,1)S(1)} %add_whole.5.refs_0_.kept_ref), channel_id=1, source_target_pairs={{0,8},{1,3},{2,10},{3,1},{4,12},{5,7},{6,14},{7,5},{8,0},{9,11},{1... | collective-permute-start | bytes 196616 | tf_op jit(solution)/shard_map/ppermute | solution.py:381
  63.6 13.1 %collective-permute-start.18 = (bf16[8,64,256]{2,1,0:T(8,128)(2,1)S(1)}, bf16[8,64,256]{2,1,0:T(8,128)(2,1)S(1)}, u32[]{:S(2)}, u32[]{:S(2)}) collective-permute-start(bf16[8,64,256]{2,1,0:T(8,128)(2,1)S(1)} %get-tuple-element.59), channel_id=1, source_target_pairs={{0,1},{1,0},{2,3},{3,2},{4,5},{5,4},{6,7},{7,6},{8,9},{9,8},{10,11... | collective-permute-start | bytes 786440 | tf_op jit(solution)/shard_map/ppermute | solution.py:346
  65.9 4.8 %collective-permute-start.27 = (bf16[128,256]{1,0:T(8,128)(2,1)S(1)}, bf16[128,256]{1,0:T(8,128)(2,1)S(1)}, u32[]{:S(2)}, u32[]{:S(2)}) collective-permute-start(bf16[128,256]{1,0:T(8,128)(2,1)S(1)} %add_whole.7.refs_0_.mine_ref), channel_id=1, source_target_pairs={{0,4},{1,9},{2,6},{3,11},{4,0},{5,13},{6,2},{7,15},{8,12},{9,1},{1... | collective-permute-start | bytes 196616 | tf_op jit(solution)/shard_map/ppermute | solution.py:381
  67.8 5.1 %collective-permute-start.29 = (bf16[256,256]{1,0:T(8,128)(2,1)S(1)}, bf16[256,256]{1,0:T(8,128)(2,1)S(1)}, u32[]{:S(2)}, u32[]{:S(2)}) collective-permute-start(bf16[256,256]{1,0:T(8,128)(2,1)S(1)} %get-tuple-element.69), channel_id=1, source_target_pairs={{0,1},{1,0},{2,3},{3,2},{4,5},{5,4},{6,7},{7,6},{8,9},{9,8},{10,11... | collective-permute-start | bytes 393224 | tf_op jit(solution)/shard_map/ppermute | solution.py:346
  70.8 5.0 %collective-permute-start.28 = (bf16[256,256]{1,0:T(8,128)(2,1)S(1)}, bf16[256,256]{1,0:T(8,128)(2,1)S(1)}, u32[]{:S(2)}, u32[]{:S(2)}) collective-permute-start(bf16[256,256]{1,0:T(8,128)(2,1)S(1)} %join.3.mine_ref), channel_id=1, source_target_pairs={{0,2},{1,5},{2,0},{3,7},{4,6},{5,1},{6,4},{7,3},{8,10},{9,13},{10,... | collective-permute-start | bytes 393224 | tf_op jit(solution)/shard_map/ppermute | solution.py:381
  71.9 6.0 %collective-permute-start.26 = (bf16[256,256]{1,0:T(8,128)(2,1)S(1)}, bf16[256,256]{1,0:T(8,128)(2,1)S(1)}, u32[]{:S(2)}, u32[]{:S(2)}) collective-permute-start(bf16[256,256]{1,0:T(8,128)(2,1)S(1)} %join.2.mine_ref.refs_0_), channel_id=1, source_target_pairs={{0,2},{1,5},{2,0},{3,7},{4,6},{5,1},{6,4},{7,3},{8,10},{9,13},{10,... | collective-permute-start | bytes 393224 | tf_op jit(solution)/shard_map/ppermute | solution.py:381
  (17 other events, 70.9 us)

commit v9 on v8

--- a/solution.py
+++ b/solution.py
@@ -143,7 +143,10 @@
     write_packed(total, (own_ref, even_ref, odd_ref))
 
 
-def local_kernel(own_ref, oth_ref, cot_ref, out_ref, out_other_ref, base_ref, grad_ref, grad_other_ref):
+def local_kernel(
+    own_ref, oth_ref, cot_ref, out_ref, out_other_ref,
+    base_ref, grad_ref, grad_other_ref,
+):
     rows = own_ref.shape[0]
     r = lax.axis_index("rep")
     cot = cot_ref[:, pl.ds(pl.multiple_of(r * rows, rows), rows)]
@@ -303,23 +306,28 @@
     grad_ref[...] = jnp.where(low, other, mine)[:channels].astype(F32)
 
 
-def pair_kernel(after_ref, proj_ref, east_ref, pair_ref):
-    pair_ref[0] = proj_ref[...]
-    pair_ref[1] = east_ref[...]
-
-
-def pick_kernel(device_ref, slot_ref, pair_ref, even_ref, odd_ref, mine_ref, theirs_ref):
-    r = lax.axis_index("rep")
-    tables = (pair_ref, even_ref, odd_ref)
+def pack_kernel(after_ref, proj_ref, even_ref, odd_ref, out_ref):
+    for k, part in enumerate((proj_ref, even_ref, odd_ref)):
+        out_ref[k] = part[...]
+
+
+def pick_kernel(device_ref, slot_ref, after_ref, own_ref, east_ref, mine_ref, theirs_ref):
+    r = lax.axis_index("rep")
     blocks = mine_ref.shape[0]
-    per = pair_ref.shape[0]
+    slots = own_ref.shape[0] // 3
     for out_ref, first in ((mine_ref, r * blocks), (theirs_ref, (1 - r) * blocks)):
         for i in range(blocks):
-            at = entry_of(device_ref, slot_ref, first + i, per // 2)
-            for k, table in enumerate(tables):
-                @pl.when(at // per == k)
-                def _(k=k, i=i, at=at, table=table, out_ref=out_ref):
-                    out_ref[i] = table[at - k * per]
+            at = entry_of(device_ref, slot_ref, first + i, slots)
+            side = lax.div(at, 2 * slots)
+            rest = at - side * 2 * slots
+
+            @pl.when(rest < slots)
+            def _(i=i, at=side * slots + rest, out_ref=out_ref):
+                out_ref[i] = own_ref[at]
+
+            @pl.when(rest >= slots)
+            def _(i=i, at=side * slots + rest - slots, out_ref=out_ref):
+                out_ref[i] = east_ref[at]
 
 
 def decode_kernel(tiles_ref, base_ref, mine_ref, got_ref, out_ref, picked):
@@ -438,7 +446,7 @@
             scratch=[
                 pltpu.VMEM((6 * slots, half, width), F32), pltpu.VMEM((grid_rows, width), BF16),
             ],
-        )(device, slot, after, grid_t, interp_tiles, weight)
+        )(*routes, after, grid_t, interp_tiles, weight)
 
     own_a, even_a, odd_a, hidden_a = encode(back_own, in_hbm(w_embed))
     even_in_a, odd_in_a = to_even(even_a), to_odd(odd_a)
@@ -448,6 +456,17 @@
     out_other, up_other, down_other = swap_rep(out_t), swap_rep(w_up), swap_rep(w_down)
     embed_shape = (slots, 2, half, width)
     mesh_other = swap_rep(mesh_embed)
+
+    second = pl.BlockSpec((1, nodes, width), lambda i: (1, 0, 0))
+
+    def add_east(after, *terms):
+        return call(
+            add_kernel, "add_east", [anywhere()] * len(after) + [second] * 3, whole((nodes, width)),
+            shape_of((nodes, width), BF16), 3 * nodes * width, 6e5, grid=(1,),
+        )(*after, *terms)
+
+    send_a = add_east((back_moved,), own_a, even_in_a, odd_in_a)
+    moved_a = to_east(send_a)
 
     base, local, local_other = call(
         local_kernel, "local_terms", [vmem()] * 5, [vmem()] * 3,
@@ -455,17 +474,7 @@
         4 * my_rows * latent * channels, 4e6,
     )(hidden_a, hidden_b, cot_t, out_t, out_other)
 
-    second = pl.BlockSpec((1, nodes, width), lambda i: (1, 0, 0))
-
-    def add_east(after, *terms):
-        return call(
-            add_kernel, "add_east", [anywhere()] + [second] * 3, whole((nodes, width)),
-            shape_of((nodes, width), BF16), 3 * nodes * width, 6e5, grid=(1,),
-        )(after, *terms)
-
-    send_a = add_east(back_moved, own_a, even_in_a, odd_in_a)
-    moved_a = to_east(send_a)
-    send_b = add_east(moved_a, own_b, even_in_b, odd_in_b)
+    send_b = add_east((moved_a,), own_b, even_in_b, odd_in_b)
     moved_b = to_east(send_b)
 
     back_even, back_odd = call(
@@ -496,7 +505,7 @@
         back_own, back_moved, back_even_in, back_odd_in, local, local_other, *weights,
     )
 
-    east = lax.ppermute(proj, "lon", west_pairs)
+    proj_even, proj_odd = to_even(proj), to_odd(proj)
     hold = lambda rows: [pltpu.VMEM((rows, width), F32)]
     up_keep, up_give, outer_keep, outer_give = call(
         terms_kernel, "sum_terms", [vmem()] * 2, [vmem()] * 4,
@@ -510,8 +519,6 @@
     def step_call(kernel, name, chain, step, out_rows, scratch=()):
         kept, given = chain[0], chain[-1]
         after = [latest] if latest is not None else []
-        if chain is chains[1]:
-            after += [[pair], [pair_even, pair_odd]][step] if step < 2 and len(chain) == 2 else []
         made = call(
             kernel, name, [vmem()] * 2 + [anywhere()] * len(after), [vmem()] * len(out_rows),
             [shape_of((rows, width), BF16) for rows in out_rows], 1, 1, scratch=scratch,
@@ -521,12 +528,12 @@
     for step in range(count):
         for c in range(2):
             rows = chains[c][0].shape[0]
-            if step == 0 and c == 1:
-                pair = call(
-                    pair_kernel, "pair_nodes", [anywhere()] + [vmem()] * 2, vmem(), shape_of((2, nodes, padded), BF16),
-                    1, 1,
-                )(up_give, proj, east)
-                pair_even, pair_odd = to_even(pair), to_odd(pair)
+            if step == 1 and c == 0:
+                trio = call(
+                    pack_kernel, "pack_nodes", [anywhere()] + [vmem()] * 3, vmem(),
+                    shape_of((3, nodes, padded), BF16), 1, 1,
+                )(latest, proj, proj_even, proj_odd)
+                east_trio = lax.ppermute(trio, "lon", west_pairs)
             if step == 0:
                 chains[c] = step_call(
                     functools.partial(halving_kernel, 1), "halve", chains[c], step,
@@ -535,6 +542,7 @@
             else:
                 chains[c] = step_call(whole_kernel, "add_whole", chains[c], step, [rows])
             latest = chains[c][-1]
+    after_pick = chains[1][-1]
     for c in range(2):
         rows = chains[c][0].shape[0]
         chains[c] = step_call(
@@ -556,11 +564,11 @@
         name="place_mesh",
     )(swap_rep(mesh_give), mesh_filled).reshape(mesh_embed.shape)
 
-    table_shape = (2 * slots, half, padded)
+    table_shape = (3 * slots, half, padded)
     mine_picked, theirs_picked = call(
-        pick_kernel, "pick_nodes", [smem()] * 2 + [vmem()] * 3, [vmem()] * 2,
-        [shape_of((blocks // 2, half, padded), BF16)] * 2, 1, 1, weight=5e9,
-    )(device, slot, *[table.reshape(table_shape) for table in (pair, pair_even, pair_odd)])
+        pick_kernel, "pick_nodes", [smem()] * 2 + [anywhere()] + [vmem()] * 2, [vmem()] * 2,
+        [shape_of((blocks // 2, half, padded), BF16)] * 2, 1, 1,
+    )(device, slot, after_pick, trio.reshape(table_shape), east_trio.reshape(table_shape))
     grid_out_t = call(
         decode_kernel, "decode", [vmem()] * 4, vmem(),
         shape_of((channels, my_rows), BF16), 2 * my_rows * tile_rows * padded, 4e6,
@@ -570,11 +578,11 @@
     grad_down, grad_out = call(
         finish_outer_kernel, "finish_outer", [anywhere()] + [vmem()] * 4, [vmem()] * 2,
         [shape_of((width, latent), F32), shape_of((channels, width), F32)], 1, 1,
-    )(grid_out_t, outer_mine, outer_theirs, out_t, out_other)
+    )(in_hbm(grid_out_t), outer_mine, outer_theirs, out_t, out_other)
     grad_up = call(
-        functools.partial(join_kernel, 0), "finish_up", [vmem()] * 2, vmem(),
+        functools.partial(join_kernel, 0), "finish_up", [vmem()] * 2 + [anywhere()], vmem(),
         shape_of((latent, width), F32), 1, 1,
-    )(up_mine, up_theirs)
+    )(up_mine, up_theirs, in_hbm(grid_out_t))
     return (grid_out_t.T, grad_out.T, grad_up, grad_down, grad_mesh)
 
 

time: 80.2 us -> 78.5 us (0.979)
  starting transfers between devices: 37.9 us -> 34.6 us
  waiting for transfers between devices: 22.1 us -> 24.5 us
  local copies, waits for them, and re-layouts: 1.72 us -> 0.69 us
    ppermute x16, waiting for transfers between devices: 9.2 us -> 13.9 us  [along(): return lambda value: lax.ppermute(value, axis, pairs)]
    ppermute x1, waiting for transfers between devices: 3.82 us -> 0.01 us  [per_device(): east_trio = lax.ppermute(trio, 'lon', west_pairs)]
    ppermute x10, starting transfers between devices: 15.4 us -> 12.3 us  [sum_swap(): return lax.ppermute(value, ('lat', 'lon', 'rep'), pairs)]
    ppermute x10, waiting for transfers between devices: 9.07 us -> 10.6 us  [sum_swap(): return lax.ppermute(value, ('lat', 'lon', 'rep'), pairs)]
    unnamed x22 -> x20, local copies, waits for them, and re-layouts: 1.72 us -> 0.69 us
where the time goes in v9:
time: 78.5 us; the launch traced here: 78.2 us
  starting transfers between devices  34.6 us (44%)
  waiting for transfers between devices  24.5 us (31%)
  Pallas kernels  17.5 us (22%)
  between operations  0.96 us (1%)
    ppermute x16, starting transfers between devices, along(): return lambda value: lax.ppermute(value, axis, pairs)  17 us
    ppermute x16, waiting for transfers between devices, along(): return lambda value: lax.ppermute(value, axis, pairs)  13.9 us
    ppermute x10, starting transfers between devices, sum_swap(): return lax.ppermute(value, ('lat', 'lon', 'rep'), pairs)  12.3 us
    ppermute x10, waiting for transfers between devices, sum_swap(): return lax.ppermute(value, ('lat', 'lon', 'rep'), pairs)  10.6 us
    pallas_call x2, Pallas kernels, encode(): call(encode_kernel, 'encode', [smem(), smem(), anywhere()] + [vmem()] * 3...  5.08 us
    ppermute x3, starting transfers between devices, per_device(): to_east = lambda value: lax.ppermute(value, 'lon', east_pairs)  4.2 us
    pallas_call x1, Pallas kernels, per_device(): call(back_kernel, 'back_messages', [smem(), smem(), anywhere(), anywhere(...  3.49 us
    pallas_call x1, Pallas kernels, per_device(): call(node_kernel, 'node_update_and_gradients', sums_specs * 2 + [whole(em...  2.85 us
  transfers between devices with their start and end apart: 30, of which 13 were waited for; matrix products, arithmetic and copies ran while one was open for 0% of the time, Pallas kernels for 12%

profile of v9, /device:TPU:0, one launch (start us, length us, event | category | flops | bytes accessed | tf_op | source)
XLA Modules:
  0.0 78.2 jit_solution(12795919174249738555)
XLA Ops:
  0.7 3.5 %back_messages.1 = (bf16[256,256]{1,0:T(8,128)(2,1)S(1)}, bf16[3,256,256]{2,1,0:T(8,128)(2,1)S(1)}, bf16[2,256,256]{2,1,0:T(8,128)(2,1)S(1)}) custom-call(s32[16]{0:T(128)} %bitcast.23, s32[16]{0:T(128)} %slot_ref.7, bf16[16,128,128]{2,1,0:T(8,128)(2,1)} %tiles_ref.7, bf16[227,2048]{1,0:T(8,128)(2,1)} %bitcast.13), custom_call_target="tpu_custom_call" | custom-call | flops 1 | bytes 1 | tf_op jit(solution)/shard_map/back_messages/pallas_call | solution.py:422
  4.1 3.0 %collective-permute-start.4 = (bf16[3,256,256]{2,1,0:T(8,128)(2,1)S(1)}, bf16[3,256,256]{2,1,0:T(8,128)(2,1)S(1)}, u32[]{:S(2)}, u32[]{:S(2)}) collective-permute-start(bf16[3,256,256]{2,1,0:T(8,128)(2,1)S(1)} %get-tuple-element.45), channel_id=1, source_target_pairs={{0,2},{2,0},{1,3},{3,1},{4,6},{6,4},{5,7},{7,5},{8,10},{10,8},{9,1... | collective-permute-start | bytes 1179656 | tf_op jit(solution)/shard_map/ppermute | solution.py:412
  7.2 2.6 %encode.2 = (bf16[2,256,256]{2,1,0:T(8,128)(2,1)S(1)}, bf16[2,256,256]{2,1,0:T(8,128)(2,1)S(1)}, bf16[2,256,256]{2,1,0:T(8,128)(2,1)S(1)}, bf16[1024,256]{1,0:T(8,128)(2,1)S(1)}) custom-call(s32[16]{0:T(128)} %bitcast.24, s32[16]{0:T(128)} %slot_ref.7, bf16[256,256]{1,0:T(8,128)(2,1)S(1)} %get-tuple-element.38.after_ref.back_ref, ...), custom_call_target="tpu_custom_call" | custom-call | flops 1 | bytes 1 | tf_op jit(solution)/shard_map/encode/pallas_call | solution.py:440
  9.8 1.6 %collective-permute-start.2 = (bf16[2,256,256]{2,1,0:T(8,128)(2,1)S(1)}, bf16[2,256,256]{2,1,0:T(8,128)(2,1)S(1)}, u32[]{:S(2)}, u32[]{:S(2)}) collective-permute-start(bf16[2,256,256]{2,1,0:T(8,128)(2,1)S(1)} %get-tuple-element.43), channel_id=1, source_target_pairs={{0,4},{4,0},{8,12},{12,8},{1,5},{5,1},{9,13},{13,9},{2,6},{6,2},{1... | collective-permute-start | bytes 786440 | tf_op jit(solution)/shard_map/ppermute | solution.py:354
  12.8 2.5 %encode.3 = (bf16[2,256,256]{2,1,0:T(8,128)(2,1)S(1)}, bf16[2,256,256]{2,1,0:T(8,128)(2,1)S(1)}, bf16[2,256,256]{2,1,0:T(8,128)(2,1)S(1)}, bf16[1024,256]{1,0:T(8,128)(2,1)S(1)}) custom-call(s32[16]{0:T(128)} %bitcast.25, s32[16]{0:T(128)} %slot_ref.7, bf16[2,256,256]{2,1,0:T(8,128)(2,1)S(1)} %get-tuple-element.40.after_ref.refs_1_.own_a, ...), custom_call_target="tpu_custom_call" | custom-call | flops 1 | bytes 1 | tf_op jit(solution)/shard_map/encode/pallas_call | solution.py:440
  15.2 3.8 %collective-permute-start.6 = (bf16[2,256,256]{2,1,0:T(8,128)(2,1)S(1)}, bf16[2,256,256]{2,1,0:T(8,128)(2,1)S(1)}, u32[]{:S(2)}, u32[]{:S(2)}) collective-permute-start(bf16[2,256,256]{2,1,0:T(8,128)(2,1)S(1)} %get-tuple-element.47), channel_id=1, source_target_pairs={{0,4},{4,0},{8,12},{12,8},{1,5},{5,1},{9,13},{13,9},{2,6},{6,2},{1... | collective-permute-start | bytes 786440 | tf_op jit(solution)/shard_map/ppermute | solution.py:354
  20.8 4.9 %collective-permute-done.6.refs_2_.even_b = bf16[2,256,256]{2,1,0:T(8,128)(2,1)S(1)} collective-permute-done((bf16[2,256,256]{2,1,0:T(8,128)(2,1)S(1)}, bf16[2,256,256]{2,1,0:T(8,128)(2,1)S(1)}, u32[]{:S(2)}, u32[]{:S(2)}) %collective-permute-start.6) | collective-permute-done | bytes 262176 | tf_op jit(solution)/shard_map/ppermute | solution.py:354
  27.4 3.4 %collective-permute-start.10 = (bf16[256,256]{1,0:T(8,128)(2,1)S(1)}, bf16[256,256]{1,0:T(8,128)(2,1)S(1)}, u32[]{:S(2)}, u32[]{:S(2)}) collective-permute-start(bf16[256,256]{1,0:T(8,128)(2,1)S(1)} %get-tuple-element.50), channel_id=1, source_target_pairs={{0,4},{4,0},{8,12},{12,8},{1,5},{5,1},{9,13},{13,9},{2,6},{6,2},{1... | collective-permute-start | bytes 393224 | tf_op jit(solution)/shard_map/ppermute | solution.py:354
  32.3 2.4 %collective-permute-done.10.back_even_ref = bf16[256,256]{1,0:T(8,128)(2,1)S(1)} collective-permute-done((bf16[256,256]{1,0:T(8,128)(2,1)S(1)}, bf16[256,256]{1,0:T(8,128)(2,1)S(1)}, u32[]{:S(2)}, u32[]{:S(2)}) %collective-permute-start.10) | collective-permute-done | bytes 131104 | tf_op jit(solution)/shard_map/ppermute | solution.py:354
  34.7 2.9 %node_update_and_gradients.1 = (bf16[256,256]{1,0:T(8,128)(2,1)S(1)}, f32[1024,256]{1,0:T(8,128)S(1)}, bf16[1024,256]{1,0:T(8,128)(2,1)S(1)}, bf16[256,256]{1,0:T(8,128)(2,1)S(1)}, f32[4,2,64,256]{3,2,1,0:T(8,128)}) custom-call(bf16[2,256,256]{2,1,0:T(8,128)(2,1)S(1)} %get-tuple-element.40.after_ref.refs_1_.own_a, ...), custom_call_target="tpu_custom_call" | custom-call | flops 1 | bytes 1 | tf_op jit(solution)/shard_map/node_update_and_gradients/pallas_call | solution.py:491
  37.6 1.9 %collective-permute-done.14.got_ref = bf16[1024,256]{1,0:T(8,128)(2,1)S(1)} collective-permute-done((bf16[1024,256]{1,0:T(8,128)(2,1)S(1)}, bf16[1024,256]{1,0:T(8,128)(2,1)S(1)}, u32[]{:S(2)}, u32[]{:S(2)}) %collective-permute-start.14) | collective-permute-done | bytes 524320 | tf_op jit(solution)/shard_map/ppermute | solution.py:354
  39.7 1.1 %collective-permute-start.16 = (bf16[256,256]{1,0:T(8,128)(2,1)S(1)}, bf16[256,256]{1,0:T(8,128)(2,1)S(1)}, u32[]{:S(2)}, u32[]{:S(2)}) collective-permute-start(bf16[256,256]{1,0:T(8,128)(2,1)S(1)} %get-tuple-element.59), channel_id=1, source_target_pairs={{0,2},{1,5},{2,0},{3,7},{4,6},{5,1},{6,4},{7,3},{8,10},{9,13},{10,... | collective-permute-start | bytes 393224 | tf_op jit(solution)/shard_map/ppermute | solution.py:389
  41.8 3.6 %collective-permute-start.21 = (bf16[256,256]{1,0:T(8,128)(2,1)S(1)}, bf16[256,256]{1,0:T(8,128)(2,1)S(1)}, u32[]{:S(2)}, u32[]{:S(2)}) collective-permute-start(bf16[256,256]{1,0:T(8,128)(2,1)S(1)} %get-tuple-element.64.proj_ref), channel_id=1, source_target_pairs={{0,4},{4,0},{8,12},{12,8},{1,5},{5,1},{9,13},{13,9},{2,6},{6,2},{1... | collective-permute-start | bytes 393224 | tf_op jit(solution)/shard_map/ppermute | solution.py:354
  46.3 3.6 %collective-permute-done.21.even_ref = bf16[256,256]{1,0:T(8,128)(2,1)S(1)} collective-permute-done((bf16[256,256]{1,0:T(8,128)(2,1)S(1)}, bf16[256,256]{1,0:T(8,128)(2,1)S(1)}, u32[]{:S(2)}, u32[]{:S(2)}) %collective-permute-start.21) | collective-permute-done | bytes 131104 | tf_op jit(solution)/shard_map/ppermute | solution.py:354
  49.8 1.1 %collective-permute-start.23 = (bf16[3,256,256]{2,1,0:T(8,128)(2,1)S(1)}, bf16[3,256,256]{2,1,0:T(8,128)(2,1)S(1)}, u32[]{:S(2)}, u32[]{:S(2)}) collective-permute-start(bf16[3,256,256]{2,1,0:T(8,128)(2,1)S(1)} %pack_nodes.1), channel_id=1, source_target_pairs={{2,0},{0,2},{3,1},{1,3},{6,4},{4,6},{7,5},{5,7},{10,8},{8,10},{11,... | collective-permute-start | bytes 1179656 | tf_op jit(solution)/shard_map/ppermute | solution.py:536
  51.0 2.6 %collective-permute-start.18 = (bf16[128,256]{1,0:T(8,128)(2,1)S(1)}, bf16[128,256]{1,0:T(8,128)(2,1)S(1)}, u32[]{:S(2)}, u32[]{:S(2)}) collective-permute-start(bf16[128,256]{1,0:T(8,128)(2,1)S(1)} %get-tuple-element.60.refs_0_), channel_id=1, source_target_pairs={{0,4},{1,9},{2,6},{3,11},{4,0},{5,13},{6,2},{7,15},{8,12},{9,1},{1... | collective-permute-start | bytes 196616 | tf_op jit(solution)/shard_map/ppermute | solution.py:389
  53.6 2.2 %collective-permute-done.18.got_ref = bf16[128,256]{1,0:T(8,128)(2,1)S(1)} collective-permute-done((bf16[128,256]{1,0:T(8,128)(2,1)S(1)}, bf16[128,256]{1,0:T(8,128)(2,1)S(1)}, u32[]{:S(2)}, u32[]{:S(2)}) %collective-permute-start.18) | collective-permute-done | bytes 65568 | tf_op jit(solution)/shard_map/ppermute | solution.py:389
  55.8 2.8 %collective-permute-start.20 = (bf16[128,256]{1,0:T(8,128)(2,1)S(1)}, bf16[128,256]{1,0:T(8,128)(2,1)S(1)}, u32[]{:S(2)}, u32[]{:S(2)}) collective-permute-start(bf16[128,256]{1,0:T(8,128)(2,1)S(1)} %add_whole.4.refs_0_.kept_ref), channel_id=1, source_target_pairs={{0,8},{1,3},{2,10},{3,1},{4,12},{5,7},{6,14},{7,5},{8,0},{9,11},{1... | collective-permute-start | bytes 196616 | tf_op jit(solution)/shard_map/ppermute | solution.py:389
  59.3 1.8 %collective-permute-done.20.got_ref = bf16[128,256]{1,0:T(8,128)(2,1)S(1)} collective-permute-done((bf16[128,256]{1,0:T(8,128)(2,1)S(1)}, bf16[128,256]{1,0:T(8,128)(2,1)S(1)}, u32[]{:S(2)}, u32[]{:S(2)}) %collective-permute-start.20) | collective-permute-done | bytes 65568 | tf_op jit(solution)/shard_map/ppermute | solution.py:389
  61.1 3.1 %collective-permute-done.19.got_ref = bf16[128,256]{1,0:T(8,128)(2,1)S(1)} collective-permute-done((bf16[128,256]{1,0:T(8,128)(2,1)S(1)}, bf16[128,256]{1,0:T(8,128)(2,1)S(1)}, u32[]{:S(2)}, u32[]{:S(2)}) %collective-permute-start.19) | collective-permute-done | bytes 65568 | tf_op jit(solution)/shard_map/ppermute | solution.py:389
  66.1 1.9 %collective-permute-start.27 = (bf16[128,256]{1,0:T(8,128)(2,1)S(1)}, bf16[128,256]{1,0:T(8,128)(2,1)S(1)}, u32[]{:S(2)}, u32[]{:S(2)}) collective-permute-start(bf16[128,256]{1,0:T(8,128)(2,1)S(1)} %add_whole.7.after_ref.refs_0_.mine_ref), channel_id=1, source_target_pairs={{0,4},{1,9},{2,6},{3,11},{4,0},{5,13},{6,2},{7,15},{8,12},{9,1},{1... | collective-permute-start | bytes 196616 | tf_op jit(solution)/shard_map/ppermute | solution.py:389
  68.8 1.8 %collective-permute-done.25.got_ref = bf16[128,256]{1,0:T(8,128)(2,1)S(1)} collective-permute-done((bf16[128,256]{1,0:T(8,128)(2,1)S(1)}, bf16[128,256]{1,0:T(8,128)(2,1)S(1)}, u32[]{:S(2)}, u32[]{:S(2)}) %collective-permute-start.25) | collective-permute-done | bytes 65568 | tf_op jit(solution)/shard_map/ppermute | solution.py:389
  70.6 1.0 %collective-permute-start.26 = (bf16[256,256]{1,0:T(8,128)(2,1)S(1)}, bf16[256,256]{1,0:T(8,128)(2,1)S(1)}, u32[]{:S(2)}, u32[]{:S(2)}) collective-permute-start(bf16[256,256]{1,0:T(8,128)(2,1)S(1)} %join.2.mine_ref.refs_0_), channel_id=1, source_target_pairs={{0,2},{1,5},{2,0},{3,7},{4,6},{5,1},{6,4},{7,3},{8,10},{9,13},{10,... | collective-permute-start | bytes 393224 | tf_op jit(solution)/shard_map/ppermute | solution.py:389
  74.1 1.2 %decode.1.after_ref.refs_0_ = bf16[227,1024]{1,0:T(8,128)(2,1)} custom-call(bf16[16,128,128]{2,1,0:T(8,128)(2,1)S(1)} %copy-done, f32[227,1024]{1,0:T(8,128)S(1)} %get-tuple-element.42.base_ref, bf16[8,64,256]{2,1,0:T(8,128)(2,1)S(1)} %get-tuple-element.65.mine_ref, bf16[8,64,256]{2,1,0:T(8,128)(2,1)S(1)} %collective-permute-done.24.got_ref), custom_call_target="tpu_custom_call" | custom-call | flops 1 | bytes 1 | tf_op jit(solution)/shard_map/decode/pallas_call | solution.py:572
  (79 shorter events, 17.1 us)
Async XLA Ops:
  4.1 15.8 %collective-permute-start.4 = (bf16[3,256,256]{2,1,0:T(8,128)(2,1)S(1)}, bf16[3,256,256]{2,1,0:T(8,128)(2,1)S(1)}, u32[]{:S(2)}, u32[]{:S(2)}) collective-permute-start(bf16[3,256,256]{2,1,0:T(8,128)(2,1)S(1)} %get-tuple-element.45), channel_id=1, source_target_pairs={{0,2},{2,0},{1,3},{3,1},{4,6},{6,4},{5,7},{7,5},{8,10},{10,8},{9,1... | collective-permute-start | bytes 1179656 | tf_op jit(solution)/shard_map/ppermute | solution.py:412
  9.8 10.1 %collective-permute-start.2 = (bf16[2,256,256]{2,1,0:T(8,128)(2,1)S(1)}, bf16[2,256,256]{2,1,0:T(8,128)(2,1)S(1)}, u32[]{:S(2)}, u32[]{:S(2)}) collective-permute-start(bf16[2,256,256]{2,1,0:T(8,128)(2,1)S(1)} %get-tuple-element.43), channel_id=1, source_target_pairs={{0,4},{4,0},{8,12},{12,8},{1,5},{5,1},{9,13},{13,9},{2,6},{6,2},{1... | collective-permute-start | bytes 786440 | tf_op jit(solution)/shard_map/ppermute | solution.py:354
  11.4 8.5 %collective-permute-start.3 = (bf16[2,256,256]{2,1,0:T(8,128)(2,1)S(1)}, bf16[2,256,256]{2,1,0:T(8,128)(2,1)S(1)}, u32[]{:S(2)}, u32[]{:S(2)}) collective-permute-start(bf16[2,256,256]{2,1,0:T(8,128)(2,1)S(1)} %get-tuple-element.44), channel_id=1, source_target_pairs={{0,0},{4,8},{8,4},{12,12},{1,1},{5,9},{9,5},{13,13},{2,2},{6,10},{... | collective-permute-start | bytes 786440 | tf_op jit(solution)/shard_map/ppermute | solution.py:354
  15.2 10.5 %collective-permute-start.6 = (bf16[2,256,256]{2,1,0:T(8,128)(2,1)S(1)}, bf16[2,256,256]{2,1,0:T(8,128)(2,1)S(1)}, u32[]{:S(2)}, u32[]{:S(2)}) collective-permute-start(bf16[2,256,256]{2,1,0:T(8,128)(2,1)S(1)} %get-tuple-element.47), channel_id=1, source_target_pairs={{0,4},{4,0},{8,12},{12,8},{1,5},{5,1},{9,13},{13,9},{2,6},{6,2},{1... | collective-permute-start | bytes 786440 | tf_op jit(solution)/shard_map/ppermute | solution.py:354
  19.0 6.7 %collective-permute-start.7 = (bf16[2,256,256]{2,1,0:T(8,128)(2,1)S(1)}, bf16[2,256,256]{2,1,0:T(8,128)(2,1)S(1)}, u32[]{:S(2)}, u32[]{:S(2)}) collective-permute-start(bf16[2,256,256]{2,1,0:T(8,128)(2,1)S(1)} %get-tuple-element.48), channel_id=1, source_target_pairs={{0,0},{4,8},{8,4},{12,12},{1,1},{5,9},{9,5},{13,13},{2,2},{6,10},{... | collective-permute-start | bytes 786440 | tf_op jit(solution)/shard_map/ppermute | solution.py:354
  19.9 11.0 %collective-permute-start.9 = (bf16[512,256]{1,0:T(8,128)(2,1)S(1)}, bf16[512,256]{1,0:T(8,128)(2,1)S(1)}, u32[]{:S(2)}, u32[]{:S(2)}) collective-permute-start(bf16[512,256]{1,0:T(8,128)(2,1)S(1)} %copy-done.4), channel_id=1, source_target_pairs={{0,1},{1,0},{2,3},{3,2},{4,5},{5,4},{6,7},{7,6},{8,9},{9,8},{10,11... | collective-permute-start | bytes 786440 | tf_op jit(solution)/shard_map/ppermute | solution.py:354
  20.0 6.2 %collective-permute-start.5 = (bf16[256,256]{1,0:T(8,128)(2,1)S(1)}, bf16[256,256]{1,0:T(8,128)(2,1)S(1)}, u32[]{:S(2)}, u32[]{:S(2)}) collective-permute-start(bf16[256,256]{1,0:T(8,128)(2,1)S(1)} %add_east.2), channel_id=1, source_target_pairs={{0,2},{2,0},{1,3},{3,1},{4,6},{6,4},{5,7},{7,5},{8,10},{10,8},{9,1... | collective-permute-start | bytes 393224 | tf_op jit(solution)/shard_map/ppermute | solution.py:412
  20.6 11.7 %collective-permute-start.12 = (bf16[512,256]{1,0:T(8,128)(2,1)S(1)}, bf16[512,256]{1,0:T(8,128)(2,1)S(1)}, u32[]{:S(2)}, u32[]{:S(2)}) collective-permute-start(bf16[512,256]{1,0:T(8,128)(2,1)S(1)} %copy-done.5), channel_id=1, source_target_pairs={{0,1},{1,0},{2,3},{3,2},{4,5},{5,4},{6,7},{7,6},{8,9},{9,8},{10,11... | collective-permute-start | bytes 786440 | tf_op jit(solution)/shard_map/ppermute | solution.py:354
  25.7 6.6 %collective-permute-start.13 = (bf16[256,512]{1,0:T(8,128)(2,1)S(1)}, bf16[256,512]{1,0:T(8,128)(2,1)S(1)}, u32[]{:S(2)}, u32[]{:S(2)}) collective-permute-start(bf16[256,512]{1,0:T(8,128)(2,1)S(1)} %copy-done.6), channel_id=1, source_target_pairs={{0,1},{1,0},{2,3},{3,2},{4,5},{5,4},{6,7},{7,6},{8,9},{9,8},{10,11... | collective-permute-start | bytes 786440 | tf_op jit(solution)/shard_map/ppermute | solution.py:354
  26.3 6.0 %collective-permute-start.8 = (bf16[256,256]{1,0:T(8,128)(2,1)S(1)}, bf16[256,256]{1,0:T(8,128)(2,1)S(1)}, u32[]{:S(2)}, u32[]{:S(2)}) collective-permute-start(bf16[256,256]{1,0:T(8,128)(2,1)S(1)} %add_east.3.after_ref), channel_id=1, source_target_pairs={{0,2},{2,0},{1,3},{3,1},{4,6},{6,4},{5,7},{7,5},{8,10},{10,8},{9,1... | collective-permute-start | bytes 393224 | tf_op jit(solution)/shard_map/ppermute | solution.py:412
  27.4 7.2 %collective-permute-start.10 = (bf16[256,256]{1,0:T(8,128)(2,1)S(1)}, bf16[256,256]{1,0:T(8,128)(2,1)S(1)}, u32[]{:S(2)}, u32[]{:S(2)}) collective-permute-start(bf16[256,256]{1,0:T(8,128)(2,1)S(1)} %get-tuple-element.50), channel_id=1, source_target_pairs={{0,4},{4,0},{8,12},{12,8},{1,5},{5,1},{9,13},{13,9},{2,6},{6,2},{1... | collective-permute-start | bytes 393224 | tf_op jit(solution)/shard_map/ppermute | solution.py:354
  39.7 6.4 %collective-permute-start.16 = (bf16[256,256]{1,0:T(8,128)(2,1)S(1)}, bf16[256,256]{1,0:T(8,128)(2,1)S(1)}, u32[]{:S(2)}, u32[]{:S(2)}) collective-permute-start(bf16[256,256]{1,0:T(8,128)(2,1)S(1)} %get-tuple-element.59), channel_id=1, source_target_pairs={{0,2},{1,5},{2,0},{3,7},{4,6},{5,1},{6,4},{7,3},{8,10},{9,13},{10,... | collective-permute-start | bytes 393224 | tf_op jit(solution)/shard_map/ppermute | solution.py:389
  40.8 5.4 %collective-permute-start.15 = (bf16[256,256]{1,0:T(8,128)(2,1)S(1)}, bf16[256,256]{1,0:T(8,128)(2,1)S(1)}, u32[]{:S(2)}, u32[]{:S(2)}) collective-permute-start(bf16[256,256]{1,0:T(8,128)(2,1)S(1)} %get-tuple-element.57), channel_id=1, source_target_pairs={{0,2},{1,5},{2,0},{3,7},{4,6},{5,1},{6,4},{7,3},{8,10},{9,13},{10,... | collective-permute-start | bytes 393224 | tf_op jit(solution)/shard_map/ppermute | solution.py:389
  41.8 8.0 %collective-permute-start.21 = (bf16[256,256]{1,0:T(8,128)(2,1)S(1)}, bf16[256,256]{1,0:T(8,128)(2,1)S(1)}, u32[]{:S(2)}, u32[]{:S(2)}) collective-permute-start(bf16[256,256]{1,0:T(8,128)(2,1)S(1)} %get-tuple-element.64.proj_ref), channel_id=1, source_target_pairs={{0,4},{4,0},{8,12},{12,8},{1,5},{5,1},{9,13},{13,9},{2,6},{6,2},{1... | collective-permute-start | bytes 393224 | tf_op jit(solution)/shard_map/ppermute | solution.py:354
  49.8 14.3 %collective-permute-start.23 = (bf16[3,256,256]{2,1,0:T(8,128)(2,1)S(1)}, bf16[3,256,256]{2,1,0:T(8,128)(2,1)S(1)}, u32[]{:S(2)}, u32[]{:S(2)}) collective-permute-start(bf16[3,256,256]{2,1,0:T(8,128)(2,1)S(1)} %pack_nodes.1), channel_id=1, source_target_pairs={{2,0},{0,2},{3,1},{1,3},{6,4},{4,6},{7,5},{5,7},{10,8},{8,10},{11,... | collective-permute-start | bytes 1179656 | tf_op jit(solution)/shard_map/ppermute | solution.py:536
  51.0 4.8 %collective-permute-start.18 = (bf16[128,256]{1,0:T(8,128)(2,1)S(1)}, bf16[128,256]{1,0:T(8,128)(2,1)S(1)}, u32[]{:S(2)}, u32[]{:S(2)}) collective-permute-start(bf16[128,256]{1,0:T(8,128)(2,1)S(1)} %get-tuple-element.60.refs_0_), channel_id=1, source_target_pairs={{0,4},{1,9},{2,6},{3,11},{4,0},{5,13},{6,2},{7,15},{8,12},{9,1},{1... | collective-permute-start | bytes 196616 | tf_op jit(solution)/shard_map/ppermute | solution.py:389
  53.6 5.0 %collective-permute-start.17 = (bf16[128,256]{1,0:T(8,128)(2,1)S(1)}, bf16[128,256]{1,0:T(8,128)(2,1)S(1)}, u32[]{:S(2)}, u32[]{:S(2)}) collective-permute-start(bf16[128,256]{1,0:T(8,128)(2,1)S(1)} %get-tuple-element.62.refs_0_.after_ref), channel_id=1, source_target_pairs={{0,4},{1,9},{2,6},{3,11},{4,0},{5,13},{6,2},{7,15},{8,12},{9,1},{1... | collective-permute-start | bytes 196616 | tf_op jit(solution)/shard_map/ppermute | solution.py:389
  55.8 5.2 %collective-permute-start.20 = (bf16[128,256]{1,0:T(8,128)(2,1)S(1)}, bf16[128,256]{1,0:T(8,128)(2,1)S(1)}, u32[]{:S(2)}, u32[]{:S(2)}) collective-permute-start(bf16[128,256]{1,0:T(8,128)(2,1)S(1)} %add_whole.4.refs_0_.kept_ref), channel_id=1, source_target_pairs={{0,8},{1,3},{2,10},{3,1},{4,12},{5,7},{6,14},{7,5},{8,0},{9,11},{1... | collective-permute-start | bytes 196616 | tf_op jit(solution)/shard_map/ppermute | solution.py:389
  58.6 5.5 %collective-permute-start.19 = (bf16[128,256]{1,0:T(8,128)(2,1)S(1)}, bf16[128,256]{1,0:T(8,128)(2,1)S(1)}, u32[]{:S(2)}, u32[]{:S(2)}) collective-permute-start(bf16[128,256]{1,0:T(8,128)(2,1)S(1)} %add_whole.5.refs_0_.kept_ref), channel_id=1, source_target_pairs={{0,8},{1,3},{2,10},{3,1},{4,12},{5,7},{6,14},{7,5},{8,0},{9,11},{1... | collective-permute-start | bytes 196616 | tf_op jit(solution)/shard_map/ppermute | solution.py:389
  65.8 8.3 %collective-permute-start.24 = (bf16[8,64,256]{2,1,0:T(8,128)(2,1)S(1)}, bf16[8,64,256]{2,1,0:T(8,128)(2,1)S(1)}, u32[]{:S(2)}, u32[]{:S(2)}) collective-permute-start(bf16[8,64,256]{2,1,0:T(8,128)(2,1)S(1)} %get-tuple-element.66), channel_id=1, source_target_pairs={{0,1},{1,0},{2,3},{3,2},{4,5},{5,4},{6,7},{7,6},{8,9},{9,8},{10,11... | collective-permute-start | bytes 786440 | tf_op jit(solution)/shard_map/ppermute | solution.py:354
  66.1 6.2 %collective-permute-start.27 = (bf16[128,256]{1,0:T(8,128)(2,1)S(1)}, bf16[128,256]{1,0:T(8,128)(2,1)S(1)}, u32[]{:S(2)}, u32[]{:S(2)}) collective-permute-start(bf16[128,256]{1,0:T(8,128)(2,1)S(1)} %add_whole.7.after_ref.refs_0_.mine_ref), channel_id=1, source_target_pairs={{0,4},{1,9},{2,6},{3,11},{4,0},{5,13},{6,2},{7,15},{8,12},{9,1},{1... | collective-permute-start | bytes 196616 | tf_op jit(solution)/shard_map/ppermute | solution.py:389
  68.0 5.4 %collective-permute-start.29 = (bf16[256,256]{1,0:T(8,128)(2,1)S(1)}, bf16[256,256]{1,0:T(8,128)(2,1)S(1)}, u32[]{:S(2)}, u32[]{:S(2)}) collective-permute-start(bf16[256,256]{1,0:T(8,128)(2,1)S(1)} %get-tuple-element.69), channel_id=1, source_target_pairs={{0,1},{1,0},{2,3},{3,2},{4,5},{5,4},{6,7},{7,6},{8,9},{9,8},{10,11... | collective-permute-start | bytes 393224 | tf_op jit(solution)/shard_map/ppermute | solution.py:354
  70.6 5.0 %collective-permute-start.26 = (bf16[256,256]{1,0:T(8,128)(2,1)S(1)}, bf16[256,256]{1,0:T(8,128)(2,1)S(1)}, u32[]{:S(2)}, u32[]{:S(2)}) collective-permute-start(bf16[256,256]{1,0:T(8,128)(2,1)S(1)} %join.2.mine_ref.refs_0_), channel_id=1, source_target_pairs={{0,2},{1,5},{2,0},{3,7},{4,6},{5,1},{6,4},{7,3},{8,10},{9,13},{10,... | collective-permute-start | bytes 393224 | tf_op jit(solution)/shard_map/ppermute | solution.py:389
  72.3 5.0 %collective-permute-start.28 = (bf16[256,256]{1,0:T(8,128)(2,1)S(1)}, bf16[256,256]{1,0:T(8,128)(2,1)S(1)}, u32[]{:S(2)}, u32[]{:S(2)}) collective-permute-start(bf16[256,256]{1,0:T(8,128)(2,1)S(1)} %join.3.mine_ref), channel_id=1, source_target_pairs={{0,2},{1,5},{2,0},{3,7},{4,6},{5,1},{6,4},{7,3},{8,10},{9,13},{10,... | collective-permute-start | bytes 393224 | tf_op jit(solution)/shard_map/ppermute | solution.py:389
  (16 other events, 70.1 us)

commit v10 on v9

--- a/solution.py
+++ b/solution.py
@@ -143,10 +143,8 @@
     write_packed(total, (own_ref, even_ref, odd_ref))
 
 
-def local_kernel(
-    own_ref, oth_ref, cot_ref, out_ref, out_other_ref,
-    base_ref, grad_ref, grad_other_ref,
-):
+def local_kernel(*refs):
+    own_ref, oth_ref, cot_ref, out_ref, out_other_ref, base_ref, grad_ref, grad_other_ref = refs[-8:]
     rows = own_ref.shape[0]
     r = lax.axis_index("rep")
     cot = cot_ref[:, pl.ds(pl.multiple_of(r * rows, rows), rows)]
@@ -223,6 +221,15 @@
         back_own += dot_last(pre_grad, up_own)
         back_oth += dot_last(pre_grad, up_oth)
 
+    back = jnp.concatenate([back_own, back_oth], axis=1)
+    slope = (
+        back - jnp.mean(back, axis=-1, keepdims=True)
+        - norm * jnp.mean(back * norm, axis=-1, keepdims=True)
+    ) * inverse
+    mesh_half[...] = (grad_own.astype(F32) + slope[:, :width]).reshape(mesh_half.shape)
+    mesh_give_ref[...] = (grad_oth.astype(F32) + slope[:, width:]).astype(mesh_give_ref.dtype)
+    copy = pltpu.make_async_copy(mesh_half, mesh_ref.at[:, r], mesh_sem)
+    copy.start()
     mesh_own = (states[0] + update_own).astype(BF16)
     mesh_oth = (states[1] + update_oth).astype(BF16)
     proj = dot_last(mesh_own, out_ref[...]) + dot_last(mesh_oth, out_other_ref[...])
@@ -234,16 +241,6 @@
         grad = dot_rows(cot, mesh)
         o_ref[start : 2 * latent, :] = grad.astype(o_ref.dtype)
         o_ref[start : start + channels, :] = (grad[:channels] + local[...]).astype(o_ref.dtype)
-
-    back = jnp.concatenate([back_own, back_oth], axis=1)
-    slope = (
-        back - jnp.mean(back, axis=-1, keepdims=True)
-        - norm * jnp.mean(back * norm, axis=-1, keepdims=True)
-    ) * inverse
-    mesh_half[...] = (grad_own.astype(F32) + slope[:, :width]).reshape(mesh_half.shape)
-    mesh_give_ref[...] = (grad_oth.astype(F32) + slope[:, width:]).astype(mesh_give_ref.dtype)
-    copy = pltpu.make_async_copy(mesh_half, mesh_ref.at[:, r], mesh_sem)
-    copy.start()
     copy.wait()
 
 
@@ -311,35 +308,28 @@
         out_ref[k] = part[...]
 
 
-def pick_kernel(device_ref, slot_ref, after_ref, own_ref, east_ref, mine_ref, theirs_ref):
+def hold_kernel(after_ref, value_ref, out_ref):
+    out_ref[...] = value_ref[...]
+
+
+def decode_kernel(device_ref, slot_ref, tiles_ref, base_ref, *refs):
+    tables, (out_ref, picked) = refs[:4], refs[4:]
     r = lax.axis_index("rep")
-    blocks = mine_ref.shape[0]
-    slots = own_ref.shape[0] // 3
-    for out_ref, first in ((mine_ref, r * blocks), (theirs_ref, (1 - r) * blocks)):
-        for i in range(blocks):
-            at = entry_of(device_ref, slot_ref, first + i, slots)
-            side = lax.div(at, 2 * slots)
-            rest = at - side * 2 * slots
-
-            @pl.when(rest < slots)
-            def _(i=i, at=side * slots + rest, out_ref=out_ref):
-                out_ref[i] = own_ref[at]
-
-            @pl.when(rest >= slots)
-            def _(i=i, at=side * slots + rest - slots, out_ref=out_ref):
-                out_ref[i] = east_ref[at]
-
-
-def decode_kernel(tiles_ref, base_ref, mine_ref, got_ref, out_ref, picked):
-    r = lax.axis_index("rep")
-    blocks, half = mine_ref.shape[:2]
-    rows = tiles_ref.shape[1]
+    blocks, rows = picked.shape[:2]
+    half = rows // 2
+    slots = tables[0].shape[0] // 3
     channels = out_ref.shape[0]
-    own = pl.ds(pl.multiple_of(r * half, half), half)
-    other = pl.ds(pl.multiple_of((1 - r) * half, half), half)
     for i in range(blocks):
-        picked[i, own, :] = mine_ref[i]
-        picked[i, other, :] = got_ref[i]
+        at = entry_of(device_ref, slot_ref, r * blocks + i, slots)
+        side = lax.div(at, 2 * slots)
+        rest = at - side * 2 * slots
+        for east in range(2):
+            @pl.when(lax.div(rest, slots) == east)
+            def _(i=i, at=side * slots + rest - east * slots, east=east):
+                own = pl.ds(pl.multiple_of(r * half, half), half)
+                other = pl.ds(pl.multiple_of((1 - r) * half, half), half)
+                picked[i, own, :] = tables[east][at]
+                picked[i, other, :] = tables[2 + east][at]
     for i in range(blocks):
         cols = slice(i * rows, (i + 1) * rows)
         decoded = dot_last(picked[i].T, tiles_ref[r * blocks + i])
@@ -465,23 +455,23 @@
             shape_of((nodes, width), BF16), 3 * nodes * width, 6e5, grid=(1,),
         )(*after, *terms)
 
-    send_a = add_east((back_moved,), own_a, even_in_a, odd_in_a)
+    send_a = add_east((own_b,), own_a, even_in_a, odd_in_a)
     moved_a = to_east(send_a)
-
-    base, local, local_other = call(
-        local_kernel, "local_terms", [vmem()] * 5, [vmem()] * 3,
-        [shape_of((channels, my_rows), F32)] + [shape_of((channels, width), F32)] * 2,
-        4 * my_rows * latent * channels, 4e6,
-    )(hidden_a, hidden_b, cot_t, out_t, out_other)
-
-    send_b = add_east((moved_a,), own_b, even_in_b, odd_in_b)
-    moved_b = to_east(send_b)
 
     back_even, back_odd = call(
         sides_kernel, "add_sides", [anywhere(), vmem(), vmem()], [vmem()] * 2,
         [shape_of((nodes, padded), BF16)] * 2, 3 * nodes * width, 1e6,
-    )(send_b, back_side, back_moved)
+    )(own_b, back_side, back_moved)
     back_even_in, back_odd_in = to_even(back_even), to_odd(back_odd)
+
+    base, local, local_other = call(
+        local_kernel, "local_terms", [anywhere()] * 3 + [vmem()] * 5, [vmem()] * 3,
+        [shape_of((channels, my_rows), F32)] + [shape_of((channels, width), F32)] * 2,
+        4 * my_rows * latent * channels, 4e6,
+    )(moved_a, back_even_in, back_odd_in, hidden_a, hidden_b, cot_t, out_t, out_other)
+
+    send_b = add_east((local,), own_b, even_in_b, odd_in_b)
+    moved_b = to_east(send_b)
 
     first = pl.BlockSpec((1, nodes, width), lambda i: (0, 0, 0))
     sums_specs = [first] * 3 + [whole((nodes, width))]
@@ -528,7 +518,7 @@
     for step in range(count):
         for c in range(2):
             rows = chains[c][0].shape[0]
-            if step == 1 and c == 0:
+            if step == 2 and c == 0:
                 trio = call(
                     pack_kernel, "pack_nodes", [anywhere()] + [vmem()] * 3, vmem(),
                     shape_of((3, nodes, padded), BF16), 1, 1,
@@ -542,7 +532,6 @@
             else:
                 chains[c] = step_call(whole_kernel, "add_whole", chains[c], step, [rows])
             latest = chains[c][-1]
-    after_pick = chains[1][-1]
     for c in range(2):
         rows = chains[c][0].shape[0]
         chains[c] = step_call(
@@ -565,15 +554,16 @@
     )(swap_rep(mesh_give), mesh_filled).reshape(mesh_embed.shape)
 
     table_shape = (3 * slots, half, padded)
-    mine_picked, theirs_picked = call(
-        pick_kernel, "pick_nodes", [smem()] * 2 + [anywhere()] + [vmem()] * 2, [vmem()] * 2,
-        [shape_of((blocks // 2, half, padded), BF16)] * 2, 1, 1,
-    )(device, slot, after_pick, trio.reshape(table_shape), east_trio.reshape(table_shape))
+    east_trio = call(
+        hold_kernel, "hold_nodes", [anywhere(), vmem()], vmem(),
+        shape_of((3, nodes, padded), BF16), 1, 1,
+    )(outer_mine, east_trio)
+    tables = (trio, east_trio, swap_rep(trio), swap_rep(east_trio))
     grid_out_t = call(
-        decode_kernel, "decode", [vmem()] * 4, vmem(),
-        shape_of((channels, my_rows), BF16), 2 * my_rows * tile_rows * padded, 4e6,
+        decode_kernel, "decode", [smem()] * 2 + [vmem()] * 6, vmem(),
+        shape_of((channels, my_rows), BF16), 1, 1,
         scratch=[pltpu.VMEM((blocks // 2, tile_rows, padded), BF16)],
-    )(interp_tiles, base, mine_picked, swap_rep(theirs_picked))
+    )(*routes, interp_tiles, base, *[table.reshape(table_shape) for table in tables])
 
     grad_down, grad_out = call(
         finish_outer_kernel, "finish_outer", [anywhere()] + [vmem()] * 4, [vmem()] * 2,

time: 78.5 us -> 84.7 us (1.079)
  starting transfers between devices: 34.6 us -> 42 us
    ppermute x16 -> x17, starting transfers between devices: 17 us -> 25.9 us  [along(): return lambda value: lax.ppermute(value, axis, pairs)]
    ppermute x16 -> x17, waiting for transfers between devices: 13.9 us -> 6.08 us  [along(): return lambda value: lax.ppermute(value, axis, pairs)]
    ppermute x3, waiting for transfers between devices: 0.01 us -> 7.14 us  [per_device(): to_east = lambda value: lax.ppermute(value, 'lon', east_pairs)]
    ppermute x10, starting transfers between devices: 12.3 us -> 11.3 us  [sum_swap(): return lax.ppermute(value, ('lat', 'lon', 'rep'), pairs)]
  transfers between devices with their start and end apart: 30 -> 31, of which waited for: 13 -> 11; matrix products, arithmetic and copies ran while one was open for 0% -> 0% of each run, Pallas kernels for 12% -> 11%
where the time goes in v10:
time: 84.7 us; the launch traced here: 84.4 us
  starting transfers between devices  42 us (50%)
  waiting for transfers between devices  24.2 us (29%)
  Pallas kernels  17.3 us (20%)
  between operations  0.95 us (1%)
    ppermute x17, starting transfers between devices, along(): return lambda value: lax.ppermute(value, axis, pairs)  25.9 us
    ppermute x10, starting transfers between devices, sum_swap(): return lax.ppermute(value, ('lat', 'lon', 'rep'), pairs)  11.3 us
    ppermute x10, waiting for transfers between devices, sum_swap(): return lax.ppermute(value, ('lat', 'lon', 'rep'), pairs)  11 us
    ppermute x3, waiting for transfers between devices, per_device(): to_east = lambda value: lax.ppermute(value, 'lon', east_pairs)  7.14 us
    ppermute x17, waiting for transfers between devices, along(): return lambda value: lax.ppermute(value, axis, pairs)  6.08 us
    pallas_call x2, Pallas kernels, encode(): call(encode_kernel, 'encode', [smem(), smem(), anywhere()] + [vmem()] * 3...  4.93 us
    ppermute x3, starting transfers between devices, per_device(): to_east = lambda value: lax.ppermute(value, 'lon', east_pairs)  4.2 us
    pallas_call x1, Pallas kernels, per_device(): call(back_kernel, 'back_messages', [smem(), smem(), anywhere(), anywhere(...  3.49 us
  transfers between devices with their start and end apart: 31, of which 11 were waited for; matrix products, arithmetic and copies ran while one was open for 0% of the time, Pallas kernels for 11%

profile of v10, /device:TPU:0, one launch (start us, length us, event | category | flops | bytes accessed | tf_op | source)
XLA Modules:
  0.0 84.4 jit_solution(10266902451299903597)
XLA Ops:
  0.7 3.5 %back_messages.1 = (bf16[256,256]{1,0:T(8,128)(2,1)S(1)}, bf16[3,256,256]{2,1,0:T(8,128)(2,1)S(1)}, bf16[2,256,256]{2,1,0:T(8,128)(2,1)S(1)}) custom-call(s32[16]{0:T(128)} %bitcast.29, s32[16]{0:T(128)} %slot_ref.7, bf16[16,128,128]{2,1,0:T(8,128)(2,1)} %tiles_ref.7, bf16[227,2048]{1,0:T(8,128)(2,1)} %bitcast.13), custom_call_target="tpu_custom_call" | custom-call | flops 1 | bytes 1 | tf_op jit(solution)/shard_map/back_messages/pallas_call | solution.py:412
  4.1 3.0 %collective-permute-start.4 = (bf16[3,256,256]{2,1,0:T(8,128)(2,1)S(1)}, bf16[3,256,256]{2,1,0:T(8,128)(2,1)S(1)}, u32[]{:S(2)}, u32[]{:S(2)}) collective-permute-start(bf16[3,256,256]{2,1,0:T(8,128)(2,1)S(1)} %get-tuple-element.42), channel_id=1, source_target_pairs={{0,2},{2,0},{1,3},{3,1},{4,6},{6,4},{5,7},{7,5},{8,10},{10,8},{9,1... | collective-permute-start | bytes 1179656 | tf_op jit(solution)/shard_map/ppermute | solution.py:402
  7.2 2.6 %encode.2 = (bf16[2,256,256]{2,1,0:T(8,128)(2,1)S(1)}, bf16[2,256,256]{2,1,0:T(8,128)(2,1)S(1)}, bf16[2,256,256]{2,1,0:T(8,128)(2,1)S(1)}, bf16[1024,256]{1,0:T(8,128)(2,1)S(1)}) custom-call(s32[16]{0:T(128)} %bitcast.30, s32[16]{0:T(128)} %slot_ref.7, bf16[256,256]{1,0:T(8,128)(2,1)S(1)} %get-tuple-element.36.after_ref.back_ref, ...), custom_call_target="tpu_custom_call" | custom-call | flops 1 | bytes 1 | tf_op jit(solution)/shard_map/encode/pallas_call | solution.py:430
  9.8 1.6 %collective-permute-start.1 = (bf16[2,256,256]{2,1,0:T(8,128)(2,1)S(1)}, bf16[2,256,256]{2,1,0:T(8,128)(2,1)S(1)}, u32[]{:S(2)}, u32[]{:S(2)}) collective-permute-start(bf16[2,256,256]{2,1,0:T(8,128)(2,1)S(1)} %get-tuple-element.39), channel_id=1, source_target_pairs={{0,4},{4,0},{8,12},{12,8},{1,5},{5,1},{9,13},{13,9},{2,6},{6,2},{1... | collective-permute-start | bytes 786440 | tf_op jit(solution)/shard_map/ppermute | solution.py:344
  13.5 2.3 %encode.3 = (bf16[2,256,256]{2,1,0:T(8,128)(2,1)S(1)}, bf16[2,256,256]{2,1,0:T(8,128)(2,1)S(1)}, bf16[2,256,256]{2,1,0:T(8,128)(2,1)S(1)}, bf16[1024,256]{1,0:T(8,128)(2,1)S(1)}) custom-call(s32[16]{0:T(128)} %bitcast.31, s32[16]{0:T(128)} %slot_ref.7, bf16[2,256,256]{2,1,0:T(8,128)(2,1)S(1)} %get-tuple-element.37.after_ref.refs_1_.own_a, ...), custom_call_target="tpu_custom_call" | custom-call | flops 1 | bytes 1 | tf_op jit(solution)/shard_map/encode/pallas_call | solution.py:430
  15.8 4.4 %collective-permute-start.8 = (bf16[2,256,256]{2,1,0:T(8,128)(2,1)S(1)}, bf16[2,256,256]{2,1,0:T(8,128)(2,1)S(1)}, u32[]{:S(2)}, u32[]{:S(2)}) collective-permute-start(bf16[2,256,256]{2,1,0:T(8,128)(2,1)S(1)} %get-tuple-element.48), channel_id=1, source_target_pairs={{0,4},{4,0},{8,12},{12,8},{1,5},{5,1},{9,13},{13,9},{2,6},{6,2},{1... | collective-permute-start | bytes 786440 | tf_op jit(solution)/shard_map/ppermute | solution.py:344
  21.7 1.8 %collective-permute-start.5 = (bf16[256,256]{1,0:T(8,128)(2,1)S(1)}, bf16[256,256]{1,0:T(8,128)(2,1)S(1)}, u32[]{:S(2)}, u32[]{:S(2)}) collective-permute-start(bf16[256,256]{1,0:T(8,128)(2,1)S(1)} %get-tuple-element.43), channel_id=1, source_target_pairs={{0,4},{4,0},{8,12},{12,8},{1,5},{5,1},{9,13},{13,9},{2,6},{6,2},{1... | collective-permute-start | bytes 393224 | tf_op jit(solution)/shard_map/ppermute | solution.py:344
  24.2 2.2 %collective-permute-done.3.refs_0_.moved_a = bf16[256,256]{1,0:T(8,128)(2,1)S(1)} collective-permute-done((bf16[256,256]{1,0:T(8,128)(2,1)S(1)}, bf16[256,256]{1,0:T(8,128)(2,1)S(1)}, u32[]{:S(2)}, u32[]{:S(2)}) %collective-permute-start.3) | collective-permute-done | bytes 131104 | tf_op jit(solution)/shard_map/ppermute | solution.py:402
  26.4 3.3 %collective-permute-done.5.refs_1_.back_even_ref = bf16[256,256]{1,0:T(8,128)(2,1)S(1)} collective-permute-done((bf16[256,256]{1,0:T(8,128)(2,1)S(1)}, bf16[256,256]{1,0:T(8,128)(2,1)S(1)}, u32[]{:S(2)}, u32[]{:S(2)}) %collective-permute-start.5) | collective-permute-done | bytes 131104 | tf_op jit(solution)/shard_map/ppermute | solution.py:344
  31.6 4.9 %collective-permute-done.10.moved_b = bf16[256,256]{1,0:T(8,128)(2,1)S(1)} collective-permute-done((bf16[256,256]{1,0:T(8,128)(2,1)S(1)}, bf16[256,256]{1,0:T(8,128)(2,1)S(1)}, u32[]{:S(2)}, u32[]{:S(2)}) %collective-permute-start.10) | collective-permute-done | bytes 131104 | tf_op jit(solution)/shard_map/ppermute | solution.py:402
  36.6 2.8 %node_update_and_gradients.1 = (bf16[256,256]{1,0:T(8,128)(2,1)S(1)}, f32[1024,256]{1,0:T(8,128)S(1)}, bf16[1024,256]{1,0:T(8,128)(2,1)S(1)}, bf16[256,256]{1,0:T(8,128)(2,1)S(1)}, f32[4,2,64,256]{3,2,1,0:T(8,128)}) custom-call(bf16[2,256,256]{2,1,0:T(8,128)(2,1)S(1)} %get-tuple-element.37.after_ref.refs_1_.own_a, ...), custom_call_target="tpu_custom_call" | custom-call | flops 1 | bytes 1 | tf_op jit(solution)/shard_map/node_update_and_gradients/pallas_call | solution.py:481
  39.5 1.9 %collective-permute-done.14.got_ref = bf16[1024,256]{1,0:T(8,128)(2,1)S(1)} collective-permute-done((bf16[1024,256]{1,0:T(8,128)(2,1)S(1)}, bf16[1024,256]{1,0:T(8,128)(2,1)S(1)}, u32[]{:S(2)}, u32[]{:S(2)}) %collective-permute-start.14) | collective-permute-done | bytes 524320 | tf_op jit(solution)/shard_map/ppermute | solution.py:344
  42.2 1.5 %collective-permute-start.15 = (bf16[256,256]{1,0:T(8,128)(2,1)S(1)}, bf16[256,256]{1,0:T(8,128)(2,1)S(1)}, u32[]{:S(2)}, u32[]{:S(2)}) collective-permute-start(bf16[256,256]{1,0:T(8,128)(2,1)S(1)} %get-tuple-element.55), channel_id=1, source_target_pairs={{0,2},{1,5},{2,0},{3,7},{4,6},{5,1},{6,4},{7,3},{8,10},{9,13},{10,... | collective-permute-start | bytes 393224 | tf_op jit(solution)/shard_map/ppermute | solution.py:379
  44.4 5.2 %collective-permute-start.19 = (bf16[256,256]{1,0:T(8,128)(2,1)S(1)}, bf16[256,256]{1,0:T(8,128)(2,1)S(1)}, u32[]{:S(2)}, u32[]{:S(2)}) collective-permute-start(bf16[256,256]{1,0:T(8,128)(2,1)S(1)} %get-tuple-element.62.proj_ref), channel_id=1, source_target_pairs={{0,4},{4,0},{8,12},{12,8},{1,5},{5,1},{9,13},{13,9},{2,6},{6,2},{1... | collective-permute-start | bytes 393224 | tf_op jit(solution)/shard_map/ppermute | solution.py:344
  50.4 1.4 %collective-permute-start.17 = (bf16[128,256]{1,0:T(8,128)(2,1)S(1)}, bf16[128,256]{1,0:T(8,128)(2,1)S(1)}, u32[]{:S(2)}, u32[]{:S(2)}) collective-permute-start(bf16[128,256]{1,0:T(8,128)(2,1)S(1)} %get-tuple-element.60.refs_0_), channel_id=1, source_target_pairs={{0,4},{1,9},{2,6},{3,11},{4,0},{5,13},{6,2},{7,15},{8,12},{9,1},{1... | collective-permute-start | bytes 196616 | tf_op jit(solution)/shard_map/ppermute | solution.py:379
  51.8 2.3 %collective-permute-done.18.got_ref = bf16[128,256]{1,0:T(8,128)(2,1)S(1)} collective-permute-done((bf16[128,256]{1,0:T(8,128)(2,1)S(1)}, bf16[128,256]{1,0:T(8,128)(2,1)S(1)}, u32[]{:S(2)}, u32[]{:S(2)}) %collective-permute-start.18) | collective-permute-done | bytes 65568 | tf_op jit(solution)/shard_map/ppermute | solution.py:379
  55.8 3.1 %collective-permute-start.21 = (bf16[128,256]{1,0:T(8,128)(2,1)S(1)}, bf16[128,256]{1,0:T(8,128)(2,1)S(1)}, u32[]{:S(2)}, u32[]{:S(2)}) collective-permute-start(bf16[128,256]{1,0:T(8,128)(2,1)S(1)} %add_whole.4.refs_0_.kept_ref), channel_id=1, source_target_pairs={{0,8},{1,3},{2,10},{3,1},{4,12},{5,7},{6,14},{7,5},{8,0},{9,11},{1... | collective-permute-start | bytes 196616 | tf_op jit(solution)/shard_map/ppermute | solution.py:379
  58.9 2.2 %collective-permute-done.21.got_ref = bf16[128,256]{1,0:T(8,128)(2,1)S(1)} collective-permute-done((bf16[128,256]{1,0:T(8,128)(2,1)S(1)}, bf16[128,256]{1,0:T(8,128)(2,1)S(1)}, u32[]{:S(2)}, u32[]{:S(2)}) %collective-permute-start.21) | collective-permute-done | bytes 65568 | tf_op jit(solution)/shard_map/ppermute | solution.py:379
  61.2 1.8 %collective-permute-start.22 = (bf16[128,256]{1,0:T(8,128)(2,1)S(1)}, bf16[128,256]{1,0:T(8,128)(2,1)S(1)}, u32[]{:S(2)}, u32[]{:S(2)}) collective-permute-start(bf16[128,256]{1,0:T(8,128)(2,1)S(1)} %add_whole.6.refs_0_.mine_ref), channel_id=1, source_target_pairs={{0,4},{1,9},{2,6},{3,11},{4,0},{5,13},{6,2},{7,15},{8,12},{9,1},{1... | collective-permute-start | bytes 196616 | tf_op jit(solution)/shard_map/ppermute | solution.py:379
  63.0 4.9 %collective-permute-start.25 = (bf16[3,256,256]{2,1,0:T(8,128)(2,1)S(1)}, bf16[3,256,256]{2,1,0:T(8,128)(2,1)S(1)}, u32[]{:S(2)}, u32[]{:S(2)}) collective-permute-start(bf16[3,256,256]{2,1,0:T(8,128)(2,1)S(1)} %pack_nodes.1), channel_id=1, source_target_pairs={{0,1},{1,0},{2,3},{3,2},{4,5},{5,4},{6,7},{7,6},{8,9},{9,8},{10,11... | collective-permute-start | bytes 1179656 | tf_op jit(solution)/shard_map/ppermute | solution.py:344
  68.0 4.0 %collective-permute-start.26 = (bf16[3,256,256]{2,1,0:T(8,128)(2,1)S(1)}, bf16[3,256,256]{2,1,0:T(8,128)(2,1)S(1)}, u32[]{:S(2)}, u32[]{:S(2)}) collective-permute-start(bf16[3,256,256]{2,1,0:T(8,128)(2,1)S(1)} %hold_nodes.1), channel_id=1, source_target_pairs={{0,1},{1,0},{2,3},{3,2},{4,5},{5,4},{6,7},{7,6},{8,9},{9,8},{10,11... | collective-permute-start | bytes 1179656 | tf_op jit(solution)/shard_map/ppermute | solution.py:344
  72.2 4.8 %collective-permute-done.28.got_ref = bf16[128,256]{1,0:T(8,128)(2,1)S(1)} collective-permute-done((bf16[128,256]{1,0:T(8,128)(2,1)S(1)}, bf16[128,256]{1,0:T(8,128)(2,1)S(1)}, u32[]{:S(2)}, u32[]{:S(2)}) %collective-permute-start.28) | collective-permute-done | bytes 65568 | tf_op jit(solution)/shard_map/ppermute | solution.py:379
  77.6 1.5 %collective-permute-start.27 = (bf16[256,256]{1,0:T(8,128)(2,1)S(1)}, bf16[256,256]{1,0:T(8,128)(2,1)S(1)}, u32[]{:S(2)}, u32[]{:S(2)}) collective-permute-start(bf16[256,256]{1,0:T(8,128)(2,1)S(1)} %join.2.after_ref.mine_ref.refs_0_), channel_id=1, source_target_pairs={{0,2},{1,5},{2,0},{3,7},{4,6},{5,1},{6,4},{7,3},{8,10},{9,13},{10,... | collective-permute-start | bytes 393224 | tf_op jit(solution)/shard_map/ppermute | solution.py:379
  79.8 2.0 %decode.1.after_ref.refs_0_ = bf16[227,1024]{1,0:T(8,128)(2,1)} custom-call(s32[16]{0:T(128)} %bitcast.32, s32[16]{0:T(128)} %slot_ref.7, bf16[16,128,128]{2,1,0:T(8,128)(2,1)S(1)} %copy-done, f32[227,1024]{1,0:T(8,128)S(1)} %get-tuple-element.47.base_ref, bf16[12,64,256]{2,1,0:T(8,128)(2,1)S(1)} %bitcast.18, bf16[12,64,256]{2,1,0:T(8,128)(2,1)S(1)} %bitcast.17, ...), custom_call_target="tpu_custom_call" | custom-call | flops 1 | bytes 1 | tf_op jit(solution)/shard_map/decode/pallas_call | solution.py:562
  (77 shorter events, 14.2 us)
Async XLA Ops:
  4.1 17.5 %collective-permute-start.4 = (bf16[3,256,256]{2,1,0:T(8,128)(2,1)S(1)}, bf16[3,256,256]{2,1,0:T(8,128)(2,1)S(1)}, u32[]{:S(2)}, u32[]{:S(2)}) collective-permute-start(bf16[3,256,256]{2,1,0:T(8,128)(2,1)S(1)} %get-tuple-element.42), channel_id=1, source_target_pairs={{0,2},{2,0},{1,3},{3,1},{4,6},{6,4},{5,7},{7,5},{8,10},{10,8},{9,1... | collective-permute-start | bytes 1179656 | tf_op jit(solution)/shard_map/ppermute | solution.py:402
  9.8 10.5 %collective-permute-start.1 = (bf16[2,256,256]{2,1,0:T(8,128)(2,1)S(1)}, bf16[2,256,256]{2,1,0:T(8,128)(2,1)S(1)}, u32[]{:S(2)}, u32[]{:S(2)}) collective-permute-start(bf16[2,256,256]{2,1,0:T(8,128)(2,1)S(1)} %get-tuple-element.39), channel_id=1, source_target_pairs={{0,4},{4,0},{8,12},{12,8},{1,5},{5,1},{9,13},{13,9},{2,6},{6,2},{1... | collective-permute-start | bytes 786440 | tf_op jit(solution)/shard_map/ppermute | solution.py:344
  11.4 9.5 %collective-permute-start.2 = (bf16[2,256,256]{2,1,0:T(8,128)(2,1)S(1)}, bf16[2,256,256]{2,1,0:T(8,128)(2,1)S(1)}, u32[]{:S(2)}, u32[]{:S(2)}) collective-permute-start(bf16[2,256,256]{2,1,0:T(8,128)(2,1)S(1)} %get-tuple-element.40), channel_id=1, source_target_pairs={{0,0},{4,8},{8,4},{12,12},{1,1},{5,9},{9,5},{13,13},{2,2},{6,10},{... | collective-permute-start | bytes 786440 | tf_op jit(solution)/shard_map/ppermute | solution.py:344
  12.2 11.3 %collective-permute-start.7 = (bf16[227,256]{1,0:T(8,128)(2,1)S(1)}, bf16[227,256]{1,0:T(8,128)(2,1)S(1)}, u32[]{:S(2)}, u32[]{:S(2)}) collective-permute-start(bf16[227,256]{1,0:T(8,128)(2,1)S(1)} %bitcast.19), channel_id=1, source_target_pairs={{0,1},{1,0},{2,3},{3,2},{4,5},{5,4},{6,7},{7,6},{8,9},{9,8},{10,11... | collective-permute-start | bytes 348680 | tf_op jit(solution)/shard_map/ppermute | solution.py:344
  15.8 15.1 %collective-permute-start.8 = (bf16[2,256,256]{2,1,0:T(8,128)(2,1)S(1)}, bf16[2,256,256]{2,1,0:T(8,128)(2,1)S(1)}, u32[]{:S(2)}, u32[]{:S(2)}) collective-permute-start(bf16[2,256,256]{2,1,0:T(8,128)(2,1)S(1)} %get-tuple-element.48), channel_id=1, source_target_pairs={{0,4},{4,0},{8,12},{12,8},{1,5},{5,1},{9,13},{13,9},{2,6},{6,2},{1... | collective-permute-start | bytes 786440 | tf_op jit(solution)/shard_map/ppermute | solution.py:344
  20.3 10.7 %collective-permute-start.9 = (bf16[2,256,256]{2,1,0:T(8,128)(2,1)S(1)}, bf16[2,256,256]{2,1,0:T(8,128)(2,1)S(1)}, u32[]{:S(2)}, u32[]{:S(2)}) collective-permute-start(bf16[2,256,256]{2,1,0:T(8,128)(2,1)S(1)} %get-tuple-element.49), channel_id=1, source_target_pairs={{0,0},{4,8},{8,4},{12,12},{1,1},{5,9},{9,5},{13,13},{2,2},{6,10},{... | collective-permute-start | bytes 786440 | tf_op jit(solution)/shard_map/ppermute | solution.py:344
  21.0 5.3 %collective-permute-start.3 = (bf16[256,256]{1,0:T(8,128)(2,1)S(1)}, bf16[256,256]{1,0:T(8,128)(2,1)S(1)}, u32[]{:S(2)}, u32[]{:S(2)}) collective-permute-start(bf16[256,256]{1,0:T(8,128)(2,1)S(1)} %add_east.2), channel_id=1, source_target_pairs={{0,2},{2,0},{1,3},{3,1},{4,6},{6,4},{5,7},{7,5},{8,10},{10,8},{9,1... | collective-permute-start | bytes 393224 | tf_op jit(solution)/shard_map/ppermute | solution.py:402
  21.7 8.0 %collective-permute-start.5 = (bf16[256,256]{1,0:T(8,128)(2,1)S(1)}, bf16[256,256]{1,0:T(8,128)(2,1)S(1)}, u32[]{:S(2)}, u32[]{:S(2)}) collective-permute-start(bf16[256,256]{1,0:T(8,128)(2,1)S(1)} %get-tuple-element.43), channel_id=1, source_target_pairs={{0,4},{4,0},{8,12},{12,8},{1,5},{5,1},{9,13},{13,9},{2,6},{6,2},{1... | collective-permute-start | bytes 393224 | tf_op jit(solution)/shard_map/ppermute | solution.py:344
  23.5 6.2 %collective-permute-start.6 = (bf16[256,256]{1,0:T(8,128)(2,1)S(1)}, bf16[256,256]{1,0:T(8,128)(2,1)S(1)}, u32[]{:S(2)}, u32[]{:S(2)}) collective-permute-start(bf16[256,256]{1,0:T(8,128)(2,1)S(1)} %get-tuple-element.44), channel_id=1, source_target_pairs={{0,0},{4,8},{8,4},{12,12},{1,1},{5,9},{9,5},{13,13},{2,2},{6,10},{... | collective-permute-start | bytes 393224 | tf_op jit(solution)/shard_map/ppermute | solution.py:344
  26.4 5.3 %collective-permute-start.11 = (bf16[512,256]{1,0:T(8,128)(2,1)S(1)}, bf16[512,256]{1,0:T(8,128)(2,1)S(1)}, u32[]{:S(2)}, u32[]{:S(2)}) collective-permute-start(bf16[512,256]{1,0:T(8,128)(2,1)S(1)} %copy-done.4), channel_id=1, source_target_pairs={{0,1},{1,0},{2,3},{3,2},{4,5},{5,4},{6,7},{7,6},{8,9},{9,8},{10,11... | collective-permute-start | bytes 786440 | tf_op jit(solution)/shard_map/ppermute | solution.py:344
  31.0 5.5 %collective-permute-start.10 = (bf16[256,256]{1,0:T(8,128)(2,1)S(1)}, bf16[256,256]{1,0:T(8,128)(2,1)S(1)}, u32[]{:S(2)}, u32[]{:S(2)}) collective-permute-start(bf16[256,256]{1,0:T(8,128)(2,1)S(1)} %add_east.3), channel_id=1, source_target_pairs={{0,2},{2,0},{1,3},{3,1},{4,6},{6,4},{5,7},{7,5},{8,10},{10,8},{9,1... | collective-permute-start | bytes 393224 | tf_op jit(solution)/shard_map/ppermute | solution.py:402
  41.6 7.9 %collective-permute-start.16 = (bf16[256,256]{1,0:T(8,128)(2,1)S(1)}, bf16[256,256]{1,0:T(8,128)(2,1)S(1)}, u32[]{:S(2)}, u32[]{:S(2)}) collective-permute-start(bf16[256,256]{1,0:T(8,128)(2,1)S(1)} %get-tuple-element.57), channel_id=1, source_target_pairs={{0,2},{1,5},{2,0},{3,7},{4,6},{5,1},{6,4},{7,3},{8,10},{9,13},{10,... | collective-permute-start | bytes 393224 | tf_op jit(solution)/shard_map/ppermute | solution.py:379
  42.2 8.1 %collective-permute-start.15 = (bf16[256,256]{1,0:T(8,128)(2,1)S(1)}, bf16[256,256]{1,0:T(8,128)(2,1)S(1)}, u32[]{:S(2)}, u32[]{:S(2)}) collective-permute-start(bf16[256,256]{1,0:T(8,128)(2,1)S(1)} %get-tuple-element.55), channel_id=1, source_target_pairs={{0,2},{1,5},{2,0},{3,7},{4,6},{5,1},{6,4},{7,3},{8,10},{9,13},{10,... | collective-permute-start | bytes 393224 | tf_op jit(solution)/shard_map/ppermute | solution.py:379
  43.7 11.4 %collective-permute-start.20 = (bf16[256,256]{1,0:T(8,128)(2,1)S(1)}, bf16[256,256]{1,0:T(8,128)(2,1)S(1)}, u32[]{:S(2)}, u32[]{:S(2)}) collective-permute-start(bf16[256,256]{1,0:T(8,128)(2,1)S(1)} %get-tuple-element.62.proj_ref), channel_id=1, source_target_pairs={{0,0},{4,8},{8,4},{12,12},{1,1},{5,9},{9,5},{13,13},{2,2},{6,10},{... | collective-permute-start | bytes 393224 | tf_op jit(solution)/shard_map/ppermute | solution.py:344
  44.4 10.8 %collective-permute-start.19 = (bf16[256,256]{1,0:T(8,128)(2,1)S(1)}, bf16[256,256]{1,0:T(8,128)(2,1)S(1)}, u32[]{:S(2)}, u32[]{:S(2)}) collective-permute-start(bf16[256,256]{1,0:T(8,128)(2,1)S(1)} %get-tuple-element.62.proj_ref), channel_id=1, source_target_pairs={{0,4},{4,0},{8,12},{12,8},{1,5},{5,1},{9,13},{13,9},{2,6},{6,2},{1... | collective-permute-start | bytes 393224 | tf_op jit(solution)/shard_map/ppermute | solution.py:344
  55.2 12.8 %collective-permute-start.24 = (bf16[3,256,256]{2,1,0:T(8,128)(2,1)S(1)}, bf16[3,256,256]{2,1,0:T(8,128)(2,1)S(1)}, u32[]{:S(2)}, u32[]{:S(2)}) collective-permute-start(bf16[3,256,256]{2,1,0:T(8,128)(2,1)S(1)} %pack_nodes.1), channel_id=1, source_target_pairs={{2,0},{0,2},{3,1},{1,3},{6,4},{4,6},{7,5},{5,7},{10,8},{8,10},{11,... | collective-permute-start | bytes 1179656 | tf_op jit(solution)/shard_map/ppermute | solution.py:526
  55.8 5.4 %collective-permute-start.21 = (bf16[128,256]{1,0:T(8,128)(2,1)S(1)}, bf16[128,256]{1,0:T(8,128)(2,1)S(1)}, u32[]{:S(2)}, u32[]{:S(2)}) collective-permute-start(bf16[128,256]{1,0:T(8,128)(2,1)S(1)} %add_whole.4.refs_0_.kept_ref), channel_id=1, source_target_pairs={{0,8},{1,3},{2,10},{3,1},{4,12},{5,7},{6,14},{7,5},{8,0},{9,11},{1... | collective-permute-start | bytes 196616 | tf_op jit(solution)/shard_map/ppermute | solution.py:379
  58.9 9.0 %collective-permute-start.23 = (bf16[128,256]{1,0:T(8,128)(2,1)S(1)}, bf16[128,256]{1,0:T(8,128)(2,1)S(1)}, u32[]{:S(2)}, u32[]{:S(2)}) collective-permute-start(bf16[128,256]{1,0:T(8,128)(2,1)S(1)} %add_whole.5.after_ref.refs_0_.kept_ref), channel_id=1, source_target_pairs={{0,8},{1,3},{2,10},{3,1},{4,12},{5,7},{6,14},{7,5},{8,0},{9,11},{1... | collective-permute-start | bytes 196616 | tf_op jit(solution)/shard_map/ppermute | solution.py:379
  61.2 6.8 %collective-permute-start.22 = (bf16[128,256]{1,0:T(8,128)(2,1)S(1)}, bf16[128,256]{1,0:T(8,128)(2,1)S(1)}, u32[]{:S(2)}, u32[]{:S(2)}) collective-permute-start(bf16[128,256]{1,0:T(8,128)(2,1)S(1)} %add_whole.6.refs_0_.mine_ref), channel_id=1, source_target_pairs={{0,4},{1,9},{2,6},{3,11},{4,0},{5,13},{6,2},{7,15},{8,12},{9,1},{1... | collective-permute-start | bytes 196616 | tf_op jit(solution)/shard_map/ppermute | solution.py:379
  63.0 16.8 %collective-permute-start.25 = (bf16[3,256,256]{2,1,0:T(8,128)(2,1)S(1)}, bf16[3,256,256]{2,1,0:T(8,128)(2,1)S(1)}, u32[]{:S(2)}, u32[]{:S(2)}) collective-permute-start(bf16[3,256,256]{2,1,0:T(8,128)(2,1)S(1)} %pack_nodes.1), channel_id=1, source_target_pairs={{0,1},{1,0},{2,3},{3,2},{4,5},{5,4},{6,7},{7,6},{8,9},{9,8},{10,11... | collective-permute-start | bytes 1179656 | tf_op jit(solution)/shard_map/ppermute | solution.py:344
  68.0 11.8 %collective-permute-start.26 = (bf16[3,256,256]{2,1,0:T(8,128)(2,1)S(1)}, bf16[3,256,256]{2,1,0:T(8,128)(2,1)S(1)}, u32[]{:S(2)}, u32[]{:S(2)}) collective-permute-start(bf16[3,256,256]{2,1,0:T(8,128)(2,1)S(1)} %hold_nodes.1), channel_id=1, source_target_pairs={{0,1},{1,0},{2,3},{3,2},{4,5},{5,4},{6,7},{7,6},{8,9},{9,8},{10,11... | collective-permute-start | bytes 1179656 | tf_op jit(solution)/shard_map/ppermute | solution.py:344
  72.0 7.1 %collective-permute-start.30 = (bf16[256,256]{1,0:T(8,128)(2,1)S(1)}, bf16[256,256]{1,0:T(8,128)(2,1)S(1)}, u32[]{:S(2)}, u32[]{:S(2)}) collective-permute-start(bf16[256,256]{1,0:T(8,128)(2,1)S(1)} %get-tuple-element.65), channel_id=1, source_target_pairs={{0,1},{1,0},{2,3},{3,2},{4,5},{5,4},{6,7},{7,6},{8,9},{9,8},{10,11... | collective-permute-start | bytes 393224 | tf_op jit(solution)/shard_map/ppermute | solution.py:344
  77.0 5.0 %collective-permute-start.29 = (bf16[256,256]{1,0:T(8,128)(2,1)S(1)}, bf16[256,256]{1,0:T(8,128)(2,1)S(1)}, u32[]{:S(2)}, u32[]{:S(2)}) collective-permute-start(bf16[256,256]{1,0:T(8,128)(2,1)S(1)} %join.3.mine_ref), channel_id=1, source_target_pairs={{0,2},{1,5},{2,0},{3,7},{4,6},{5,1},{6,4},{7,3},{8,10},{9,13},{10,... | collective-permute-start | bytes 393224 | tf_op jit(solution)/shard_map/ppermute | solution.py:379
  77.6 5.8 %collective-permute-start.27 = (bf16[256,256]{1,0:T(8,128)(2,1)S(1)}, bf16[256,256]{1,0:T(8,128)(2,1)S(1)}, u32[]{:S(2)}, u32[]{:S(2)}) collective-permute-start(bf16[256,256]{1,0:T(8,128)(2,1)S(1)} %join.2.after_ref.mine_ref.refs_0_), channel_id=1, source_target_pairs={{0,2},{1,5},{2,0},{3,7},{4,6},{5,1},{6,4},{7,3},{8,10},{9,13},{10,... | collective-permute-start | bytes 393224 | tf_op jit(solution)/shard_map/ppermute | solution.py:379
  (15 other events, 74.6 us)

commit v11 on v9

--- a/solution.py
+++ b/solution.py
@@ -518,7 +518,7 @@
 
     def step_call(kernel, name, chain, step, out_rows, scratch=()):
         kept, given = chain[0], chain[-1]
-        after = [latest] if latest is not None else []
+        after = [latest] if latest is not None else [proj_even, proj_odd]
         made = call(
             kernel, name, [vmem()] * 2 + [anywhere()] * len(after), [vmem()] * len(out_rows),
             [shape_of((rows, width), BF16) for rows in out_rows], 1, 1, scratch=scratch,
@@ -568,7 +568,7 @@
     mine_picked, theirs_picked = call(
         pick_kernel, "pick_nodes", [smem()] * 2 + [anywhere()] + [vmem()] * 2, [vmem()] * 2,
         [shape_of((blocks // 2, half, padded), BF16)] * 2, 1, 1,
-    )(device, slot, after_pick, trio.reshape(table_shape), east_trio.reshape(table_shape))
+    )(*routes, after_pick, trio.reshape(table_shape), east_trio.reshape(table_shape))
     grid_out_t = call(
         decode_kernel, "decode", [vmem()] * 4, vmem(),
         shape_of((channels, my_rows), BF16), 2 * my_rows * tile_rows * padded, 4e6,

time: 78.5 us -> 76.6 us (0.976)
  waiting for transfers between devices: 24.5 us -> 23.5 us
    ppermute x16, waiting for transfers between devices: 13.9 us -> 9.55 us  [along(): return lambda value: lax.ppermute(value, axis, pairs)]
    ppermute x10, waiting for transfers between devices: 10.6 us -> 14 us  [sum_swap(): return lax.ppermute(value, ('lat', 'lon', 'rep'), pairs)]
  transfers between devices with their start and end apart: 30 -> 30, of which waited for: 13 -> 15; matrix products, arithmetic and copies ran while one was open for 0% -> 0% of each run, Pallas kernels for 12% -> 12%
where the time goes in v11:
time: 76.6 us; the launch traced here: 76.3 us
  starting transfers between devices  34.2 us (45%)
  waiting for transfers between devices  23.5 us (31%)
  Pallas kernels  17.6 us (23%)
  between operations  0.93 us (1%)
    ppermute x16, starting transfers between devices, along(): return lambda value: lax.ppermute(value, axis, pairs)  17.1 us
    ppermute x10, waiting for transfers between devices, sum_swap(): return lax.ppermute(value, ('lat', 'lon', 'rep'), pairs)  14 us
    ppermute x10, starting transfers between devices, sum_swap(): return lax.ppermute(value, ('lat', 'lon', 'rep'), pairs)  11.8 us
    ppermute x16, waiting for transfers between devices, along(): return lambda value: lax.ppermute(value, axis, pairs)  9.55 us
    pallas_call x2, Pallas kernels, encode(): call(encode_kernel, 'encode', [smem(), smem(), anywhere()] + [vmem()] * 3...  5.08 us
    ppermute x3, starting transfers between devices, per_device(): to_east = lambda value: lax.ppermute(value, 'lon', east_pairs)  4.2 us
    pallas_call x1, Pallas kernels, per_device(): call(back_kernel, 'back_messages', [smem(), smem(), anywhere(), anywhere(...  3.49 us
    pallas_call x1, Pallas kernels, per_device(): call(node_kernel, 'node_update_and_gradients', sums_specs * 2 + [whole(em...  2.85 us
  transfers between devices with their start and end apart: 30, of which 15 were waited for; matrix products, arithmetic and copies ran while one was open for 0% of the time, Pallas kernels for 12%

profile of v11, /device:TPU:0, one launch (start us, length us, event | category | flops | bytes accessed | tf_op | source)
XLA Modules:
  0.0 76.3 jit_solution(1657160444958238030)
XLA Ops:
  0.7 3.5 %back_messages.1 = (bf16[256,256]{1,0:T(8,128)(2,1)S(1)}, bf16[3,256,256]{2,1,0:T(8,128)(2,1)S(1)}, bf16[2,256,256]{2,1,0:T(8,128)(2,1)S(1)}) custom-call(s32[16]{0:T(128)} %bitcast.25, s32[16]{0:T(128)} %slot_ref.7, bf16[16,128,128]{2,1,0:T(8,128)(2,1)} %tiles_ref.7, bf16[227,2048]{1,0:T(8,128)(2,1)} %bitcast.13), custom_call_target="tpu_custom_call" | custom-call | flops 1 | bytes 1 | tf_op jit(solution)/shard_map/back_messages/pallas_call | solution.py:422
  4.1 3.0 %collective-permute-start.4 = (bf16[3,256,256]{2,1,0:T(8,128)(2,1)S(1)}, bf16[3,256,256]{2,1,0:T(8,128)(2,1)S(1)}, u32[]{:S(2)}, u32[]{:S(2)}) collective-permute-start(bf16[3,256,256]{2,1,0:T(8,128)(2,1)S(1)} %get-tuple-element.45), channel_id=1, source_target_pairs={{0,2},{2,0},{1,3},{3,1},{4,6},{6,4},{5,7},{7,5},{8,10},{10,8},{9,1... | collective-permute-start | bytes 1179656 | tf_op jit(solution)/shard_map/ppermute | solution.py:412
  7.2 2.6 %encode.2 = (bf16[2,256,256]{2,1,0:T(8,128)(2,1)S(1)}, bf16[2,256,256]{2,1,0:T(8,128)(2,1)S(1)}, bf16[2,256,256]{2,1,0:T(8,128)(2,1)S(1)}, bf16[1024,256]{1,0:T(8,128)(2,1)S(1)}) custom-call(s32[16]{0:T(128)} %bitcast.26, s32[16]{0:T(128)} %slot_ref.7, bf16[256,256]{1,0:T(8,128)(2,1)S(1)} %get-tuple-element.38.after_ref.back_ref, ...), custom_call_target="tpu_custom_call" | custom-call | flops 1 | bytes 1 | tf_op jit(solution)/shard_map/encode/pallas_call | solution.py:440
  9.8 1.6 %collective-permute-start.2 = (bf16[2,256,256]{2,1,0:T(8,128)(2,1)S(1)}, bf16[2,256,256]{2,1,0:T(8,128)(2,1)S(1)}, u32[]{:S(2)}, u32[]{:S(2)}) collective-permute-start(bf16[2,256,256]{2,1,0:T(8,128)(2,1)S(1)} %get-tuple-element.43), channel_id=1, source_target_pairs={{0,4},{4,0},{8,12},{12,8},{1,5},{5,1},{9,13},{13,9},{2,6},{6,2},{1... | collective-permute-start | bytes 786440 | tf_op jit(solution)/shard_map/ppermute | solution.py:354
  12.8 2.5 %encode.3 = (bf16[2,256,256]{2,1,0:T(8,128)(2,1)S(1)}, bf16[2,256,256]{2,1,0:T(8,128)(2,1)S(1)}, bf16[2,256,256]{2,1,0:T(8,128)(2,1)S(1)}, bf16[1024,256]{1,0:T(8,128)(2,1)S(1)}) custom-call(s32[16]{0:T(128)} %bitcast.27, s32[16]{0:T(128)} %slot_ref.7, bf16[2,256,256]{2,1,0:T(8,128)(2,1)S(1)} %get-tuple-element.40.after_ref.refs_1_.own_a, ...), custom_call_target="tpu_custom_call" | custom-call | flops 1 | bytes 1 | tf_op jit(solution)/shard_map/encode/pallas_call | solution.py:440
  15.2 3.8 %collective-permute-start.6 = (bf16[2,256,256]{2,1,0:T(8,128)(2,1)S(1)}, bf16[2,256,256]{2,1,0:T(8,128)(2,1)S(1)}, u32[]{:S(2)}, u32[]{:S(2)}) collective-permute-start(bf16[2,256,256]{2,1,0:T(8,128)(2,1)S(1)} %get-tuple-element.47), channel_id=1, source_target_pairs={{0,4},{4,0},{8,12},{12,8},{1,5},{5,1},{9,13},{13,9},{2,6},{6,2},{1... | collective-permute-start | bytes 786440 | tf_op jit(solution)/shard_map/ppermute | solution.py:354
  20.8 4.9 %collective-permute-done.6.refs_2_.even_b = bf16[2,256,256]{2,1,0:T(8,128)(2,1)S(1)} collective-permute-done((bf16[2,256,256]{2,1,0:T(8,128)(2,1)S(1)}, bf16[2,256,256]{2,1,0:T(8,128)(2,1)S(1)}, u32[]{:S(2)}, u32[]{:S(2)}) %collective-permute-start.6) | collective-permute-done | bytes 262176 | tf_op jit(solution)/shard_map/ppermute | solution.py:354
  27.4 3.4 %collective-permute-start.10 = (bf16[256,256]{1,0:T(8,128)(2,1)S(1)}, bf16[256,256]{1,0:T(8,128)(2,1)S(1)}, u32[]{:S(2)}, u32[]{:S(2)}) collective-permute-start(bf16[256,256]{1,0:T(8,128)(2,1)S(1)} %get-tuple-element.50), channel_id=1, source_target_pairs={{0,4},{4,0},{8,12},{12,8},{1,5},{5,1},{9,13},{13,9},{2,6},{6,2},{1... | collective-permute-start | bytes 393224 | tf_op jit(solution)/shard_map/ppermute | solution.py:354
  32.3 2.4 %collective-permute-done.10.back_even_ref = bf16[256,256]{1,0:T(8,128)(2,1)S(1)} collective-permute-done((bf16[256,256]{1,0:T(8,128)(2,1)S(1)}, bf16[256,256]{1,0:T(8,128)(2,1)S(1)}, u32[]{:S(2)}, u32[]{:S(2)}) %collective-permute-start.10) | collective-permute-done | bytes 131104 | tf_op jit(solution)/shard_map/ppermute | solution.py:354
  34.7 2.9 %node_update_and_gradients.1 = (bf16[256,256]{1,0:T(8,128)(2,1)S(1)}, f32[1024,256]{1,0:T(8,128)S(1)}, bf16[1024,256]{1,0:T(8,128)(2,1)S(1)}, bf16[256,256]{1,0:T(8,128)(2,1)S(1)}, f32[4,2,64,256]{3,2,1,0:T(8,128)}) custom-call(bf16[2,256,256]{2,1,0:T(8,128)(2,1)S(1)} %get-tuple-element.40.after_ref.refs_1_.own_a, ...), custom_call_target="tpu_custom_call" | custom-call | flops 1 | bytes 1 | tf_op jit(solution)/shard_map/node_update_and_gradients/pallas_call | solution.py:491
  37.6 3.7 %collective-permute-start.17 = (bf16[256,256]{1,0:T(8,128)(2,1)S(1)}, bf16[256,256]{1,0:T(8,128)(2,1)S(1)}, u32[]{:S(2)}, u32[]{:S(2)}) collective-permute-start(bf16[256,256]{1,0:T(8,128)(2,1)S(1)} %get-tuple-element.60.proj_ref), channel_id=1, source_target_pairs={{0,4},{4,0},{8,12},{12,8},{1,5},{5,1},{9,13},{13,9},{2,6},{6,2},{1... | collective-permute-start | bytes 393224 | tf_op jit(solution)/shard_map/ppermute | solution.py:354
  42.2 1.1 %collective-permute-start.16 = (bf16[256,256]{1,0:T(8,128)(2,1)S(1)}, bf16[256,256]{1,0:T(8,128)(2,1)S(1)}, u32[]{:S(2)}, u32[]{:S(2)}) collective-permute-start(bf16[256,256]{1,0:T(8,128)(2,1)S(1)} %get-tuple-element.59), channel_id=1, source_target_pairs={{0,2},{1,5},{2,0},{3,7},{4,6},{5,1},{6,4},{7,3},{8,10},{9,13},{10,... | collective-permute-start | bytes 393224 | tf_op jit(solution)/shard_map/ppermute | solution.py:389
  44.3 1.1 %collective-permute-done.17.refs_0_.even_ref = bf16[256,256]{1,0:T(8,128)(2,1)S(1)} collective-permute-done((bf16[256,256]{1,0:T(8,128)(2,1)S(1)}, bf16[256,256]{1,0:T(8,128)(2,1)S(1)}, u32[]{:S(2)}, u32[]{:S(2)}) %collective-permute-start.17) | collective-permute-done | bytes 131104 | tf_op jit(solution)/shard_map/ppermute | solution.py:354
  45.4 1.8 %collective-permute-done.16.got_ref = bf16[256,256]{1,0:T(8,128)(2,1)S(1)} collective-permute-done((bf16[256,256]{1,0:T(8,128)(2,1)S(1)}, bf16[256,256]{1,0:T(8,128)(2,1)S(1)}, u32[]{:S(2)}, u32[]{:S(2)}) %collective-permute-start.16) | collective-permute-done | bytes 131104 | tf_op jit(solution)/shard_map/ppermute | solution.py:389
  47.3 1.3 %collective-permute-done.15.got_ref = bf16[256,256]{1,0:T(8,128)(2,1)S(1)} collective-permute-done((bf16[256,256]{1,0:T(8,128)(2,1)S(1)}, bf16[256,256]{1,0:T(8,128)(2,1)S(1)}, u32[]{:S(2)}, u32[]{:S(2)}) %collective-permute-start.15) | collective-permute-done | bytes 131104 | tf_op jit(solution)/shard_map/ppermute | solution.py:389
  48.7 1.1 %collective-permute-start.23 = (bf16[3,256,256]{2,1,0:T(8,128)(2,1)S(1)}, bf16[3,256,256]{2,1,0:T(8,128)(2,1)S(1)}, u32[]{:S(2)}, u32[]{:S(2)}) collective-permute-start(bf16[3,256,256]{2,1,0:T(8,128)(2,1)S(1)} %pack_nodes.1), channel_id=1, source_target_pairs={{2,0},{0,2},{3,1},{1,3},{6,4},{4,6},{7,5},{5,7},{10,8},{8,10},{11,... | collective-permute-start | bytes 1179656 | tf_op jit(solution)/shard_map/ppermute | solution.py:536
  49.9 2.5 %collective-permute-start.20 = (bf16[128,256]{1,0:T(8,128)(2,1)S(1)}, bf16[128,256]{1,0:T(8,128)(2,1)S(1)}, u32[]{:S(2)}, u32[]{:S(2)}) collective-permute-start(bf16[128,256]{1,0:T(8,128)(2,1)S(1)} %get-tuple-element.61.refs_0_), channel_id=1, source_target_pairs={{0,4},{1,9},{2,6},{3,11},{4,0},{5,13},{6,2},{7,15},{8,12},{9,1},{1... | collective-permute-start | bytes 196616 | tf_op jit(solution)/shard_map/ppermute | solution.py:389
  52.4 2.2 %collective-permute-done.20.got_ref = bf16[128,256]{1,0:T(8,128)(2,1)S(1)} collective-permute-done((bf16[128,256]{1,0:T(8,128)(2,1)S(1)}, bf16[128,256]{1,0:T(8,128)(2,1)S(1)}, u32[]{:S(2)}, u32[]{:S(2)}) %collective-permute-start.20) | collective-permute-done | bytes 65568 | tf_op jit(solution)/shard_map/ppermute | solution.py:389
  54.6 2.4 %collective-permute-start.22 = (bf16[128,256]{1,0:T(8,128)(2,1)S(1)}, bf16[128,256]{1,0:T(8,128)(2,1)S(1)}, u32[]{:S(2)}, u32[]{:S(2)}) collective-permute-start(bf16[128,256]{1,0:T(8,128)(2,1)S(1)} %add_whole.4.refs_0_.kept_ref), channel_id=1, source_target_pairs={{0,8},{1,3},{2,10},{3,1},{4,12},{5,7},{6,14},{7,5},{8,0},{9,11},{1... | collective-permute-start | bytes 196616 | tf_op jit(solution)/shard_map/ppermute | solution.py:389
  57.8 2.1 %collective-permute-done.22.got_ref = bf16[128,256]{1,0:T(8,128)(2,1)S(1)} collective-permute-done((bf16[128,256]{1,0:T(8,128)(2,1)S(1)}, bf16[128,256]{1,0:T(8,128)(2,1)S(1)}, u32[]{:S(2)}, u32[]{:S(2)}) %collective-permute-start.22) | collective-permute-done | bytes 65568 | tf_op jit(solution)/shard_map/ppermute | solution.py:389
  59.9 2.8 %collective-permute-done.21.got_ref = bf16[128,256]{1,0:T(8,128)(2,1)S(1)} collective-permute-done((bf16[128,256]{1,0:T(8,128)(2,1)S(1)}, bf16[128,256]{1,0:T(8,128)(2,1)S(1)}, u32[]{:S(2)}, u32[]{:S(2)}) %collective-permute-start.21) | collective-permute-done | bytes 65568 | tf_op jit(solution)/shard_map/ppermute | solution.py:389
  64.3 1.8 %collective-permute-start.27 = (bf16[128,256]{1,0:T(8,128)(2,1)S(1)}, bf16[128,256]{1,0:T(8,128)(2,1)S(1)}, u32[]{:S(2)}, u32[]{:S(2)}) collective-permute-start(bf16[128,256]{1,0:T(8,128)(2,1)S(1)} %add_whole.7.after_ref.refs_0_.mine_ref), channel_id=1, source_target_pairs={{0,4},{1,9},{2,6},{3,11},{4,0},{5,13},{6,2},{7,15},{8,12},{9,1},{1... | collective-permute-start | bytes 196616 | tf_op jit(solution)/shard_map/ppermute | solution.py:389
  66.8 1.8 %collective-permute-done.25.got_ref = bf16[128,256]{1,0:T(8,128)(2,1)S(1)} collective-permute-done((bf16[128,256]{1,0:T(8,128)(2,1)S(1)}, bf16[128,256]{1,0:T(8,128)(2,1)S(1)}, u32[]{:S(2)}, u32[]{:S(2)}) %collective-permute-start.25) | collective-permute-done | bytes 65568 | tf_op jit(solution)/shard_map/ppermute | solution.py:389
  72.2 1.2 %decode.1.after_ref.refs_0_ = bf16[227,1024]{1,0:T(8,128)(2,1)} custom-call(bf16[16,128,128]{2,1,0:T(8,128)(2,1)S(1)} %copy-done, f32[227,1024]{1,0:T(8,128)S(1)} %get-tuple-element.42.base_ref, bf16[8,64,256]{2,1,0:T(8,128)(2,1)S(1)} %get-tuple-element.65.mine_ref, bf16[8,64,256]{2,1,0:T(8,128)(2,1)S(1)} %collective-permute-done.24.got_ref), custom_call_target="tpu_custom_call" | custom-call | flops 1 | bytes 1 | tf_op jit(solution)/shard_map/decode/pallas_call | solution.py:572
  (75 shorter events, 17.7 us)
Async XLA Ops:
  4.1 15.8 %collective-permute-start.4 = (bf16[3,256,256]{2,1,0:T(8,128)(2,1)S(1)}, bf16[3,256,256]{2,1,0:T(8,128)(2,1)S(1)}, u32[]{:S(2)}, u32[]{:S(2)}) collective-permute-start(bf16[3,256,256]{2,1,0:T(8,128)(2,1)S(1)} %get-tuple-element.45), channel_id=1, source_target_pairs={{0,2},{2,0},{1,3},{3,1},{4,6},{6,4},{5,7},{7,5},{8,10},{10,8},{9,1... | collective-permute-start | bytes 1179656 | tf_op jit(solution)/shard_map/ppermute | solution.py:412
  9.8 10.1 %collective-permute-start.2 = (bf16[2,256,256]{2,1,0:T(8,128)(2,1)S(1)}, bf16[2,256,256]{2,1,0:T(8,128)(2,1)S(1)}, u32[]{:S(2)}, u32[]{:S(2)}) collective-permute-start(bf16[2,256,256]{2,1,0:T(8,128)(2,1)S(1)} %get-tuple-element.43), channel_id=1, source_target_pairs={{0,4},{4,0},{8,12},{12,8},{1,5},{5,1},{9,13},{13,9},{2,6},{6,2},{1... | collective-permute-start | bytes 786440 | tf_op jit(solution)/shard_map/ppermute | solution.py:354
  11.4 8.5 %collective-permute-start.3 = (bf16[2,256,256]{2,1,0:T(8,128)(2,1)S(1)}, bf16[2,256,256]{2,1,0:T(8,128)(2,1)S(1)}, u32[]{:S(2)}, u32[]{:S(2)}) collective-permute-start(bf16[2,256,256]{2,1,0:T(8,128)(2,1)S(1)} %get-tuple-element.44), channel_id=1, source_target_pairs={{0,0},{4,8},{8,4},{12,12},{1,1},{5,9},{9,5},{13,13},{2,2},{6,10},{... | collective-permute-start | bytes 786440 | tf_op jit(solution)/shard_map/ppermute | solution.py:354
  15.2 10.5 %collective-permute-start.6 = (bf16[2,256,256]{2,1,0:T(8,128)(2,1)S(1)}, bf16[2,256,256]{2,1,0:T(8,128)(2,1)S(1)}, u32[]{:S(2)}, u32[]{:S(2)}) collective-permute-start(bf16[2,256,256]{2,1,0:T(8,128)(2,1)S(1)} %get-tuple-element.47), channel_id=1, source_target_pairs={{0,4},{4,0},{8,12},{12,8},{1,5},{5,1},{9,13},{13,9},{2,6},{6,2},{1... | collective-permute-start | bytes 786440 | tf_op jit(solution)/shard_map/ppermute | solution.py:354
  19.0 6.7 %collective-permute-start.7 = (bf16[2,256,256]{2,1,0:T(8,128)(2,1)S(1)}, bf16[2,256,256]{2,1,0:T(8,128)(2,1)S(1)}, u32[]{:S(2)}, u32[]{:S(2)}) collective-permute-start(bf16[2,256,256]{2,1,0:T(8,128)(2,1)S(1)} %get-tuple-element.48), channel_id=1, source_target_pairs={{0,0},{4,8},{8,4},{12,12},{1,1},{5,9},{9,5},{13,13},{2,2},{6,10},{... | collective-permute-start | bytes 786440 | tf_op jit(solution)/shard_map/ppermute | solution.py:354
  19.9 11.0 %collective-permute-start.9 = (bf16[512,256]{1,0:T(8,128)(2,1)S(1)}, bf16[512,256]{1,0:T(8,128)(2,1)S(1)}, u32[]{:S(2)}, u32[]{:S(2)}) collective-permute-start(bf16[512,256]{1,0:T(8,128)(2,1)S(1)} %copy-done.4), channel_id=1, source_target_pairs={{0,1},{1,0},{2,3},{3,2},{4,5},{5,4},{6,7},{7,6},{8,9},{9,8},{10,11... | collective-permute-start | bytes 786440 | tf_op jit(solution)/shard_map/ppermute | solution.py:354
  20.0 6.2 %collective-permute-start.5 = (bf16[256,256]{1,0:T(8,128)(2,1)S(1)}, bf16[256,256]{1,0:T(8,128)(2,1)S(1)}, u32[]{:S(2)}, u32[]{:S(2)}) collective-permute-start(bf16[256,256]{1,0:T(8,128)(2,1)S(1)} %add_east.2), channel_id=1, source_target_pairs={{0,2},{2,0},{1,3},{3,1},{4,6},{6,4},{5,7},{7,5},{8,10},{10,8},{9,1... | collective-permute-start | bytes 393224 | tf_op jit(solution)/shard_map/ppermute | solution.py:412
  20.6 11.7 %collective-permute-start.12 = (bf16[512,256]{1,0:T(8,128)(2,1)S(1)}, bf16[512,256]{1,0:T(8,128)(2,1)S(1)}, u32[]{:S(2)}, u32[]{:S(2)}) collective-permute-start(bf16[512,256]{1,0:T(8,128)(2,1)S(1)} %copy-done.5), channel_id=1, source_target_pairs={{0,1},{1,0},{2,3},{3,2},{4,5},{5,4},{6,7},{7,6},{8,9},{9,8},{10,11... | collective-permute-start | bytes 786440 | tf_op jit(solution)/shard_map/ppermute | solution.py:354
  25.7 6.6 %collective-permute-start.13 = (bf16[256,512]{1,0:T(8,128)(2,1)S(1)}, bf16[256,512]{1,0:T(8,128)(2,1)S(1)}, u32[]{:S(2)}, u32[]{:S(2)}) collective-permute-start(bf16[256,512]{1,0:T(8,128)(2,1)S(1)} %copy-done.6), channel_id=1, source_target_pairs={{0,1},{1,0},{2,3},{3,2},{4,5},{5,4},{6,7},{7,6},{8,9},{9,8},{10,11... | collective-permute-start | bytes 786440 | tf_op jit(solution)/shard_map/ppermute | solution.py:354
  26.3 6.0 %collective-permute-start.8 = (bf16[256,256]{1,0:T(8,128)(2,1)S(1)}, bf16[256,256]{1,0:T(8,128)(2,1)S(1)}, u32[]{:S(2)}, u32[]{:S(2)}) collective-permute-start(bf16[256,256]{1,0:T(8,128)(2,1)S(1)} %add_east.3.after_ref), channel_id=1, source_target_pairs={{0,2},{2,0},{1,3},{3,1},{4,6},{6,4},{5,7},{7,5},{8,10},{10,8},{9,1... | collective-permute-start | bytes 393224 | tf_op jit(solution)/shard_map/ppermute | solution.py:412
  27.4 7.2 %collective-permute-start.10 = (bf16[256,256]{1,0:T(8,128)(2,1)S(1)}, bf16[256,256]{1,0:T(8,128)(2,1)S(1)}, u32[]{:S(2)}, u32[]{:S(2)}) collective-permute-start(bf16[256,256]{1,0:T(8,128)(2,1)S(1)} %get-tuple-element.50), channel_id=1, source_target_pairs={{0,4},{4,0},{8,12},{12,8},{1,5},{5,1},{9,13},{13,9},{2,6},{6,2},{1... | collective-permute-start | bytes 393224 | tf_op jit(solution)/shard_map/ppermute | solution.py:354
  37.6 7.8 %collective-permute-start.17 = (bf16[256,256]{1,0:T(8,128)(2,1)S(1)}, bf16[256,256]{1,0:T(8,128)(2,1)S(1)}, u32[]{:S(2)}, u32[]{:S(2)}) collective-permute-start(bf16[256,256]{1,0:T(8,128)(2,1)S(1)} %get-tuple-element.60.proj_ref), channel_id=1, source_target_pairs={{0,4},{4,0},{8,12},{12,8},{1,5},{5,1},{9,13},{13,9},{2,6},{6,2},{1... | collective-permute-start | bytes 393224 | tf_op jit(solution)/shard_map/ppermute | solution.py:354
  42.2 5.0 %collective-permute-start.16 = (bf16[256,256]{1,0:T(8,128)(2,1)S(1)}, bf16[256,256]{1,0:T(8,128)(2,1)S(1)}, u32[]{:S(2)}, u32[]{:S(2)}) collective-permute-start(bf16[256,256]{1,0:T(8,128)(2,1)S(1)} %get-tuple-element.59), channel_id=1, source_target_pairs={{0,2},{1,5},{2,0},{3,7},{4,6},{5,1},{6,4},{7,3},{8,10},{9,13},{10,... | collective-permute-start | bytes 393224 | tf_op jit(solution)/shard_map/ppermute | solution.py:389
  43.3 5.3 %collective-permute-start.15 = (bf16[256,256]{1,0:T(8,128)(2,1)S(1)}, bf16[256,256]{1,0:T(8,128)(2,1)S(1)}, u32[]{:S(2)}, u32[]{:S(2)}) collective-permute-start(bf16[256,256]{1,0:T(8,128)(2,1)S(1)} %get-tuple-element.57), channel_id=1, source_target_pairs={{0,2},{1,5},{2,0},{3,7},{4,6},{5,1},{6,4},{7,3},{8,10},{9,13},{10,... | collective-permute-start | bytes 393224 | tf_op jit(solution)/shard_map/ppermute | solution.py:389
  48.7 14.0 %collective-permute-start.23 = (bf16[3,256,256]{2,1,0:T(8,128)(2,1)S(1)}, bf16[3,256,256]{2,1,0:T(8,128)(2,1)S(1)}, u32[]{:S(2)}, u32[]{:S(2)}) collective-permute-start(bf16[3,256,256]{2,1,0:T(8,128)(2,1)S(1)} %pack_nodes.1), channel_id=1, source_target_pairs={{2,0},{0,2},{3,1},{1,3},{6,4},{4,6},{7,5},{5,7},{10,8},{8,10},{11,... | collective-permute-start | bytes 1179656 | tf_op jit(solution)/shard_map/ppermute | solution.py:536
  49.9 4.8 %collective-permute-start.20 = (bf16[128,256]{1,0:T(8,128)(2,1)S(1)}, bf16[128,256]{1,0:T(8,128)(2,1)S(1)}, u32[]{:S(2)}, u32[]{:S(2)}) collective-permute-start(bf16[128,256]{1,0:T(8,128)(2,1)S(1)} %get-tuple-element.61.refs_0_), channel_id=1, source_target_pairs={{0,4},{1,9},{2,6},{3,11},{4,0},{5,13},{6,2},{7,15},{8,12},{9,1},{1... | collective-permute-start | bytes 196616 | tf_op jit(solution)/shard_map/ppermute | solution.py:389
  52.4 4.8 %collective-permute-start.19 = (bf16[128,256]{1,0:T(8,128)(2,1)S(1)}, bf16[128,256]{1,0:T(8,128)(2,1)S(1)}, u32[]{:S(2)}, u32[]{:S(2)}) collective-permute-start(bf16[128,256]{1,0:T(8,128)(2,1)S(1)} %get-tuple-element.63.refs_0_.after_ref), channel_id=1, source_target_pairs={{0,4},{1,9},{2,6},{3,11},{4,0},{5,13},{6,2},{7,15},{8,12},{9,1},{1... | collective-permute-start | bytes 196616 | tf_op jit(solution)/shard_map/ppermute | solution.py:389
  54.6 5.2 %collective-permute-start.22 = (bf16[128,256]{1,0:T(8,128)(2,1)S(1)}, bf16[128,256]{1,0:T(8,128)(2,1)S(1)}, u32[]{:S(2)}, u32[]{:S(2)}) collective-permute-start(bf16[128,256]{1,0:T(8,128)(2,1)S(1)} %add_whole.4.refs_0_.kept_ref), channel_id=1, source_target_pairs={{0,8},{1,3},{2,10},{3,1},{4,12},{5,7},{6,14},{7,5},{8,0},{9,11},{1... | collective-permute-start | bytes 196616 | tf_op jit(solution)/shard_map/ppermute | solution.py:389
  57.2 5.6 %collective-permute-start.21 = (bf16[128,256]{1,0:T(8,128)(2,1)S(1)}, bf16[128,256]{1,0:T(8,128)(2,1)S(1)}, u32[]{:S(2)}, u32[]{:S(2)}) collective-permute-start(bf16[128,256]{1,0:T(8,128)(2,1)S(1)} %add_whole.5.refs_0_.kept_ref), channel_id=1, source_target_pairs={{0,8},{1,3},{2,10},{3,1},{4,12},{5,7},{6,14},{7,5},{8,0},{9,11},{1... | collective-permute-start | bytes 196616 | tf_op jit(solution)/shard_map/ppermute | solution.py:389
  63.9 8.3 %collective-permute-start.24 = (bf16[8,64,256]{2,1,0:T(8,128)(2,1)S(1)}, bf16[8,64,256]{2,1,0:T(8,128)(2,1)S(1)}, u32[]{:S(2)}, u32[]{:S(2)}) collective-permute-start(bf16[8,64,256]{2,1,0:T(8,128)(2,1)S(1)} %get-tuple-element.66), channel_id=1, source_target_pairs={{0,1},{1,0},{2,3},{3,2},{4,5},{5,4},{6,7},{7,6},{8,9},{9,8},{10,11... | collective-permute-start | bytes 786440 | tf_op jit(solution)/shard_map/ppermute | solution.py:354
  64.3 6.1 %collective-permute-start.27 = (bf16[128,256]{1,0:T(8,128)(2,1)S(1)}, bf16[128,256]{1,0:T(8,128)(2,1)S(1)}, u32[]{:S(2)}, u32[]{:S(2)}) collective-permute-start(bf16[128,256]{1,0:T(8,128)(2,1)S(1)} %add_whole.7.after_ref.refs_0_.mine_ref), channel_id=1, source_target_pairs={{0,4},{1,9},{2,6},{3,11},{4,0},{5,13},{6,2},{7,15},{8,12},{9,1},{1... | collective-permute-start | bytes 196616 | tf_op jit(solution)/shard_map/ppermute | solution.py:389
  66.1 5.4 %collective-permute-start.29 = (bf16[256,256]{1,0:T(8,128)(2,1)S(1)}, bf16[256,256]{1,0:T(8,128)(2,1)S(1)}, u32[]{:S(2)}, u32[]{:S(2)}) collective-permute-start(bf16[256,256]{1,0:T(8,128)(2,1)S(1)} %get-tuple-element.69), channel_id=1, source_target_pairs={{0,1},{1,0},{2,3},{3,2},{4,5},{5,4},{6,7},{7,6},{8,9},{9,8},{10,11... | collective-permute-start | bytes 393224 | tf_op jit(solution)/shard_map/ppermute | solution.py:354
  68.6 5.0 %collective-permute-start.26 = (bf16[256,256]{1,0:T(8,128)(2,1)S(1)}, bf16[256,256]{1,0:T(8,128)(2,1)S(1)}, u32[]{:S(2)}, u32[]{:S(2)}) collective-permute-start(bf16[256,256]{1,0:T(8,128)(2,1)S(1)} %join.2.mine_ref.refs_0_), channel_id=1, source_target_pairs={{0,2},{1,5},{2,0},{3,7},{4,6},{5,1},{6,4},{7,3},{8,10},{9,13},{10,... | collective-permute-start | bytes 393224 | tf_op jit(solution)/shard_map/ppermute | solution.py:389
  70.4 5.0 %collective-permute-start.28 = (bf16[256,256]{1,0:T(8,128)(2,1)S(1)}, bf16[256,256]{1,0:T(8,128)(2,1)S(1)}, u32[]{:S(2)}, u32[]{:S(2)}) collective-permute-start(bf16[256,256]{1,0:T(8,128)(2,1)S(1)} %join.3.mine_ref), channel_id=1, source_target_pairs={{0,2},{1,5},{2,0},{3,7},{4,6},{5,1},{6,4},{7,3},{8,10},{9,13},{10,... | collective-permute-start | bytes 393224 | tf_op jit(solution)/shard_map/ppermute | solution.py:389
  (14 other events, 71.0 us)

commit v12 on v11

--- a/solution.py
+++ b/solution.py
@@ -273,11 +273,6 @@
         put_halves(added(keep_ref[part, :], got_ref[part, :]), 0, *outs[2 * chain :][:2], hold)
 
 
-def halving_kernel(step, kept_ref, got_ref, *refs):
-    keep_ref, give_ref, hold = refs[-3:]
-    put_halves(added(kept_ref[...], got_ref[...]), step, keep_ref, give_ref, hold)
-
-
 def whole_kernel(kept_ref, got_ref, *refs):
     refs[-1][...] = added(kept_ref[...], got_ref[...]).astype(refs[-1].dtype)
 
@@ -516,14 +511,14 @@
     chains = [[outer_keep, outer_give], [up_keep, up_give]]
     latest = None
 
-    def step_call(kernel, name, chain, step, out_rows, scratch=()):
+    def step_call(chain, step, rows):
         kept, given = chain[0], chain[-1]
         after = [latest] if latest is not None else [proj_even, proj_odd]
         made = call(
-            kernel, name, [vmem()] * 2 + [anywhere()] * len(after), [vmem()] * len(out_rows),
-            [shape_of((rows, width), BF16) for rows in out_rows], 1, 1, scratch=scratch,
+            whole_kernel, "add_whole", [vmem()] * 2 + [anywhere()] * len(after), vmem(),
+            shape_of((rows, width), BF16), 1, 1,
         )(kept, sum_swap(given, step), *after)
-        return list(made)
+        return [made]
 
     for step in range(count):
         for c in range(2):
@@ -534,21 +529,9 @@
                     shape_of((3, nodes, padded), BF16), 1, 1,
                 )(latest, proj, proj_even, proj_odd)
                 east_trio = lax.ppermute(trio, "lon", west_pairs)
-            if step == 0:
-                chains[c] = step_call(
-                    functools.partial(halving_kernel, 1), "halve", chains[c], step,
-                    [rows // 2] * 2, hold(rows),
-                )
-            else:
-                chains[c] = step_call(whole_kernel, "add_whole", chains[c], step, [rows])
+            chains[c] = step_call(chains[c], step, rows)
             latest = chains[c][-1]
     after_pick = chains[1][-1]
-    for c in range(2):
-        rows = chains[c][0].shape[0]
-        chains[c] = step_call(
-            functools.partial(join_kernel, 1), "join", chains[c], 1, [2 * rows]
-        )
-        latest = chains[c][-1]
     (outer_mine,), (up_mine,) = chains
     outer_theirs, up_theirs = sum_swap(outer_mine, 0), sum_swap(up_mine, 0)
 

time: 76.6 us -> 76 us (level)
  starting transfers between devices: 34.2 us -> 33.3 us
    ppermute x10 -> x8, starting transfers between devices: 11.8 us -> 11.1 us  [sum_swap(): return lax.ppermute(value, ('lat', 'lon', 'rep'), pairs)]
    ppermute x10 -> x8, waiting for transfers between devices: 14 us -> 14.4 us  [sum_swap(): return lax.ppermute(value, ('lat', 'lon', 'rep'), pairs)]
  transfers between devices with their start and end apart: 30 -> 28, of which waited for: 15 -> 12; matrix products, arithmetic and copies ran while one was open for 0% -> 0% of each run, Pallas kernels for 12% -> 12%
where the time goes in v12:
time: 76 us; the launch traced here: 75.7 us
  starting transfers between devices  33.3 us (44%)
  waiting for transfers between devices  23.9 us (31%)
  Pallas kernels  17.6 us (23%)
  between operations  0.92 us (1%)
    ppermute x16, starting transfers between devices, along(): return lambda value: lax.ppermute(value, axis, pairs)  16.8 us
    ppermute x8, waiting for transfers between devices, sum_swap(): return lax.ppermute(value, ('lat', 'lon', 'rep'), pairs)  14.4 us
    ppermute x8, starting transfers between devices, sum_swap(): return lax.ppermute(value, ('lat', 'lon', 'rep'), pairs)  11.1 us
    ppermute x16, waiting for transfers between devices, along(): return lambda value: lax.ppermute(value, axis, pairs)  9.54 us
    pallas_call x2, Pallas kernels, encode(): call(encode_kernel, 'encode', [smem(), smem(), anywhere()] + [vmem()] * 3...  5.08 us
    ppermute x3, starting transfers between devices, per_device(): to_east = lambda value: lax.ppermute(value, 'lon', east_pairs)  4.21 us
    pallas_call x1, Pallas kernels, per_device(): call(back_kernel, 'back_messages', [smem(), smem(), anywhere(), anywhere(...  3.49 us
    pallas_call x1, Pallas kernels, per_device(): call(node_kernel, 'node_update_and_gradients', sums_specs * 2 + [whole(em...  2.85 us
  transfers between devices with their start and end apart: 28, of which 12 were waited for; matrix products, arithmetic and copies ran while one was open for 0% of the time, Pallas kernels for 12%

profile of v12, /device:TPU:0, one launch (start us, length us, event | category | flops | bytes accessed | tf_op | source)
XLA Modules:
  0.0 75.7 jit_solution(13192627541515506054)
XLA Ops:
  0.7 3.5 %back_messages.1 = (bf16[256,256]{1,0:T(8,128)(2,1)S(1)}, bf16[3,256,256]{2,1,0:T(8,128)(2,1)S(1)}, bf16[2,256,256]{2,1,0:T(8,128)(2,1)S(1)}) custom-call(s32[16]{0:T(128)} %bitcast.25, s32[16]{0:T(128)} %slot_ref.7, bf16[16,128,128]{2,1,0:T(8,128)(2,1)} %tiles_ref.7, bf16[227,2048]{1,0:T(8,128)(2,1)} %bitcast.13), custom_call_target="tpu_custom_call" | custom-call | flops 1 | bytes 1 | tf_op jit(solution)/shard_map/back_messages/pallas_call | solution.py:417
  4.1 3.0 %collective-permute-start.4 = (bf16[3,256,256]{2,1,0:T(8,128)(2,1)S(1)}, bf16[3,256,256]{2,1,0:T(8,128)(2,1)S(1)}, u32[]{:S(2)}, u32[]{:S(2)}) collective-permute-start(bf16[3,256,256]{2,1,0:T(8,128)(2,1)S(1)} %get-tuple-element.41), channel_id=1, source_target_pairs={{0,2},{2,0},{1,3},{3,1},{4,6},{6,4},{5,7},{7,5},{8,10},{10,8},{9,1... | collective-permute-start | bytes 1179656 | tf_op jit(solution)/shard_map/ppermute | solution.py:407
  7.2 2.6 %encode.2 = (bf16[2,256,256]{2,1,0:T(8,128)(2,1)S(1)}, bf16[2,256,256]{2,1,0:T(8,128)(2,1)S(1)}, bf16[2,256,256]{2,1,0:T(8,128)(2,1)S(1)}, bf16[1024,256]{1,0:T(8,128)(2,1)S(1)}) custom-call(s32[16]{0:T(128)} %bitcast.26, s32[16]{0:T(128)} %slot_ref.7, bf16[256,256]{1,0:T(8,128)(2,1)S(1)} %get-tuple-element.34.after_ref.back_ref, ...), custom_call_target="tpu_custom_call" | custom-call | flops 1 | bytes 1 | tf_op jit(solution)/shard_map/encode/pallas_call | solution.py:435
  9.8 1.6 %collective-permute-start.2 = (bf16[2,256,256]{2,1,0:T(8,128)(2,1)S(1)}, bf16[2,256,256]{2,1,0:T(8,128)(2,1)S(1)}, u32[]{:S(2)}, u32[]{:S(2)}) collective-permute-start(bf16[2,256,256]{2,1,0:T(8,128)(2,1)S(1)} %get-tuple-element.39), channel_id=1, source_target_pairs={{0,4},{4,0},{8,12},{12,8},{1,5},{5,1},{9,13},{13,9},{2,6},{6,2},{1... | collective-permute-start | bytes 786440 | tf_op jit(solution)/shard_map/ppermute | solution.py:349
  12.8 2.5 %encode.3 = (bf16[2,256,256]{2,1,0:T(8,128)(2,1)S(1)}, bf16[2,256,256]{2,1,0:T(8,128)(2,1)S(1)}, bf16[2,256,256]{2,1,0:T(8,128)(2,1)S(1)}, bf16[1024,256]{1,0:T(8,128)(2,1)S(1)}) custom-call(s32[16]{0:T(128)} %bitcast.27, s32[16]{0:T(128)} %slot_ref.7, bf16[2,256,256]{2,1,0:T(8,128)(2,1)S(1)} %get-tuple-element.36.after_ref.refs_1_.own_a, ...), custom_call_target="tpu_custom_call" | custom-call | flops 1 | bytes 1 | tf_op jit(solution)/shard_map/encode/pallas_call | solution.py:435
  15.2 3.8 %collective-permute-start.6 = (bf16[2,256,256]{2,1,0:T(8,128)(2,1)S(1)}, bf16[2,256,256]{2,1,0:T(8,128)(2,1)S(1)}, u32[]{:S(2)}, u32[]{:S(2)}) collective-permute-start(bf16[2,256,256]{2,1,0:T(8,128)(2,1)S(1)} %get-tuple-element.43), channel_id=1, source_target_pairs={{0,4},{4,0},{8,12},{12,8},{1,5},{5,1},{9,13},{13,9},{2,6},{6,2},{1... | collective-permute-start | bytes 786440 | tf_op jit(solution)/shard_map/ppermute | solution.py:349
  20.8 4.9 %collective-permute-done.6.refs_2_.even_b = bf16[2,256,256]{2,1,0:T(8,128)(2,1)S(1)} collective-permute-done((bf16[2,256,256]{2,1,0:T(8,128)(2,1)S(1)}, bf16[2,256,256]{2,1,0:T(8,128)(2,1)S(1)}, u32[]{:S(2)}, u32[]{:S(2)}) %collective-permute-start.6) | collective-permute-done | bytes 262176 | tf_op jit(solution)/shard_map/ppermute | solution.py:349
  27.4 3.4 %collective-permute-start.10 = (bf16[256,256]{1,0:T(8,128)(2,1)S(1)}, bf16[256,256]{1,0:T(8,128)(2,1)S(1)}, u32[]{:S(2)}, u32[]{:S(2)}) collective-permute-start(bf16[256,256]{1,0:T(8,128)(2,1)S(1)} %get-tuple-element.46), channel_id=1, source_target_pairs={{0,4},{4,0},{8,12},{12,8},{1,5},{5,1},{9,13},{13,9},{2,6},{6,2},{1... | collective-permute-start | bytes 393224 | tf_op jit(solution)/shard_map/ppermute | solution.py:349
  32.3 2.4 %collective-permute-done.10.back_even_ref = bf16[256,256]{1,0:T(8,128)(2,1)S(1)} collective-permute-done((bf16[256,256]{1,0:T(8,128)(2,1)S(1)}, bf16[256,256]{1,0:T(8,128)(2,1)S(1)}, u32[]{:S(2)}, u32[]{:S(2)}) %collective-permute-start.10) | collective-permute-done | bytes 131104 | tf_op jit(solution)/shard_map/ppermute | solution.py:349
  34.7 2.8 %node_update_and_gradients.1 = (bf16[256,256]{1,0:T(8,128)(2,1)S(1)}, f32[1024,256]{1,0:T(8,128)S(1)}, bf16[1024,256]{1,0:T(8,128)(2,1)S(1)}, bf16[256,256]{1,0:T(8,128)(2,1)S(1)}, f32[4,2,64,256]{3,2,1,0:T(8,128)}) custom-call(bf16[2,256,256]{2,1,0:T(8,128)(2,1)S(1)} %get-tuple-element.36.after_ref.refs_1_.own_a, ...), custom_call_target="tpu_custom_call" | custom-call | flops 1 | bytes 1 | tf_op jit(solution)/shard_map/node_update_and_gradients/pallas_call | solution.py:486
  37.6 3.7 %collective-permute-start.17 = (bf16[256,256]{1,0:T(8,128)(2,1)S(1)}, bf16[256,256]{1,0:T(8,128)(2,1)S(1)}, u32[]{:S(2)}, u32[]{:S(2)}) collective-permute-start(bf16[256,256]{1,0:T(8,128)(2,1)S(1)} %get-tuple-element.56.proj_ref), channel_id=1, source_target_pairs={{0,4},{4,0},{8,12},{12,8},{1,5},{5,1},{9,13},{13,9},{2,6},{6,2},{1... | collective-permute-start | bytes 393224 | tf_op jit(solution)/shard_map/ppermute | solution.py:349
  42.2 1.1 %collective-permute-start.16 = (bf16[256,256]{1,0:T(8,128)(2,1)S(1)}, bf16[256,256]{1,0:T(8,128)(2,1)S(1)}, u32[]{:S(2)}, u32[]{:S(2)}) collective-permute-start(bf16[256,256]{1,0:T(8,128)(2,1)S(1)} %get-tuple-element.55), channel_id=1, source_target_pairs={{0,2},{1,5},{2,0},{3,7},{4,6},{5,1},{6,4},{7,3},{8,10},{9,13},{10,... | collective-permute-start | bytes 393224 | tf_op jit(solution)/shard_map/ppermute | solution.py:384
  44.3 1.1 %collective-permute-done.17.refs_0_.even_ref = bf16[256,256]{1,0:T(8,128)(2,1)S(1)} collective-permute-done((bf16[256,256]{1,0:T(8,128)(2,1)S(1)}, bf16[256,256]{1,0:T(8,128)(2,1)S(1)}, u32[]{:S(2)}, u32[]{:S(2)}) %collective-permute-start.17) | collective-permute-done | bytes 131104 | tf_op jit(solution)/shard_map/ppermute | solution.py:349
  45.4 1.8 %collective-permute-done.16.got_ref = bf16[256,256]{1,0:T(8,128)(2,1)S(1)} collective-permute-done((bf16[256,256]{1,0:T(8,128)(2,1)S(1)}, bf16[256,256]{1,0:T(8,128)(2,1)S(1)}, u32[]{:S(2)}, u32[]{:S(2)}) %collective-permute-start.16) | collective-permute-done | bytes 131104 | tf_op jit(solution)/shard_map/ppermute | solution.py:384
  47.3 1.4 %collective-permute-done.15.got_ref = bf16[256,256]{1,0:T(8,128)(2,1)S(1)} collective-permute-done((bf16[256,256]{1,0:T(8,128)(2,1)S(1)}, bf16[256,256]{1,0:T(8,128)(2,1)S(1)}, u32[]{:S(2)}, u32[]{:S(2)}) %collective-permute-start.15) | collective-permute-done | bytes 131104 | tf_op jit(solution)/shard_map/ppermute | solution.py:384
  48.7 1.1 %collective-permute-start.23 = (bf16[3,256,256]{2,1,0:T(8,128)(2,1)S(1)}, bf16[3,256,256]{2,1,0:T(8,128)(2,1)S(1)}, u32[]{:S(2)}, u32[]{:S(2)}) collective-permute-start(bf16[3,256,256]{2,1,0:T(8,128)(2,1)S(1)} %pack_nodes.1), channel_id=1, source_target_pairs={{2,0},{0,2},{3,1},{1,3},{6,4},{4,6},{7,5},{5,7},{10,8},{8,10},{11,... | collective-permute-start | bytes 1179656 | tf_op jit(solution)/shard_map/ppermute | solution.py:531
  49.8 2.5 %collective-permute-start.20 = (bf16[256,256]{1,0:T(8,128)(2,1)S(1)}, bf16[256,256]{1,0:T(8,128)(2,1)S(1)}, u32[]{:S(2)}, u32[]{:S(2)}) collective-permute-start(bf16[256,256]{1,0:T(8,128)(2,1)S(1)} %add_whole.6.refs_0_.kept_ref), channel_id=1, source_target_pairs={{0,4},{1,9},{2,6},{3,11},{4,0},{5,13},{6,2},{7,15},{8,12},{9,1},{1... | collective-permute-start | bytes 393224 | tf_op jit(solution)/shard_map/ppermute | solution.py:384
  52.4 3.7 %collective-permute-done.20.got_ref = bf16[256,256]{1,0:T(8,128)(2,1)S(1)} collective-permute-done((bf16[256,256]{1,0:T(8,128)(2,1)S(1)}, bf16[256,256]{1,0:T(8,128)(2,1)S(1)}, u32[]{:S(2)}, u32[]{:S(2)}) %collective-permute-start.20) | collective-permute-done | bytes 131104 | tf_op jit(solution)/shard_map/ppermute | solution.py:384
  56.1 3.0 %collective-permute-start.22 = (bf16[256,256]{1,0:T(8,128)(2,1)S(1)}, bf16[256,256]{1,0:T(8,128)(2,1)S(1)}, u32[]{:S(2)}, u32[]{:S(2)}) collective-permute-start(bf16[256,256]{1,0:T(8,128)(2,1)S(1)} %add_whole.8.refs_0_.kept_ref), channel_id=1, source_target_pairs={{0,8},{1,3},{2,10},{3,1},{4,12},{5,7},{6,14},{7,5},{8,0},{9,11},{1... | collective-permute-start | bytes 393224 | tf_op jit(solution)/shard_map/ppermute | solution.py:384
  59.1 1.5 %collective-permute-start.21 = (bf16[256,256]{1,0:T(8,128)(2,1)S(1)}, bf16[256,256]{1,0:T(8,128)(2,1)S(1)}, u32[]{:S(2)}, u32[]{:S(2)}) collective-permute-start(bf16[256,256]{1,0:T(8,128)(2,1)S(1)} %add_whole.9.refs_0_.kept_ref), channel_id=1, source_target_pairs={{0,8},{1,3},{2,10},{3,1},{4,12},{5,7},{6,14},{7,5},{8,0},{9,11},{1... | collective-permute-start | bytes 393224 | tf_op jit(solution)/shard_map/ppermute | solution.py:384
  60.6 1.4 %collective-permute-done.22.got_ref = bf16[256,256]{1,0:T(8,128)(2,1)S(1)} collective-permute-done((bf16[256,256]{1,0:T(8,128)(2,1)S(1)}, bf16[256,256]{1,0:T(8,128)(2,1)S(1)}, u32[]{:S(2)}, u32[]{:S(2)}) %collective-permute-start.22) | collective-permute-done | bytes 131104 | tf_op jit(solution)/shard_map/ppermute | solution.py:384
  62.1 4.7 %collective-permute-done.21.got_ref = bf16[256,256]{1,0:T(8,128)(2,1)S(1)} collective-permute-done((bf16[256,256]{1,0:T(8,128)(2,1)S(1)}, bf16[256,256]{1,0:T(8,128)(2,1)S(1)}, u32[]{:S(2)}, u32[]{:S(2)}) %collective-permute-start.21) | collective-permute-done | bytes 131104 | tf_op jit(solution)/shard_map/ppermute | solution.py:384
  66.8 1.1 %pick_nodes.1 = (bf16[8,64,256]{2,1,0:T(8,128)(2,1)S(1)}, bf16[8,64,256]{2,1,0:T(8,128)(2,1)S(1)}) custom-call(s32[16]{0:T(128)} %bitcast.28, s32[16]{0:T(128)} %slot_ref.7, bf16[256,256]{1,0:T(8,128)(2,1)S(1)} %add_whole.11.after_ref.mine_ref, bf16[12,64,256]{2,1,0:T(8,128)(2,1)S(1)} %bitcast.15, bf16[12,64,256]{2,1,0:T(8,128)(2,1)S(1)} %bitcast.20), custom_call_target="tpu_custom_call" | custom-call | flops 1 | bytes 1 | tf_op jit(solution)/shard_map/pick_nodes/pallas_call | solution.py:551
  71.3 1.2 %decode.1.after_ref.refs_0_ = bf16[227,1024]{1,0:T(8,128)(2,1)} custom-call(bf16[16,128,128]{2,1,0:T(8,128)(2,1)S(1)} %copy-done, f32[227,1024]{1,0:T(8,128)S(1)} %get-tuple-element.38.base_ref, bf16[8,64,256]{2,1,0:T(8,128)(2,1)S(1)} %get-tuple-element.57.mine_ref, bf16[8,64,256]{2,1,0:T(8,128)(2,1)S(1)} %collective-permute-done.24.got_ref), custom_call_target="tpu_custom_call" | custom-call | flops 1 | bytes 1 | tf_op jit(solution)/shard_map/decode/pallas_call | solution.py:555
  (69 shorter events, 14.9 us)
Async XLA Ops:
  4.1 15.8 %collective-permute-start.4 = (bf16[3,256,256]{2,1,0:T(8,128)(2,1)S(1)}, bf16[3,256,256]{2,1,0:T(8,128)(2,1)S(1)}, u32[]{:S(2)}, u32[]{:S(2)}) collective-permute-start(bf16[3,256,256]{2,1,0:T(8,128)(2,1)S(1)} %get-tuple-element.41), channel_id=1, source_target_pairs={{0,2},{2,0},{1,3},{3,1},{4,6},{6,4},{5,7},{7,5},{8,10},{10,8},{9,1... | collective-permute-start | bytes 1179656 | tf_op jit(solution)/shard_map/ppermute | solution.py:407
  9.8 10.1 %collective-permute-start.2 = (bf16[2,256,256]{2,1,0:T(8,128)(2,1)S(1)}, bf16[2,256,256]{2,1,0:T(8,128)(2,1)S(1)}, u32[]{:S(2)}, u32[]{:S(2)}) collective-permute-start(bf16[2,256,256]{2,1,0:T(8,128)(2,1)S(1)} %get-tuple-element.39), channel_id=1, source_target_pairs={{0,4},{4,0},{8,12},{12,8},{1,5},{5,1},{9,13},{13,9},{2,6},{6,2},{1... | collective-permute-start | bytes 786440 | tf_op jit(solution)/shard_map/ppermute | solution.py:349
  11.4 8.5 %collective-permute-start.3 = (bf16[2,256,256]{2,1,0:T(8,128)(2,1)S(1)}, bf16[2,256,256]{2,1,0:T(8,128)(2,1)S(1)}, u32[]{:S(2)}, u32[]{:S(2)}) collective-permute-start(bf16[2,256,256]{2,1,0:T(8,128)(2,1)S(1)} %get-tuple-element.40), channel_id=1, source_target_pairs={{0,0},{4,8},{8,4},{12,12},{1,1},{5,9},{9,5},{13,13},{2,2},{6,10},{... | collective-permute-start | bytes 786440 | tf_op jit(solution)/shard_map/ppermute | solution.py:349
  15.2 10.5 %collective-permute-start.6 = (bf16[2,256,256]{2,1,0:T(8,128)(2,1)S(1)}, bf16[2,256,256]{2,1,0:T(8,128)(2,1)S(1)}, u32[]{:S(2)}, u32[]{:S(2)}) collective-permute-start(bf16[2,256,256]{2,1,0:T(8,128)(2,1)S(1)} %get-tuple-element.43), channel_id=1, source_target_pairs={{0,4},{4,0},{8,12},{12,8},{1,5},{5,1},{9,13},{13,9},{2,6},{6,2},{1... | collective-permute-start | bytes 786440 | tf_op jit(solution)/shard_map/ppermute | solution.py:349
  19.0 6.7 %collective-permute-start.7 = (bf16[2,256,256]{2,1,0:T(8,128)(2,1)S(1)}, bf16[2,256,256]{2,1,0:T(8,128)(2,1)S(1)}, u32[]{:S(2)}, u32[]{:S(2)}) collective-permute-start(bf16[2,256,256]{2,1,0:T(8,128)(2,1)S(1)} %get-tuple-element.44), channel_id=1, source_target_pairs={{0,0},{4,8},{8,4},{12,12},{1,1},{5,9},{9,5},{13,13},{2,2},{6,10},{... | collective-permute-start | bytes 786440 | tf_op jit(solution)/shard_map/ppermute | solution.py:349
  19.9 11.0 %collective-permute-start.9 = (bf16[512,256]{1,0:T(8,128)(2,1)S(1)}, bf16[512,256]{1,0:T(8,128)(2,1)S(1)}, u32[]{:S(2)}, u32[]{:S(2)}) collective-permute-start(bf16[512,256]{1,0:T(8,128)(2,1)S(1)} %copy-done.4), channel_id=1, source_target_pairs={{0,1},{1,0},{2,3},{3,2},{4,5},{5,4},{6,7},{7,6},{8,9},{9,8},{10,11... | collective-permute-start | bytes 786440 | tf_op jit(solution)/shard_map/ppermute | solution.py:349
  20.0 6.2 %collective-permute-start.5 = (bf16[256,256]{1,0:T(8,128)(2,1)S(1)}, bf16[256,256]{1,0:T(8,128)(2,1)S(1)}, u32[]{:S(2)}, u32[]{:S(2)}) collective-permute-start(bf16[256,256]{1,0:T(8,128)(2,1)S(1)} %add_east.2), channel_id=1, source_target_pairs={{0,2},{2,0},{1,3},{3,1},{4,6},{6,4},{5,7},{7,5},{8,10},{10,8},{9,1... | collective-permute-start | bytes 393224 | tf_op jit(solution)/shard_map/ppermute | solution.py:407
  20.6 11.6 %collective-permute-start.12 = (bf16[512,256]{1,0:T(8,128)(2,1)S(1)}, bf16[512,256]{1,0:T(8,128)(2,1)S(1)}, u32[]{:S(2)}, u32[]{:S(2)}) collective-permute-start(bf16[512,256]{1,0:T(8,128)(2,1)S(1)} %copy-done.5), channel_id=1, source_target_pairs={{0,1},{1,0},{2,3},{3,2},{4,5},{5,4},{6,7},{7,6},{8,9},{9,8},{10,11... | collective-permute-start | bytes 786440 | tf_op jit(solution)/shard_map/ppermute | solution.py:349
  25.7 6.6 %collective-permute-start.13 = (bf16[256,512]{1,0:T(8,128)(2,1)S(1)}, bf16[256,512]{1,0:T(8,128)(2,1)S(1)}, u32[]{:S(2)}, u32[]{:S(2)}) collective-permute-start(bf16[256,512]{1,0:T(8,128)(2,1)S(1)} %copy-done.6), channel_id=1, source_target_pairs={{0,1},{1,0},{2,3},{3,2},{4,5},{5,4},{6,7},{7,6},{8,9},{9,8},{10,11... | collective-permute-start | bytes 786440 | tf_op jit(solution)/shard_map/ppermute | solution.py:349
  26.3 6.0 %collective-permute-start.8 = (bf16[256,256]{1,0:T(8,128)(2,1)S(1)}, bf16[256,256]{1,0:T(8,128)(2,1)S(1)}, u32[]{:S(2)}, u32[]{:S(2)}) collective-permute-start(bf16[256,256]{1,0:T(8,128)(2,1)S(1)} %add_east.3.after_ref), channel_id=1, source_target_pairs={{0,2},{2,0},{1,3},{3,1},{4,6},{6,4},{5,7},{7,5},{8,10},{10,8},{9,1... | collective-permute-start | bytes 393224 | tf_op jit(solution)/shard_map/ppermute | solution.py:407
  27.4 7.2 %collective-permute-start.10 = (bf16[256,256]{1,0:T(8,128)(2,1)S(1)}, bf16[256,256]{1,0:T(8,128)(2,1)S(1)}, u32[]{:S(2)}, u32[]{:S(2)}) collective-permute-start(bf16[256,256]{1,0:T(8,128)(2,1)S(1)} %get-tuple-element.46), channel_id=1, source_target_pairs={{0,4},{4,0},{8,12},{12,8},{1,5},{5,1},{9,13},{13,9},{2,6},{6,2},{1... | collective-permute-start | bytes 393224 | tf_op jit(solution)/shard_map/ppermute | solution.py:349
  30.9 3.8 %collective-permute-start.11 = (bf16[256,256]{1,0:T(8,128)(2,1)S(1)}, bf16[256,256]{1,0:T(8,128)(2,1)S(1)}, u32[]{:S(2)}, u32[]{:S(2)}) collective-permute-start(bf16[256,256]{1,0:T(8,128)(2,1)S(1)} %get-tuple-element.47), channel_id=1, source_target_pairs={{0,0},{4,8},{8,4},{12,12},{1,1},{5,9},{9,5},{13,13},{2,2},{6,10},{... | collective-permute-start | bytes 393224 | tf_op jit(solution)/shard_map/ppermute | solution.py:349
  37.6 4.4 %collective-permute-start.14 = (bf16[1024,256]{1,0:T(8,128)(2,1)S(1)}, bf16[1024,256]{1,0:T(8,128)(2,1)S(1)}, u32[]{:S(2)}, u32[]{:S(2)}) collective-permute-start(bf16[1024,256]{1,0:T(8,128)(2,1)S(1)} %get-tuple-element.51), channel_id=1, source_target_pairs={{0,1},{1,0},{2,3},{3,2},{4,5},{5,4},{6,7},{7,6},{8,9},{9,8},{10,11... | collective-permute-start | bytes 1572872 | tf_op jit(solution)/shard_map/ppermute | solution.py:349
  37.6 7.8 %collective-permute-start.17 = (bf16[256,256]{1,0:T(8,128)(2,1)S(1)}, bf16[256,256]{1,0:T(8,128)(2,1)S(1)}, u32[]{:S(2)}, u32[]{:S(2)}) collective-permute-start(bf16[256,256]{1,0:T(8,128)(2,1)S(1)} %get-tuple-element.56.proj_ref), channel_id=1, source_target_pairs={{0,4},{4,0},{8,12},{12,8},{1,5},{5,1},{9,13},{13,9},{2,6},{6,2},{1... | collective-permute-start | bytes 393224 | tf_op jit(solution)/shard_map/ppermute | solution.py:349
  41.3 4.1 %collective-permute-start.18 = (bf16[256,256]{1,0:T(8,128)(2,1)S(1)}, bf16[256,256]{1,0:T(8,128)(2,1)S(1)}, u32[]{:S(2)}, u32[]{:S(2)}) collective-permute-start(bf16[256,256]{1,0:T(8,128)(2,1)S(1)} %get-tuple-element.56.proj_ref), channel_id=1, source_target_pairs={{0,0},{4,8},{8,4},{12,12},{1,1},{5,9},{9,5},{13,13},{2,2},{6,10},{... | collective-permute-start | bytes 393224 | tf_op jit(solution)/shard_map/ppermute | solution.py:349
  42.2 5.0 %collective-permute-start.16 = (bf16[256,256]{1,0:T(8,128)(2,1)S(1)}, bf16[256,256]{1,0:T(8,128)(2,1)S(1)}, u32[]{:S(2)}, u32[]{:S(2)}) collective-permute-start(bf16[256,256]{1,0:T(8,128)(2,1)S(1)} %get-tuple-element.55), channel_id=1, source_target_pairs={{0,2},{1,5},{2,0},{3,7},{4,6},{5,1},{6,4},{7,3},{8,10},{9,13},{10,... | collective-permute-start | bytes 393224 | tf_op jit(solution)/shard_map/ppermute | solution.py:384
  43.3 5.3 %collective-permute-start.15 = (bf16[256,256]{1,0:T(8,128)(2,1)S(1)}, bf16[256,256]{1,0:T(8,128)(2,1)S(1)}, u32[]{:S(2)}, u32[]{:S(2)}) collective-permute-start(bf16[256,256]{1,0:T(8,128)(2,1)S(1)} %get-tuple-element.53), channel_id=1, source_target_pairs={{0,2},{1,5},{2,0},{3,7},{4,6},{5,1},{6,4},{7,3},{8,10},{9,13},{10,... | collective-permute-start | bytes 393224 | tf_op jit(solution)/shard_map/ppermute | solution.py:384
  48.7 18.1 %collective-permute-start.23 = (bf16[3,256,256]{2,1,0:T(8,128)(2,1)S(1)}, bf16[3,256,256]{2,1,0:T(8,128)(2,1)S(1)}, u32[]{:S(2)}, u32[]{:S(2)}) collective-permute-start(bf16[3,256,256]{2,1,0:T(8,128)(2,1)S(1)} %pack_nodes.1), channel_id=1, source_target_pairs={{2,0},{0,2},{3,1},{1,3},{6,4},{4,6},{7,5},{5,7},{10,8},{8,10},{11,... | collective-permute-start | bytes 1179656 | tf_op jit(solution)/shard_map/ppermute | solution.py:531
  49.8 6.2 %collective-permute-start.20 = (bf16[256,256]{1,0:T(8,128)(2,1)S(1)}, bf16[256,256]{1,0:T(8,128)(2,1)S(1)}, u32[]{:S(2)}, u32[]{:S(2)}) collective-permute-start(bf16[256,256]{1,0:T(8,128)(2,1)S(1)} %add_whole.6.refs_0_.kept_ref), channel_id=1, source_target_pairs={{0,4},{1,9},{2,6},{3,11},{4,0},{5,13},{6,2},{7,15},{8,12},{9,1},{1... | collective-permute-start | bytes 393224 | tf_op jit(solution)/shard_map/ppermute | solution.py:384
  52.4 6.7 %collective-permute-start.19 = (bf16[256,256]{1,0:T(8,128)(2,1)S(1)}, bf16[256,256]{1,0:T(8,128)(2,1)S(1)}, u32[]{:S(2)}, u32[]{:S(2)}) collective-permute-start(bf16[256,256]{1,0:T(8,128)(2,1)S(1)} %add_whole.7.refs_0_.kept_ref.after_ref), channel_id=1, source_target_pairs={{0,4},{1,9},{2,6},{3,11},{4,0},{5,13},{6,2},{7,15},{8,12},{9,1},{1... | collective-permute-start | bytes 393224 | tf_op jit(solution)/shard_map/ppermute | solution.py:384
  56.1 5.9 %collective-permute-start.22 = (bf16[256,256]{1,0:T(8,128)(2,1)S(1)}, bf16[256,256]{1,0:T(8,128)(2,1)S(1)}, u32[]{:S(2)}, u32[]{:S(2)}) collective-permute-start(bf16[256,256]{1,0:T(8,128)(2,1)S(1)} %add_whole.8.refs_0_.kept_ref), channel_id=1, source_target_pairs={{0,8},{1,3},{2,10},{3,1},{4,12},{5,7},{6,14},{7,5},{8,0},{9,11},{1... | collective-permute-start | bytes 393224 | tf_op jit(solution)/shard_map/ppermute | solution.py:384
  59.1 7.7 %collective-permute-start.21 = (bf16[256,256]{1,0:T(8,128)(2,1)S(1)}, bf16[256,256]{1,0:T(8,128)(2,1)S(1)}, u32[]{:S(2)}, u32[]{:S(2)}) collective-permute-start(bf16[256,256]{1,0:T(8,128)(2,1)S(1)} %add_whole.9.refs_0_.kept_ref), channel_id=1, source_target_pairs={{0,8},{1,3},{2,10},{3,1},{4,12},{5,7},{6,14},{7,5},{8,0},{9,11},{1... | collective-permute-start | bytes 393224 | tf_op jit(solution)/shard_map/ppermute | solution.py:384
  68.5 5.0 %collective-permute-start.25 = (bf16[256,256]{1,0:T(8,128)(2,1)S(1)}, bf16[256,256]{1,0:T(8,128)(2,1)S(1)}, u32[]{:S(2)}, u32[]{:S(2)}) collective-permute-start(bf16[256,256]{1,0:T(8,128)(2,1)S(1)} %add_whole.10.refs_0_.mine_ref), channel_id=1, source_target_pairs={{0,2},{1,5},{2,0},{3,7},{4,6},{5,1},{6,4},{7,3},{8,10},{9,13},{10,... | collective-permute-start | bytes 393224 | tf_op jit(solution)/shard_map/ppermute | solution.py:384
  69.5 5.4 %collective-permute-start.26 = (bf16[256,256]{1,0:T(8,128)(2,1)S(1)}, bf16[256,256]{1,0:T(8,128)(2,1)S(1)}, u32[]{:S(2)}, u32[]{:S(2)}) collective-permute-start(bf16[256,256]{1,0:T(8,128)(2,1)S(1)} %add_whole.11.after_ref.mine_ref), channel_id=1, source_target_pairs={{0,2},{1,5},{2,0},{3,7},{4,6},{5,1},{6,4},{7,3},{8,10},{9,13},{10,... | collective-permute-start | bytes 393224 | tf_op jit(solution)/shard_map/ppermute | solution.py:384
  (12 other events, 59.8 us)

commit v13 on v12

--- a/solution.py
+++ b/solution.py
@@ -123,10 +123,8 @@
         east_ref[k] = block.reshape(east_ref.shape[1:]).astype(east_ref.dtype)
 
 
-def encode_kernel(
-    device_ref, slot_ref, after_ref, grid_ref, tiles_ref, weight_ref,
-    own_ref, even_ref, odd_ref, hidden_ref, total, hold,
-):
+def encode_kernel(device_ref, slot_ref, after_ref, grid_ref, tiles_ref, weight_ref, *refs):
+    extra, (own_ref, even_ref, odd_ref, hidden_ref, total, hold) = refs[:-6], refs[-6:]
     blocks, rows = tiles_ref.shape[:2]
     slots = total.shape[0] // 6
     step_rows = blocks * rows // STEPS
@@ -140,7 +138,11 @@
             total[at] += dot(node_half(tiles_ref[b], r), hold[b * rows : (b + 1) * rows, :])
     mine = hidden_ref.shape[0]
     hidden_ref[...] = hold[pl.ds(pl.multiple_of(r * mine, mine), mine), :]
-    write_packed(total, (own_ref, even_ref, odd_ref))
+    write_packed(total, (own_ref, even_ref.at[:2], odd_ref.at[:2]))
+    if extra:
+        side_ref, moved_ref = extra
+        even_ref[2] = added(side_ref[0], moved_ref[1]).astype(even_ref.dtype)
+        odd_ref[2] = added(side_ref[1], moved_ref[2]).astype(odd_ref.dtype)
 
 
 def local_kernel(
@@ -165,11 +167,6 @@
 def add_kernel(*refs):
     a, b, c, out = refs[-4:]
     out[...] = added(a[0], b[0], c[0]).astype(out.dtype)
-
-
-def sides_kernel(after_ref, side_ref, moved_ref, even_ref, odd_ref):
-    even_ref[...] = added(side_ref[0], moved_ref[1]).astype(even_ref.dtype)
-    odd_ref[...] = added(side_ref[1], moved_ref[2]).astype(odd_ref.dtype)
 
 
 def node_kernel(
@@ -197,7 +194,7 @@
     norm = centered * inverse
     normed = norm.astype(BF16)
 
-    cot = added(back_ref[...], back_moved_ref[0], back_even_ref[...], back_odd_ref[...]).astype(BF16)
+    cot = added(back_ref[...], back_moved_ref[0], back_even_ref[0], back_odd_ref[0]).astype(BF16)
     terms = cot[:, :channels]
     grad_own = dot(terms, out_ref[...]).astype(BF16)
     grad_oth = dot(terms, out_other_ref[...]).astype(BF16)
@@ -431,21 +428,23 @@
     )(*routes, tiles_in, cot_in_t)
     back_moved = to_east(back_east)
 
-    def encode(after, weight):
+    def encode(after, weight, *extra):
+        sent = (3,) + pair_shape[1:] if extra else pair_shape
         return call(
             encode_kernel, "encode",
-            [smem(), smem(), anywhere()] + [vmem()] * 3,
+            [smem(), smem(), anywhere()] + [vmem()] * (3 + len(extra)),
             [vmem()] * 4,
-            [shape_of(pair_shape, BF16)] * 3 + [shape_of((my_rows, width), BF16)],
+            [shape_of(pair_shape, BF16)] + [shape_of(sent, BF16)] * 2
+            + [shape_of((my_rows, width), BF16)],
             1, 1,
             scratch=[
                 pltpu.VMEM((6 * slots, half, width), F32), pltpu.VMEM((grid_rows, width), BF16),
             ],
-        )(*routes, after, grid_t, interp_tiles, weight)
+        )(*routes, after, grid_t, interp_tiles, weight, *extra)
 
     own_a, even_a, odd_a, hidden_a = encode(back_own, in_hbm(w_embed))
     even_in_a, odd_in_a = to_even(even_a), to_odd(odd_a)
-    own_b, even_b, odd_b, hidden_b = encode(own_a, embed_other)
+    own_b, even_b, odd_b, hidden_b = encode(own_a, embed_other, back_side, back_moved)
     even_in_b, odd_in_b = to_even(even_b), to_odd(odd_b)
 
     out_other, up_other, down_other = swap_rep(out_t), swap_rep(w_up), swap_rep(w_down)
@@ -460,7 +459,7 @@
             shape_of((nodes, width), BF16), 3 * nodes * width, 6e5, grid=(1,),
         )(*after, *terms)
 
-    send_a = add_east((back_moved,), own_a, even_in_a, odd_in_a)
+    send_a = add_east((own_b,), own_a, even_in_a, odd_in_a)
     moved_a = to_east(send_a)
 
     base, local, local_other = call(
@@ -471,12 +470,6 @@
 
     send_b = add_east((moved_a,), own_b, even_in_b, odd_in_b)
     moved_b = to_east(send_b)
-
-    back_even, back_odd = call(
-        sides_kernel, "add_sides", [anywhere(), vmem(), vmem()], [vmem()] * 2,
-        [shape_of((nodes, padded), BF16)] * 2, 3 * nodes * width, 1e6,
-    )(send_b, back_side, back_moved)
-    back_even_in, back_odd_in = to_even(back_even), to_odd(back_odd)
 
     first = pl.BlockSpec((1, nodes, width), lambda i: (0, 0, 0))
     sums_specs = [first] * 3 + [whole((nodes, width))]
@@ -486,7 +479,8 @@
     proj, keep, give, mesh_give, mesh_filled = call(
         node_kernel, "node_update_and_gradients",
         sums_specs * 2 + [whole(embed_shape)] * 2
-        + [back_spec, pl.BlockSpec((1, nodes, padded), lambda i: (0, 0, 0)), back_spec, back_spec]
+        + [back_spec, pl.BlockSpec((1, nodes, padded), lambda i: (0, 0, 0))]
+        + [pl.BlockSpec((1, nodes, padded), lambda i: (2, 0, 0))] * 2
         + [whole((channels, width))] * 2 + [whole(w.shape) for w in weights],
         [whole((nodes, padded))] + [whole((2 * latent, width))] * 2
         + [whole((nodes, width)), anywhere()],
@@ -497,7 +491,7 @@
     )(
         own_a, even_in_a, odd_in_a, moved_a, own_b, even_in_b, odd_in_b, moved_b,
         mesh_embed.reshape(embed_shape), mesh_other.reshape(embed_shape),
-        back_own, back_moved, back_even_in, back_odd_in, local, local_other, *weights,
+        back_own, back_moved, even_in_b, odd_in_b, local, local_other, *weights,
     )
 
     proj_even, proj_odd = to_even(proj), to_odd(proj)

time: 76 us -> 78.9 us (1.038)
  waiting for transfers between devices: 23.9 us -> 32.4 us
  starting transfers between devices: 33.3 us -> 27.8 us
    ppermute x3, waiting for transfers between devices: 0.01 us -> 8.05 us  [per_device(): to_east = lambda value: lax.ppermute(value, 'lon', east_pairs)]
    ppermute x8, starting transfers between devices: 11.1 us -> 7.48 us  [sum_swap(): return lax.ppermute(value, ('lat', 'lon', 'rep'), pairs)]
    ppermute x16 -> x14, starting transfers between devices: 16.8 us -> 13.6 us  [along(): return lambda value: lax.ppermute(value, axis, pairs)]
    ppermute x8, waiting for transfers between devices: 14.4 us -> 16.4 us  [sum_swap(): return lax.ppermute(value, ('lat', 'lon', 'rep'), pairs)]
    ppermute x16 -> x14, waiting for transfers between devices: 9.54 us -> 7.92 us  [along(): return lambda value: lax.ppermute(value, axis, pairs)]
    ppermute x3, starting transfers between devices: 4.21 us -> 5.28 us  [per_device(): to_east = lambda value: lax.ppermute(value, 'lon', east_pairs)]
    pallas_call x3 -> x2, Pallas kernels: 5.14 us -> 5.03 us  [encode(): call(encode_kernel, 'encode', [smem(), smem(), anywhere()] + [vmem()] * (...]
  transfers between devices with their start and end apart: 28 -> 26, of which waited for: 12 -> 15; matrix products, arithmetic and copies ran while one was open for 0% -> 0% of each run, Pallas kernels for 12% -> 11%
where the time goes in v13:
time: 78.9 us; the launch traced here: 78.7 us
  waiting for transfers between devices  32.4 us (41%)
  starting transfers between devices  27.8 us (35%)
  Pallas kernels  17.5 us (22%)
  between operations  0.92 us (1%)
    ppermute x8, waiting for transfers between devices, sum_swap(): return lax.ppermute(value, ('lat', 'lon', 'rep'), pairs)  16.4 us
    ppermute x14, starting transfers between devices, along(): return lambda value: lax.ppermute(value, axis, pairs)  13.6 us
    ppermute x3, waiting for transfers between devices, per_device(): to_east = lambda value: lax.ppermute(value, 'lon', east_pairs)  8.05 us
    ppermute x14, waiting for transfers between devices, along(): return lambda value: lax.ppermute(value, axis, pairs)  7.92 us
    ppermute x8, starting transfers between devices, sum_swap(): return lax.ppermute(value, ('lat', 'lon', 'rep'), pairs)  7.48 us
    ppermute x3, starting transfers between devices, per_device(): to_east = lambda value: lax.ppermute(value, 'lon', east_pairs)  5.28 us
    pallas_call x2, Pallas kernels, encode(): call(encode_kernel, 'encode', [smem(), smem(), anywhere()] + [vmem()] * (...  5.03 us
    pallas_call x1, Pallas kernels, per_device(): call(back_kernel, 'back_messages', [smem(), smem(), anywhere(), anywhere(...  3.49 us
  transfers between devices with their start and end apart: 26, of which 15 were waited for; matrix products, arithmetic and copies ran while one was open for 0% of the time, Pallas kernels for 11%

profile of v13, /device:TPU:0, one launch (start us, length us, event | category | flops | bytes accessed | tf_op | source)
XLA Modules:
  0.0 78.7 jit_solution(17268599501386717071)
XLA Ops:
  0.7 3.5 %back_messages.1 = (bf16[256,256]{1,0:T(8,128)(2,1)S(1)}, bf16[3,256,256]{2,1,0:T(8,128)(2,1)S(1)}, bf16[2,256,256]{2,1,0:T(8,128)(2,1)S(1)}) custom-call(s32[16]{0:T(128)} %bitcast.25, s32[16]{0:T(128)} %slot_ref.7, bf16[16,128,128]{2,1,0:T(8,128)(2,1)} %tiles_ref.7, bf16[227,2048]{1,0:T(8,128)(2,1)} %bitcast.13), custom_call_target="tpu_custom_call" | custom-call | flops 1 | bytes 1 | tf_op jit(solution)/shard_map/back_messages/pallas_call | solution.py:414
  4.1 3.0 %collective-permute-start.1 = (bf16[3,256,256]{2,1,0:T(8,128)(2,1)S(1)}, bf16[3,256,256]{2,1,0:T(8,128)(2,1)S(1)}, u32[]{:S(2)}, u32[]{:S(2)}) collective-permute-start(bf16[3,256,256]{2,1,0:T(8,128)(2,1)S(1)} %get-tuple-element.36), channel_id=1, source_target_pairs={{0,2},{2,0},{1,3},{3,1},{4,6},{6,4},{5,7},{7,5},{8,10},{10,8},{9,1... | collective-permute-start | bytes 1179656 | tf_op jit(solution)/shard_map/ppermute | solution.py:404
  7.2 2.6 %encode.2 = (bf16[2,256,256]{2,1,0:T(8,128)(2,1)S(1)}, bf16[2,256,256]{2,1,0:T(8,128)(2,1)S(1)}, bf16[2,256,256]{2,1,0:T(8,128)(2,1)S(1)}, bf16[1024,256]{1,0:T(8,128)(2,1)S(1)}) custom-call(s32[16]{0:T(128)} %bitcast.26, s32[16]{0:T(128)} %slot_ref.7, bf16[256,256]{1,0:T(8,128)(2,1)S(1)} %get-tuple-element.32.after_ref.back_ref, ...), custom_call_target="tpu_custom_call" | custom-call | flops 1 | bytes 1 | tf_op jit(solution)/shard_map/encode/pallas_call | solution.py:433
  9.8 1.6 %collective-permute-start.3 = (bf16[2,256,256]{2,1,0:T(8,128)(2,1)S(1)}, bf16[2,256,256]{2,1,0:T(8,128)(2,1)S(1)}, u32[]{:S(2)}, u32[]{:S(2)}) collective-permute-start(bf16[2,256,256]{2,1,0:T(8,128)(2,1)S(1)} %get-tuple-element.39), channel_id=1, source_target_pairs={{0,4},{4,0},{8,12},{12,8},{1,5},{5,1},{9,13},{13,9},{2,6},{6,2},{1... | collective-permute-start | bytes 786440 | tf_op jit(solution)/shard_map/ppermute | solution.py:346
  13.5 2.8 %collective-permute-done.1.refs_1_.back_moved_ref = bf16[3,256,256]{2,1,0:T(8,128)(2,1)S(1)} collective-permute-done((bf16[3,256,256]{2,1,0:T(8,128)(2,1)S(1)}, bf16[3,256,256]{2,1,0:T(8,128)(2,1)S(1)}, u32[]{:S(2)}, u32[]{:S(2)}) %collective-permute-start.1) | collective-permute-done | bytes 393248 | tf_op jit(solution)/shard_map/ppermute | solution.py:404
  16.3 2.4 %encode.3 = (bf16[2,256,256]{2,1,0:T(8,128)(2,1)S(1)}, bf16[3,256,256]{2,1,0:T(8,128)(2,1)S(1)}, bf16[3,256,256]{2,1,0:T(8,128)(2,1)S(1)}, bf16[1024,256]{1,0:T(8,128)(2,1)S(1)}) custom-call(s32[16]{0:T(128)} %bitcast.27, s32[16]{0:T(128)} %slot_ref.7, bf16[2,256,256]{2,1,0:T(8,128)(2,1)S(1)} %get-tuple-element.34.after_ref.refs_1_.own_a, ...), custom_call_target="tpu_custom_call" | custom-call | flops 1 | bytes 1 | tf_op jit(solution)/shard_map/encode/pallas_call | solution.py:433
  18.7 1.9 %collective-permute-start.6 = (bf16[3,256,256]{2,1,0:T(8,128)(2,1)S(1)}, bf16[3,256,256]{2,1,0:T(8,128)(2,1)S(1)}, u32[]{:S(2)}, u32[]{:S(2)}) collective-permute-start(bf16[3,256,256]{2,1,0:T(8,128)(2,1)S(1)} %get-tuple-element.42), channel_id=1, source_target_pairs={{0,4},{4,0},{8,12},{12,8},{1,5},{5,1},{9,13},{13,9},{2,6},{6,2},{1... | collective-permute-start | bytes 1179656 | tf_op jit(solution)/shard_map/ppermute | solution.py:346
  21.4 1.6 %collective-permute-start.5 = (bf16[256,256]{1,0:T(8,128)(2,1)S(1)}, bf16[256,256]{1,0:T(8,128)(2,1)S(1)}, u32[]{:S(2)}, u32[]{:S(2)}) collective-permute-start(bf16[256,256]{1,0:T(8,128)(2,1)S(1)} %add_east.2), channel_id=1, source_target_pairs={{0,2},{2,0},{1,3},{3,1},{4,6},{6,4},{5,7},{7,5},{8,10},{10,8},{9,1... | collective-permute-start | bytes 393224 | tf_op jit(solution)/shard_map/ppermute | solution.py:404
  23.5 3.1 %collective-permute-done.5.refs_0_.moved_a = bf16[256,256]{1,0:T(8,128)(2,1)S(1)} collective-permute-done((bf16[256,256]{1,0:T(8,128)(2,1)S(1)}, bf16[256,256]{1,0:T(8,128)(2,1)S(1)}, u32[]{:S(2)}, u32[]{:S(2)}) %collective-permute-start.5) | collective-permute-done | bytes 131104 | tf_op jit(solution)/shard_map/ppermute | solution.py:404
  26.5 3.3 %collective-permute-done.6.refs_2_.even_b.back_even_ref = bf16[3,256,256]{2,1,0:T(8,128)(2,1)S(1)} collective-permute-done((bf16[3,256,256]{2,1,0:T(8,128)(2,1)S(1)}, bf16[3,256,256]{2,1,0:T(8,128)(2,1)S(1)}, u32[]{:S(2)}, u32[]{:S(2)}) %collective-permute-start.6) | collective-permute-done | bytes 393248 | tf_op jit(solution)/shard_map/ppermute | solution.py:346
  30.6 1.3 %collective-permute-done.2.out_other_ref = bf16[227,256]{1,0:T(8,128)(2,1)S(1)} collective-permute-done((bf16[227,256]{1,0:T(8,128)(2,1)S(1)}, bf16[227,256]{1,0:T(8,128)(2,1)S(1)}, u32[]{:S(2)}, u32[]{:S(2)}) %collective-permute-start.2) | collective-permute-done | bytes 116256 | tf_op jit(solution)/shard_map/ppermute | solution.py:346
  32.7 2.2 %collective-permute-done.8.moved_b = bf16[256,256]{1,0:T(8,128)(2,1)S(1)} collective-permute-done((bf16[256,256]{1,0:T(8,128)(2,1)S(1)}, bf16[256,256]{1,0:T(8,128)(2,1)S(1)}, u32[]{:S(2)}, u32[]{:S(2)}) %collective-permute-start.8) | collective-permute-done | bytes 131104 | tf_op jit(solution)/shard_map/ppermute | solution.py:404
  34.9 2.9 %node_update_and_gradients.1 = (bf16[256,256]{1,0:T(8,128)(2,1)S(1)}, f32[1024,256]{1,0:T(8,128)S(1)}, bf16[1024,256]{1,0:T(8,128)(2,1)S(1)}, bf16[256,256]{1,0:T(8,128)(2,1)S(1)}, f32[4,2,64,256]{3,2,1,0:T(8,128)}) custom-call(bf16[2,256,256]{2,1,0:T(8,128)(2,1)S(1)} %get-tuple-element.34.after_ref.refs_1_.own_a, ...), custom_call_target="tpu_custom_call" | custom-call | flops 1 | bytes 1 | tf_op jit(solution)/shard_map/node_update_and_gradients/pallas_call | solution.py:479
  38.5 6.8 %collective-permute-start.15 = (bf16[256,256]{1,0:T(8,128)(2,1)S(1)}, bf16[256,256]{1,0:T(8,128)(2,1)S(1)}, u32[]{:S(2)}, u32[]{:S(2)}) collective-permute-start(bf16[256,256]{1,0:T(8,128)(2,1)S(1)} %get-tuple-element.52.proj_ref), channel_id=1, source_target_pairs={{0,4},{4,0},{8,12},{12,8},{1,5},{5,1},{9,13},{13,9},{2,6},{6,2},{1... | collective-permute-start | bytes 393224 | tf_op jit(solution)/shard_map/ppermute | solution.py:346
  45.5 1.6 %collective-permute-start.14 = (bf16[256,256]{1,0:T(8,128)(2,1)S(1)}, bf16[256,256]{1,0:T(8,128)(2,1)S(1)}, u32[]{:S(2)}, u32[]{:S(2)}) collective-permute-start(bf16[256,256]{1,0:T(8,128)(2,1)S(1)} %get-tuple-element.51), channel_id=1, source_target_pairs={{0,2},{1,5},{2,0},{3,7},{4,6},{5,1},{6,4},{7,3},{8,10},{9,13},{10,... | collective-permute-start | bytes 393224 | tf_op jit(solution)/shard_map/ppermute | solution.py:381
  47.6 2.0 %collective-permute-done.15.refs_0_.even_ref = bf16[256,256]{1,0:T(8,128)(2,1)S(1)} collective-permute-done((bf16[256,256]{1,0:T(8,128)(2,1)S(1)}, bf16[256,256]{1,0:T(8,128)(2,1)S(1)}, u32[]{:S(2)}, u32[]{:S(2)}) %collective-permute-start.15) | collective-permute-done | bytes 131104 | tf_op jit(solution)/shard_map/ppermute | solution.py:346
  50.6 1.4 %collective-permute-done.13.got_ref = bf16[256,256]{1,0:T(8,128)(2,1)S(1)} collective-permute-done((bf16[256,256]{1,0:T(8,128)(2,1)S(1)}, bf16[256,256]{1,0:T(8,128)(2,1)S(1)}, u32[]{:S(2)}, u32[]{:S(2)}) %collective-permute-start.13) | collective-permute-done | bytes 131104 | tf_op jit(solution)/shard_map/ppermute | solution.py:381
  52.1 1.5 %collective-permute-start.21 = (bf16[3,256,256]{2,1,0:T(8,128)(2,1)S(1)}, bf16[3,256,256]{2,1,0:T(8,128)(2,1)S(1)}, u32[]{:S(2)}, u32[]{:S(2)}) collective-permute-start(bf16[3,256,256]{2,1,0:T(8,128)(2,1)S(1)} %pack_nodes.1), channel_id=1, source_target_pairs={{2,0},{0,2},{3,1},{1,3},{6,4},{4,6},{7,5},{5,7},{10,8},{8,10},{11,... | collective-permute-start | bytes 1179656 | tf_op jit(solution)/shard_map/ppermute | solution.py:525
  53.6 2.0 %collective-permute-start.17 = (bf16[256,256]{1,0:T(8,128)(2,1)S(1)}, bf16[256,256]{1,0:T(8,128)(2,1)S(1)}, u32[]{:S(2)}, u32[]{:S(2)}) collective-permute-start(bf16[256,256]{1,0:T(8,128)(2,1)S(1)} %add_whole.7.refs_0_.kept_ref.after_ref), channel_id=1, source_target_pairs={{0,4},{1,9},{2,6},{3,11},{4,0},{5,13},{6,2},{7,15},{8,12},{9,1},{1... | collective-permute-start | bytes 393224 | tf_op jit(solution)/shard_map/ppermute | solution.py:381
  55.6 4.6 %collective-permute-done.18.got_ref = bf16[256,256]{1,0:T(8,128)(2,1)S(1)} collective-permute-done((bf16[256,256]{1,0:T(8,128)(2,1)S(1)}, bf16[256,256]{1,0:T(8,128)(2,1)S(1)}, u32[]{:S(2)}, u32[]{:S(2)}) %collective-permute-start.18) | collective-permute-done | bytes 131104 | tf_op jit(solution)/shard_map/ppermute | solution.py:381
  60.3 1.7 %collective-permute-done.17.got_ref = bf16[256,256]{1,0:T(8,128)(2,1)S(1)} collective-permute-done((bf16[256,256]{1,0:T(8,128)(2,1)S(1)}, bf16[256,256]{1,0:T(8,128)(2,1)S(1)}, u32[]{:S(2)}, u32[]{:S(2)}) %collective-permute-start.17) | collective-permute-done | bytes 131104 | tf_op jit(solution)/shard_map/ppermute | solution.py:381
  63.3 3.4 %collective-permute-done.20.got_ref = bf16[256,256]{1,0:T(8,128)(2,1)S(1)} collective-permute-done((bf16[256,256]{1,0:T(8,128)(2,1)S(1)}, bf16[256,256]{1,0:T(8,128)(2,1)S(1)}, u32[]{:S(2)}, u32[]{:S(2)}) %collective-permute-start.20) | collective-permute-done | bytes 131104 | tf_op jit(solution)/shard_map/ppermute | solution.py:381
  66.7 2.8 %collective-permute-done.19.got_ref = bf16[256,256]{1,0:T(8,128)(2,1)S(1)} collective-permute-done((bf16[256,256]{1,0:T(8,128)(2,1)S(1)}, bf16[256,256]{1,0:T(8,128)(2,1)S(1)}, u32[]{:S(2)}, u32[]{:S(2)}) %collective-permute-start.19) | collective-permute-done | bytes 131104 | tf_op jit(solution)/shard_map/ppermute | solution.py:381
  71.9 1.3 %collective-permute-start.23 = (bf16[256,256]{1,0:T(8,128)(2,1)S(1)}, bf16[256,256]{1,0:T(8,128)(2,1)S(1)}, u32[]{:S(2)}, u32[]{:S(2)}) collective-permute-start(bf16[256,256]{1,0:T(8,128)(2,1)S(1)} %add_whole.10.refs_0_.mine_ref), channel_id=1, source_target_pairs={{0,2},{1,5},{2,0},{3,7},{4,6},{5,1},{6,4},{7,3},{8,10},{9,13},{10,... | collective-permute-start | bytes 393224 | tf_op jit(solution)/shard_map/ppermute | solution.py:381
  (64 shorter events, 16.6 us)
Async XLA Ops:
  4.1 12.1 %collective-permute-start.1 = (bf16[3,256,256]{2,1,0:T(8,128)(2,1)S(1)}, bf16[3,256,256]{2,1,0:T(8,128)(2,1)S(1)}, u32[]{:S(2)}, u32[]{:S(2)}) collective-permute-start(bf16[3,256,256]{2,1,0:T(8,128)(2,1)S(1)} %get-tuple-element.36), channel_id=1, source_target_pairs={{0,2},{2,0},{1,3},{3,1},{4,6},{6,4},{5,7},{7,5},{8,10},{10,8},{9,1... | collective-permute-start | bytes 1179656 | tf_op jit(solution)/shard_map/ppermute | solution.py:404
  9.8 11.5 %collective-permute-start.3 = (bf16[2,256,256]{2,1,0:T(8,128)(2,1)S(1)}, bf16[2,256,256]{2,1,0:T(8,128)(2,1)S(1)}, u32[]{:S(2)}, u32[]{:S(2)}) collective-permute-start(bf16[2,256,256]{2,1,0:T(8,128)(2,1)S(1)} %get-tuple-element.39), channel_id=1, source_target_pairs={{0,4},{4,0},{8,12},{12,8},{1,5},{5,1},{9,13},{13,9},{2,6},{6,2},{1... | collective-permute-start | bytes 786440 | tf_op jit(solution)/shard_map/ppermute | solution.py:346
  11.4 9.8 %collective-permute-start.4 = (bf16[2,256,256]{2,1,0:T(8,128)(2,1)S(1)}, bf16[2,256,256]{2,1,0:T(8,128)(2,1)S(1)}, u32[]{:S(2)}, u32[]{:S(2)}) collective-permute-start(bf16[2,256,256]{2,1,0:T(8,128)(2,1)S(1)} %get-tuple-element.40), channel_id=1, source_target_pairs={{0,0},{4,8},{8,4},{12,12},{1,1},{5,9},{9,5},{13,13},{2,2},{6,10},{... | collective-permute-start | bytes 786440 | tf_op jit(solution)/shard_map/ppermute | solution.py:346
  18.7 11.1 %collective-permute-start.6 = (bf16[3,256,256]{2,1,0:T(8,128)(2,1)S(1)}, bf16[3,256,256]{2,1,0:T(8,128)(2,1)S(1)}, u32[]{:S(2)}, u32[]{:S(2)}) collective-permute-start(bf16[3,256,256]{2,1,0:T(8,128)(2,1)S(1)} %get-tuple-element.42), channel_id=1, source_target_pairs={{0,4},{4,0},{8,12},{12,8},{1,5},{5,1},{9,13},{13,9},{2,6},{6,2},{1... | collective-permute-start | bytes 1179656 | tf_op jit(solution)/shard_map/ppermute | solution.py:346
  20.6 9.2 %collective-permute-start.7 = (bf16[3,256,256]{2,1,0:T(8,128)(2,1)S(1)}, bf16[3,256,256]{2,1,0:T(8,128)(2,1)S(1)}, u32[]{:S(2)}, u32[]{:S(2)}) collective-permute-start(bf16[3,256,256]{2,1,0:T(8,128)(2,1)S(1)} %get-tuple-element.43), channel_id=1, source_target_pairs={{0,0},{4,8},{8,4},{12,12},{1,1},{5,9},{9,5},{13,13},{2,2},{6,10},{... | collective-permute-start | bytes 1179656 | tf_op jit(solution)/shard_map/ppermute | solution.py:346
  21.4 5.1 %collective-permute-start.5 = (bf16[256,256]{1,0:T(8,128)(2,1)S(1)}, bf16[256,256]{1,0:T(8,128)(2,1)S(1)}, u32[]{:S(2)}, u32[]{:S(2)}) collective-permute-start(bf16[256,256]{1,0:T(8,128)(2,1)S(1)} %add_east.2), channel_id=1, source_target_pairs={{0,2},{2,0},{1,3},{3,1},{4,6},{6,4},{5,7},{7,5},{8,10},{10,8},{9,1... | collective-permute-start | bytes 393224 | tf_op jit(solution)/shard_map/ppermute | solution.py:404
  23.0 9.7 %collective-permute-start.9 = (bf16[512,256]{1,0:T(8,128)(2,1)S(1)}, bf16[512,256]{1,0:T(8,128)(2,1)S(1)}, u32[]{:S(2)}, u32[]{:S(2)}) collective-permute-start(bf16[512,256]{1,0:T(8,128)(2,1)S(1)} %copy-done.4), channel_id=1, source_target_pairs={{0,1},{1,0},{2,3},{3,2},{4,5},{5,4},{6,7},{7,6},{8,9},{9,8},{10,11... | collective-permute-start | bytes 786440 | tf_op jit(solution)/shard_map/ppermute | solution.py:346
  23.0 9.7 %collective-permute-start.10 = (bf16[512,256]{1,0:T(8,128)(2,1)S(1)}, bf16[512,256]{1,0:T(8,128)(2,1)S(1)}, u32[]{:S(2)}, u32[]{:S(2)}) collective-permute-start(bf16[512,256]{1,0:T(8,128)(2,1)S(1)} %copy-done.5), channel_id=1, source_target_pairs={{0,1},{1,0},{2,3},{3,2},{4,5},{5,4},{6,7},{7,6},{8,9},{9,8},{10,11... | collective-permute-start | bytes 786440 | tf_op jit(solution)/shard_map/ppermute | solution.py:346
  26.5 6.1 %collective-permute-start.11 = (bf16[256,512]{1,0:T(8,128)(2,1)S(1)}, bf16[256,512]{1,0:T(8,128)(2,1)S(1)}, u32[]{:S(2)}, u32[]{:S(2)}) collective-permute-start(bf16[256,512]{1,0:T(8,128)(2,1)S(1)} %copy-done.6), channel_id=1, source_target_pairs={{0,1},{1,0},{2,3},{3,2},{4,5},{5,4},{6,7},{7,6},{8,9},{9,8},{10,11... | collective-permute-start | bytes 786440 | tf_op jit(solution)/shard_map/ppermute | solution.py:346
  29.9 5.0 %collective-permute-start.8 = (bf16[256,256]{1,0:T(8,128)(2,1)S(1)}, bf16[256,256]{1,0:T(8,128)(2,1)S(1)}, u32[]{:S(2)}, u32[]{:S(2)}) collective-permute-start(bf16[256,256]{1,0:T(8,128)(2,1)S(1)} %add_east.3), channel_id=1, source_target_pairs={{0,2},{2,0},{1,3},{3,1},{4,6},{6,4},{5,7},{7,5},{8,10},{10,8},{9,1... | collective-permute-start | bytes 393224 | tf_op jit(solution)/shard_map/ppermute | solution.py:404
  37.8 7.6 %collective-permute-start.12 = (bf16[1024,256]{1,0:T(8,128)(2,1)S(1)}, bf16[1024,256]{1,0:T(8,128)(2,1)S(1)}, u32[]{:S(2)}, u32[]{:S(2)}) collective-permute-start(bf16[1024,256]{1,0:T(8,128)(2,1)S(1)} %get-tuple-element.47), channel_id=1, source_target_pairs={{0,1},{1,0},{2,3},{3,2},{4,5},{5,4},{6,7},{7,6},{8,9},{9,8},{10,11... | collective-permute-start | bytes 1572872 | tf_op jit(solution)/shard_map/ppermute | solution.py:346
  37.8 9.8 %collective-permute-start.16 = (bf16[256,256]{1,0:T(8,128)(2,1)S(1)}, bf16[256,256]{1,0:T(8,128)(2,1)S(1)}, u32[]{:S(2)}, u32[]{:S(2)}) collective-permute-start(bf16[256,256]{1,0:T(8,128)(2,1)S(1)} %get-tuple-element.52.proj_ref), channel_id=1, source_target_pairs={{0,0},{4,8},{8,4},{12,12},{1,1},{5,9},{9,5},{13,13},{2,2},{6,10},{... | collective-permute-start | bytes 393224 | tf_op jit(solution)/shard_map/ppermute | solution.py:346
  38.5 11.1 %collective-permute-start.15 = (bf16[256,256]{1,0:T(8,128)(2,1)S(1)}, bf16[256,256]{1,0:T(8,128)(2,1)S(1)}, u32[]{:S(2)}, u32[]{:S(2)}) collective-permute-start(bf16[256,256]{1,0:T(8,128)(2,1)S(1)} %get-tuple-element.52.proj_ref), channel_id=1, source_target_pairs={{0,4},{4,0},{8,12},{12,8},{1,5},{5,1},{9,13},{13,9},{2,6},{6,2},{1... | collective-permute-start | bytes 393224 | tf_op jit(solution)/shard_map/ppermute | solution.py:346
  45.5 5.0 %collective-permute-start.14 = (bf16[256,256]{1,0:T(8,128)(2,1)S(1)}, bf16[256,256]{1,0:T(8,128)(2,1)S(1)}, u32[]{:S(2)}, u32[]{:S(2)}) collective-permute-start(bf16[256,256]{1,0:T(8,128)(2,1)S(1)} %get-tuple-element.51), channel_id=1, source_target_pairs={{0,2},{1,5},{2,0},{3,7},{4,6},{5,1},{6,4},{7,3},{8,10},{9,13},{10,... | collective-permute-start | bytes 393224 | tf_op jit(solution)/shard_map/ppermute | solution.py:381
  47.1 5.0 %collective-permute-start.13 = (bf16[256,256]{1,0:T(8,128)(2,1)S(1)}, bf16[256,256]{1,0:T(8,128)(2,1)S(1)}, u32[]{:S(2)}, u32[]{:S(2)}) collective-permute-start(bf16[256,256]{1,0:T(8,128)(2,1)S(1)} %get-tuple-element.49), channel_id=1, source_target_pairs={{0,2},{1,5},{2,0},{3,7},{4,6},{5,1},{6,4},{7,3},{8,10},{9,13},{10,... | collective-permute-start | bytes 393224 | tf_op jit(solution)/shard_map/ppermute | solution.py:381
  52.1 17.5 %collective-permute-start.21 = (bf16[3,256,256]{2,1,0:T(8,128)(2,1)S(1)}, bf16[3,256,256]{2,1,0:T(8,128)(2,1)S(1)}, u32[]{:S(2)}, u32[]{:S(2)}) collective-permute-start(bf16[3,256,256]{2,1,0:T(8,128)(2,1)S(1)} %pack_nodes.1), channel_id=1, source_target_pairs={{2,0},{0,2},{3,1},{1,3},{6,4},{4,6},{7,5},{5,7},{10,8},{8,10},{11,... | collective-permute-start | bytes 1179656 | tf_op jit(solution)/shard_map/ppermute | solution.py:525
  53.6 6.6 %collective-permute-start.18 = (bf16[256,256]{1,0:T(8,128)(2,1)S(1)}, bf16[256,256]{1,0:T(8,128)(2,1)S(1)}, u32[]{:S(2)}, u32[]{:S(2)}) collective-permute-start(bf16[256,256]{1,0:T(8,128)(2,1)S(1)} %add_whole.6.refs_0_.kept_ref), channel_id=1, source_target_pairs={{0,4},{1,9},{2,6},{3,11},{4,0},{5,13},{6,2},{7,15},{8,12},{9,1},{1... | collective-permute-start | bytes 393224 | tf_op jit(solution)/shard_map/ppermute | solution.py:381
  53.6 8.4 %collective-permute-start.17 = (bf16[256,256]{1,0:T(8,128)(2,1)S(1)}, bf16[256,256]{1,0:T(8,128)(2,1)S(1)}, u32[]{:S(2)}, u32[]{:S(2)}) collective-permute-start(bf16[256,256]{1,0:T(8,128)(2,1)S(1)} %add_whole.7.refs_0_.kept_ref.after_ref), channel_id=1, source_target_pairs={{0,4},{1,9},{2,6},{3,11},{4,0},{5,13},{6,2},{7,15},{8,12},{9,1},{1... | collective-permute-start | bytes 393224 | tf_op jit(solution)/shard_map/ppermute | solution.py:381
  60.2 6.5 %collective-permute-start.20 = (bf16[256,256]{1,0:T(8,128)(2,1)S(1)}, bf16[256,256]{1,0:T(8,128)(2,1)S(1)}, u32[]{:S(2)}, u32[]{:S(2)}) collective-permute-start(bf16[256,256]{1,0:T(8,128)(2,1)S(1)} %add_whole.8.refs_0_.kept_ref), channel_id=1, source_target_pairs={{0,8},{1,3},{2,10},{3,1},{4,12},{5,7},{6,14},{7,5},{8,0},{9,11},{1... | collective-permute-start | bytes 393224 | tf_op jit(solution)/shard_map/ppermute | solution.py:381
  62.1 7.4 %collective-permute-start.19 = (bf16[256,256]{1,0:T(8,128)(2,1)S(1)}, bf16[256,256]{1,0:T(8,128)(2,1)S(1)}, u32[]{:S(2)}, u32[]{:S(2)}) collective-permute-start(bf16[256,256]{1,0:T(8,128)(2,1)S(1)} %add_whole.9.refs_0_.kept_ref), channel_id=1, source_target_pairs={{0,8},{1,3},{2,10},{3,1},{4,12},{5,7},{6,14},{7,5},{8,0},{9,11},{1... | collective-permute-start | bytes 393224 | tf_op jit(solution)/shard_map/ppermute | solution.py:381
  70.7 3.3 %collective-permute-start.22 = (bf16[8,64,256]{2,1,0:T(8,128)(2,1)S(1)}, bf16[8,64,256]{2,1,0:T(8,128)(2,1)S(1)}, u32[]{:S(2)}, u32[]{:S(2)}) collective-permute-start(bf16[8,64,256]{2,1,0:T(8,128)(2,1)S(1)} %get-tuple-element.54), channel_id=1, source_target_pairs={{0,1},{1,0},{2,3},{3,2},{4,5},{5,4},{6,7},{7,6},{8,9},{9,8},{10,11... | collective-permute-start | bytes 786440 | tf_op jit(solution)/shard_map/ppermute | solution.py:346
  70.8 2.5 %collective-permute-start.25 = (bf16[256,256]{1,0:T(8,128)(2,1)S(1)}, bf16[256,256]{1,0:T(8,128)(2,1)S(1)}, u32[]{:S(2)}, u32[]{:S(2)}) collective-permute-start(bf16[256,256]{1,0:T(8,128)(2,1)S(1)} %get-tuple-element.57), channel_id=1, source_target_pairs={{0,1},{1,0},{2,3},{3,2},{4,5},{5,4},{6,7},{7,6},{8,9},{9,8},{10,11... | collective-permute-start | bytes 393224 | tf_op jit(solution)/shard_map/ppermute | solution.py:346
  71.3 5.0 %collective-permute-start.24 = (bf16[256,256]{1,0:T(8,128)(2,1)S(1)}, bf16[256,256]{1,0:T(8,128)(2,1)S(1)}, u32[]{:S(2)}, u32[]{:S(2)}) collective-permute-start(bf16[256,256]{1,0:T(8,128)(2,1)S(1)} %add_whole.11.after_ref.mine_ref), channel_id=1, source_target_pairs={{0,2},{1,5},{2,0},{3,7},{4,6},{5,1},{6,4},{7,3},{8,10},{9,13},{10,... | collective-permute-start | bytes 393224 | tf_op jit(solution)/shard_map/ppermute | solution.py:381
  71.9 5.7 %collective-permute-start.23 = (bf16[256,256]{1,0:T(8,128)(2,1)S(1)}, bf16[256,256]{1,0:T(8,128)(2,1)S(1)}, u32[]{:S(2)}, u32[]{:S(2)}) collective-permute-start(bf16[256,256]{1,0:T(8,128)(2,1)S(1)} %add_whole.10.refs_0_.mine_ref), channel_id=1, source_target_pairs={{0,2},{1,5},{2,0},{3,7},{4,6},{5,1},{6,4},{7,3},{8,10},{9,13},{10,... | collective-permute-start | bytes 393224 | tf_op jit(solution)/shard_map/ppermute | solution.py:381
  (10 other events, 49.1 us)

commit v14 on v12

--- a/solution.py
+++ b/solution.py
@@ -90,8 +90,8 @@
 
 
 def back_kernel(
-    device_ref, slot_ref, tiles_ref, cot_ref, own_ref, east_ref, side_ref,
-    total, tiles, cots, tile_sems, cot_sems,
+    device_ref, slot_ref, tiles_ref, cot_ref, weight_ref, own_ref, east_ref, side_ref, held_ref,
+    total, tiles, cots, tile_sems, cot_sems, weight_sem,
 ):
     blocks, rows = tiles.shape[0], tiles.shape[1]
     count = blocks // STEPS
@@ -108,6 +108,8 @@
         ))
         for copy in copies[-1]:
             copy.start()
+    weight_copy = pltpu.make_async_copy(weight_ref, held_ref, weight_sem)
+    weight_copy.start()
     total[...] = jnp.zeros_like(total)
     for b in range(blocks):
         if b % count == 0:
@@ -121,6 +123,7 @@
     for k in range(3):
         block = total[(2 * k + 1) * slots : (2 * k + 2) * slots]
         east_ref[k] = block.reshape(east_ref.shape[1:]).astype(east_ref.dtype)
+    weight_copy.wait()
 
 
 def encode_kernel(
@@ -412,14 +415,12 @@
     routes = (in_hbm(device), in_hbm(slot))
     tiles_in, grid_in_t, cot_in_t = in_hbm(interp_tiles), in_hbm(grid_t), in_hbm(cot_t)
     pair_shape = (2, nodes, width)
-    embed_other = swap_rep(w_embed)
-
-    back_own, back_east, back_side = call(
+    back_own, back_east, back_side, embed_own = call(
         back_kernel, "back_messages",
-        [smem(), smem(), anywhere(), anywhere()],
-        [vmem()] * 3,
+        [smem(), smem(), anywhere(), anywhere(), anywhere()],
+        [vmem()] * 4,
         [shape_of((nodes, padded), BF16), shape_of((3, nodes, padded), BF16),
-         shape_of((2, nodes, padded), BF16)],
+         shape_of((2, nodes, padded), BF16), shape_of((channels, width), BF16)],
         1, 1,
         scratch=[
             pltpu.VMEM((6 * slots, half, padded), F32),
@@ -427,9 +428,11 @@
             pltpu.VMEM(cot_t.shape, BF16),
             pltpu.SemaphoreType.DMA((STEPS,)),
             pltpu.SemaphoreType.DMA((STEPS,)),
+            pltpu.SemaphoreType.DMA,
         ],
-    )(*routes, tiles_in, cot_in_t)
+    )(*routes, tiles_in, cot_in_t, in_hbm(w_embed))
     back_moved = to_east(back_east)
+    embed_other = swap_rep(embed_own)
 
     def encode(after, weight):
         return call(
@@ -443,7 +446,7 @@
             ],
         )(*routes, after, grid_t, interp_tiles, weight)
 
-    own_a, even_a, odd_a, hidden_a = encode(back_own, in_hbm(w_embed))
+    own_a, even_a, odd_a, hidden_a = encode(back_own, embed_own)
     even_in_a, odd_in_a = to_even(even_a), to_odd(odd_a)
     own_b, even_b, odd_b, hidden_b = encode(own_a, embed_other)
     even_in_b, odd_in_b = to_even(even_b), to_odd(odd_b)

time: 76 us -> 75.7 us (level)
  no operation moved by 1% of the time
where the time goes in v14:
time: 75.7 us; the launch traced here: 75.4 us
  starting transfers between devices  33.3 us (44%)
  waiting for transfers between devices  23.9 us (32%)
  Pallas kernels  17.3 us (23%)
  between operations  0.92 us (1%)
    ppermute x16, starting transfers between devices, along(): return lambda value: lax.ppermute(value, axis, pairs)  16.8 us
    ppermute x8, waiting for transfers between devices, sum_swap(): return lax.ppermute(value, ('lat', 'lon', 'rep'), pairs)  14.4 us
    ppermute x8, starting transfers between devices, sum_swap(): return lax.ppermute(value, ('lat', 'lon', 'rep'), pairs)  11.1 us
    ppermute x16, waiting for transfers between devices, along(): return lambda value: lax.ppermute(value, axis, pairs)  9.53 us
    pallas_call x2, Pallas kernels, encode(): call(encode_kernel, 'encode', [smem(), smem(), anywhere()] + [vmem()] * 3...  4.76 us
    ppermute x3, starting transfers between devices, per_device(): to_east = lambda value: lax.ppermute(value, 'lon', east_pairs)  4.21 us
    pallas_call x1, Pallas kernels, per_device(): call(back_kernel, 'back_messages', [smem(), smem(), anywhere(), anywhere(...  3.5 us
    pallas_call x1, Pallas kernels, per_device(): call(node_kernel, 'node_update_and_gradients', sums_specs * 2 + [whole(em...  2.85 us
  transfers between devices with their start and end apart: 28, of which 12 were waited for; matrix products, arithmetic and copies ran while one was open for 0% of the time, Pallas kernels for 12%

profile of v14, /device:TPU:0, one launch (start us, length us, event | category | flops | bytes accessed | tf_op | source)
XLA Modules:
  0.0 75.4 jit_solution(13390144572697186895)
XLA Ops:
  0.7 3.5 %back_messages.1 = (bf16[256,256]{1,0:T(8,128)(2,1)S(1)}, bf16[3,256,256]{2,1,0:T(8,128)(2,1)S(1)}, bf16[2,256,256]{2,1,0:T(8,128)(2,1)S(1)}, bf16[227,256]{1,0:T(8,128)(2,1)S(1)}) custom-call(s32[16]{0:T(128)} %bitcast.25, s32[16]{0:T(128)} %slot_ref.7, bf16[16,128,128]{2,1,0:T(8,128)(2,1)} %tiles_ref.7, bf16[227,2048]{1,0:T(8,128)(2,1)} %bitcast.13, ...), custom_call_target="tpu_custom_call" | custom-call | flops 1 | bytes 1 | tf_op jit(solution)/shard_map/back_messages/pallas_call | solution.py:418
  4.2 3.0 %collective-permute-start.4 = (bf16[3,256,256]{2,1,0:T(8,128)(2,1)S(1)}, bf16[3,256,256]{2,1,0:T(8,128)(2,1)S(1)}, u32[]{:S(2)}, u32[]{:S(2)}) collective-permute-start(bf16[3,256,256]{2,1,0:T(8,128)(2,1)S(1)} %get-tuple-element.43), channel_id=1, source_target_pairs={{0,2},{2,0},{1,3},{3,1},{4,6},{6,4},{5,7},{7,5},{8,10},{10,8},{9,1... | collective-permute-start | bytes 1179656 | tf_op jit(solution)/shard_map/ppermute | solution.py:410
  7.2 2.3 %encode.2 = (bf16[2,256,256]{2,1,0:T(8,128)(2,1)S(1)}, bf16[2,256,256]{2,1,0:T(8,128)(2,1)S(1)}, bf16[2,256,256]{2,1,0:T(8,128)(2,1)S(1)}, bf16[1024,256]{1,0:T(8,128)(2,1)S(1)}) custom-call(s32[16]{0:T(128)} %bitcast.26, s32[16]{0:T(128)} %slot_ref.7, bf16[256,256]{1,0:T(8,128)(2,1)S(1)} %get-tuple-element.35.after_ref.back_ref, ...), custom_call_target="tpu_custom_call" | custom-call | flops 1 | bytes 1 | tf_op jit(solution)/shard_map/encode/pallas_call | solution.py:438
  9.5 1.6 %collective-permute-start.2 = (bf16[2,256,256]{2,1,0:T(8,128)(2,1)S(1)}, bf16[2,256,256]{2,1,0:T(8,128)(2,1)S(1)}, u32[]{:S(2)}, u32[]{:S(2)}) collective-permute-start(bf16[2,256,256]{2,1,0:T(8,128)(2,1)S(1)} %get-tuple-element.41), channel_id=1, source_target_pairs={{0,4},{4,0},{8,12},{12,8},{1,5},{5,1},{9,13},{13,9},{2,6},{6,2},{1... | collective-permute-start | bytes 786440 | tf_op jit(solution)/shard_map/ppermute | solution.py:352
  12.5 2.4 %encode.3 = (bf16[2,256,256]{2,1,0:T(8,128)(2,1)S(1)}, bf16[2,256,256]{2,1,0:T(8,128)(2,1)S(1)}, bf16[2,256,256]{2,1,0:T(8,128)(2,1)S(1)}, bf16[1024,256]{1,0:T(8,128)(2,1)S(1)}) custom-call(s32[16]{0:T(128)} %bitcast.27, s32[16]{0:T(128)} %slot_ref.7, bf16[2,256,256]{2,1,0:T(8,128)(2,1)S(1)} %get-tuple-element.38.after_ref.refs_1_.own_a, ...), custom_call_target="tpu_custom_call" | custom-call | flops 1 | bytes 1 | tf_op jit(solution)/shard_map/encode/pallas_call | solution.py:438
  14.9 3.8 %collective-permute-start.6 = (bf16[2,256,256]{2,1,0:T(8,128)(2,1)S(1)}, bf16[2,256,256]{2,1,0:T(8,128)(2,1)S(1)}, u32[]{:S(2)}, u32[]{:S(2)}) collective-permute-start(bf16[2,256,256]{2,1,0:T(8,128)(2,1)S(1)} %get-tuple-element.45), channel_id=1, source_target_pairs={{0,4},{4,0},{8,12},{12,8},{1,5},{5,1},{9,13},{13,9},{2,6},{6,2},{1... | collective-permute-start | bytes 786440 | tf_op jit(solution)/shard_map/ppermute | solution.py:352
  20.5 4.9 %collective-permute-done.6.refs_2_.even_b = bf16[2,256,256]{2,1,0:T(8,128)(2,1)S(1)} collective-permute-done((bf16[2,256,256]{2,1,0:T(8,128)(2,1)S(1)}, bf16[2,256,256]{2,1,0:T(8,128)(2,1)S(1)}, u32[]{:S(2)}, u32[]{:S(2)}) %collective-permute-start.6) | collective-permute-done | bytes 262176 | tf_op jit(solution)/shard_map/ppermute | solution.py:352
  27.1 3.4 %collective-permute-start.10 = (bf16[256,256]{1,0:T(8,128)(2,1)S(1)}, bf16[256,256]{1,0:T(8,128)(2,1)S(1)}, u32[]{:S(2)}, u32[]{:S(2)}) collective-permute-start(bf16[256,256]{1,0:T(8,128)(2,1)S(1)} %get-tuple-element.48), channel_id=1, source_target_pairs={{0,4},{4,0},{8,12},{12,8},{1,5},{5,1},{9,13},{13,9},{2,6},{6,2},{1... | collective-permute-start | bytes 393224 | tf_op jit(solution)/shard_map/ppermute | solution.py:352
  32.0 2.4 %collective-permute-done.10.back_even_ref = bf16[256,256]{1,0:T(8,128)(2,1)S(1)} collective-permute-done((bf16[256,256]{1,0:T(8,128)(2,1)S(1)}, bf16[256,256]{1,0:T(8,128)(2,1)S(1)}, u32[]{:S(2)}, u32[]{:S(2)}) %collective-permute-start.10) | collective-permute-done | bytes 131104 | tf_op jit(solution)/shard_map/ppermute | solution.py:352
  34.4 2.9 %node_update_and_gradients.1 = (bf16[256,256]{1,0:T(8,128)(2,1)S(1)}, f32[1024,256]{1,0:T(8,128)S(1)}, bf16[1024,256]{1,0:T(8,128)(2,1)S(1)}, bf16[256,256]{1,0:T(8,128)(2,1)S(1)}, f32[4,2,64,256]{3,2,1,0:T(8,128)}) custom-call(bf16[2,256,256]{2,1,0:T(8,128)(2,1)S(1)} %get-tuple-element.38.after_ref.refs_1_.own_a, ...), custom_call_target="tpu_custom_call" | custom-call | flops 1 | bytes 1 | tf_op jit(solution)/shard_map/node_update_and_gradients/pallas_call | solution.py:489
  37.3 3.7 %collective-permute-start.17 = (bf16[256,256]{1,0:T(8,128)(2,1)S(1)}, bf16[256,256]{1,0:T(8,128)(2,1)S(1)}, u32[]{:S(2)}, u32[]{:S(2)}) collective-permute-start(bf16[256,256]{1,0:T(8,128)(2,1)S(1)} %get-tuple-element.58.proj_ref), channel_id=1, source_target_pairs={{0,4},{4,0},{8,12},{12,8},{1,5},{5,1},{9,13},{13,9},{2,6},{6,2},{1... | collective-permute-start | bytes 393224 | tf_op jit(solution)/shard_map/ppermute | solution.py:352
  41.9 1.1 %collective-permute-start.16 = (bf16[256,256]{1,0:T(8,128)(2,1)S(1)}, bf16[256,256]{1,0:T(8,128)(2,1)S(1)}, u32[]{:S(2)}, u32[]{:S(2)}) collective-permute-start(bf16[256,256]{1,0:T(8,128)(2,1)S(1)} %get-tuple-element.57), channel_id=1, source_target_pairs={{0,2},{1,5},{2,0},{3,7},{4,6},{5,1},{6,4},{7,3},{8,10},{9,13},{10,... | collective-permute-start | bytes 393224 | tf_op jit(solution)/shard_map/ppermute | solution.py:387
  44.0 1.1 %collective-permute-done.17.refs_0_.even_ref = bf16[256,256]{1,0:T(8,128)(2,1)S(1)} collective-permute-done((bf16[256,256]{1,0:T(8,128)(2,1)S(1)}, bf16[256,256]{1,0:T(8,128)(2,1)S(1)}, u32[]{:S(2)}, u32[]{:S(2)}) %collective-permute-start.17) | collective-permute-done | bytes 131104 | tf_op jit(solution)/shard_map/ppermute | solution.py:352
  45.1 1.8 %collective-permute-done.16.got_ref = bf16[256,256]{1,0:T(8,128)(2,1)S(1)} collective-permute-done((bf16[256,256]{1,0:T(8,128)(2,1)S(1)}, bf16[256,256]{1,0:T(8,128)(2,1)S(1)}, u32[]{:S(2)}, u32[]{:S(2)}) %collective-permute-start.16) | collective-permute-done | bytes 131104 | tf_op jit(solution)/shard_map/ppermute | solution.py:387
  47.0 1.4 %collective-permute-done.15.got_ref = bf16[256,256]{1,0:T(8,128)(2,1)S(1)} collective-permute-done((bf16[256,256]{1,0:T(8,128)(2,1)S(1)}, bf16[256,256]{1,0:T(8,128)(2,1)S(1)}, u32[]{:S(2)}, u32[]{:S(2)}) %collective-permute-start.15) | collective-permute-done | bytes 131104 | tf_op jit(solution)/shard_map/ppermute | solution.py:387
  48.4 1.1 %collective-permute-start.23 = (bf16[3,256,256]{2,1,0:T(8,128)(2,1)S(1)}, bf16[3,256,256]{2,1,0:T(8,128)(2,1)S(1)}, u32[]{:S(2)}, u32[]{:S(2)}) collective-permute-start(bf16[3,256,256]{2,1,0:T(8,128)(2,1)S(1)} %pack_nodes.1), channel_id=1, source_target_pairs={{2,0},{0,2},{3,1},{1,3},{6,4},{4,6},{7,5},{5,7},{10,8},{8,10},{11,... | collective-permute-start | bytes 1179656 | tf_op jit(solution)/shard_map/ppermute | solution.py:534
  49.5 2.5 %collective-permute-start.20 = (bf16[256,256]{1,0:T(8,128)(2,1)S(1)}, bf16[256,256]{1,0:T(8,128)(2,1)S(1)}, u32[]{:S(2)}, u32[]{:S(2)}) collective-permute-start(bf16[256,256]{1,0:T(8,128)(2,1)S(1)} %add_whole.6.refs_0_.kept_ref), channel_id=1, source_target_pairs={{0,4},{1,9},{2,6},{3,11},{4,0},{5,13},{6,2},{7,15},{8,12},{9,1},{1... | collective-permute-start | bytes 393224 | tf_op jit(solution)/shard_map/ppermute | solution.py:387
  52.1 3.7 %collective-permute-done.20.got_ref = bf16[256,256]{1,0:T(8,128)(2,1)S(1)} collective-permute-done((bf16[256,256]{1,0:T(8,128)(2,1)S(1)}, bf16[256,256]{1,0:T(8,128)(2,1)S(1)}, u32[]{:S(2)}, u32[]{:S(2)}) %collective-permute-start.20) | collective-permute-done | bytes 131104 | tf_op jit(solution)/shard_map/ppermute | solution.py:387
  55.8 2.9 %collective-permute-start.22 = (bf16[256,256]{1,0:T(8,128)(2,1)S(1)}, bf16[256,256]{1,0:T(8,128)(2,1)S(1)}, u32[]{:S(2)}, u32[]{:S(2)}) collective-permute-start(bf16[256,256]{1,0:T(8,128)(2,1)S(1)} %add_whole.8.refs_0_.kept_ref), channel_id=1, source_target_pairs={{0,8},{1,3},{2,10},{3,1},{4,12},{5,7},{6,14},{7,5},{8,0},{9,11},{1... | collective-permute-start | bytes 393224 | tf_op jit(solution)/shard_map/ppermute | solution.py:387
  58.8 1.5 %collective-permute-start.21 = (bf16[256,256]{1,0:T(8,128)(2,1)S(1)}, bf16[256,256]{1,0:T(8,128)(2,1)S(1)}, u32[]{:S(2)}, u32[]{:S(2)}) collective-permute-start(bf16[256,256]{1,0:T(8,128)(2,1)S(1)} %add_whole.9.refs_0_.kept_ref), channel_id=1, source_target_pairs={{0,8},{1,3},{2,10},{3,1},{4,12},{5,7},{6,14},{7,5},{8,0},{9,11},{1... | collective-permute-start | bytes 393224 | tf_op jit(solution)/shard_map/ppermute | solution.py:387
  60.3 1.4 %collective-permute-done.22.got_ref = bf16[256,256]{1,0:T(8,128)(2,1)S(1)} collective-permute-done((bf16[256,256]{1,0:T(8,128)(2,1)S(1)}, bf16[256,256]{1,0:T(8,128)(2,1)S(1)}, u32[]{:S(2)}, u32[]{:S(2)}) %collective-permute-start.22) | collective-permute-done | bytes 131104 | tf_op jit(solution)/shard_map/ppermute | solution.py:387
  61.8 4.7 %collective-permute-done.21.got_ref = bf16[256,256]{1,0:T(8,128)(2,1)S(1)} collective-permute-done((bf16[256,256]{1,0:T(8,128)(2,1)S(1)}, bf16[256,256]{1,0:T(8,128)(2,1)S(1)}, u32[]{:S(2)}, u32[]{:S(2)}) %collective-permute-start.21) | collective-permute-done | bytes 131104 | tf_op jit(solution)/shard_map/ppermute | solution.py:387
  66.5 1.1 %pick_nodes.1 = (bf16[8,64,256]{2,1,0:T(8,128)(2,1)S(1)}, bf16[8,64,256]{2,1,0:T(8,128)(2,1)S(1)}) custom-call(s32[16]{0:T(128)} %bitcast.28, s32[16]{0:T(128)} %slot_ref.7, bf16[256,256]{1,0:T(8,128)(2,1)S(1)} %add_whole.11.after_ref.mine_ref, bf16[12,64,256]{2,1,0:T(8,128)(2,1)S(1)} %bitcast.15, bf16[12,64,256]{2,1,0:T(8,128)(2,1)S(1)} %bitcast.20), custom_call_target="tpu_custom_call" | custom-call | flops 1 | bytes 1 | tf_op jit(solution)/shard_map/pick_nodes/pallas_call | solution.py:554
  71.0 1.2 %decode.1.after_ref.refs_0_ = bf16[227,1024]{1,0:T(8,128)(2,1)} custom-call(bf16[16,128,128]{2,1,0:T(8,128)(2,1)S(1)} %copy-done, f32[227,1024]{1,0:T(8,128)S(1)} %get-tuple-element.40.base_ref, bf16[8,64,256]{2,1,0:T(8,128)(2,1)S(1)} %get-tuple-element.59.mine_ref, bf16[8,64,256]{2,1,0:T(8,128)(2,1)S(1)} %collective-permute-done.24.got_ref), custom_call_target="tpu_custom_call" | custom-call | flops 1 | bytes 1 | tf_op jit(solution)/shard_map/decode/pallas_call | solution.py:558
  (67 shorter events, 14.9 us)
Async XLA Ops:
  4.2 15.5 %collective-permute-start.4 = (bf16[3,256,256]{2,1,0:T(8,128)(2,1)S(1)}, bf16[3,256,256]{2,1,0:T(8,128)(2,1)S(1)}, u32[]{:S(2)}, u32[]{:S(2)}) collective-permute-start(bf16[3,256,256]{2,1,0:T(8,128)(2,1)S(1)} %get-tuple-element.43), channel_id=1, source_target_pairs={{0,2},{2,0},{1,3},{3,1},{4,6},{6,4},{5,7},{7,5},{8,10},{10,8},{9,1... | collective-permute-start | bytes 1179656 | tf_op jit(solution)/shard_map/ppermute | solution.py:410
  9.5 10.1 %collective-permute-start.2 = (bf16[2,256,256]{2,1,0:T(8,128)(2,1)S(1)}, bf16[2,256,256]{2,1,0:T(8,128)(2,1)S(1)}, u32[]{:S(2)}, u32[]{:S(2)}) collective-permute-start(bf16[2,256,256]{2,1,0:T(8,128)(2,1)S(1)} %get-tuple-element.41), channel_id=1, source_target_pairs={{0,4},{4,0},{8,12},{12,8},{1,5},{5,1},{9,13},{13,9},{2,6},{6,2},{1... | collective-permute-start | bytes 786440 | tf_op jit(solution)/shard_map/ppermute | solution.py:352
  11.1 8.5 %collective-permute-start.3 = (bf16[2,256,256]{2,1,0:T(8,128)(2,1)S(1)}, bf16[2,256,256]{2,1,0:T(8,128)(2,1)S(1)}, u32[]{:S(2)}, u32[]{:S(2)}) collective-permute-start(bf16[2,256,256]{2,1,0:T(8,128)(2,1)S(1)} %get-tuple-element.42), channel_id=1, source_target_pairs={{0,0},{4,8},{8,4},{12,12},{1,1},{5,9},{9,5},{13,13},{2,2},{6,10},{... | collective-permute-start | bytes 786440 | tf_op jit(solution)/shard_map/ppermute | solution.py:352
  14.9 10.5 %collective-permute-start.6 = (bf16[2,256,256]{2,1,0:T(8,128)(2,1)S(1)}, bf16[2,256,256]{2,1,0:T(8,128)(2,1)S(1)}, u32[]{:S(2)}, u32[]{:S(2)}) collective-permute-start(bf16[2,256,256]{2,1,0:T(8,128)(2,1)S(1)} %get-tuple-element.45), channel_id=1, source_target_pairs={{0,4},{4,0},{8,12},{12,8},{1,5},{5,1},{9,13},{13,9},{2,6},{6,2},{1... | collective-permute-start | bytes 786440 | tf_op jit(solution)/shard_map/ppermute | solution.py:352
  18.7 6.7 %collective-permute-start.7 = (bf16[2,256,256]{2,1,0:T(8,128)(2,1)S(1)}, bf16[2,256,256]{2,1,0:T(8,128)(2,1)S(1)}, u32[]{:S(2)}, u32[]{:S(2)}) collective-permute-start(bf16[2,256,256]{2,1,0:T(8,128)(2,1)S(1)} %get-tuple-element.46), channel_id=1, source_target_pairs={{0,0},{4,8},{8,4},{12,12},{1,1},{5,9},{9,5},{13,13},{2,2},{6,10},{... | collective-permute-start | bytes 786440 | tf_op jit(solution)/shard_map/ppermute | solution.py:352
  19.6 11.0 %collective-permute-start.9 = (bf16[512,256]{1,0:T(8,128)(2,1)S(1)}, bf16[512,256]{1,0:T(8,128)(2,1)S(1)}, u32[]{:S(2)}, u32[]{:S(2)}) collective-permute-start(bf16[512,256]{1,0:T(8,128)(2,1)S(1)} %copy-done.4), channel_id=1, source_target_pairs={{0,1},{1,0},{2,3},{3,2},{4,5},{5,4},{6,7},{7,6},{8,9},{9,8},{10,11... | collective-permute-start | bytes 786440 | tf_op jit(solution)/shard_map/ppermute | solution.py:352
  19.7 6.2 %collective-permute-start.5 = (bf16[256,256]{1,0:T(8,128)(2,1)S(1)}, bf16[256,256]{1,0:T(8,128)(2,1)S(1)}, u32[]{:S(2)}, u32[]{:S(2)}) collective-permute-start(bf16[256,256]{1,0:T(8,128)(2,1)S(1)} %add_east.2), channel_id=1, source_target_pairs={{0,2},{2,0},{1,3},{3,1},{4,6},{6,4},{5,7},{7,5},{8,10},{10,8},{9,1... | collective-permute-start | bytes 393224 | tf_op jit(solution)/shard_map/ppermute | solution.py:410
  20.3 11.6 %collective-permute-start.12 = (bf16[512,256]{1,0:T(8,128)(2,1)S(1)}, bf16[512,256]{1,0:T(8,128)(2,1)S(1)}, u32[]{:S(2)}, u32[]{:S(2)}) collective-permute-start(bf16[512,256]{1,0:T(8,128)(2,1)S(1)} %copy-done.5), channel_id=1, source_target_pairs={{0,1},{1,0},{2,3},{3,2},{4,5},{5,4},{6,7},{7,6},{8,9},{9,8},{10,11... | collective-permute-start | bytes 786440 | tf_op jit(solution)/shard_map/ppermute | solution.py:352
  25.4 6.6 %collective-permute-start.13 = (bf16[256,512]{1,0:T(8,128)(2,1)S(1)}, bf16[256,512]{1,0:T(8,128)(2,1)S(1)}, u32[]{:S(2)}, u32[]{:S(2)}) collective-permute-start(bf16[256,512]{1,0:T(8,128)(2,1)S(1)} %copy-done.6), channel_id=1, source_target_pairs={{0,1},{1,0},{2,3},{3,2},{4,5},{5,4},{6,7},{7,6},{8,9},{9,8},{10,11... | collective-permute-start | bytes 786440 | tf_op jit(solution)/shard_map/ppermute | solution.py:352
  26.0 6.0 %collective-permute-start.8 = (bf16[256,256]{1,0:T(8,128)(2,1)S(1)}, bf16[256,256]{1,0:T(8,128)(2,1)S(1)}, u32[]{:S(2)}, u32[]{:S(2)}) collective-permute-start(bf16[256,256]{1,0:T(8,128)(2,1)S(1)} %add_east.3.after_ref), channel_id=1, source_target_pairs={{0,2},{2,0},{1,3},{3,1},{4,6},{6,4},{5,7},{7,5},{8,10},{10,8},{9,1... | collective-permute-start | bytes 393224 | tf_op jit(solution)/shard_map/ppermute | solution.py:410
  27.1 7.2 %collective-permute-start.10 = (bf16[256,256]{1,0:T(8,128)(2,1)S(1)}, bf16[256,256]{1,0:T(8,128)(2,1)S(1)}, u32[]{:S(2)}, u32[]{:S(2)}) collective-permute-start(bf16[256,256]{1,0:T(8,128)(2,1)S(1)} %get-tuple-element.48), channel_id=1, source_target_pairs={{0,4},{4,0},{8,12},{12,8},{1,5},{5,1},{9,13},{13,9},{2,6},{6,2},{1... | collective-permute-start | bytes 393224 | tf_op jit(solution)/shard_map/ppermute | solution.py:352
  30.6 3.8 %collective-permute-start.11 = (bf16[256,256]{1,0:T(8,128)(2,1)S(1)}, bf16[256,256]{1,0:T(8,128)(2,1)S(1)}, u32[]{:S(2)}, u32[]{:S(2)}) collective-permute-start(bf16[256,256]{1,0:T(8,128)(2,1)S(1)} %get-tuple-element.49), channel_id=1, source_target_pairs={{0,0},{4,8},{8,4},{12,12},{1,1},{5,9},{9,5},{13,13},{2,2},{6,10},{... | collective-permute-start | bytes 393224 | tf_op jit(solution)/shard_map/ppermute | solution.py:352
  37.2 4.4 %collective-permute-start.14 = (bf16[1024,256]{1,0:T(8,128)(2,1)S(1)}, bf16[1024,256]{1,0:T(8,128)(2,1)S(1)}, u32[]{:S(2)}, u32[]{:S(2)}) collective-permute-start(bf16[1024,256]{1,0:T(8,128)(2,1)S(1)} %get-tuple-element.53), channel_id=1, source_target_pairs={{0,1},{1,0},{2,3},{3,2},{4,5},{5,4},{6,7},{7,6},{8,9},{9,8},{10,11... | collective-permute-start | bytes 1572872 | tf_op jit(solution)/shard_map/ppermute | solution.py:352
  37.3 7.8 %collective-permute-start.17 = (bf16[256,256]{1,0:T(8,128)(2,1)S(1)}, bf16[256,256]{1,0:T(8,128)(2,1)S(1)}, u32[]{:S(2)}, u32[]{:S(2)}) collective-permute-start(bf16[256,256]{1,0:T(8,128)(2,1)S(1)} %get-tuple-element.58.proj_ref), channel_id=1, source_target_pairs={{0,4},{4,0},{8,12},{12,8},{1,5},{5,1},{9,13},{13,9},{2,6},{6,2},{1... | collective-permute-start | bytes 393224 | tf_op jit(solution)/shard_map/ppermute | solution.py:352
  41.0 4.1 %collective-permute-start.18 = (bf16[256,256]{1,0:T(8,128)(2,1)S(1)}, bf16[256,256]{1,0:T(8,128)(2,1)S(1)}, u32[]{:S(2)}, u32[]{:S(2)}) collective-permute-start(bf16[256,256]{1,0:T(8,128)(2,1)S(1)} %get-tuple-element.58.proj_ref), channel_id=1, source_target_pairs={{0,0},{4,8},{8,4},{12,12},{1,1},{5,9},{9,5},{13,13},{2,2},{6,10},{... | collective-permute-start | bytes 393224 | tf_op jit(solution)/shard_map/ppermute | solution.py:352
  41.9 5.0 %collective-permute-start.16 = (bf16[256,256]{1,0:T(8,128)(2,1)S(1)}, bf16[256,256]{1,0:T(8,128)(2,1)S(1)}, u32[]{:S(2)}, u32[]{:S(2)}) collective-permute-start(bf16[256,256]{1,0:T(8,128)(2,1)S(1)} %get-tuple-element.57), channel_id=1, source_target_pairs={{0,2},{1,5},{2,0},{3,7},{4,6},{5,1},{6,4},{7,3},{8,10},{9,13},{10,... | collective-permute-start | bytes 393224 | tf_op jit(solution)/shard_map/ppermute | solution.py:387
  43.0 5.3 %collective-permute-start.15 = (bf16[256,256]{1,0:T(8,128)(2,1)S(1)}, bf16[256,256]{1,0:T(8,128)(2,1)S(1)}, u32[]{:S(2)}, u32[]{:S(2)}) collective-permute-start(bf16[256,256]{1,0:T(8,128)(2,1)S(1)} %get-tuple-element.55), channel_id=1, source_target_pairs={{0,2},{1,5},{2,0},{3,7},{4,6},{5,1},{6,4},{7,3},{8,10},{9,13},{10,... | collective-permute-start | bytes 393224 | tf_op jit(solution)/shard_map/ppermute | solution.py:387
  48.4 18.1 %collective-permute-start.23 = (bf16[3,256,256]{2,1,0:T(8,128)(2,1)S(1)}, bf16[3,256,256]{2,1,0:T(8,128)(2,1)S(1)}, u32[]{:S(2)}, u32[]{:S(2)}) collective-permute-start(bf16[3,256,256]{2,1,0:T(8,128)(2,1)S(1)} %pack_nodes.1), channel_id=1, source_target_pairs={{2,0},{0,2},{3,1},{1,3},{6,4},{4,6},{7,5},{5,7},{10,8},{8,10},{11,... | collective-permute-start | bytes 1179656 | tf_op jit(solution)/shard_map/ppermute | solution.py:534
  49.5 6.2 %collective-permute-start.20 = (bf16[256,256]{1,0:T(8,128)(2,1)S(1)}, bf16[256,256]{1,0:T(8,128)(2,1)S(1)}, u32[]{:S(2)}, u32[]{:S(2)}) collective-permute-start(bf16[256,256]{1,0:T(8,128)(2,1)S(1)} %add_whole.6.refs_0_.kept_ref), channel_id=1, source_target_pairs={{0,4},{1,9},{2,6},{3,11},{4,0},{5,13},{6,2},{7,15},{8,12},{9,1},{1... | collective-permute-start | bytes 393224 | tf_op jit(solution)/shard_map/ppermute | solution.py:387
  52.1 6.7 %collective-permute-start.19 = (bf16[256,256]{1,0:T(8,128)(2,1)S(1)}, bf16[256,256]{1,0:T(8,128)(2,1)S(1)}, u32[]{:S(2)}, u32[]{:S(2)}) collective-permute-start(bf16[256,256]{1,0:T(8,128)(2,1)S(1)} %add_whole.7.refs_0_.kept_ref.after_ref), channel_id=1, source_target_pairs={{0,4},{1,9},{2,6},{3,11},{4,0},{5,13},{6,2},{7,15},{8,12},{9,1},{1... | collective-permute-start | bytes 393224 | tf_op jit(solution)/shard_map/ppermute | solution.py:387
  55.8 5.9 %collective-permute-start.22 = (bf16[256,256]{1,0:T(8,128)(2,1)S(1)}, bf16[256,256]{1,0:T(8,128)(2,1)S(1)}, u32[]{:S(2)}, u32[]{:S(2)}) collective-permute-start(bf16[256,256]{1,0:T(8,128)(2,1)S(1)} %add_whole.8.refs_0_.kept_ref), channel_id=1, source_target_pairs={{0,8},{1,3},{2,10},{3,1},{4,12},{5,7},{6,14},{7,5},{8,0},{9,11},{1... | collective-permute-start | bytes 393224 | tf_op jit(solution)/shard_map/ppermute | solution.py:387
  58.8 7.7 %collective-permute-start.21 = (bf16[256,256]{1,0:T(8,128)(2,1)S(1)}, bf16[256,256]{1,0:T(8,128)(2,1)S(1)}, u32[]{:S(2)}, u32[]{:S(2)}) collective-permute-start(bf16[256,256]{1,0:T(8,128)(2,1)S(1)} %add_whole.9.refs_0_.kept_ref), channel_id=1, source_target_pairs={{0,8},{1,3},{2,10},{3,1},{4,12},{5,7},{6,14},{7,5},{8,0},{9,11},{1... | collective-permute-start | bytes 393224 | tf_op jit(solution)/shard_map/ppermute | solution.py:387
  68.2 5.0 %collective-permute-start.25 = (bf16[256,256]{1,0:T(8,128)(2,1)S(1)}, bf16[256,256]{1,0:T(8,128)(2,1)S(1)}, u32[]{:S(2)}, u32[]{:S(2)}) collective-permute-start(bf16[256,256]{1,0:T(8,128)(2,1)S(1)} %add_whole.10.refs_0_.mine_ref), channel_id=1, source_target_pairs={{0,2},{1,5},{2,0},{3,7},{4,6},{5,1},{6,4},{7,3},{8,10},{9,13},{10,... | collective-permute-start | bytes 393224 | tf_op jit(solution)/shard_map/ppermute | solution.py:387
  69.2 5.4 %collective-permute-start.26 = (bf16[256,256]{1,0:T(8,128)(2,1)S(1)}, bf16[256,256]{1,0:T(8,128)(2,1)S(1)}, u32[]{:S(2)}, u32[]{:S(2)}) collective-permute-start(bf16[256,256]{1,0:T(8,128)(2,1)S(1)} %add_whole.11.after_ref.mine_ref), channel_id=1, source_target_pairs={{0,2},{1,5},{2,0},{3,7},{4,6},{5,1},{6,4},{7,3},{8,10},{9,13},{10,... | collective-permute-start | bytes 393224 | tf_op jit(solution)/shard_map/ppermute | solution.py:387
  (11 other events, 55.6 us)
